TPU v7x, 32 devices: a whole 2x2x4 slice. The times are simulated.
32 devices in a mesh: seq: 2 (over x), clips: 16 (over z, y, core).
Axes of the slice: x: 2, y: 2, z: 4, core: 2. Of those that a mesh axis runs over, the one named last changes fastest.
Arguments:
- tokens: bfloat16 [2, 16384, 768], P('seq', 'clips'), may hold values from -6 to 6
- clip_class: int32 [16], P('clips'), may hold values from 0 to 1
- w_qkv: bfloat16 [768, 2304], P(('seq', 'clips')), may hold values from -0.21875 to 0.21875
- w_out: bfloat16 [768, 768], P(('seq', 'clips')), may hold values from -3.5 to 3.5
- w_up: bfloat16 [768, 3072], P(('seq', 'clips')), may hold values from -0.21875 to 0.21875
- w_down: bfloat16 [3072, 768], P(('seq', 'clips')), may hold values from -0.109375 to 0.109375
- norm_gains: bfloat16 [768, 2], P(('seq', 'clips')), may hold values from 0.5 to 1.5
- cotangent: bfloat16 [2, 16384, 768], P('seq', 'clips'), may hold values from -6 to 6
Outputs:
- output_tokens: bfloat16 [2, 16384, 768], P('seq', 'clips')
- grad_tokens: bfloat16 [2, 16384, 768], P('seq', 'clips')
- grad_w_qkv: float32 [768, 2304], P(('seq', 'clips'))
- grad_w_out: float32 [768, 768], P(('seq', 'clips'))
- grad_w_up: float32 [768, 3072], P(('seq', 'clips'))
- grad_w_down: float32 [3072, 768], P(('seq', 'clips'))
- grad_norm_gains: float32 [768, 2], P(('seq', 'clips'))
Inputs may be any that keep to these rules, and one draw needn't show every extreme that they name: `clip_class`: 0 means the group holds clips of 512 patches, 1 clips of half as many; each clip's patches are split evenly in time over the seq axis.
All inputs are finite; a program needn't handle non-finite values.
Results may differ from a plain program's by a relative error of at most 0.014.
Values may be sent and summed in bfloat16 or wider, within the bound.
No kernel may reach another device: no remote copies, remote signals or barrier semaphores. Data moves between devices by JAX's collectives and lax.ppermute only.
A program may use at most 192 MiB of HBM per device.

v0:
```python
import jax
import jax.numpy as jnp
from jax import lax
from jax.sharding import PartitionSpec as P

HEAD_DIM = 64
CLIP = 512


EPSILON = 1e-05


def norm_apply(values, scales):
    average = jnp.mean(values, axis=-1, keepdims=True)
    centered = values - average
    spread = jnp.mean(centered * centered, axis=-1, keepdims=True)
    return centered * lax.rsqrt(spread + EPSILON) * scales


def gelu_exact(values):
    return jax.nn.gelu(values, approximate=False)


def inner_rows(left, right):
    return lax.dot_general(
        left, right, (((0,), (0,)), ((), ())), preferred_element_type=jnp.float32
    )


def times_transposed(left, right):
    return lax.dot_general(
        left, right, (((1,), (1,)), ((), ())), preferred_element_type=jnp.float32
    )


def clips_per_block(clip_total, query_len):
    count = min(clip_total, max(1, 512 // query_len))
    while clip_total % count != 0:
        count = count - 1
    return count


def attention_forward(queries, keys, values, query_len, key_len):
    row_count, model_width = queries.shape
    head_count = model_width // HEAD_DIM
    score_scale = HEAD_DIM ** (-0.5)
    clip_total = row_count // query_len
    per_block = clips_per_block(clip_total, query_len)
    block_count = clip_total // per_block
    query_blocks = queries.reshape(block_count, per_block, query_len, head_count, HEAD_DIM)
    key_blocks = keys.reshape(block_count, per_block, key_len, head_count, HEAD_DIM)
    value_blocks = values.reshape(block_count, per_block, key_len, head_count, HEAD_DIM)

    def one_block(pieces):
        query_block, key_block, value_block = pieces
        scores = (
            jnp.einsum(
                "cqhe,ckhe->chqk", query_block, key_block, preferred_element_type=jnp.float32
            )
            * score_scale
        )
        top_score = jnp.max(scores, axis=-1, keepdims=True)
        raised = jnp.exp(scores - top_score)
        row_total = jnp.sum(raised, axis=-1, keepdims=True)
        soft_low = (raised / row_total).astype(jnp.bfloat16)
        mixed_heads = jnp.einsum(
            "chqk,ckhe->cqhe", soft_low, value_block, preferred_element_type=jnp.float32
        )
        log_total = (top_score[..., 0] + jnp.log(row_total[..., 0])).transpose(0, 2, 1)
        return (mixed_heads, log_total)

    mixed_blocks, log_totals = lax.map(one_block, (query_blocks, key_blocks, value_blocks))
    return (mixed_blocks.reshape(row_count, model_width), log_totals.reshape(row_count, head_count))


def attention_backward(queries, keys, values, grad_attended, log_totals, query_len, key_len):
    row_count, model_width = queries.shape
    head_count = model_width // HEAD_DIM
    score_scale = HEAD_DIM ** (-0.5)
    clip_total = row_count // query_len
    per_block = clips_per_block(clip_total, query_len)
    block_count = clip_total // per_block
    query_blocks = queries.reshape(block_count, per_block, query_len, head_count, HEAD_DIM)
    key_blocks = keys.reshape(block_count, per_block, key_len, head_count, HEAD_DIM)
    value_blocks = values.reshape(block_count, per_block, key_len, head_count, HEAD_DIM)
    grad_blocks = grad_attended.reshape(block_count, per_block, query_len, head_count, HEAD_DIM)
    total_blocks = log_totals.reshape(block_count, per_block, query_len, head_count)

    def one_block(pieces):
        query_block, key_block, value_block, grad_block, total_block = pieces
        scores = (
            jnp.einsum(
                "cqhe,ckhe->chqk", query_block, key_block, preferred_element_type=jnp.float32
            )
            * score_scale
        )
        soft_weights = jnp.exp(scores - total_block.transpose(0, 2, 1)[..., None])
        soft_low = soft_weights.astype(jnp.bfloat16)
        value_grad = jnp.einsum(
            "chqk,cqhe->ckhe", soft_low, grad_block, preferred_element_type=jnp.float32
        )
        grad_soft = jnp.einsum(
            "cqhe,ckhe->chqk", grad_block, value_block, preferred_element_type=jnp.float32
        )
        grad_scores = (
            soft_weights * (grad_soft - jnp.sum(soft_weights * grad_soft, axis=-1, keepdims=True))
        ).astype(jnp.bfloat16)
        key_grad = (
            jnp.einsum(
                "chqk,cqhe->ckhe", grad_scores, query_block, preferred_element_type=jnp.float32
            )
            * score_scale
        )
        query_grad = (
            jnp.einsum(
                "chqk,ckhe->cqhe", grad_scores, key_block, preferred_element_type=jnp.float32
            )
            * score_scale
        )
        return (query_grad, key_grad, value_grad)

    query_grads, key_grads, value_grads = lax.map(
        one_block, (query_blocks, key_blocks, value_blocks, grad_blocks, total_blocks)
    )
    key_rows = clip_total * key_len
    return (
        query_grads.reshape(row_count, model_width),
        key_grads.reshape(key_rows, model_width),
        value_grads.reshape(key_rows, model_width),
    )


def to_clips(rows, shard_count, query_len):
    width = rows.shape[1]
    clip_total = rows.shape[0] // (shard_count * query_len)
    return (
        rows.reshape(shard_count, clip_total, query_len, width)
        .transpose(1, 0, 2, 3)
        .reshape(rows.shape[0], width)
    )


def from_clips(rows, shard_count, query_len):
    width = rows.shape[1]
    clip_total = rows.shape[0] // (shard_count * query_len)
    return (
        rows.reshape(clip_total, shard_count, query_len, width)
        .transpose(1, 0, 2, 3)
        .reshape(rows.shape[0], width)
    )


def body(tokens, clip_class, w_qkv, w_out, w_up, w_down, norm_gains, cotangent):
    time_shards = lax.axis_size("seq")
    model_width = tokens.shape[2]
    token_rows = tokens[0]
    cotangent_rows = cotangent[0]
    inputs = token_rows.astype(jnp.float32)
    full_qkv, full_out, full_up, full_down, full_gains = (
        lax.all_gather(w_qkv, ("seq", "clips"), axis=0, tiled=True),
        lax.all_gather(w_out, ("seq", "clips"), axis=0, tiled=True),
        lax.all_gather(w_up, ("seq", "clips"), axis=0, tiled=True),
        lax.all_gather(w_down, ("seq", "clips"), axis=0, tiled=True),
        lax.all_gather(norm_gains, ("seq", "clips"), axis=0, tiled=True),
    )
    gains_float = full_gains.astype(jnp.float32)
    is_long = clip_class[0] == 0
    normed_first = norm_apply(inputs, gains_float[:, 0]).astype(jnp.bfloat16)
    packed = jnp.dot(normed_first, full_qkv, preferred_element_type=jnp.float32).astype(
        jnp.bfloat16
    )
    queries = packed[:, :model_width]
    keys_local = packed[:, model_width : 2 * model_width]
    values_local = packed[:, 2 * model_width :]
    keys_all, values_all = (
        lax.all_gather(keys_local, "seq", axis=0, tiled=True),
        lax.all_gather(values_local, "seq", axis=0, tiled=True),
    )

    def forward_for(query_len):

        def forward_run(query_rows, key_rows, value_rows):
            return attention_forward(
                query_rows,
                to_clips(key_rows, time_shards, query_len),
                to_clips(value_rows, time_shards, query_len),
                query_len,
                time_shards * query_len,
            )

        return forward_run

    def backward_for(query_len):

        def backward_run(query_rows, key_rows, value_rows, grad_rows, total_rows):
            query_grad, key_grad, value_grad = attention_backward(
                query_rows,
                to_clips(key_rows, time_shards, query_len),
                to_clips(value_rows, time_shards, query_len),
                grad_rows,
                total_rows,
                query_len,
                time_shards * query_len,
            )
            return (
                query_grad,
                from_clips(key_grad, time_shards, query_len),
                from_clips(value_grad, time_shards, query_len),
            )

        return backward_run

    long_len = CLIP // time_shards
    short_len = CLIP // (2 * time_shards)
    mixed_rows, log_totals = lax.cond(
        is_long, forward_for(long_len), forward_for(short_len), queries, keys_all, values_all
    )
    attended = mixed_rows.astype(jnp.bfloat16)
    hidden = inputs + jnp.dot(attended, full_out, preferred_element_type=jnp.float32)
    normed_second = norm_apply(hidden, gains_float[:, 1]).astype(jnp.bfloat16)
    up_values = jnp.dot(normed_second, full_up, preferred_element_type=jnp.float32)
    active = gelu_exact(up_values).astype(jnp.bfloat16)
    result = hidden + jnp.dot(active, full_down, preferred_element_type=jnp.float32)
    output_rows = result.astype(jnp.bfloat16)
    back_qkv, back_out, back_up, back_down, back_gains = (
        lax.all_gather(w_qkv, ("seq", "clips"), axis=0, tiled=True),
        lax.all_gather(w_out, ("seq", "clips"), axis=0, tiled=True),
        lax.all_gather(w_up, ("seq", "clips"), axis=0, tiled=True),
        lax.all_gather(w_down, ("seq", "clips"), axis=0, tiled=True),
        lax.all_gather(norm_gains, ("seq", "clips"), axis=0, tiled=True),
    )
    back_gains_float = back_gains.astype(jnp.float32)
    upstream = cotangent_rows.astype(jnp.float32)
    grad_second = upstream.astype(jnp.bfloat16)
    grad_down = inner_rows(active, grad_second)
    grad_active = times_transposed(grad_second, back_down)
    unused_active, gelu_pullback = jax.vjp(gelu_exact, up_values)
    grad_up_values = gelu_pullback(grad_active)[0].astype(jnp.bfloat16)
    grad_up = inner_rows(normed_second, grad_up_values)
    grad_normed_second = times_transposed(grad_up_values, back_up)
    unused_second, norm_pullback_second = jax.vjp(norm_apply, hidden, back_gains_float[:, 1])
    hidden_part, gain_grad_second = norm_pullback_second(grad_normed_second)
    grad_hidden = upstream + hidden_part
    grad_first = grad_hidden.astype(jnp.bfloat16)
    grad_out = inner_rows(attended, grad_first)
    grad_attended = times_transposed(grad_first, back_out).astype(jnp.bfloat16)
    query_grad, key_terms, value_terms = lax.cond(
        is_long,
        backward_for(long_len),
        backward_for(short_len),
        queries,
        keys_all,
        values_all,
        grad_attended,
        log_totals,
    )
    key_grad, value_grad = (
        lax.psum_scatter(
            key_terms.astype(jnp.bfloat16), "seq", scatter_dimension=0, tiled=True
        ).astype(jnp.float32),
        lax.psum_scatter(
            value_terms.astype(jnp.bfloat16), "seq", scatter_dimension=0, tiled=True
        ).astype(jnp.float32),
    )
    grad_packed = jnp.concatenate([query_grad, key_grad, value_grad], axis=1).astype(jnp.bfloat16)
    grad_qkv = inner_rows(normed_first, grad_packed)
    grad_normed_first = times_transposed(grad_packed, back_qkv)
    unused_first, norm_pullback_first = jax.vjp(norm_apply, inputs, back_gains_float[:, 0])
    input_part, gain_grad_first = norm_pullback_first(grad_normed_first)
    grad_rows = (grad_hidden + input_part).astype(jnp.bfloat16)
    grad_gains = jnp.stack([gain_grad_first, gain_grad_second], axis=1)
    owned_qkv, owned_out, owned_up, owned_down, owned_gains = (
        lax.psum_scatter(grad_qkv, ("seq", "clips"), scatter_dimension=0, tiled=True),
        lax.psum_scatter(grad_out, ("seq", "clips"), scatter_dimension=0, tiled=True),
        lax.psum_scatter(grad_up, ("seq", "clips"), scatter_dimension=0, tiled=True),
        lax.psum_scatter(grad_down, ("seq", "clips"), scatter_dimension=0, tiled=True),
        lax.psum_scatter(grad_gains, ("seq", "clips"), scatter_dimension=0, tiled=True),
    )
    output_tokens = output_rows[None]
    grad_tokens = grad_rows[None]
    return (output_tokens, grad_tokens, owned_qkv, owned_out, owned_up, owned_down, owned_gains)


def solution(mesh):
    return jax.shard_map(
        body,
        mesh=mesh,
        in_specs=(
            P("seq", "clips", None),
            P("clips"),
            P(("seq", "clips"), None),
            P(("seq", "clips"), None),
            P(("seq", "clips"), None),
            P(("seq", "clips"), None),
            P(("seq", "clips"), None),
            P("seq", "clips", None),
        ),
        out_specs=(
            P("seq", "clips", None),
            P("seq", "clips", None),
            P(("seq", "clips"), None),
            P(("seq", "clips"), None),
            P(("seq", "clips"), None),
            P(("seq", "clips"), None),
            P(("seq", "clips"), None),
        ),
        check_vma=False,
    )
```

profile of v0, /device:TPU:0, one launch (start us, length us, event | category | flops | bytes accessed | tf_op | source)
XLA Modules:
  0.0 1130.5 jit_solution(15051737498739773418)
XLA Ops:
  7.9 43.3 %all-gather = bf16[32,24,2]{1,2,0:T(2,128)(2,1)S(1)} all-gather(bf16[1,24,2]{1,2,0:T(2,128)(2,1)} %bitcast.377), channel_id=1, replica_groups=mesh['seq'=2,'clips'=16] {'seq','clips'}, dimensions={0}, use_global_device_ids=true | all-gather | bytes 3168 | tf_op jit(solution)/shard_map/all_gather | solution.py:164
  55.2 18.6 %all-gather.8.cloned.1.call-done = bf16[768,2304]{1,0:T(8,128)(2,1)} async-done(((bf16[24,2304]{1,0:T(8,128)(2,1)}), bf16[768,2304]{1,0:T(8,128)(2,1)}) %all-gather.8.cloned.1.call-update) | async-done | bytes 3538960 | tf_op jit(solution)/shard_map/all_gather | solution.py:160
  73.8 6.3 convolution_convert_fusion
  87.3 39.1 %all-gather.12.cloned.1.call-done = bf16[2048,768]{1,0:T(8,128)(2,1)} async-done(((bf16[1024,768]{1,0:T(8,128)(2,1)}), bf16[2048,768]{1,0:T(8,128)(2,1)}) %all-gather.12.cloned.1.call-update) | async-done | bytes 3145744 | tf_op jit(solution)/shard_map/all_gather | solution.py:177
  126.3 47.1 %all-gather.10.cloned.1.call-done = bf16[2048,768]{1,0:T(8,128)(2,1)} async-done(((bf16[1024,768]{1,0:T(8,128)(2,1)}), bf16[2048,768]{1,0:T(8,128)(2,1)}) %all-gather.10.cloned.1.call-update) | async-done | bytes 3145744 | tf_op jit(solution)/shard_map/all_gather | solution.py:176
  173.4 63.3 %conditional.4 = (f32[1024,12]{1,0:T(8,128)S(1)}, bf16[1024,768]{0,1:T(8,128)(2,1)}) conditional(s32[]{:T(128)} %bitcast.67, (bf16[1024,768]{1,0:T(8,128)(2,1)}, bf16[2048,768]{1,0:T(8,128)(2,1)}, bf16[2048,768]{1,0:T(8,128)(2,1)}) %tuple.50, (bf16[1024,768]{1,0:T(8,128)(2,1)}, bf16[2048,768]{1,0:T(8,128)(2,1)}, bf16[2048,768]{1,0:T(8,128)(2,1)}) %tuple.50), branch_computations={%region_2.7_spmd, %region_7.12_spmd} | conditional | flops 833611776 | bytes 139535696
  173.6 8.7 copy.129
  182.3 6.1 reshape.169
  188.5 5.5 copy.130
  194.0 6.1 reshape.172
  201.8 4.0 reshape.170
  205.7 25.4 %while.49 = (s32[]{:T(128)}, bf16[2,2,256,12,64]{2,4,3,1,0:T(8,128)(2,1)}, f32[2,2,256,12]{2,3,1,0:T(8,128)S(1)}, bf16[2,2,512,12,64]{2,4,3,1,0:T(8,128)(2,1)}, ...) while((s32[]{:T(128)}, ...), condition=%wide.region_11.11_spmd, body=%wide.region_8.10_spmd.sunk | while | flops 833611776 | bytes 70231216 | solution.py:72
  209.5 3.1 fusion.156
  212.6 4.7 bitcast_dynamic-update-slice_fusion.26
  222.2 3.1 fusion.156
  225.3 4.7 bitcast_dynamic-update-slice_fusion.26
  231.4 3.0 copy.133
  237.6 3.7 fusion.103
  241.8 53.9 %all-gather.16.cloned.1.call-done = bf16[768,3072]{1,0:T(8,128)(2,1)} async-done(((bf16[24,3072]{1,0:T(8,128)(2,1)}), bf16[768,3072]{1,0:T(8,128)(2,1)}) %all-gather.16.cloned.1.call-update) | async-done | bytes 4718608 | tf_op jit(solution)/shard_map/all_gather | solution.py:162
  295.7 37.2 %multiply_convert_fusion.2 = (bf16[1024,3072]{1,0:T(8,128)(2,1)}, f32[1024,3072]{1,0:T(8,128)}, f32[1024,3072]{1,0:T(8,128)}) fusion(bf16[768,3072]{1,0:T(8,128)(2,1)} %all-gather.16.cloned.1.call-done, f32[1024,768]{0,1:T(8,128)S(1)} %get-tuple-element.501, f32[768]{0:T(1024)S(1)} %copy-done.52, f32[1024]{0:T(1024)S(1)} %fusion.97, ...), kind=kOutput, calls=%fused_computation.93 | convolution fusion | flops 5039456256 | bytes 39332864 | tf_op jit(solution)/shard_map/dot_general | solution.py:221
  332.9 28.0 %all-gather.18.cloned.1.call-done = bf16[3072,768]{1,0:T(8,128)(2,1)} async-done(((bf16[96,768]{1,0:T(8,128)(2,1)}), bf16[3072,768]{1,0:T(8,128)(2,1)}) %all-gather.18.cloned.1.call-update) | async-done | bytes 4718608 | tf_op jit(solution)/shard_map/all_gather | solution.py:163
  360.8 17.5 %add_convert_fusion = bf16[1024,3072]{1,0:T(8,128)(2,1)} fusion(f32[1024,3072]{1,0:T(8,128)} %get-tuple-element.484, f32[1024,3072]{1,0:T(8,128)} %get-tuple-element.502, bf16[3072,768]{1,0:T(8,128)(2,1)} %all-gather.18.cloned.1.call-done, bf16[1,1024,768]{2,1,0:T(8,128)(2,1)} %param.27), kind=kOutput, calls=%fused_computation.92 | convolution fusion | flops 4875878400 | bytes 37748736 | tf_op jit(solution)/shard_map/dot_general | solution.py:31
  378.3 8.7 multiply_reduce_fusion.4
  390.3 2.6 convolution_convert_fusion.1
  392.9 124.5 %conditional.10 = (bf16[2048,768]{1,0:T(8,128)(2,1)}, bf16[2048,768]{1,0:T(8,128)(2,1)S(1)}, bf16[1024,768]{0,1:T(8,128)(2,1)}) conditional(s32[]{:T(128)} %bitcast.67, (bf16[1024,768]{1,0:T(8,128)(2,1)}, bf16[2048,768]{1,0:T(8,128)(2,1)}, bf16[2048,768]{1,0:T(8,128)(2,1)S(1)}, bf16[1024,768]{1,0:T(8,128)(2,1)}, f32[1024,12]{1,0:T(8,128)}) %tuple.192, ...), branch_computations={%region_16.20_spmd, %region_20.24_spmd} | conditional | flops 2052188160 | bytes 245646752 | solution.py:247
  394.3 2.6 copy.161
  396.9 3.9 reshape.191
  403.3 3.8 reshape.189
  407.2 5.5 copy.143
  412.7 6.2 reshape.193
  418.9 5.5 copy.142
  424.4 4.6 reshape.188
  429.0 53.3 %while.51 = (s32[]{:T(128)}, bf16[2,2,256,12,64]{2,4,3,1,0:T(8,128)(2,1)}, bf16[2,2,512,12,64]{2,4,3,1,0:T(8,128)(2,1)}, bf16[2,2,512,12,64]{2,4,3,1,0:T(8,128)(...) while((s32[]{:T(128)}, ...), condition=%wide.region_23.23_spmd, body=%wide.region_21.22_spmd.sunk | while | flops 2052188160 | bytes 163759392 | solution.py:122
  429.0 2.7 constant_dynamic-slice_fusion.11
  433.5 3.5 bitcast_dynamic-update-slice_fusion.22
  437.1 7.0 multiply_reduce_fusion.11
  444.1 6.7 multiply_convert_fusion.8
  455.7 2.7 constant_dynamic-slice_fusion.11
  460.2 3.5 bitcast_dynamic-update-slice_fusion.22
  463.7 7.0 multiply_reduce_fusion.11
  470.7 6.7 multiply_convert_fusion.8
  482.3 5.5 reshape.197
  487.8 6.9 copy.148
  494.8 4.2 copy.149
  499.0 3.8 reshape.202
  502.8 5.5 reshape.195
  508.3 8.7 copy.147
  517.3 4.8 copy.163
  522.2 2.9 copy.164
  525.3 5.1 fusion.104
  530.6 10.4 fusion.98
  542.4 10.2 fusion.88
  555.2 9.3 reduce-scatter.8.cloned.1.call-done
  564.5 2.7 constant_dynamic-update-slice_fusion.1
  567.2 43.1 %reduce-scatter.10.cloned.1.call-done = bf16[1024,768]{0,1:T(8,128)(2,1)} async-done(((bf16[2048,768]{0,1:T(8,128)(2,1)}), bf16[1024,768]{0,1:T(8,128)(2,1)}) %reduce-scatter.10.cloned.1.call-update) | async-done | bytes 1572880 | tf_op jit(solution)/shard_map/reduce_scatter | solution.py:261
  610.2 2.7 constant_dynamic-update-slice_fusion
  613.0 8.5 fusion.93
  622.1 9.2 fusion.91
  633.0 6.9 fusion.85
  645.5 39.6 %all-reduce = f32[768,2]{0,1:T(2,128)S(1)} all-reduce(f32[768,2]{0,1:T(2,128)S(1)} %pad_maximum_fusion), channel_id=8, replica_groups=mesh['seq'=2,'clips'=16] {'seq','clips'}, use_global_device_ids=true, to_apply=%region_34.35.clone | all-reduce | flops 1536 | bytes 12288
  685.7 29.6 %reduce-scatter.14.cloned.1.call-done = f32[24,768]{1,0:T(8,128)} async-done(((f32[768,768]{1,0:T(8,128)}), f32[24,768]{1,0:T(8,128)}) %reduce-scatter.14.cloned.1.call-update) | async-done | bytes 73744 | tf_op jit(solution)/shard_map/reduce_scatter | solution.py:274
  715.3 142.0 %reduce-scatter.16.cloned.1.call-done = f32[24,3072]{1,0:T(8,128)} async-done(((f32[768,3072]{1,0:T(8,128)}), f32[24,3072]{1,0:T(8,128)}) %reduce-scatter.16.cloned.1.call-update) | async-done | bytes 294928 | tf_op jit(solution)/shard_map/reduce_scatter | solution.py:275
  857.2 141.2 %reduce-scatter.18.cloned.1.call-done = f32[96,768]{1,0:T(8,128)} async-done(((f32[3072,768]{1,0:T(8,128)}), f32[96,768]{1,0:T(8,128)}) %reduce-scatter.18.cloned.1.call-update) | async-done | bytes 294928 | tf_op jit(solution)/shard_map/reduce_scatter | solution.py:276
  998.4 125.1 %reduce-scatter.12.cloned.1.call-done = f32[24,2304]{1,0:T(8,128)} async-done(((f32[768,2304]{1,0:T(8,128)}), f32[24,2304]{1,0:T(8,128)}) %reduce-scatter.12.cloned.1.call-update) | async-done | bytes 221200 | tf_op jit(solution)/shard_map/reduce_scatter | solution.py:273
  (184 shorter events, 59.6 us)
Async XLA Ops:
  7.2 66.6 %all-gather.8.cloned.1.call-start = ((), (), s32[]{:S(2)}) async-start(), calls=%async_computation.6 | async-start | bytes 3649536 | tf_op jit(solution)/shard_map/all_gather | solution.py:160
  7.9 118.4 %all-gather.12.cloned.1.call-start = ((), (), s32[]{:S(2)}) async-start(), calls=%async_computation.8 | async-start | bytes 4718592 | tf_op jit(solution)/shard_map/all_gather | solution.py:177
  53.2 26.9 %copy-start.5 = (bf16[1,1024,768]{1,2,0:T(8,128)(2,1)}, bf16[1,1024,768]{1,2,0:T(8,128)(2,1)S(1)}, u32[]{:S(2)}) copy-start(bf16[1,1024,768]{1,2,0:T(8,128)(2,1)S(1)} %copy.150) | copy-start | bytes 4718596
  53.9 26.3 %copy-start.42 = (f32[768]{0:T(1024)}, f32[768]{0:T(1024)S(1)}, u32[]{:S(2)}) copy-start(f32[768]{0:T(1024)S(1)} %get-tuple-element.420) | copy-start | bytes 9220
  54.2 26.0 %copy-start.40 = (f32[1024]{0:T(1024)}, f32[1024]{0:T(1024)S(1)}, u32[]{:S(2)}) copy-start(f32[1024]{0:T(1024)S(1)} %broadcast_multiply_fusion.1) | copy-start | bytes 12292
  55.2 24.9 %copy-start.44 = (f32[1024]{0:T(1024)}, f32[1024]{0:T(1024)S(1)}, u32[]{:S(2)}) copy-start(f32[1024]{0:T(1024)S(1)} %fusion.96) | copy-start | bytes 12292
  82.4 3.2 copy-start.29
  82.5 91.0 %all-gather.10.cloned.1.call-start = ((), (), s32[]{:S(2)}) async-start(), calls=%async_computation.7 | async-start | bytes 4718592 | tf_op jit(solution)/shard_map/all_gather | solution.py:176
  83.2 153.5 %all-gather.14.cloned.1.call-start = ((), (), s32[]{:S(2)}) async-start(), calls=%async_computation.9 | async-start | bytes 1216512 | tf_op jit(solution)/shard_map/all_gather | solution.py:161
  83.8 211.9 %all-gather.16.cloned.1.call-start = ((), (), s32[]{:S(2)}) async-start(), calls=%async_computation.10 | async-start | bytes 4866048 | tf_op jit(solution)/shard_map/all_gather | solution.py:162
  84.4 276.4 %all-gather.18.cloned.1.call-start = ((), (), s32[]{:S(2)}) async-start(), calls=%async_computation.11 | async-start | bytes 4866048 | tf_op jit(solution)/shard_map/all_gather | solution.py:163
  84.9 479.6 %reduce-scatter.8.cloned.1.call-start = ((), (), s32[]{:S(2)}) async-start(), calls=%async_computation.12 | async-start | bytes 4718592 | tf_op jit(solution)/shard_map/reduce_scatter | solution.py:258
  182.3 6.1 copy-start.2
  194.0 6.1 copy-start.8
  201.7 4.0 copy-start.11
  209.5 3.1 copy-start.22
  209.5 3.1 copy-start.37
  217.3 1.1 copy-start.38
  222.2 3.1 copy-start.22
  222.2 3.1 copy-start.37
  230.0 1.1 copy-start.38
  236.7 0.8 copy-start.20
  241.3 145.6 %copy-start.17 = (f32[1024,768]{0,1:T(8,128)}, f32[1024,768]{0,1:T(8,128)S(1)}, u32[]{:S(2)}) copy-start(f32[1024,768]{0,1:T(8,128)S(1)} %get-tuple-element.501) | copy-start | bytes 9437188
  241.3 54.3 %copy-start.52 = (f32[768]{0:T(1024)S(1)}, f32[768]{0:T(1024)}, u32[]{:S(2)}) copy-start(f32[768]{0:T(1024)} %get-tuple-element.419) | copy-start | bytes 9220
  241.4 145.6 %copy-start.46 = (f32[1024]{0:T(1024)}, f32[1024]{0:T(1024)S(1)}, u32[]{:S(2)}) copy-start(f32[1024]{0:T(1024)S(1)} %broadcast_multiply_fusion) | copy-start | bytes 12292
  241.8 145.2 %copy-start.54 = (f32[1024]{0:T(1024)}, f32[1024]{0:T(1024)S(1)}, u32[]{:S(2)}) copy-start(f32[1024]{0:T(1024)S(1)} %fusion.97) | copy-start | bytes 12292
  360.8 17.5 %copy-start.57 = (bf16[768,3072]{1,0:T(8,128)(2,1)S(1)}, bf16[768,3072]{1,0:T(8,128)(2,1)}, u32[]{:S(2)}) copy-start(bf16[768,3072]{1,0:T(8,128)(2,1)} %all-gather.16.cloned.1.call-done) | copy-start | bytes 14155780
  387.0 1.4 copy-start.15
  387.9 1.7 copy-start.13
  387.9 1.7 copy-start.50
  388.4 1.9 copy-start.58
  390.3 2.6 copy-start.39
  390.3 2.6 copy-start
  412.7 6.2 copy-start.4
  433.5 3.5 copy-start.10
  444.0 6.7 copy-start.33
  450.8 2.1 copy-start.27
  452.8 1.2 copy-start.34
  454.0 1.7 copy-start.28
  460.2 3.5 copy-start.10
  470.7 6.7 copy-start.33
  477.4 2.1 copy-start.27
  479.5 1.2 copy-start.34
  480.6 1.7 copy-start.28
  522.2 88.1 %reduce-scatter.10.cloned.1.call-start = ((), (), s32[]{:S(2)}) async-start(), calls=%async_computation.13 | async-start | bytes 4718592 | tf_op jit(solution)/shard_map/reduce_scatter | solution.py:261
  525.2 5.3 copy-start.18
  525.2 5.3 copy-start.47
  525.2 5.3 copy-start.53
  525.2 5.3 copy-start.55
  525.2 190.0 %reduce-scatter.14.cloned.1.call-start = ((), (), s32[]{:S(2)}) async-start(), calls=%async_computation.15 | async-start | bytes 2433024 | tf_op jit(solution)/shard_map/reduce_scatter | solution.py:274
  530.5 326.8 %reduce-scatter.16.cloned.1.call-start = ((), (), s32[]{:S(2)}) async-start(), calls=%async_computation.16 | async-start | bytes 9732096 | tf_op jit(solution)/shard_map/reduce_scatter | solution.py:275
  541.0 1.4 copy-start.30
  541.0 457.4 %reduce-scatter.18.cloned.1.call-start = ((), (), s32[]{:S(2)}) async-start(), calls=%async_computation.17 | async-start | bytes 9732096 | tf_op jit(solution)/shard_map/reduce_scatter | solution.py:276
  552.6 1.4 copy-start.19
  552.6 570.9 %reduce-scatter.12.cloned.1.call-start = ((), (), s32[]{:S(2)}) async-start(), calls=%async_computation.14 | async-start | bytes 7299072 | tf_op jit(solution)/shard_map/reduce_scatter | solution.py:273
  555.2 57.7 %copy-start.6 = (bf16[1,1024,768]{1,2,0:T(8,128)(2,1)S(1)}, bf16[1,1024,768]{1,2,0:T(8,128)(2,1)}, u32[]{:S(2)}) copy-start(bf16[1,1024,768]{1,2,0:T(8,128)(2,1)} %copy-done.5) | copy-start | bytes 4718596
  555.2 57.7 %copy-start.41 = (f32[1024]{0:T(1024)S(1)}, f32[1024]{0:T(1024)}, u32[]{:S(2)}) copy-start(f32[1024]{0:T(1024)} %copy-done.40) | copy-start | bytes 12292
  555.2 57.7 %copy-start.43 = (f32[768]{0:T(1024)S(1)}, f32[768]{0:T(1024)}, u32[]{:S(2)}) copy-start(f32[768]{0:T(1024)} %copy-done.42) | copy-start | bytes 9220
  555.2 57.7 %copy-start.45 = (f32[1024]{0:T(1024)S(1)}, f32[1024]{0:T(1024)}, u32[]{:S(2)}) copy-start(f32[1024]{0:T(1024)} %copy-done.44) | copy-start | bytes 12292
  621.5 0.7 copy-start.56
  633.0 6.9 copy-start.49
  639.9 1.9 copy-start.14
  639.9 2.4 copy-start.16
  639.9 2.4 copy-start.51
  (1 other events, 0.6 us)
Sparse Core Ops, SparseCore 0:
  10.9 62.8 all-gather.7
  82.6 43.7 all-gather.11
  128.5 44.9 all-gather.9
  176.2 54.1 all-gather.13
  233.1 62.5 all-gather.15
  298.4 62.3 all-gather.17
  522.3 42.1 reduce-scatter.7
  566.8 43.3 reduce-scatter.9
  616.1 99.1 reduce-scatter.13
  722.6 134.6 reduce-scatter.15
  863.7 134.6 reduce-scatter.17
  1005.5 117.9 reduce-scatter.11
where the time goes:
time: 1140 us; the launch traced here: 1130 us
  waiting for transfers between devices  680 us (60%)
  matrix products  171 us (15%)
  local copies, waits for them, and re-layouts  155 us (14%)
  blocking collectives  82.8 us (7%)
  other arithmetic  25.2 us (2%)
  between operations  15.4 us (1%)
    reduce_scatter x1, waiting for transfers between devices, body(): lax.psum_scatter(grad_up, ('seq', 'clips'), scatter_dimension=0, tiled=True)  142 us
    reduce_scatter x1, waiting for transfers between devices, body(): lax.psum_scatter(grad_down, ('seq', 'clips'), scatter_dimension=0, tiled=...  141 us
    reduce_scatter x1, waiting for transfers between devices, body(): lax.psum_scatter(grad_qkv, ('seq', 'clips'), scatter_dimension=0, tiled=T...  125 us
    all_gather x1, waiting for transfers between devices, body(): lax.all_gather(w_up, ('seq', 'clips'), axis=0, tiled=True)  53.9 us
    all_gather x1, waiting for transfers between devices, body(): lax.all_gather(keys_local, 'seq', axis=0, tiled=True)  47.1 us
    all_gather x1, blocking collectives, body(): lax.all_gather(norm_gains, ('seq', 'clips'), axis=0, tiled=True)  43.3 us
    reduce_scatter x1, waiting for transfers between devices, body(): lax.psum_scatter(value_terms.astype(jnp.bfloat16), 'seq', scatter_dimensi...  43.1 us
    unnamed x1, blocking collectives  39.6 us
  transfers between devices with their start and end apart: 12, of which 11 were waited for; matrix products, arithmetic and copies ran while one was open for 15% of the time, Pallas kernels for 0%

commit v1 on v0

v1 whole, which is shorter than its diff:
```python
import functools

import jax
import jax.numpy as jnp
from jax import lax
from jax.experimental import pallas as pl
from jax.experimental.pallas import tpu as pltpu
from jax.sharding import PartitionSpec as P

HEAD_DIM = 64
CLIP = 512
EPSILON = 1e-05
AXES = ("seq", "clips")
LOG2E = 1.4426950408889634
SCORE_SCALE = HEAD_DIM ** (-0.5)
BF16 = jnp.bfloat16
F32 = jnp.float32
VMEM_BYTES = 58 * 1024 * 1024


class Grid:
    def __init__(self, seq, clips):
        self.nx = seq
        self.clips = clips
        pairs = clips // 2
        bits = pairs.bit_length() - 1
        self.ny = 2 ** (bits // 3)
        self.nz = pairs // self.ny
        self.sizes = {"x": self.nx, "y": self.ny, "z": self.nz}
        self.chips = self.nx * self.ny * self.nz

    def index(self, x, z, y, c):
        return x * self.clips + (z * self.ny + y) * 2 + c

    def shift(self, axis, k):
        pairs = []
        for x in range(self.nx):
            for z in range(self.nz):
                for y in range(self.ny):
                    for c in range(2):
                        t = {"x": x, "y": y, "z": z}
                        t[axis] = (t[axis] + k) % self.sizes[axis]
                        pairs.append((self.index(x, z, y, c), self.index(t["x"], t["z"], t["y"], c)))
        return pairs

    def core_swap(self):
        return [(i, i ^ 1) for i in range(self.nx * self.clips)]

    def here(self):
        x = lax.axis_index("seq")
        rest = lax.axis_index("clips")
        return {"x": x, "z": rest // (2 * self.ny), "y": (rest // 2) % self.ny, "c": rest % 2}


def rel_of(grid, coords):
    return (coords["x"] * grid.ny + coords["y"]) * grid.nz + coords["z"]


def after(value, *earlier):
    return lax.optimization_barrier((value,) + earlier)[0]


def exchange(grid, parts, axis):
    moved = []
    for k in range(1, grid.sizes[axis]):
        for array, spots in parts:
            moved.append((lax.ppermute(array, AXES, grid.shift(axis, k)), [{**s, axis: k} for s in spots]))
    return moved


def joined_parts(parts):
    if len(parts) == 1:
        return parts[0]
    return (jnp.concatenate([a for a, _ in parts], axis=0), [s for _, spots in parts for s in spots])


def gather_along_z(grid, piece):
    parts = [(piece[None], [{"x": 0, "y": 0, "z": 0}])]
    parts = parts + exchange(grid, parts, "z")
    cut = max(1, (3 * len(parts)) // 4)
    return joined_parts(parts[:cut]), joined_parts(parts[cut:])


def scatter_sum(grid, mine, other):
    got = lax.ppermute(other, AXES, grid.core_swap())
    shape = (grid.ny, grid.nx, grid.nz) + mine.shape[1:]
    mine, got = mine.reshape(shape), got.reshape(shape)
    cut = max(1, (3 * grid.nz) // 4)
    kept = []
    for lo, hi, first in ((0, cut, "y"), (cut, grid.nz, "x")):
        second = "x" if first == "y" else "y"
        current = [mine[:, :, lo:hi], got[:, :, lo:hi]]
        for axis in (first, second):
            dim = 0 if axis == "y" else 1 - (first == "y")
            pieces = [
                [lax.index_in_dim(c, k, dim, keepdims=False) for c in current] for k in range(grid.sizes[axis])
            ]
            received = [
                lax.ppermute(add_all(pieces[k]).astype(BF16), AXES, grid.shift(axis, k))
                for k in range(1, grid.sizes[axis])
            ]
            current = pieces[0] + received
        kept.append(current)
    final = []
    for k in range(grid.nz):
        group = kept[0] if k < cut else kept[1]
        at = k if k < cut else k - cut
        total = add_all([c[at] for c in group])
        final.append(total if k == 0 else lax.ppermute(total.astype(BF16), AXES, grid.shift("z", k)))
    return add_all(final)


def add_all(items):
    total = items[0].astype(F32)
    for item in items[1:]:
        total = total + item.astype(F32)
    return total


def nn(a, b):
    return lax.dot_general(a, b, (((1,), (0,)), ((), ())), preferred_element_type=F32)


def nt(a, b):
    return lax.dot_general(a, b, (((1,), (1,)), ((), ())), preferred_element_type=F32)


def tn(a, b):
    return lax.dot_general(a, b, (((0,), (0,)), ((), ())), preferred_element_type=F32)


def normalized(values):
    centered = values - jnp.mean(values, axis=-1, keepdims=True)
    spread = jnp.mean(centered * centered, axis=-1, keepdims=True)
    root = lax.rsqrt(spread + EPSILON)
    return centered * root, root


def norm_back(z, root, scaled):
    return root * (
        scaled
        - jnp.mean(scaled, axis=-1, keepdims=True)
        - z * jnp.mean(scaled * z, axis=-1, keepdims=True)
    )


class Pieces:
    def __init__(self, chips, mine, theirs, fields):
        self.chips = chips
        self.arrays = [a for a, _ in mine] + [a for a, _ in theirs]
        self.spots = [s for _, s in mine] + [s for _, s in theirs]
        self.count_mine = len(mine)
        self.rows = self.arrays[0].shape[1]
        self.fields = fields

    def copies(self, wanted):
        total = 0
        for n, spots in enumerate(self.spots):
            for name, column, width, gain in self.fields:
                if name in wanted and not (gain and n >= self.count_mine):
                    total += len(spots)
        return total

    def start(self, refs, tab, wanted, sems, first):
        core = tab[2 * self.chips]
        started = {name: [] for name in wanted}
        n_sem = first
        for n, spots in enumerate(self.spots):
            for name, column, width, gain in self.fields:
                if name not in wanted or (gain and n >= self.count_mine):
                    continue
                for k, r in enumerate(spots):
                    row = pl.multiple_of(tab[r] * self.rows, 16)
                    if gain:
                        place = wanted[name].at[pl.ds(row, self.rows), :]
                    else:
                        side = core if n < self.count_mine else 1 - core
                        col = pl.multiple_of(side * width, 128)
                        place = wanted[name].at[pl.ds(row, self.rows), pl.ds(col, width)]
                    copy = pltpu.make_async_copy(
                        refs[n].at[k, :, column : column + width], place, sems.at[n_sem]
                    )
                    copy.start()
                    started[name].append(copy)
                    n_sem += 1
        return started


def wait_all(copies):
    for copy in copies:
        copy.wait()


def emit(value, side, first_chip, rows, mine, other, columns, tab, chips):
    rel = side ^ tab[2 * chips]
    height = value.shape[0]
    low = value.astype(BF16)

    def put(ref):
        if rows >= height:
            ref[0, pl.ds(first_chip, height), columns] = low
        else:
            for a in range(height // rows):
                ref[tab[chips + first_chip + a], :, columns] = low[a * rows : (a + 1) * rows]

    @pl.when(rel == 0)
    def _():
        put(mine)

    @pl.when(rel != 0)
    def _():
        put(other)


def place_of(row, rows, chips):
    return row if chips == 1 else row // rows


def input_kernel(pieces, n_refs, chips, tab, own, got, *refs):
    sources, refs = refs[:n_refs], refs[n_refs:]
    packed, normed, gains, w_qkv, gain_cols, sems = refs
    i = pl.program_id(0)
    steps = pl.num_programs(0)
    width = own.shape[1]

    @pl.when(i == 0)
    def _():
        started = pieces.start(sources, tab, {"gain": gain_cols, "qkv": w_qkv}, sems, 0)
        wait_all(started["gain"])
        pick = (
            lax.broadcasted_iota(jnp.int32, (8, 128), 0) == lax.broadcasted_iota(jnp.int32, (8, 128), 1)
        ).astype(BF16)
        gains[...] = nt(pick, gain_cols[...])
        wait_all(started["qkv"])

    x = jnp.where(i < steps // 2, own[...], got[...]).astype(F32)
    z, _ = normalized(x)
    low = (z * gains[0:1, :]).astype(BF16)
    normed[...] = low
    for c in range(3):
        cols = slice(c * width, (c + 1) * width)
        packed[:, cols] = nn(low, w_qkv[:, cols]).astype(BF16)


def pair_of(ref, n):
    return ref[:, 0, :, 128 * n : 128 * (n + 1)].reshape(512, 128)


def fill_bias(bias, short):
    row_clip = (lax.broadcasted_iota(jnp.int32, (512, 512), 0) // 128) % 2
    col_clip = (lax.broadcasted_iota(jnp.int32, (512, 512), 1) // 128) % 2
    apart = jnp.logical_and(row_clip != col_clip, short != 0)
    bias[...] = jnp.where(apart, -1e30, 0.0)


def attend_kernel(chips, tab, q_ref, k_ref, v_ref, attended, log_totals, bias):
    @pl.when(jnp.logical_and(pl.program_id(0) == 0, pl.program_id(1) == 0))
    def _():
        fill_bias(bias, tab[2 * chips + 1])

    lane = lax.broadcasted_iota(jnp.int32, (512, 128), 1)
    for n in range(2):
        q, k, v = pair_of(q_ref, n), pair_of(k_ref, n), pair_of(v_ref, n)
        v_t = v.T
        mixed = []
        for h in range(2):
            k_h = jnp.where((lane // 64) == h, k, jnp.zeros_like(k))
            s = nt(k_h, q) * (SCORE_SCALE * LOG2E) + bias[...]
            top_score = jnp.max(s, axis=0, keepdims=True)
            p = jnp.exp2(s - top_score)
            total = jnp.sum(p, axis=0, keepdims=True)
            mixed.append(nn(v_t[64 * h : 64 * h + 64, :], p.astype(BF16)) * (1.0 / total))
            log_totals[2 * n + h] = top_score + jnp.log2(total)
        out = jnp.concatenate(mixed, axis=0).T.astype(BF16)
        attended[:, 0, :, 128 * n : 128 * (n + 1)] = out.reshape(2, 256, 128)


ERF_P = 0.3275911 * (0.5**0.5)
ERF_A = (0.254829592 * 0.5, -0.284496736 * 0.5, 1.421413741 * 0.5, -1.453152027 * 0.5, 1.061405429 * 0.5)


def gelu_both(u):
    t = 1.0 / (1.0 + ERF_P * jnp.abs(u))
    bell = jnp.exp2(u * u * (-0.5 * LOG2E))
    poly = t * (ERF_A[0] + t * (ERF_A[1] + t * (ERF_A[2] + t * (ERF_A[3] + t * ERF_A[4]))))
    tail = poly * bell
    below = jnp.where(u < 0, tail, 1.0 - tail)
    return u * below, below + u * (bell * 0.3989422804014327)


def middle_kernel(pieces, n_refs, chips, tab, attended, own, got, gains, *refs):
    sources, refs = refs[:n_refs], refs[n_refs:]
    hidden, normed, w_out, sems = refs
    i = pl.program_id(0)

    @pl.when(i == 0)
    def _():
        wait_all(pieces.start(sources, tab, {"out": w_out}, sems, 0)["out"])

    x = jnp.where(i < pl.num_programs(0) // 2, own[...], got[...]).astype(F32)
    h = x + nn(attended[...], w_out[...])
    hidden[...] = h
    z, _ = normalized(h)
    normed[...] = (z * gains[1:2, :]).astype(BF16)


def up_kernel(pieces, n_refs, chips, rows_down, tab, normed, cot_own, cot_got, *refs):
    sources, refs = refs[:n_refs], refs[n_refs:]
    active, slope, down_mine, down_other, w_up, sems = refs
    half, width = cot_own.shape
    j = pl.program_id(0)

    @pl.when(j == 0)
    def _():
        wait_all(pieces.start(sources, tab, {"up": w_up}, sems, 0)["up"])

    cols = pl.ds(pl.multiple_of(j * width, 128), width)

    @pl.loop(0, 2 * half // 256)
    def _(i):
        rows = pl.ds(pl.multiple_of(i * 256, 256), 256)
        a, s = gelu_both(nn(normed[rows, :], w_up[:, cols]))
        active[rows, :] = a.astype(BF16)
        slope[rows, :] = s.astype(BF16)

    for m in range(2):
        piece = slice(384 * m, 384 * (m + 1))
        grad = tn(active[:half, piece], cot_own[...]) + tn(active[half:, piece], cot_got[...])
        start = place_of(width * j + 384 * m, rows_down, chips)
        emit(grad[:, : width // 2], 0, start, rows_down, down_mine, down_other, slice(None), tab, chips)
        emit(grad[:, width // 2 :], 1, start, rows_down, down_mine, down_other, slice(None), tab, chips)


def down_back_kernel(pieces, n_refs, chips, rows_up, tab, cot_own, cot_got, normed, slope, *refs):
    sources, refs = refs[:n_refs], refs[n_refs:]
    grad_up, up_mine, up_other, w_down, sems = refs
    half, width = cot_own.shape
    j = pl.program_id(0)
    steps = pl.num_programs(0)

    @pl.when(j == 0)
    def _():
        wait_all(pieces.start(sources, tab, {"down": w_down}, sems, 0)["down"])

    w_rows = pl.ds(pl.multiple_of(j * width, 256), width)
    for part, cot in enumerate((cot_own, cot_got)):
        @pl.loop(0, half // 256)
        def _(i):
            inner = pl.ds(pl.multiple_of(i * 256, 256), 256)
            rows = pl.ds(pl.multiple_of(part * half + i * 256, 256), 256)
            grad_up[rows, :] = (nt(cot[inner, :], w_down[w_rows, :]) * slope[rows, :].astype(F32)).astype(BF16)

    side = j // (steps // 2)
    offset = lax.rem(j, steps // 2) * width
    for m in range(2):
        grad = tn(normed[:, 384 * m : 384 * (m + 1)], grad_up[...])
        start = place_of(384 * m, rows_up, chips)
        emit(grad, side, start, rows_up, up_mine, up_other, pl.ds(pl.multiple_of(offset, 128), width), tab, chips)


def up_back_kernel(pieces, n_refs, chips, rows_up, tab, grad_up, attended, gains, cot_own, cot_got, hidden, *refs):
    sources, refs = refs[:n_refs], refs[n_refs:]
    grad_hidden, grad_att, out_mine, out_other, w_up, w_out, total_out, sems = refs
    i = pl.program_id(0)
    steps = pl.num_programs(0)
    width = hidden.shape[1]

    @pl.when(i == 0)
    def _():
        started = pieces.start(sources, tab, {"up": w_up, "out": w_out}, sems, 0)
        total_out[...] = jnp.zeros_like(total_out)
        wait_all(started["up"])
        wait_all(started["out"])

    cot = jnp.where(i < steps // 2, cot_own[...], cot_got[...]).astype(F32)
    e = nt(grad_up[...], w_up[...])
    z, root = normalized(hidden[...])
    total = cot + norm_back(z, root, e * gains[1:2, :])
    grad_hidden[...] = total
    low = total.astype(BF16)
    grad_att[...] = nt(low, w_out[...]).astype(BF16)
    total_out[...] += tn(attended[...], low)

    @pl.when(i == steps - 1)
    def _():
        for m in range(2):
            start = place_of(384 * m, rows_up, chips)
            for side in range(2):
                value = total_out[384 * m : 384 * (m + 1), side * (width // 2) : (side + 1) * (width // 2)]
                emit(value, side, start, rows_up, out_mine, out_other, slice(None), tab, chips)


def output_kernel(pieces, n_refs, chips, tab, active, hidden, *refs):
    sources, refs = refs[:n_refs], refs[n_refs:]
    out, w_down, sems = refs

    @pl.when(pl.program_id(0) == 0)
    def _():
        wait_all(pieces.start(sources, tab, {"down": w_down}, sems, 0)["down"])

    out[...] = (hidden[...] + nn(active[...], w_down[...])).astype(BF16)


def attend_back_kernel(chips, tab, q_ref, k_ref, v_ref, o_ref, d_ref, log_totals, grad_q_ref, grad_k_ref, grad_v_ref, bias):
    @pl.when(jnp.logical_and(pl.program_id(0) == 0, pl.program_id(1) == 0))
    def _():
        fill_bias(bias, tab[2 * chips + 1])

    lane = lax.broadcasted_iota(jnp.int32, (512, 128), 1)
    for n in range(2):
        q, k, v, o, d = [pair_of(r, n) for r in (q_ref, k_ref, v_ref, o_ref, d_ref)]
        k_t = k.T
        dots = (o.astype(F32) * d.astype(F32)).T
        grad_q, grad_k, grad_v = [], [], []
        for h in range(2):
            here = (lane // 64) == h
            zero = jnp.zeros_like(k)
            s = nt(jnp.where(here, k, zero), q) * (SCORE_SCALE * LOG2E) + bias[...]
            p = jnp.exp2(s - log_totals[2 * n + h])
            grad_v.append(nn(p.astype(BF16), jnp.where(here, d, zero)))
            grad_p = nt(jnp.where(here, v, zero), d)
            delta = jnp.sum(dots[64 * h : 64 * h + 64, :], axis=0, keepdims=True)
            grad_s = (p * (grad_p - delta)).astype(BF16)
            grad_k.append(nn(grad_s, jnp.where(here, q, zero)))
            grad_q.append(nn(k_t[64 * h : 64 * h + 64, :], grad_s))

        def put(ref, value):
            ref[:, 0, :, 128 * n : 128 * (n + 1)] = value.astype(BF16).reshape(2, 256, 128)

        put(grad_q_ref, jnp.concatenate(grad_q, axis=0).T * SCORE_SCALE)
        put(grad_k_ref, (grad_k[0] + grad_k[1]) * SCORE_SCALE)
        put(grad_v_ref, grad_v[0] + grad_v[1])


def qkv_grad_kernel(chips, rows_qkv, tab, normed, grad_q, grad_k, grad_v, mine, other):
    width = normed.shape[1]
    near = width // 2
    for n, ref in enumerate((grad_q, grad_k, grad_v)):
        for m in range(2):
            grad = tn(normed[:, 384 * m : 384 * (m + 1)], ref[...])
            start = place_of(384 * m, rows_qkv, chips)
            for part in range(2):
                at = n * width + part * near
                side, column = at // (3 * near), at % (3 * near)
                value = grad[:, part * near : (part + 1) * near]
                emit(value, side, start, rows_qkv, mine, other, slice(column, column + near), tab, chips)


def first_kernel(pieces, n_refs, chips, tab, own, got, gains, grad_q, grad_k, grad_v, grad_hidden, *refs):
    sources, refs = refs[:n_refs], refs[n_refs:]
    out, w_qkv, sems = refs
    i = pl.program_id(0)
    width = own.shape[1]

    @pl.when(i == 0)
    def _():
        wait_all(pieces.start(sources, tab, {"qkv": w_qkv}, sems, 0)["qkv"])

    x = jnp.where(i < pl.num_programs(0) // 2, own[...], got[...]).astype(F32)
    e = nt(grad_q[...], w_qkv[:, :width])
    e += nt(grad_k[...], w_qkv[:, width : 2 * width])
    e += nt(grad_v[...], w_qkv[:, 2 * width :])
    z, root = normalized(x)
    out[...] = (grad_hidden[...] + norm_back(z, root, e * gains[0:1, :])).astype(BF16)


def whole(shape):
    return pl.BlockSpec(shape, lambda *_: (0,) * len(shape))


def call(kernel, tab, inputs, piece_arrays, outs, scratch, grid=(1,), cost=0):
    specs = [spec or whole(a.shape) for a, spec in inputs]
    specs = specs + [pl.BlockSpec(memory_space=pl.ANY) for _ in piece_arrays]
    moved = sum(a.size * a.dtype.itemsize for a, _ in inputs) + sum(a.size * a.dtype.itemsize for a in piece_arrays)
    moved += sum(o.size * o.dtype.itemsize for o, _ in outs)
    return pl.pallas_call(
        kernel,
        out_shape=[o for o, _ in outs],
        grid_spec=pltpu.PrefetchScalarGridSpec(
            num_scalar_prefetch=1,
            grid=grid,
            in_specs=specs,
            out_specs=[spec or whole(o.shape) for o, spec in outs],
            scratch_shapes=scratch,
        ),
        compiler_params=pltpu.CompilerParams(
            dimension_semantics=("arbitrary",) * len(grid), vmem_limit_bytes=VMEM_BYTES
        ),
        cost_estimate=pl.CostEstimate(flops=cost, bytes_accessed=moved, transcendentals=0),
    )(tab, *[a for a, _ in inputs], *piece_arrays)


def body(grid, tokens, clip_class, w_qkv, w_out, w_up, w_down, norm_gains, cotangent):
    rows, width = tokens.shape[1:]
    half = rows // 2
    ff = w_up.shape[1]
    here = grid.here()
    mx = here["x"]
    fast = (2 * w_qkv.shape[0]) % 16 == 0 and (2 * w_down.shape[0]) % 16 == 0
    chips = grid.chips if fast else 1

    def split(array):
        own = lax.dynamic_slice(array[0], (mx * half, 0), (half, width))
        away = lax.dynamic_slice(array[0], ((1 - mx) * half, 0), (half, width))
        return own, away

    swap_x = [(0, 1), (1, 0)]
    tok_own, tok_away = split(tokens)
    cot_own, cot_away = split(cotangent)

    if fast:
        spots = [(x, y, z) for x in range(grid.nx) for y in range(grid.ny) for z in range(grid.nz)]
        chip_at = [
            (((mx - x) % grid.nx) * grid.nz + ((here["z"] - z) % grid.nz)) * grid.ny + ((here["y"] - y) % grid.ny)
            for x, y, z in spots
        ]
        place_at = []
        for a in range(chips):
            x, z, y = a // (grid.nz * grid.ny), (a // grid.ny) % grid.nz, a % grid.ny
            rx, rz, ry = (x - mx) % grid.nx, (z - here["z"]) % grid.nz, (y - here["y"]) % grid.ny
            place_at.append((ry * grid.nx + rx) * grid.nz + rz)
        core = here["c"]
    else:
        chip_at, place_at, core = [jnp.int32(0)], [jnp.int32(0)], jnp.int32(0)
    tab = jnp.stack([jnp.asarray(v, jnp.int32) for v in chip_at + place_at + [core, clip_class[0]]])

    def side_of(weight, side):
        wide = weight.shape[1] // 2
        return lax.dynamic_slice(weight, (0, side * wide), (weight.shape[0], wide))

    gain_block = jnp.pad(norm_gains, ((0, 0), (0, 126)))
    fields_a = [("qkv", 0, 3 * width // 2, False), ("gain", 3 * width // 2, 128, True)]
    fields_b = [("up", 0, ff // 2, False), ("out", ff // 2, width // 2, False)]
    fields_c = [("down", 0, width // 2, False)]
    swap_core = functools.partial(lax.ppermute, axis_name=AXES, perm=grid.core_swap())
    tok_got = lax.ppermute(tok_away, "seq", swap_x)

    if fast:
        def sides(side):
            return (
                jnp.concatenate([side_of(w_qkv, side), gain_block], axis=1),
                jnp.concatenate([side_of(w_up, side), side_of(w_out, side)], axis=1),
                side_of(w_down, side),
            )

        def with_partner(keep, give):
            other = swap_core(give)
            return jnp.concatenate(
                [jnp.where(core == 0, keep, other), jnp.where(core == 0, other, keep)], axis=0
            )

        pieces = [with_partner(k, g) for k, g in zip(sides(core), sides(1 - core))]
        pieces_a, pieces_b, pieces_c = pieces

        def plane(x_first, y_first):
            near = exchange(grid, [x_first], "x"), exchange(grid, [y_first], "y")
            straight = exchange(grid, [x_first], "y"), exchange(grid, [y_first], "x")
            return near, straight

        def corners(near):
            return exchange(grid, near[0], "y") + exchange(grid, near[1], "x")

        def finish(mine, fields):
            mine = [(a, [rel_of(grid, s) for s in spots]) for a, spots in mine]
            theirs = [(swap_core(a), s) for a, s in mine]
            return Pieces(chips, mine, theirs, fields)

        z_a = gather_along_z(grid, pieces_a)
        near_a, straight_a = plane(*z_a)
        far_a = corners(near_a)
        z_b = gather_along_z(grid, after(pieces_b, z_a[0][0], z_a[1][0]))
        z_c = gather_along_z(grid, after(pieces_c, z_b[0][0], z_b[1][0]))
        group_a = finish(list(z_a) + near_a[0] + near_a[1] + straight_a[0] + straight_a[1] + far_a, fields_a)

        def held(parts, *earlier):
            arrays = lax.optimization_barrier(tuple(a for a, _ in parts) + earlier)
            return [(a, s) for a, (_, s) in zip(arrays, parts)]

        near_b, straight_b = plane(*held(z_b, *[a for a, _ in far_a]))
        cot_away = after(cot_away, *[a for a, _ in far_a])
        cot_got = lax.ppermute(cot_away, "seq", swap_x)
    else:
        full = [lax.all_gather(w, AXES, axis=0, tiled=True) for w in (w_qkv, w_out, w_up, w_down, gain_block)]

        def natural(parts, fields):
            sides = []
            for side in range(2):
                cut = [p if p.shape[1] == 128 else p[:, side * (p.shape[1] // 2) : (side + 1) * (p.shape[1] // 2)] for p in parts]
                sides.append([(jnp.concatenate(cut, axis=1)[None], [0])])
            return Pieces(1, sides[0], sides[1], fields)

        group_a = natural([full[0], full[4]], fields_a)
        group_b = natural([full[2], full[1]], fields_b)
        group_c = natural([full[3]], fields_c)
        cot_got = lax.ppermute(cot_away, "seq", swap_x)

    sds = jax.ShapeDtypeStruct
    heads = width // HEAD_DIM
    rows_a, rows_c = (2 * w_qkv.shape[0], 2 * w_down.shape[0]) if fast else (width, ff)
    dma = pltpu.SemaphoreType.DMA
    vmem = pltpu.VMEM
    tiles = rows // 256
    tile = lambda columns: pl.BlockSpec((256, columns), lambda i, t: (i, 0))
    own_tile = pl.BlockSpec((256, width), lambda i, t: (jnp.minimum(i, tiles // 2 - 1), 0))
    got_tile = pl.BlockSpec((256, width), lambda i, t: (jnp.maximum(i - tiles // 2, 0), 0))
    chunk = pl.BlockSpec((rows, width), lambda j, t: (0, j))
    low = lambda *shape: sds(shape, BF16)

    packed, normed_first, gains = call(
        functools.partial(input_kernel, group_a, len(group_a.arrays), chips),
        tab,
        [(tok_own, own_tile), (tok_got, got_tile)],
        group_a.arrays,
        [(low(rows, 3 * width), tile(3 * width)), (low(rows, width), tile(width)), (sds((8, width), F32), None)],
        [vmem((width, 3 * width), BF16), vmem((width, 128), BF16), dma((group_a.copies(("qkv", "gain")),))],
        grid=(tiles,),
        cost=2 * rows * width * 3 * width,
    )

    clip_blocks = half // 256
    by_clip = lambda a: a.reshape(2, clip_blocks, 256, a.shape[1])
    heads_at = lambda base: pl.BlockSpec((2, 1, 256, 256), lambda b, g, t: (0, b, 0, base + g))
    totals_at = pl.BlockSpec((4, 1, 512), lambda b, g, t: (b * (heads // 4) + g, 0, 0))
    clip_shape = low(2, clip_blocks, 256, width)
    step = width // 256
    qkv_in = [(by_clip(packed), heads_at(0)), (by_clip(packed), heads_at(step)), (by_clip(packed), heads_at(2 * step))]
    if fast:
        qkv_in = [(after(a, *[x for x, _ in near_b[0] + near_b[1]]), s) for a, s in qkv_in[:1]] + qkv_in[1:]
        far_b = corners(near_b)
    attended, log_totals = call(
        functools.partial(attend_kernel, chips),
        tab,
        qkv_in,
        [],
        [(clip_shape, heads_at(0)), (sds((clip_blocks * heads, 1, 512), F32), totals_at)],
        [vmem((512, 512), F32)],
        grid=(clip_blocks, heads // 4),
        cost=8 * rows * 512 * width,
    )
    attended = attended.reshape(rows, width)

    if fast:
        parts_b = list(z_b) + near_b[0] + near_b[1] + straight_b[0] + straight_b[1] + far_b
        group_b = finish(parts_b, fields_b)
        near_c, straight_c = plane(*held(z_c, *[a for a, _ in far_b]))

    hidden, normed_second = call(
        functools.partial(middle_kernel, group_b, len(group_b.arrays), chips),
        tab,
        [(attended, tile(width)), (tok_own, own_tile), (tok_got, got_tile), (gains, None)],
        group_b.arrays,
        [(sds((rows, width), F32), tile(width)), (low(rows, width), tile(width))],
        [vmem((width, width), BF16), dma((group_b.copies(("out",)),))],
        grid=(tiles,),
        cost=2 * rows * width * width,
    )

    if fast:
        normed_up = after(normed_second, *[x for x, _ in near_c[0] + near_c[1]])
        far_c = corners(near_c)
    else:
        normed_up = normed_second
    steps = ff // width
    down_out = low(chips, rows_c, width // 2)
    active, slope, down_mine, down_other = call(
        functools.partial(up_kernel, group_b, len(group_b.arrays), chips, rows_c),
        tab,
        [(normed_up, None), (cot_own, None), (cot_got, None)],
        group_b.arrays,
        [(low(rows, ff), chunk), (low(rows, ff), chunk), (down_out, None), (down_out, None)],
        [vmem((width, ff), BF16), dma((group_b.copies(("up",)),))],
        grid=(steps,),
        cost=4 * rows * width * ff,
    )

    def sums(mine, other):
        if fast:
            total = scatter_sum(grid, mine, other)
            height = total.shape[0] // 2
            keep = lax.dynamic_slice(total, (core * height, 0), (height, total.shape[1]))
            away = lax.dynamic_slice(total, ((1 - core) * height, 0), (height, total.shape[1]))
            got = swap_core(away.astype(BF16)).astype(F32)
            return jnp.where(core == 0, keep, got), jnp.where(core == 0, got, keep)
        whole_sum = jnp.concatenate([mine[0], other[0]], axis=1)
        total = lax.psum_scatter(whole_sum, AXES, scatter_dimension=0, tiled=True).astype(F32)
        return total[:, : total.shape[1] // 2], total[:, total.shape[1] // 2 :]

    left, right = sums(down_mine, down_other)
    owned_down = jnp.concatenate([left, right], axis=1)

    if fast:
        group_c = finish(list(z_c) + near_c[0] + near_c[1] + straight_c[0] + straight_c[1] + far_c, fields_c)
    up_out = low(chips, rows_a, ff // 2)
    grad_up, up_mine, up_other = call(
        functools.partial(down_back_kernel, group_c, len(group_c.arrays), chips, rows_a),
        tab,
        [(cot_own, None), (cot_got, None), (normed_second, None), (slope, chunk)],
        group_c.arrays,
        [(low(rows, ff), chunk), (up_out, None), (up_out, None)],
        [vmem((ff, width), BF16), dma((group_c.copies(("down",)),))],
        grid=(steps,),
        cost=4 * rows * width * ff,
    )
    small_out = low(chips, rows_a, width // 2)
    grad_hidden, grad_att, out_mine, out_other = call(
        functools.partial(up_back_kernel, group_b, len(group_b.arrays), chips, rows_a),
        tab,
        [
            (grad_up, tile(ff)), (attended, tile(width)), (gains, None), (cot_own, own_tile), (cot_got, got_tile),
            (hidden, tile(width)),
        ],
        group_b.arrays,
        [(sds((rows, width), F32), tile(width)), (low(rows, width), tile(width)), (small_out, None), (small_out, None)],
        [vmem((width, ff), BF16), vmem((width, width), BF16), vmem((width, width), F32), dma((group_b.copies(("up", "out")),))],
        grid=(tiles,),
        cost=2 * rows * width * ff + 4 * rows * width * width,
    )
    left, right = sums(
        jnp.concatenate([up_mine, out_mine], axis=2), jnp.concatenate([up_other, out_other], axis=2)
    )
    owned_up = jnp.concatenate([left[:, : ff // 2], right[:, : ff // 2]], axis=1)
    owned_out = jnp.concatenate([left[:, ff // 2 :], right[:, ff // 2 :]], axis=1)

    def joined(both):
        own, away = both[:half], both[half:]
        back = lax.ppermute(away, "seq", swap_x)
        first = mx == 0
        return jnp.concatenate([jnp.where(first, own, back), jnp.where(first, back, own)], axis=0)[None]

    (outputs,) = call(
        functools.partial(output_kernel, group_c, len(group_c.arrays), chips),
        tab,
        [(active, tile(ff)), (hidden, tile(width))],
        group_c.arrays,
        [(low(rows, width), tile(width))],
        [vmem((ff, width), BF16), dma((group_c.copies(("down",)),))],
        grid=(tiles,),
        cost=2 * rows * width * ff,
    )
    output_tokens = joined(outputs)

    grads = call(
        functools.partial(attend_back_kernel, chips),
        tab,
        [
            (by_clip(packed), heads_at(0)), (by_clip(packed), heads_at(step)), (by_clip(packed), heads_at(2 * step)),
            (by_clip(attended), heads_at(0)), (by_clip(grad_att), heads_at(0)), (log_totals, totals_at),
        ],
        [],
        [(clip_shape, heads_at(0))] * 3,
        [vmem((512, 512), F32)],
        grid=(clip_blocks, heads // 4),
        cost=30 * rows * 512 * width,
    )
    grads = [g.reshape(rows, width) for g in grads]
    qkv_out = low(chips, rows_a, 3 * width // 2)
    qkv_mine, qkv_other = call(
        functools.partial(qkv_grad_kernel, chips, rows_a),
        tab,
        [(normed_first, None)] + [(g, None) for g in grads],
        [],
        [(qkv_out, None), (qkv_out, None)],
        [],
        cost=2 * rows * width * 3 * width,
    )
    left, right = sums(qkv_mine, qkv_other)
    owned_qkv = jnp.concatenate([left, right], axis=1)

    (grad_rows,) = call(
        functools.partial(first_kernel, group_a, len(group_a.arrays), chips),
        tab,
        [(tok_own, own_tile), (tok_got, got_tile), (gains, None)] + [(g, tile(width)) for g in grads] + [(grad_hidden, tile(width))],
        group_a.arrays,
        [(low(rows, width), tile(width))],
        [vmem((width, 3 * width), BF16), dma((group_a.copies(("qkv",)),))],
        grid=(tiles,),
        cost=2 * rows * width * 3 * width,
    )
    grad_tokens = joined(grad_rows)

    scale = norm_gains.astype(F32)
    first_gain = jnp.sum(w_qkv.astype(F32) * owned_qkv, axis=1) / scale[:, 0]
    second_gain = jnp.sum(w_up.astype(F32) * owned_up, axis=1) / scale[:, 1]
    owned_gains = jnp.stack([first_gain, second_gain], axis=1)
    return (output_tokens, grad_tokens, owned_qkv, owned_out, owned_up, owned_down, owned_gains)


def solution(mesh):
    grid = Grid(mesh.shape["seq"], mesh.shape["clips"])
    shard = P(AXES, None)
    return jax.shard_map(
        functools.partial(body, grid),
        mesh=mesh,
        in_specs=(P("seq", "clips", None), P("clips"), shard, shard, shard, shard, shard, P("seq", "clips", None)),
        out_specs=(P("seq", "clips", None), P("seq", "clips", None), shard, shard, shard, shard, shard),
        check_vma=False,
    )
```

time: 1140 us -> 439 us (0.39)
  waiting for transfers between devices: 680 us -> 156 us
  Pallas kernels: 0 us -> 174 us
  matrix products: 171 us -> 0 us
  local copies, waits for them, and re-layouts: 155 us -> 16.1 us
  blocking collectives: 82.8 us -> 0 us
  starting transfers between devices: 0.65 us -> 72.1 us
  between operations: 15.4 us -> 2.7 us
  other arithmetic: 25.2 us -> 12.9 us
    reduce_scatter x6 -> x0, waiting for transfers between devices: 490 us -> none  [the longest x1 142 us: body(): lax.psum_scatter(grad_up, ('seq', 'clips'), scatter_dimension=0, tiled=True)]
    all_gather x6 -> x0, waiting for transfers between devices: 187 us -> none  [the longest x1 53.9 us: body(): lax.all_gather(w_up, ('seq', 'clips'), axis=0, tiled=True)]
    pallas_call x0 -> x10, Pallas kernels: none -> 174 us  [call(): pl.pallas_call(kernel, out_shape=[o for o, _ in outs], grid_spec=pltpu.Pr...]
    dot_general x26 -> x0, matrix products: 171 us -> none  [the longest x1 37.2 us: body(): jnp.dot(normed_second, full_up, preferred_element_type=jnp.float32)]
    ppermute x0 -> x85, waiting for transfers between devices: none -> 156 us  [the longest x12 68.3 us: scatter_sum(): lax.ppermute(add_all(pieces[k]).astype(BF16), AXES, grid.shift(axis, k))]
    reshape x15 -> x0, local copies, waits for them, and re-layouts: 86.6 us -> none  [the longest x4 26.6 us: from_clips(): rows.reshape(clip_total, shard_count, query_len, width)]
    ppermute x0 -> x85, starting transfers between devices: none -> 72.1 us  [the longest x27 37.8 us: exchange(): lax.ppermute(array, AXES, grid.shift(axis, k))]
    all_gather x1 -> x0, blocking collectives: 43.3 us -> none  [body(): lax.all_gather(norm_gains, ('seq', 'clips'), axis=0, tiled=True)]
  transfers between devices with their start and end apart: 12 -> 85, of which waited for: 11 -> 28; matrix products, arithmetic and copies ran while one was open for 15% -> 4% of each run, Pallas kernels for 0% -> 40%
where the time goes in v1:
time: 439 us; the launch traced here: 433 us
  Pallas kernels  174 us (40%)
  waiting for transfers between devices  156 us (36%)
  starting transfers between devices  72.1 us (16%)
  local copies, waits for them, and re-layouts  16.1 us (4%)
  other arithmetic  12.9 us (3%)
    pallas_call x10, Pallas kernels, call(): pl.pallas_call(kernel, out_shape=[o for o, _ in outs], grid_spec=pltpu.Pr...  174 us
    ppermute x12, waiting for transfers between devices, scatter_sum(): lax.ppermute(add_all(pieces[k]).astype(BF16), AXES, grid.shift(axis, k))  68.3 us
    ppermute x27, waiting for transfers between devices, exchange(): lax.ppermute(array, AXES, grid.shift(axis, k))  63.4 us
    ppermute x27, starting transfers between devices, exchange(): lax.ppermute(array, AXES, grid.shift(axis, k))  37.8 us
    ppermute x9, waiting for transfers between devices, scatter_sum(): lax.ppermute(total.astype(BF16), AXES, grid.shift('z', k))  17 us
    ppermute x9, starting transfers between devices, scatter_sum(): lax.ppermute(total.astype(BF16), AXES, grid.shift('z', k))  13.2 us
    ppermute x12, starting transfers between devices, scatter_sum(): lax.ppermute(add_all(pieces[k]).astype(BF16), AXES, grid.shift(axis, k))  11.1 us
  transfers between devices with their start and end apart: 85, of which 28 were waited for; matrix products, arithmetic and copies ran while one was open for 4% of the time, Pallas kernels for 40%

profile of v1, /device:TPU:0, one launch (start us, length us, event | category | flops | bytes accessed | tf_op | source)
XLA Modules:
  0.0 433.1 jit_solution(16231750825378697945)
XLA Ops:
  6.2 3.7 collective-permute-start.3
  9.9 1.6 collective-permute-start.2
  11.5 2.2 collective-permute-start.4
  13.8 5.6 %collective-permute-done.3 = bf16[1,48,1280]{2,1,0:T(8,128)(2,1)S(1)} collective-permute-done((bf16[1,48,1280]{2,1,0:T(8,128)(2,1)S(1)}, bf16[1,48,1280]{2,1,0:T(8,128)(2,1)S(1)}, u32[]{:S(2)}, u32[]{:S(2)}) %collective-permute-start.3) | collective-permute-done | bytes 122912 | tf_op jit(solution)/shard_map/ppermute | solution.py:67
  19.4 1.8 collective-permute-start.5
  21.2 4.7 %collective-permute-start.21 = (bf16[1,48,1920]{2,1,0:T(8,128)(2,1)S(1)}, bf16[1,48,1920]{2,1,0:T(8,128)(2,1)S(1)}, u32[]{:S(2)}, u32[]{:S(2)}) collective-permute-start(bf16[1,48,1920]{2,1,0:T(8,128)(2,1)S(1)} %bitcast.313), channel_id=1, source_target_pairs={{0,8},{1,9},{2,10},{3,11},{4,12},{5,13},{6,14},{7,15},{8,0},{9,1},... | collective-permute-start | bytes 552968 | tf_op jit(solution)/shard_map/ppermute | solution.py:67
  26.0 1.5 collective-permute-start.6
  27.6 3.9 collective-permute-start.22
  32.0 6.8 %collective-permute-done.21 = bf16[1,48,1920]{2,1,0:T(8,128)(2,1)S(1)} collective-permute-done((bf16[1,48,1920]{2,1,0:T(8,128)(2,1)S(1)}, bf16[1,48,1920]{2,1,0:T(8,128)(2,1)S(1)}, u32[]{:S(2)}, u32[]{:S(2)}) %collective-permute-start.21) | collective-permute-done | bytes 184352 | tf_op jit(solution)/shard_map/ppermute | solution.py:67
  39.4 1.6 collective-permute-done.22.refs_1_
  41.1 1.7 collective-permute-start.39
  42.8 1.5 collective-permute-start.9
  46.0 1.5 collective-permute-start
  47.6 1.2 collective-permute-done.16.refs_13_
  49.3 2.1 collective-permute-done.39
  51.4 4.2 collective-permute-done.38
  56.2 4.8 %collective-permute-done.40.refs_1_ = bf16[1,192,384]{2,1,0:T(8,128)(2,1)} collective-permute-done((bf16[1,192,384]{2,1,0:T(8,128)(2,1)S(1)}, bf16[1,192,384]{2,1,0:T(8,128)(2,1)}, u32[]{:S(2)}, u32[]{:S(2)}) %collective-permute-start.40) | collective-permute-done | bytes 147488 | tf_op jit(solution)/shard_map/ppermute | solution.py:67
  62.3 1.7 collective-permute-done.18.refs_15_
  66.4 10.7 %collective-permute-done.23.refs_2_ = bf16[3,48,1920]{2,1,0:T(8,128)(2,1)S(1)} collective-permute-done((bf16[3,48,1920]{2,1,0:T(8,128)(2,1)S(1)}, bf16[3,48,1920]{2,1,0:T(8,128)(2,1)S(1)}, u32[]{:S(2)}, u32[]{:S(2)}) %collective-permute-start.23) | collective-permute-done | bytes 552992 | tf_op jit(solution)/shard_map/ppermute | solution.py:67
  77.7 1.6 collective-permute-start.24
  79.3 1.6 collective-permute-start.26
  82.5 12.0 %collective-permute-done.24.refs_3_ = bf16[1,48,1920]{2,1,0:T(8,128)(2,1)S(1)} collective-permute-done((bf16[1,48,1920]{2,1,0:T(8,128)(2,1)S(1)}, bf16[1,48,1920]{2,1,0:T(8,128)(2,1)S(1)}, u32[]{:S(2)}, u32[]{:S(2)}) %collective-permute-start.24) | collective-permute-done | bytes 184352 | tf_op jit(solution)/shard_map/ppermute | solution.py:67
  95.1 1.5 collective-permute-start.28
  96.6 10.3 %collective-permute-done.28.refs_7_ = bf16[1,48,1920]{2,1,0:T(8,128)(2,1)S(1)} collective-permute-done((bf16[1,48,1920]{2,1,0:T(8,128)(2,1)S(1)}, bf16[1,48,1920]{2,1,0:T(8,128)(2,1)S(1)}, u32[]{:S(2)}, u32[]{:S(2)}) %collective-permute-start.28) | collective-permute-done | bytes 184352 | tf_op jit(solution)/shard_map/ppermute | solution.py:67
  107.4 1.5 collective-permute-start.41
  114.6 5.3 %collective-permute-done.41.refs_2_ = bf16[3,192,384]{2,1,0:T(8,128)(2,1)} collective-permute-done((bf16[3,192,384]{2,1,0:T(8,128)(2,1)}, bf16[3,192,384]{2,1,0:T(8,128)(2,1)}, u32[]{:S(2)}, u32[]{:S(2)}) %collective-permute-start.41) | collective-permute-done | bytes 442400 | tf_op jit(solution)/shard_map/ppermute | solution.py:67
  120.8 10.9 %shard_map.135 = (bf16[1024,2304]{1,0:T(8,128)(2,1)}, bf16[1024,768]{1,0:T(8,128)(2,1)}, f32[8,768]{1,0:T(8,128)}) custom-call(s32[34]{0:T(128)} %stack.140.tab, bf16[512,768]{1,0:T(8,128)(2,1)} %get-tuple-element.91.own, bf16[512,768]{1,0:T(8,128)(2,1)} %copy-done.1, bf16[3,48,1280]{2,1,0:T(8,128)(2,1)} %copy-done.10, bf16[1,48,1280]{2,1,0:T(8,128)(2,1)} %copy-done.34, ...), custom_call_target="tpu_custom_call" | custom-call | flops 3623878656 | bytes 11821056 | tf_op jit(solution)/shard_map/pallas_call | solution.py:476
  131.7 1.6 collective-permute-start.45
  133.8 15.7 %shard_map.136 = (bf16[2,2,256,768]{3,2,1,0:T(8,128)(2,1)}, f32[24,1,512]{2,1,0:T(1,128)}) custom-call(s32[34]{0:T(128)} %stack.140.tab, bf16[2,2,256,2304]{3,2,1,0:T(8,128)(2,1)} %bitcast.263, bf16[2,2,256,2304]{3,2,1,0:T(8,128)(2,1)} %bitcast.264, bf16[2,2,256,2304]{3,2,1,0:T(8,128)(2,1)} %bitcast.265), custom_call_target="tpu_custom_call" | custom-call | flops 3221225472 | bytes 15777792 | tf_op jit(solution)/shard_map/pallas_call | solution.py:476
  149.5 7.7 %shard_map.137 = (f32[1024,768]{1,0:T(8,128)}, bf16[1024,768]{1,0:T(8,128)(2,1)}) custom-call(s32[34]{0:T(128)} %stack.140.tab, bf16[1024,768]{1,0:T(8,128)(2,1)} %bitcast.311, bf16[512,768]{1,0:T(8,128)(2,1)} %get-tuple-element.91.own, bf16[512,768]{1,0:T(8,128)(2,1)} %copy-done.1, f32[8,768]{1,0:T(8,128)} %get-tuple-element.45.gains, ...), custom_call_target="tpu_custom_call" | custom-call | flops 1207959552 | bytes 13787136 | tf_op jit(solution)/shard_map/pallas_call | solution.py:476
  158.9 33.3 %shard_map.138 = (bf16[1024,3072]{1,0:T(8,128)(2,1)}, bf16[1024,3072]{1,0:T(8,128)(2,1)}, bf16[16,192,384]{2,1,0:T(8,128)(2,1)}, bf16[16,192,384]{2,1,0:T(8,128)(2,1)}) custom-call(s32[34]{0:T(128)} %stack.140.tab, bf16[1024,768]{1,0:T(8,128)(2,1)} %get-tuple-element.50.normed, bf16[512,768]{1,0:T(8,128)(2,1)} %get-tuple-element.89.cot_own, ...), custom_call_target="tpu_custom_call" | custom-call | flops 9663676416 | bytes 26345472 | tf_op jit(solution)/shard_map/pallas_call | solution.py:476
  193.7 11.8 %shard_map.139 = bf16[1024,768]{1,0:T(8,128)(2,1)} custom-call(s32[34]{0:T(128)} %stack.140.tab, bf16[1024,3072]{1,0:T(8,128)(2,1)} %get-tuple-element.52.active, f32[1024,768]{1,0:T(8,128)} %get-tuple-element.53.hidden, bf16[3,192,384]{2,1,0:T(8,128)(2,1)} %pad_maximum_fusion.3.refs_0_, bf16[1,192,384]{2,1,0:T(8,128)(2,1)} %collective-permute-done.40.refs_1_, ...), custom_call_target="tpu_custom_call" | custom-call | flops 4831838208 | bytes 15728640 | tf_op jit(solution)/shard_map/pallas_call | solution.py:476
  206.7 1.6 collective-permute-start.56
  208.3 25.2 %shard_map.140 = (bf16[1024,3072]{1,0:T(8,128)(2,1)}, bf16[16,48,1536]{2,1,0:T(8,128)(2,1)}, bf16[16,48,1536]{2,1,0:T(8,128)(2,1)}) custom-call(s32[34]{0:T(128)} %stack.140.tab, bf16[512,768]{1,0:T(8,128)(2,1)} %get-tuple-element.89.cot_own, bf16[512,768]{1,0:T(8,128)(2,1)} %collective-permute-done.43.cot_got, bf16[1024,768]{1,0:T(8,128)(2,1)} %get-tuple-element.50.normed, ...), custom_call_target="tpu_custom_call" | custom-call | flops 9663676416 | bytes 25165824 | tf_op jit(solution)/shard_map/pallas_call | solution.py:476
  233.4 21.2 %shard_map.141 = (f32[1024,768]{1,0:T(8,128)}, bf16[1024,768]{1,0:T(8,128)(2,1)}, bf16[16,48,384]{2,1,0:T(8,128)(2,1)}, bf16[16,48,384]{2,1,0:T(8,128)(2,1)}) custom-call(s32[34]{0:T(128)} %stack.140.tab, bf16[1024,3072]{1,0:T(8,128)(2,1)} %get-tuple-element.55.grad_up, bf16[1024,768]{1,0:T(8,128)(2,1)} %bitcast.312, f32[8,768]{1,0:T(8,128)} %get-tuple-element.45.gains, ...), custom_call_target="tpu_custom_call" | custom-call | flops 7247757312 | bytes 24403968 | tf_op jit(solution)/shard_map/pallas_call | solution.py:476
  254.7 23.8 %shard_map.142 = (bf16[2,2,256,768]{3,2,1,0:T(8,128)(2,1)}, bf16[2,2,256,768]{3,2,1,0:T(8,128)(2,1)}, bf16[2,2,256,768]{3,2,1,0:T(8,128)(2,1)}) custom-call(s32[34]{0:T(128)} %stack.140.tab, bf16[2,2,256,2304]{3,2,1,0:T(8,128)(2,1)} %bitcast.266, bf16[2,2,256,2304]{3,2,1,0:T(8,128)(2,1)} %bitcast.267, bf16[2,2,256,2304]{3,2,1,0:T(8,128)(2,1)} %bitcast.268, ...), custom_call_target="tpu_custom_call" | custom-call | flops 12079595520 | bytes 22069248 | tf_op jit(solution)/shard_map/pallas_call | solution.py:476
  278.5 11.7 %shard_map.143 = bf16[1024,768]{1,0:T(8,128)(2,1)} custom-call(s32[34]{0:T(128)} %stack.140.tab, bf16[512,768]{1,0:T(8,128)(2,1)} %get-tuple-element.91.own, bf16[512,768]{1,0:T(8,128)(2,1)} %copy-done.1, f32[8,768]{1,0:T(8,128)} %get-tuple-element.45.gains, bf16[1024,768]{1,0:T(8,128)(2,1)} %bitcast.305, bf16[1024,768]{1,0:T(8,128)(2,1)} %bitcast.307, ...), custom_call_target="tpu_custom_call" | custom-call | flops 3623878656 | bytes 14966784 | tf_op jit(solution)/shard_map/pallas_call | solution.py:476
  290.2 2.1 slice.502
  292.8 12.2 %shard_map.144 = (bf16[16,48,1152]{2,1,0:T(8,128)(2,1)}, bf16[16,48,1152]{2,1,0:T(8,128)(2,1)}) custom-call(s32[34]{0:T(128)} %stack.140.tab, bf16[1024,768]{1,0:T(8,128)(2,1)} %get-tuple-element.62.normed, bf16[1024,768]{1,0:T(8,128)(2,1)} %bitcast.306, bf16[1024,768]{1,0:T(8,128)(2,1)} %bitcast.308, bf16[1024,768]{1,0:T(8,128)(2,1)} %bitcast.310), custom_call_target="tpu_custom_call" | custom-call | flops 3623878656 | bytes 9830400 | tf_op jit(solution)/shard_map/pallas_call | solution.py:476
  308.3 1.2 broadcast_select_fusion.3
  309.5 1.2 maximum_bitcast_fusion
  310.8 1.4 collective-permute-done.57
  312.1 1.2 broadcast_select_fusion.1
  313.4 1.2 maximum_bitcast_fusion.1
  315.8 1.2 collective-permute-start.77
  319.2 1.2 collective-permute-start.63
  320.5 31.1 %collective-permute-done.59 = bf16[2,3,48,1152]{3,2,1,0:T(8,128)(2,1)S(1)} collective-permute-done((bf16[2,3,48,1152]{3,2,1,0:T(8,128)(2,1)S(1)}, bf16[2,3,48,1152]{3,2,1,0:T(8,128)(2,1)S(1)}, u32[]{:S(2)}, u32[]{:S(2)}) %collective-permute-start.59) | collective-permute-done | bytes 663584 | tf_op jit(solution)/shard_map/ppermute | solution.py:99
  351.7 1.6 collective-permute-start.60
  355.5 3.8 collective-permute-done.64
  359.4 1.6 collective-permute-done.60
  361.1 3.0 collective-permute-start.65
  364.9 2.7 collective-permute-done.65
  368.2 5.1 %collective-permute-done.62 = bf16[48,1152]{1,0:T(8,128)(2,1)S(1)} collective-permute-done((bf16[48,1152]{1,0:T(8,128)(2,1)S(1)}, bf16[48,1152]{1,0:T(8,128)(2,1)S(1)}, u32[]{:S(2)}, u32[]{:S(2)}) %collective-permute-start.62) | collective-permute-done | bytes 110624 | tf_op jit(solution)/shard_map/ppermute | solution.py:109
  373.5 3.0 collective-permute-done.78
  376.8 4.2 collective-permute-start.83
  380.9 1.6 collective-permute-start.80
  382.8 1.2 collective-permute-start.68
  385.0 20.9 %collective-permute-done.68 = bf16[2,3,48,1920]{3,2,1,0:T(8,128)(2,1)S(1)} collective-permute-done((bf16[2,3,48,1920]{3,2,1,0:T(8,128)(2,1)S(1)}, bf16[2,3,48,1920]{3,2,1,0:T(8,128)(2,1)S(1)}, u32[]{:S(2)}, u32[]{:S(2)}) %collective-permute-start.68) | collective-permute-done | bytes 1105952 | tf_op jit(solution)/shard_map/ppermute | solution.py:99
  406.3 1.2 collective-permute-start.73
  407.8 4.1 collective-permute-done.73
  411.9 3.8 collective-permute-done.69
  416.0 2.7 collective-permute-start.74
  419.8 2.7 collective-permute-done.74
  422.5 6.4 %collective-permute-done.71 = bf16[48,1920]{1,0:T(8,128)(2,1)S(1)} collective-permute-done((bf16[48,1920]{1,0:T(8,128)(2,1)S(1)}, bf16[48,1920]{1,0:T(8,128)(2,1)S(1)}, u32[]{:S(2)}, u32[]{:S(2)}) %collective-permute-start.71) | collective-permute-done | bytes 184352 | tf_op jit(solution)/shard_map/ppermute | solution.py:109
  (290 shorter events, 45.5 us)
Async XLA Ops:
  5.7 21.8 %collective-permute-start.37 = (bf16[96,384]{1,0:T(8,128)(2,1)S(1)}, bf16[96,384]{1,0:T(8,128)(2,1)S(1)}, u32[]{:S(2)}, u32[]{:S(2)}) collective-permute-start(bf16[96,384]{1,0:T(8,128)(2,1)S(1)} %constant_dynamic-slice_fusion), channel_id=1, source_target_pairs={{0,1},{1,0},{2,3},{3,2},{4,5},{5,4},{6,7},{7,6},{8,9},{9,8},{10,11... | collective-permute-start | bytes 221192 | tf_op jit(solution)/shard_map/ppermute | solution.py:547
  6.2 13.2 %collective-permute-start.3 = (bf16[1,48,1280]{2,1,0:T(8,128)(2,1)S(1)}, bf16[1,48,1280]{2,1,0:T(8,128)(2,1)S(1)}, u32[]{:S(2)}, u32[]{:S(2)}) collective-permute-start(bf16[1,48,1280]{2,1,0:T(8,128)(2,1)S(1)} %maximum_bitcast_fusion.2), channel_id=1, source_target_pairs={{0,8},{1,9},{2,10},{3,11},{4,12},{5,13},{6,14},{7,15},{8,0},{9,1},... | collective-permute-start | bytes 368648 | tf_op jit(solution)/shard_map/ppermute | solution.py:67
  9.9 9.5 %collective-permute-start.2 = (bf16[1,48,1280]{2,1,0:T(8,128)(2,1)S(1)}, bf16[1,48,1280]{2,1,0:T(8,128)(2,1)S(1)}, u32[]{:S(2)}, u32[]{:S(2)}) collective-permute-start(bf16[1,48,1280]{2,1,0:T(8,128)(2,1)S(1)} %maximum_bitcast_fusion.2), channel_id=1, source_target_pairs={{0,4},{1,5},{2,6},{3,7},{4,8},{5,9},{6,10},{7,11},{8,12},{9,13},{1... | collective-permute-start | bytes 368648 | tf_op jit(solution)/shard_map/ppermute | solution.py:67
  11.5 9.8 %collective-permute-start.4 = (bf16[1,48,1280]{2,1,0:T(8,128)(2,1)S(1)}, bf16[1,48,1280]{2,1,0:T(8,128)(2,1)S(1)}, u32[]{:S(2)}, u32[]{:S(2)}) collective-permute-start(bf16[1,48,1280]{2,1,0:T(8,128)(2,1)S(1)} %maximum_bitcast_fusion.2), channel_id=1, source_target_pairs={{0,12},{1,13},{2,14},{3,15},{4,0},{5,1},{6,2},{7,3},{8,4},{9,5},{1... | collective-permute-start | bytes 368648 | tf_op jit(solution)/shard_map/ppermute | solution.py:67
  19.4 23.4 %collective-permute-start.5 = (bf16[3,48,1280]{2,1,0:T(8,128)(2,1)S(1)}, bf16[3,48,1280]{2,1,0:T(8,128)(2,1)S(1)}, u32[]{:S(2)}, u32[]{:S(2)}) collective-permute-start(bf16[3,48,1280]{2,1,0:T(8,128)(2,1)S(1)} %pad_maximum_fusion.4.refs_0_), channel_id=1, source_target_pairs={{0,16},{1,17},{2,18},{3,19},{4,20},{5,21},{6,22},{7,23},{8,24},{9,... | collective-permute-start | bytes 1105928 | tf_op jit(solution)/shard_map/ppermute | solution.py:67
  21.2 17.5 %collective-permute-start.21 = (bf16[1,48,1920]{2,1,0:T(8,128)(2,1)S(1)}, bf16[1,48,1920]{2,1,0:T(8,128)(2,1)S(1)}, u32[]{:S(2)}, u32[]{:S(2)}) collective-permute-start(bf16[1,48,1920]{2,1,0:T(8,128)(2,1)S(1)} %bitcast.313), channel_id=1, source_target_pairs={{0,8},{1,9},{2,10},{3,11},{4,12},{5,13},{6,14},{7,15},{8,0},{9,1},... | collective-permute-start | bytes 552968 | tf_op jit(solution)/shard_map/ppermute | solution.py:67
  26.0 12.8 %collective-permute-start.20 = (bf16[1,48,1920]{2,1,0:T(8,128)(2,1)S(1)}, bf16[1,48,1920]{2,1,0:T(8,128)(2,1)S(1)}, u32[]{:S(2)}, u32[]{:S(2)}) collective-permute-start(bf16[1,48,1920]{2,1,0:T(8,128)(2,1)S(1)} %bitcast.314), channel_id=1, source_target_pairs={{0,4},{1,5},{2,6},{3,7},{4,8},{5,9},{6,10},{7,11},{8,12},{9,13},{1... | collective-permute-start | bytes 552968 | tf_op jit(solution)/shard_map/ppermute | solution.py:67
  27.6 13.5 %collective-permute-start.22 = (bf16[1,48,1920]{2,1,0:T(8,128)(2,1)S(1)}, bf16[1,48,1920]{2,1,0:T(8,128)(2,1)S(1)}, u32[]{:S(2)}, u32[]{:S(2)}) collective-permute-start(bf16[1,48,1920]{2,1,0:T(8,128)(2,1)S(1)} %bitcast.315), channel_id=1, source_target_pairs={{0,12},{1,13},{2,14},{3,15},{4,0},{5,1},{6,2},{7,3},{8,4},{9,5},{1... | collective-permute-start | bytes 552968 | tf_op jit(solution)/shard_map/ppermute | solution.py:67
  31.5 9.6 %collective-permute-start.8 = (bf16[1,48,1280]{2,1,0:T(8,128)(2,1)S(1)}, bf16[1,48,1280]{2,1,0:T(8,128)(2,1)S(1)}, u32[]{:S(2)}, u32[]{:S(2)}) collective-permute-start(bf16[1,48,1280]{2,1,0:T(8,128)(2,1)S(1)} %collective-permute-done.4.refs_1_), channel_id=1, source_target_pairs={{0,16},{1,17},{2,18},{3,19},{4,20},{5,21},{6,22},{7,23},{8,24},{9,... | collective-permute-start | bytes 368648 | tf_op jit(solution)/shard_map/ppermute | solution.py:67
  41.1 10.3 %collective-permute-start.39 = (bf16[1,192,384]{2,1,0:T(8,128)(2,1)S(1)}, bf16[1,192,384]{2,1,0:T(8,128)(2,1)S(1)}, u32[]{:S(2)}, u32[]{:S(2)}) collective-permute-start(bf16[1,192,384]{2,1,0:T(8,128)(2,1)S(1)} %bitcast.317), channel_id=1, source_target_pairs={{0,8},{1,9},{2,10},{3,11},{4,12},{5,13},{6,14},{7,15},{8,0},{9,1},... | collective-permute-start | bytes 442376 | tf_op jit(solution)/shard_map/ppermute | solution.py:67
  42.8 13.4 %collective-permute-start.9 = (bf16[3,48,1280]{2,1,0:T(8,128)(2,1)S(1)}, bf16[3,48,1280]{2,1,0:T(8,128)(2,1)S(1)}, u32[]{:S(2)}, u32[]{:S(2)}) collective-permute-start(bf16[3,48,1280]{2,1,0:T(8,128)(2,1)S(1)} %collective-permute-done.5.refs_2_), channel_id=1, source_target_pairs={{0,2},{1,3},{2,0},{3,1},{4,6},{5,7},{6,4},{7,5},{8,10},{9,11},{10,... | collective-permute-start | bytes 1105928 | tf_op jit(solution)/shard_map/ppermute | solution.py:67
  46.0 20.4 %collective-permute-start = (bf16[512,768]{1,0:T(8,128)(2,1)S(1)}, bf16[512,768]{1,0:T(8,128)(2,1)S(1)}, u32[]{:S(2)}, u32[]{:S(2)}) collective-permute-start(bf16[512,768]{1,0:T(8,128)(2,1)S(1)} %get-tuple-element.90), channel_id=1, source_target_pairs={{0,16},{16,0},{1,17},{17,1},{2,18},{18,2},{3,19},{19,3},{4,20},{20... | collective-permute-start | bytes 2359304 | tf_op jit(solution)/shard_map/ppermute | solution.py:536
  48.8 12.8 %collective-permute-start.7 = (bf16[3,48,1280]{2,1,0:T(8,128)(2,1)S(1)}, bf16[3,48,1280]{2,1,0:T(8,128)(2,1)S(1)}, u32[]{:S(2)}, u32[]{:S(2)}) collective-permute-start(bf16[3,48,1280]{2,1,0:T(8,128)(2,1)S(1)} %pad_maximum_fusion.4.refs_0_), channel_id=1, source_target_pairs={{0,2},{1,3},{2,0},{3,1},{4,6},{5,7},{6,4},{7,5},{8,10},{9,11},{10,... | collective-permute-start | bytes 1105928 | tf_op jit(solution)/shard_map/ppermute | solution.py:67
  51.4 10.3 %collective-permute-start.11 = (bf16[3,48,1280]{2,1,0:T(8,128)(2,1)S(1)}, bf16[3,48,1280]{2,1,0:T(8,128)(2,1)S(1)}, u32[]{:S(2)}, u32[]{:S(2)}) collective-permute-start(bf16[3,48,1280]{2,1,0:T(8,128)(2,1)S(1)} %pad_maximum_fusion.4.refs_0_), channel_id=1, source_target_pairs={{0,1},{1,0},{2,3},{3,2},{4,5},{5,4},{6,7},{7,6},{8,9},{9,8},{10,11... | collective-permute-start | bytes 1105928 | tf_op jit(solution)/shard_map/ppermute | solution.py:565
  61.1 16.1 %collective-permute-start.23 = (bf16[3,48,1920]{2,1,0:T(8,128)(2,1)S(1)}, bf16[3,48,1920]{2,1,0:T(8,128)(2,1)S(1)}, u32[]{:S(2)}, u32[]{:S(2)}) collective-permute-start(bf16[3,48,1920]{2,1,0:T(8,128)(2,1)S(1)} %pad_maximum_fusion.2.refs_0_), channel_id=1, source_target_pairs={{0,16},{1,17},{2,18},{3,19},{4,20},{5,21},{6,22},{7,23},{8,24},{9,... | collective-permute-start | bytes 1658888 | tf_op jit(solution)/shard_map/ppermute | solution.py:67
  61.6 17.7 %collective-permute-start.29 = (bf16[3,48,1920]{2,1,0:T(8,128)(2,1)S(1)}, bf16[3,48,1920]{2,1,0:T(8,128)(2,1)S(1)}, u32[]{:S(2)}, u32[]{:S(2)}) collective-permute-start(bf16[3,48,1920]{2,1,0:T(8,128)(2,1)S(1)} %pad_maximum_fusion.2.refs_0_), channel_id=1, source_target_pairs={{0,1},{1,0},{2,3},{3,2},{4,5},{5,4},{6,7},{7,6},{8,9},{9,8},{10,11... | collective-permute-start | bytes 1658888 | tf_op jit(solution)/shard_map/ppermute | solution.py:565
  64.0 13.7 %collective-permute-start.13 = (bf16[3,48,1280]{2,1,0:T(8,128)(2,1)S(1)}, bf16[3,48,1280]{2,1,0:T(8,128)(2,1)S(1)}, u32[]{:S(2)}, u32[]{:S(2)}) collective-permute-start(bf16[3,48,1280]{2,1,0:T(8,128)(2,1)S(1)} %collective-permute-done.5.refs_2_), channel_id=1, source_target_pairs={{0,1},{1,0},{2,3},{3,2},{4,5},{5,4},{6,7},{7,6},{8,9},{9,8},{10,11... | collective-permute-start | bytes 1105928 | tf_op jit(solution)/shard_map/ppermute | solution.py:565
  64.2 13.4 %collective-permute-start.15 = (bf16[3,48,1280]{2,1,0:T(8,128)(2,1)S(1)}, bf16[3,48,1280]{2,1,0:T(8,128)(2,1)S(1)}, u32[]{:S(2)}, u32[]{:S(2)}) collective-permute-start(bf16[3,48,1280]{2,1,0:T(8,128)(2,1)S(1)} %collective-permute-done.7.refs_4_), channel_id=1, source_target_pairs={{0,1},{1,0},{2,3},{3,2},{4,5},{5,4},{6,7},{7,6},{8,9},{9,8},{10,11... | collective-permute-start | bytes 1105928 | tf_op jit(solution)/shard_map/ppermute | solution.py:565
  66.4 15.5 %collective-permute-start.48 = (bf16[3,192,384]{2,1,0:T(8,128)(2,1)}, bf16[3,192,384]{2,1,0:T(8,128)(2,1)S(1)}, u32[]{:S(2)}, u32[]{:S(2)}) collective-permute-start(bf16[3,192,384]{2,1,0:T(8,128)(2,1)} %pad_maximum_fusion.3.refs_0_), channel_id=1, source_target_pairs={{0,1},{1,0},{2,3},{3,2},{4,5},{5,4},{6,7},{7,6},{8,9},{9,8},{10,11... | collective-permute-start | bytes 1327112 | tf_op jit(solution)/shard_map/ppermute | solution.py:565
  77.1 29.7 %collective-permute-start.27 = (bf16[3,48,1920]{2,1,0:T(8,128)(2,1)S(1)}, bf16[3,48,1920]{2,1,0:T(8,128)(2,1)S(1)}, u32[]{:S(2)}, u32[]{:S(2)}) collective-permute-start(bf16[3,48,1920]{2,1,0:T(8,128)(2,1)S(1)} %collective-permute-done.23.refs_2_), channel_id=1, source_target_pairs={{0,2},{1,3},{2,0},{3,1},{4,6},{5,7},{6,4},{7,5},{8,10},{9,11},{10,... | collective-permute-start | bytes 1658888 | tf_op jit(solution)/shard_map/ppermute | solution.py:67
  77.7 18.9 %collective-permute-start.17 = (bf16[3,48,1280]{2,1,0:T(8,128)(2,1)S(1)}, bf16[3,48,1280]{2,1,0:T(8,128)(2,1)S(1)}, u32[]{:S(2)}, u32[]{:S(2)}) collective-permute-start(bf16[3,48,1280]{2,1,0:T(8,128)(2,1)S(1)} %collective-permute-done.9.refs_6_), channel_id=1, source_target_pairs={{0,1},{1,0},{2,3},{3,2},{4,5},{5,4},{6,7},{7,6},{8,9},{9,8},{10,11... | collective-permute-start | bytes 1105928 | tf_op jit(solution)/shard_map/ppermute | solution.py:565
  77.7 16.9 %collective-permute-start.24 = (bf16[1,48,1920]{2,1,0:T(8,128)(2,1)S(1)}, bf16[1,48,1920]{2,1,0:T(8,128)(2,1)S(1)}, u32[]{:S(2)}, u32[]{:S(2)}) collective-permute-start(bf16[1,48,1920]{2,1,0:T(8,128)(2,1)S(1)} %collective-permute-done.22.refs_1_), channel_id=1, source_target_pairs={{0,2},{1,3},{2,0},{3,1},{4,6},{5,7},{6,4},{7,5},{8,10},{9,11},{10,... | collective-permute-start | bytes 552968 | tf_op jit(solution)/shard_map/ppermute | solution.py:67
  79.3 15.7 %collective-permute-start.26 = (bf16[1,48,1920]{2,1,0:T(8,128)(2,1)S(1)}, bf16[1,48,1920]{2,1,0:T(8,128)(2,1)S(1)}, u32[]{:S(2)}, u32[]{:S(2)}) collective-permute-start(bf16[1,48,1920]{2,1,0:T(8,128)(2,1)S(1)} %collective-permute-done.22.refs_1_), channel_id=1, source_target_pairs={{0,16},{1,17},{2,18},{3,19},{4,20},{5,21},{6,22},{7,23},{8,24},{9,... | collective-permute-start | bytes 552968 | tf_op jit(solution)/shard_map/ppermute | solution.py:67
  81.9 30.6 %collective-permute-start.43 = (bf16[512,768]{1,0:T(8,128)(2,1)S(1)}, bf16[512,768]{1,0:T(8,128)(2,1)}, u32[]{:S(2)}, u32[]{:S(2)}) collective-permute-start(bf16[512,768]{1,0:T(8,128)(2,1)S(1)} %get-tuple-element.51), channel_id=1, source_target_pairs={{0,16},{16,0},{1,17},{17,1},{2,18},{18,2},{3,19},{19,3},{4,20},{20... | collective-permute-start | bytes 2359304 | tf_op jit(solution)/shard_map/ppermute | solution.py:581
  94.5 14.4 %collective-permute-start.25 = (bf16[3,48,1920]{2,1,0:T(8,128)(2,1)S(1)}, bf16[3,48,1920]{2,1,0:T(8,128)(2,1)}, u32[]{:S(2)}, u32[]{:S(2)}) collective-permute-start(bf16[3,48,1920]{2,1,0:T(8,128)(2,1)S(1)} %pad_maximum_fusion.2.refs_0_), channel_id=1, source_target_pairs={{0,2},{1,3},{2,0},{3,1},{4,6},{5,7},{6,4},{7,5},{8,10},{9,11},{10,... | collective-permute-start | bytes 1658888 | tf_op jit(solution)/shard_map/ppermute | solution.py:67
  95.1 11.8 %collective-permute-start.28 = (bf16[1,48,1920]{2,1,0:T(8,128)(2,1)S(1)}, bf16[1,48,1920]{2,1,0:T(8,128)(2,1)S(1)}, u32[]{:S(2)}, u32[]{:S(2)}) collective-permute-start(bf16[1,48,1920]{2,1,0:T(8,128)(2,1)S(1)} %collective-permute-done.24.refs_3_), channel_id=1, source_target_pairs={{0,16},{1,17},{2,18},{3,19},{4,20},{5,21},{6,22},{7,23},{8,24},{9,... | collective-permute-start | bytes 552968 | tf_op jit(solution)/shard_map/ppermute | solution.py:67
  96.6 10.8 %collective-permute-start.32 = (bf16[1,48,1920]{2,1,0:T(8,128)(2,1)S(1)}, bf16[1,48,1920]{2,1,0:T(8,128)(2,1)S(1)}, u32[]{:S(2)}, u32[]{:S(2)}) collective-permute-start(bf16[1,48,1920]{2,1,0:T(8,128)(2,1)S(1)} %collective-permute-done.24.refs_3_), channel_id=1, source_target_pairs={{0,1},{1,0},{2,3},{3,2},{4,5},{5,4},{6,7},{7,6},{8,9},{9,8},{10,11... | collective-permute-start | bytes 552968 | tf_op jit(solution)/shard_map/ppermute | solution.py:565
  107.4 12.5 %collective-permute-start.41 = (bf16[3,192,384]{2,1,0:T(8,128)(2,1)}, bf16[3,192,384]{2,1,0:T(8,128)(2,1)}, u32[]{:S(2)}, u32[]{:S(2)}) collective-permute-start(bf16[3,192,384]{2,1,0:T(8,128)(2,1)} %pad_maximum_fusion.3.refs_0_), channel_id=1, source_target_pairs={{0,16},{1,17},{2,18},{3,19},{4,20},{5,21},{6,22},{7,23},{8,24},{9,... | collective-permute-start | bytes 1327112 | tf_op jit(solution)/shard_map/ppermute | solution.py:67
  108.9 22.8 %collective-permute-start.33 = (bf16[3,48,1920]{2,1,0:T(8,128)(2,1)}, bf16[3,48,1920]{2,1,0:T(8,128)(2,1)}, u32[]{:S(2)}, u32[]{:S(2)}) collective-permute-start(bf16[3,48,1920]{2,1,0:T(8,128)(2,1)} %collective-permute-done.25.refs_4_), channel_id=1, source_target_pairs={{0,1},{1,0},{2,3},{3,2},{4,5},{5,4},{6,7},{7,6},{8,9},{9,8},{10,11... | collective-permute-start | bytes 1658888 | tf_op jit(solution)/shard_map/ppermute | solution.py:565
  111.1 22.7 %collective-permute-start.35 = (bf16[3,48,1920]{2,1,0:T(8,128)(2,1)S(1)}, bf16[3,48,1920]{2,1,0:T(8,128)(2,1)}, u32[]{:S(2)}, u32[]{:S(2)}) collective-permute-start(bf16[3,48,1920]{2,1,0:T(8,128)(2,1)S(1)} %collective-permute-done.27.refs_6_), channel_id=1, source_target_pairs={{0,1},{1,0},{2,3},{3,2},{4,5},{5,4},{6,7},{7,6},{8,9},{9,8},{10,11... | collective-permute-start | bytes 1658888 | tf_op jit(solution)/shard_map/ppermute | solution.py:565
  112.5 45.8 %collective-permute-start.44 = (bf16[3,192,384]{2,1,0:T(8,128)(2,1)}, bf16[3,192,384]{2,1,0:T(8,128)(2,1)S(1)}, u32[]{:S(2)}, u32[]{:S(2)}) collective-permute-start(bf16[3,192,384]{2,1,0:T(8,128)(2,1)} %pad_maximum_fusion.3.refs_0_), channel_id=1, source_target_pairs={{0,2},{1,3},{2,0},{3,1},{4,6},{5,7},{6,4},{7,5},{8,10},{9,11},{10,... | collective-permute-start | bytes 1327112 | tf_op jit(solution)/shard_map/ppermute | solution.py:67
  113.4 19.8 %collective-permute-start.42 = (bf16[1,192,384]{2,1,0:T(8,128)(2,1)}, bf16[1,192,384]{2,1,0:T(8,128)(2,1)S(1)}, u32[]{:S(2)}, u32[]{:S(2)}) collective-permute-start(bf16[1,192,384]{2,1,0:T(8,128)(2,1)} %collective-permute-done.40.refs_1_), channel_id=1, source_target_pairs={{0,2},{1,3},{2,0},{3,1},{4,6},{5,7},{6,4},{7,5},{8,10},{9,11},{10,... | collective-permute-start | bytes 442376 | tf_op jit(solution)/shard_map/ppermute | solution.py:67
  119.9 38.6 %collective-permute-start.46 = (bf16[3,192,384]{2,1,0:T(8,128)(2,1)}, bf16[3,192,384]{2,1,0:T(8,128)(2,1)S(1)}, u32[]{:S(2)}, u32[]{:S(2)}) collective-permute-start(bf16[3,192,384]{2,1,0:T(8,128)(2,1)} %collective-permute-done.41.refs_2_), channel_id=1, source_target_pairs={{0,2},{1,3},{2,0},{3,1},{4,6},{5,7},{6,4},{7,5},{8,10},{9,11},{10,... | collective-permute-start | bytes 1327112 | tf_op jit(solution)/shard_map/ppermute | solution.py:67
  131.7 25.6 %collective-permute-start.45 = (bf16[1,192,384]{2,1,0:T(8,128)(2,1)}, bf16[1,192,384]{2,1,0:T(8,128)(2,1)S(1)}, u32[]{:S(2)}, u32[]{:S(2)}) collective-permute-start(bf16[1,192,384]{2,1,0:T(8,128)(2,1)} %collective-permute-done.40.refs_1_), channel_id=1, source_target_pairs={{0,16},{1,17},{2,18},{3,19},{4,20},{5,21},{6,22},{7,23},{8,24},{9,... | collective-permute-start | bytes 442376 | tf_op jit(solution)/shard_map/ppermute | solution.py:67
  133.3 24.6 %collective-permute-start.47 = (bf16[1,192,384]{2,1,0:T(8,128)(2,1)S(1)}, bf16[1,192,384]{2,1,0:T(8,128)(2,1)S(1)}, u32[]{:S(2)}, u32[]{:S(2)}) collective-permute-start(bf16[1,192,384]{2,1,0:T(8,128)(2,1)S(1)} %collective-permute-done.42.refs_3_), channel_id=1, source_target_pairs={{0,16},{1,17},{2,18},{3,19},{4,20},{5,21},{6,22},{7,23},{8,24},{9,... | collective-permute-start | bytes 442376 | tf_op jit(solution)/shard_map/ppermute | solution.py:67
  133.8 24.1 %collective-permute-start.51 = (bf16[1,192,384]{2,1,0:T(8,128)(2,1)S(1)}, bf16[1,192,384]{2,1,0:T(8,128)(2,1)S(1)}, u32[]{:S(2)}, u32[]{:S(2)}) collective-permute-start(bf16[1,192,384]{2,1,0:T(8,128)(2,1)S(1)} %collective-permute-done.42.refs_3_), channel_id=1, source_target_pairs={{0,1},{1,0},{2,3},{3,2},{4,5},{5,4},{6,7},{7,6},{8,9},{9,8},{10,11... | collective-permute-start | bytes 442376 | tf_op jit(solution)/shard_map/ppermute | solution.py:565
  157.3 35.0 %collective-permute-start.53 = (bf16[1,192,384]{2,1,0:T(8,128)(2,1)S(1)}, bf16[1,192,384]{2,1,0:T(8,128)(2,1)S(1)}, u32[]{:S(2)}, u32[]{:S(2)}) collective-permute-start(bf16[1,192,384]{2,1,0:T(8,128)(2,1)S(1)} %collective-permute-done.45.refs_5_), channel_id=1, source_target_pairs={{0,1},{1,0},{2,3},{3,2},{4,5},{5,4},{6,7},{7,6},{8,9},{9,8},{10,11... | collective-permute-start | bytes 442376 | tf_op jit(solution)/shard_map/ppermute | solution.py:565
  157.9 34.6 %collective-permute-start.55 = (bf16[1,192,384]{2,1,0:T(8,128)(2,1)S(1)}, bf16[1,192,384]{2,1,0:T(8,128)(2,1)S(1)}, u32[]{:S(2)}, u32[]{:S(2)}) collective-permute-start(bf16[1,192,384]{2,1,0:T(8,128)(2,1)S(1)} %collective-permute-done.47.refs_7_), channel_id=1, source_target_pairs={{0,1},{1,0},{2,3},{3,2},{4,5},{5,4},{6,7},{7,6},{8,9},{9,8},{10,11... | collective-permute-start | bytes 442376 | tf_op jit(solution)/shard_map/ppermute | solution.py:565
  157.9 34.5 %collective-permute-start.50 = (bf16[3,192,384]{2,1,0:T(8,128)(2,1)}, bf16[3,192,384]{2,1,0:T(8,128)(2,1)S(1)}, u32[]{:S(2)}, u32[]{:S(2)}) collective-permute-start(bf16[3,192,384]{2,1,0:T(8,128)(2,1)} %collective-permute-done.41.refs_2_), channel_id=1, source_target_pairs={{0,1},{1,0},{2,3},{3,2},{4,5},{5,4},{6,7},{7,6},{8,9},{9,8},{10,11... | collective-permute-start | bytes 1327112 | tf_op jit(solution)/shard_map/ppermute | solution.py:565
  158.4 34.1 %collective-permute-start.52 = (bf16[3,192,384]{2,1,0:T(8,128)(2,1)S(1)}, bf16[3,192,384]{2,1,0:T(8,128)(2,1)S(1)}, u32[]{:S(2)}, u32[]{:S(2)}) collective-permute-start(bf16[3,192,384]{2,1,0:T(8,128)(2,1)S(1)} %collective-permute-done.44.refs_4_), channel_id=1, source_target_pairs={{0,1},{1,0},{2,3},{3,2},{4,5},{5,4},{6,7},{7,6},{8,9},{9,8},{10,11... | collective-permute-start | bytes 1327112 | tf_op jit(solution)/shard_map/ppermute | solution.py:565
  158.5 34.1 %collective-permute-start.54 = (bf16[3,192,384]{2,1,0:T(8,128)(2,1)S(1)}, bf16[3,192,384]{2,1,0:T(8,128)(2,1)S(1)}, u32[]{:S(2)}, u32[]{:S(2)}) collective-permute-start(bf16[3,192,384]{2,1,0:T(8,128)(2,1)S(1)} %collective-permute-done.46.refs_6_), channel_id=1, source_target_pairs={{0,1},{1,0},{2,3},{3,2},{4,5},{5,4},{6,7},{7,6},{8,9},{9,8},{10,11... | collective-permute-start | bytes 1327112 | tf_op jit(solution)/shard_map/ppermute | solution.py:565
  192.3 122.4 %collective-permute-start.76 = (bf16[16,192,384]{2,1,0:T(8,128)(2,1)}, bf16[16,192,384]{2,1,0:T(8,128)(2,1)S(1)}, u32[]{:S(2)}, u32[]{:S(2)}) collective-permute-start(bf16[16,192,384]{2,1,0:T(8,128)(2,1)} %get-tuple-element.70), channel_id=1, source_target_pairs={{0,1},{1,0},{2,3},{3,2},{4,5},{5,4},{6,7},{7,6},{8,9},{9,8},{10,11... | collective-permute-start | bytes 7077896 | tf_op jit(solution)/shard_map/ppermute | solution.py:85
  206.7 100.4 %collective-permute-start.56 = (bf16[512,768]{1,0:T(8,128)(2,1)S(1)}, bf16[512,768]{1,0:T(8,128)(2,1)}, u32[]{:S(2)}, u32[]{:S(2)}) collective-permute-start(bf16[512,768]{1,0:T(8,128)(2,1)S(1)} %slice.500), channel_id=1, source_target_pairs={{0,16},{16,0},{1,17},{17,1},{2,18},{18,2},{3,19},{19,3},{4,20},{20... | collective-permute-start | bytes 2359304 | tf_op jit(solution)/shard_map/ppermute | solution.py:726
  292.3 19.8 %collective-permute-start.57 = (bf16[512,768]{1,0:T(8,128)(2,1)}, bf16[512,768]{1,0:T(8,128)(2,1)}, u32[]{:S(2)}, u32[]{:S(2)}) collective-permute-start(bf16[512,768]{1,0:T(8,128)(2,1)} %slice.502), channel_id=1, source_target_pairs={{0,16},{16,0},{1,17},{17,1},{2,18},{18,2},{3,19},{19,3},{4,20},{20... | collective-permute-start | bytes 2359304 | tf_op jit(solution)/shard_map/ppermute | solution.py:726
  305.1 12.0 %collective-permute-start.58 = (bf16[16,48,1152]{2,1,0:T(8,128)(2,1)}, bf16[16,48,1152]{2,1,0:T(8,128)(2,1)S(1)}, u32[]{:S(2)}, u32[]{:S(2)}) collective-permute-start(bf16[16,48,1152]{2,1,0:T(8,128)(2,1)} %get-tuple-element.64), channel_id=1, source_target_pairs={{0,1},{1,0},{2,3},{3,2},{4,5},{5,4},{6,7},{7,6},{8,9},{9,8},{10,11... | collective-permute-start | bytes 5308424 | tf_op jit(solution)/shard_map/ppermute | solution.py:85
  305.3 77.2 %collective-permute-start.67 = (bf16[16,48,1920]{2,1,0:T(8,128)(2,1)S(1)}, bf16[16,48,1920]{2,1,0:T(8,128)(2,1)S(1)}, u32[]{:S(2)}, u32[]{:S(2)}) collective-permute-start(bf16[16,48,1920]{2,1,0:T(8,128)(2,1)S(1)} %pad_maximum_fusion.1), channel_id=1, source_target_pairs={{0,1},{1,0},{2,3},{3,2},{4,5},{5,4},{6,7},{7,6},{8,9},{9,8},{10,11... | collective-permute-start | bytes 8847368 | tf_op jit(solution)/shard_map/ppermute | solution.py:85
  315.8 48.3 %collective-permute-start.77 = (bf16[2,3,192,384]{3,2,1,0:T(8,128)(2,1)S(1)}, bf16[2,3,192,384]{3,2,1,0:T(8,128)(2,1)S(1)}, u32[]{:S(2)}, u32[]{:S(2)}) collective-permute-start(bf16[2,3,192,384]{3,2,1,0:T(8,128)(2,1)S(1)} %fusion.2), channel_id=1, source_target_pairs={{0,2},{1,3},{2,0},{3,1},{4,6},{5,7},{6,4},{7,5},{8,10},{9,11},{10,... | collective-permute-start | bytes 2654216 | tf_op jit(solution)/shard_map/ppermute | solution.py:99
  317.2 34.3 %collective-permute-start.59 = (bf16[2,3,48,1152]{3,2,1,0:T(8,128)(2,1)S(1)}, bf16[2,3,48,1152]{3,2,1,0:T(8,128)(2,1)S(1)}, u32[]{:S(2)}, u32[]{:S(2)}) collective-permute-start(bf16[2,3,48,1152]{3,2,1,0:T(8,128)(2,1)S(1)} %fusion.4), channel_id=1, source_target_pairs={{0,2},{1,3},{2,0},{3,1},{4,6},{5,7},{6,4},{7,5},{8,10},{9,11},{10,... | collective-permute-start | bytes 1990664 | tf_op jit(solution)/shard_map/ppermute | solution.py:99
  318.2 36.3 %collective-permute-start.81 = (bf16[2,1,192,384]{3,2,1,0:T(8,128)(2,1)S(1)}, bf16[2,1,192,384]{3,2,1,0:T(8,128)(2,1)S(1)}, u32[]{:S(2)}, u32[]{:S(2)}) collective-permute-start(bf16[2,1,192,384]{3,2,1,0:T(8,128)(2,1)S(1)} %fusion.14), channel_id=1, source_target_pairs={{0,16},{1,17},{2,18},{3,19},{4,20},{5,21},{6,22},{7,23},{8,24},{9,... | collective-permute-start | bytes 884744 | tf_op jit(solution)/shard_map/ppermute | solution.py:99
  319.2 34.0 %collective-permute-start.63 = (bf16[2,1,48,1152]{3,2,1,0:T(8,128)(2,1)S(1)}, bf16[2,1,48,1152]{3,2,1,0:T(8,128)(2,1)S(1)}, u32[]{:S(2)}, u32[]{:S(2)}) collective-permute-start(bf16[2,1,48,1152]{3,2,1,0:T(8,128)(2,1)S(1)} %fusion.22), channel_id=1, source_target_pairs={{0,16},{1,17},{2,18},{3,19},{4,20},{5,21},{6,22},{7,23},{8,24},{9,... | collective-permute-start | bytes 663560 | tf_op jit(solution)/shard_map/ppermute | solution.py:99
  351.7 9.3 %collective-permute-start.60 = (bf16[3,48,1152]{2,1,0:T(8,128)(2,1)S(1)}, bf16[3,48,1152]{2,1,0:T(8,128)(2,1)S(1)}, u32[]{:S(2)}, u32[]{:S(2)}) collective-permute-start(bf16[3,48,1152]{2,1,0:T(8,128)(2,1)S(1)} %fusion.5), channel_id=1, source_target_pairs={{0,16},{1,17},{2,18},{3,19},{4,20},{5,21},{6,22},{7,23},{8,24},{9,... | collective-permute-start | bytes 995336 | tf_op jit(solution)/shard_map/ppermute | solution.py:99
  354.6 18.9 %collective-permute-start.82 = (bf16[1,192,384]{2,1,0:T(8,128)(2,1)S(1)}, bf16[1,192,384]{2,1,0:T(8,128)(2,1)S(1)}, u32[]{:S(2)}, u32[]{:S(2)}) collective-permute-start(bf16[1,192,384]{2,1,0:T(8,128)(2,1)S(1)} %fusion.16), channel_id=1, source_target_pairs={{0,2},{1,3},{2,0},{3,1},{4,6},{5,7},{6,4},{7,5},{8,10},{9,11},{10,... | collective-permute-start | bytes 442376 | tf_op jit(solution)/shard_map/ppermute | solution.py:99
  364.1 9.2 %collective-permute-start.62 = (bf16[48,1152]{1,0:T(8,128)(2,1)S(1)}, bf16[48,1152]{1,0:T(8,128)(2,1)S(1)}, u32[]{:S(2)}, u32[]{:S(2)}) collective-permute-start(bf16[48,1152]{1,0:T(8,128)(2,1)S(1)} %get-tuple-element.82), channel_id=1, source_target_pairs={{0,8},{1,9},{2,10},{3,11},{4,12},{5,13},{6,14},{7,15},{8,0},{9,1},... | collective-permute-start | bytes 331784 | tf_op jit(solution)/shard_map/ppermute | solution.py:109
  364.1 9.2 %collective-permute-start.61 = (bf16[48,1152]{1,0:T(8,128)(2,1)S(1)}, bf16[48,1152]{1,0:T(8,128)(2,1)S(1)}, u32[]{:S(2)}, u32[]{:S(2)}) collective-permute-start(bf16[48,1152]{1,0:T(8,128)(2,1)S(1)} %get-tuple-element.81), channel_id=1, source_target_pairs={{0,4},{1,5},{2,6},{3,7},{4,8},{5,9},{6,10},{7,11},{8,12},{9,13},{1... | collective-permute-start | bytes 331784 | tf_op jit(solution)/shard_map/ppermute | solution.py:109
  373.4 10.6 %collective-permute-start.66 = (bf16[24,1152]{1,0:T(8,128)(2,1)S(1)}, bf16[24,1152]{1,0:T(8,128)(2,1)S(1)}, u32[]{:S(2)}, u32[]{:S(2)}) collective-permute-start(bf16[24,1152]{1,0:T(8,128)(2,1)S(1)} %dynamic-slice_convert_fusion.2), channel_id=1, source_target_pairs={{0,1},{1,0},{2,3},{3,2},{4,5},{5,4},{6,7},{7,6},{8,9},{9,8},{10,11... | collective-permute-start | bytes 165896 | tf_op jit(solution)/shard_map/ppermute | solution.py:682
  376.8 30.8 %collective-permute-start.83 = (bf16[192,384]{1,0:T(8,128)(2,1)S(1)}, bf16[192,384]{1,0:T(8,128)(2,1)S(1)}, u32[]{:S(2)}, u32[]{:S(2)}) collective-permute-start(bf16[192,384]{1,0:T(8,128)(2,1)S(1)} %get-tuple-element.80), channel_id=1, source_target_pairs={{0,12},{1,13},{2,14},{3,15},{4,0},{5,1},{6,2},{7,3},{8,4},{9,5},{1... | collective-permute-start | bytes 442376 | tf_op jit(solution)/shard_map/ppermute | solution.py:109
  380.9 26.6 %collective-permute-start.80 = (bf16[192,384]{1,0:T(8,128)(2,1)S(1)}, bf16[192,384]{1,0:T(8,128)(2,1)S(1)}, u32[]{:S(2)}, u32[]{:S(2)}) collective-permute-start(bf16[192,384]{1,0:T(8,128)(2,1)S(1)} %get-tuple-element.78), channel_id=1, source_target_pairs={{0,8},{1,9},{2,10},{3,11},{4,12},{5,13},{6,14},{7,15},{8,0},{9,1},... | collective-permute-start | bytes 442376 | tf_op jit(solution)/shard_map/ppermute | solution.py:109
  382.5 25.0 %collective-permute-start.79 = (bf16[192,384]{1,0:T(8,128)(2,1)S(1)}, bf16[192,384]{1,0:T(8,128)(2,1)S(1)}, u32[]{:S(2)}, u32[]{:S(2)}) collective-permute-start(bf16[192,384]{1,0:T(8,128)(2,1)S(1)} %get-tuple-element.77), channel_id=1, source_target_pairs={{0,4},{1,5},{2,6},{3,7},{4,8},{5,9},{6,10},{7,11},{8,12},{9,13},{1... | collective-permute-start | bytes 442376 | tf_op jit(solution)/shard_map/ppermute | solution.py:109
  382.8 23.1 %collective-permute-start.68 = (bf16[2,3,48,1920]{3,2,1,0:T(8,128)(2,1)S(1)}, bf16[2,3,48,1920]{3,2,1,0:T(8,128)(2,1)S(1)}, u32[]{:S(2)}, u32[]{:S(2)}) collective-permute-start(bf16[2,3,48,1920]{3,2,1,0:T(8,128)(2,1)S(1)} %fusion), channel_id=1, source_target_pairs={{0,2},{1,3},{2,0},{3,1},{4,6},{5,7},{6,4},{7,5},{8,10},{9,11},{10,... | collective-permute-start | bytes 3317768 | tf_op jit(solution)/shard_map/ppermute | solution.py:99
  384.9 21.3 %collective-permute-start.72 = (bf16[2,1,48,1920]{3,2,1,0:T(8,128)(2,1)S(1)}, bf16[2,1,48,1920]{3,2,1,0:T(8,128)(2,1)S(1)}, u32[]{:S(2)}, u32[]{:S(2)}) collective-permute-start(bf16[2,1,48,1920]{3,2,1,0:T(8,128)(2,1)S(1)} %fusion.6), channel_id=1, source_target_pairs={{0,16},{1,17},{2,18},{3,19},{4,20},{5,21},{6,22},{7,23},{8,24},{9,... | collective-permute-start | bytes 1105928 | tf_op jit(solution)/shard_map/ppermute | solution.py:99
  406.1 9.6 %collective-permute-start.69 = (bf16[3,48,1920]{2,1,0:T(8,128)(2,1)S(1)}, bf16[3,48,1920]{2,1,0:T(8,128)(2,1)S(1)}, u32[]{:S(2)}, u32[]{:S(2)}) collective-permute-start(bf16[3,48,1920]{2,1,0:T(8,128)(2,1)S(1)} %fusion.1), channel_id=1, source_target_pairs={{0,16},{1,17},{2,18},{3,19},{4,20},{5,21},{6,22},{7,23},{8,24},{9,... | collective-permute-start | bytes 1658888 | tf_op jit(solution)/shard_map/ppermute | solution.py:99
  407.7 12.1 %collective-permute-start.84 = (bf16[96,384]{1,0:T(8,128)(2,1)S(1)}, bf16[96,384]{1,0:T(8,128)(2,1)S(1)}, u32[]{:S(2)}, u32[]{:S(2)}) collective-permute-start(bf16[96,384]{1,0:T(8,128)(2,1)S(1)} %dynamic-slice_convert_fusion.1), channel_id=1, source_target_pairs={{0,1},{1,0},{2,3},{3,2},{4,5},{5,4},{6,7},{7,6},{8,9},{9,8},{10,11... | collective-permute-start | bytes 221192 | tf_op jit(solution)/shard_map/ppermute | solution.py:682
  418.7 10.3 %collective-permute-start.71 = (bf16[48,1920]{1,0:T(8,128)(2,1)S(1)}, bf16[48,1920]{1,0:T(8,128)(2,1)S(1)}, u32[]{:S(2)}, u32[]{:S(2)}) collective-permute-start(bf16[48,1920]{1,0:T(8,128)(2,1)S(1)} %get-tuple-element.76), channel_id=1, source_target_pairs={{0,8},{1,9},{2,10},{3,11},{4,12},{5,13},{6,14},{7,15},{8,0},{9,1},... | collective-permute-start | bytes 552968 | tf_op jit(solution)/shard_map/ppermute | solution.py:109
  419.5 9.4 %collective-permute-start.70 = (bf16[48,1920]{1,0:T(8,128)(2,1)S(1)}, bf16[48,1920]{1,0:T(8,128)(2,1)S(1)}, u32[]{:S(2)}, u32[]{:S(2)}) collective-permute-start(bf16[48,1920]{1,0:T(8,128)(2,1)S(1)} %get-tuple-element.75), channel_id=1, source_target_pairs={{0,4},{1,5},{2,6},{3,7},{4,8},{5,9},{6,10},{7,11},{8,12},{9,13},{1... | collective-permute-start | bytes 552968 | tf_op jit(solution)/shard_map/ppermute | solution.py:109
  (77 other events, 1255.7 us)

commit v2 on v1

--- a/solution.py
+++ b/solution.py
@@ -1,4 +1,5 @@
 import functools
+import math
 
 import jax
 import jax.numpy as jnp
@@ -16,6 +17,7 @@
 BF16 = jnp.bfloat16
 F32 = jnp.float32
 VMEM_BYTES = 58 * 1024 * 1024
+SPARE_BYTES = 10 * 1024 * 1024
 
 
 class Grid:
@@ -56,8 +58,8 @@
     return (coords["x"] * grid.ny + coords["y"]) * grid.nz + coords["z"]
 
 
-def after(value, *earlier):
-    return lax.optimization_barrier((value,) + earlier)[0]
+def together(*values):
+    return lax.optimization_barrier(values)
 
 
 def exchange(grid, parts, axis):
@@ -76,38 +78,56 @@
 
 def gather_along_z(grid, piece):
     parts = [(piece[None], [{"x": 0, "y": 0, "z": 0}])]
-    parts = parts + exchange(grid, parts, "z")
-    cut = max(1, (3 * len(parts)) // 4)
-    return joined_parts(parts[:cut]), joined_parts(parts[cut:])
-
-
-def scatter_sum(grid, mine, other):
+    return parts + exchange(grid, parts, "z")
+
+
+def lots_of(parts, cut):
+    cut = min(cut, len(parts))
+    return [joined_parts(p) for p in (parts[:cut], parts[cut:]) if p]
+
+
+def arrays_of(parts):
+    return [a for a, _ in parts]
+
+
+def with_arrays(parts, arrays):
+    return [(a, s) for a, (_, s) in zip(arrays, parts)]
+
+
+def scatter_steps(grid, mine, other, cut):
     got = lax.ppermute(other, AXES, grid.core_swap())
+    (got,) = yield [got]
     shape = (grid.ny, grid.nx, grid.nz) + mine.shape[1:]
     mine, got = mine.reshape(shape), got.reshape(shape)
-    cut = max(1, (3 * grid.nz) // 4)
-    kept = []
-    for lo, hi, first in ((0, cut, "y"), (cut, grid.nz, "x")):
-        second = "x" if first == "y" else "y"
-        current = [mine[:, :, lo:hi], got[:, :, lo:hi]]
-        for axis in (first, second):
-            dim = 0 if axis == "y" else 1 - (first == "y")
+    cut = min(cut, grid.nz)
+    lots = [(lo, hi, axes) for lo, hi, axes in ((0, cut, "yx"), (cut, grid.nz, "xy")) if hi > lo]
+    current = [[mine[:, :, lo:hi], got[:, :, lo:hi]] for lo, hi, _ in lots]
+    for step in range(2):
+        waiting = []
+        for n, (_, _, axes) in enumerate(lots):
+            axis = axes[step]
+            dim = 1 if axis == "x" and step == 0 else 0
             pieces = [
-                [lax.index_in_dim(c, k, dim, keepdims=False) for c in current] for k in range(grid.sizes[axis])
+                [lax.index_in_dim(c, k, dim, keepdims=False) for c in current[n]] for k in range(grid.sizes[axis])
             ]
             received = [
                 lax.ppermute(add_all(pieces[k]).astype(BF16), AXES, grid.shift(axis, k))
                 for k in range(1, grid.sizes[axis])
             ]
-            current = pieces[0] + received
-        kept.append(current)
+            waiting.append(received)
+            current[n] = pieces[0]
+        flat = yield [a for received in waiting for a in received]
+        flat = list(flat)
+        for n, received in enumerate(waiting):
+            current[n] = current[n] + flat[: len(received)]
+            flat = flat[len(received) :]
     final = []
     for k in range(grid.nz):
-        group = kept[0] if k < cut else kept[1]
-        at = k if k < cut else k - cut
-        total = add_all([c[at] for c in group])
+        n = 0 if k < lots[0][1] else 1
+        total = add_all([c[k - lots[n][0]] for c in current[n]])
         final.append(total if k == 0 else lax.ppermute(total.astype(BF16), AXES, grid.shift("z", k)))
-    return add_all(final)
+    final[1:] = yield final[1:]
+    yield add_all(final)
 
 
 def add_all(items):
@@ -304,25 +324,27 @@
     normed[...] = (z * gains[1:2, :]).astype(BF16)
 
 
-def up_kernel(pieces, n_refs, chips, rows_down, tab, normed, cot_own, cot_got, *refs):
-    sources, refs = refs[:n_refs], refs[n_refs:]
-    active, slope, down_mine, down_other, w_up, sems = refs
-    half, width = cot_own.shape
+def up_kernel(pieces, n_refs, chips, first, tab, normed, *refs):
+    sources, refs = refs[-n_refs - 4 : -4], refs[-4:]
+    active, slope, w_up, sems = refs
+    rows, width = normed.shape
     j = pl.program_id(0)
 
     @pl.when(j == 0)
     def _():
         wait_all(pieces.start(sources, tab, {"up": w_up}, sems, 0)["up"])
 
-    cols = pl.ds(pl.multiple_of(j * width, 128), width)
-
-    @pl.loop(0, 2 * half // 256)
-    def _(i):
-        rows = pl.ds(pl.multiple_of(i * 256, 256), 256)
+    cols = pl.ds(pl.multiple_of((first + j) * width, 128), width)
+    for i in range(rows // 256):
+        rows = slice(256 * i, 256 * (i + 1))
         a, s = gelu_both(nn(normed[rows, :], w_up[:, cols]))
         active[rows, :] = a.astype(BF16)
         slope[rows, :] = s.astype(BF16)
 
+
+def down_grad_kernel(chips, rows_down, tab, active, cot_own, cot_got, down_mine, down_other):
+    half, width = cot_own.shape
+    j = pl.program_id(0)
     for m in range(2):
         piece = slice(384 * m, 384 * (m + 1))
         grad = tn(active[:half, piece], cot_own[...]) + tn(active[half:, piece], cot_got[...])
@@ -344,10 +366,9 @@
 
     w_rows = pl.ds(pl.multiple_of(j * width, 256), width)
     for part, cot in enumerate((cot_own, cot_got)):
-        @pl.loop(0, half // 256)
-        def _(i):
-            inner = pl.ds(pl.multiple_of(i * 256, 256), 256)
-            rows = pl.ds(pl.multiple_of(part * half + i * 256, 256), 256)
+        for i in range(half // 256):
+            inner = slice(256 * i, 256 * (i + 1))
+            rows = slice(part * half + 256 * i, part * half + 256 * (i + 1))
             grad_up[rows, :] = (nt(cot[inner, :], w_down[w_rows, :]) * slope[rows, :].astype(F32)).astype(BF16)
 
     side = j // (steps // 2)
@@ -358,7 +379,7 @@
         emit(grad, side, start, rows_up, up_mine, up_other, pl.ds(pl.multiple_of(offset, 128), width), tab, chips)
 
 
-def up_back_kernel(pieces, n_refs, chips, rows_up, tab, grad_up, attended, gains, cot_own, cot_got, hidden, *refs):
+def up_back_kernel(pieces, n_refs, chips, rows_up, tab, grad_up, attended, gains, cot_own, cot_got, hidden, _mine, _other, *refs):
     sources, refs = refs[:n_refs], refs[n_refs:]
     grad_hidden, grad_att, out_mine, out_other, w_up, w_out, total_out, sems = refs
     i = pl.program_id(0)
@@ -432,35 +453,40 @@
         put(grad_v_ref, grad_v[0] + grad_v[1])
 
 
-def qkv_grad_kernel(chips, rows_qkv, tab, normed, grad_q, grad_k, grad_v, mine, other):
+def qkv_grad_kernel(chips, rows_qkv, cuts, tab, normed, *refs):
+    grads, mine, other = refs[:-2], refs[-2], refs[-1]
     width = normed.shape[1]
-    near = width // 2
-    for n, ref in enumerate((grad_q, grad_k, grad_v)):
+    wide = 3 * width // 2
+    for n, ref in enumerate(grads):
+        base = (n % 3) * width + cuts[n // 3]
+        size = ref.shape[1]
         for m in range(2):
             grad = tn(normed[:, 384 * m : 384 * (m + 1)], ref[...])
             start = place_of(384 * m, rows_qkv, chips)
-            for part in range(2):
-                at = n * width + part * near
-                side, column = at // (3 * near), at % (3 * near)
-                value = grad[:, part * near : (part + 1) * near]
-                emit(value, side, start, rows_qkv, mine, other, slice(column, column + near), tab, chips)
-
-
-def first_kernel(pieces, n_refs, chips, tab, own, got, gains, grad_q, grad_k, grad_v, grad_hidden, *refs):
-    sources, refs = refs[:n_refs], refs[n_refs:]
+            at = base
+            while at < base + size:
+                side = at // wide
+                end = min(base + size, (side + 1) * wide)
+                columns = slice(at - side * wide, end - side * wide)
+                emit(grad[:, at - base : end - base], side, start, rows_qkv, mine, other, columns, tab, chips)
+                at = end
+
+
+def first_kernel(pieces, n_refs, chips, cuts, tab, source, gains, grad_hidden, *refs):
+    n_grads = 3 * (len(cuts) - 1)
+    grads, sources, refs = refs[:n_grads], refs[n_grads : n_grads + n_refs], refs[n_grads + n_refs :]
     out, w_qkv, sems = refs
-    i = pl.program_id(0)
-    width = own.shape[1]
-
-    @pl.when(i == 0)
+    width = source.shape[1]
+
+    @pl.when(pl.program_id(0) == 0)
     def _():
         wait_all(pieces.start(sources, tab, {"qkv": w_qkv}, sems, 0)["qkv"])
 
-    x = jnp.where(i < pl.num_programs(0) // 2, own[...], got[...]).astype(F32)
-    e = nt(grad_q[...], w_qkv[:, :width])
-    e += nt(grad_k[...], w_qkv[:, width : 2 * width])
-    e += nt(grad_v[...], w_qkv[:, 2 * width :])
-    z, root = normalized(x)
+    e = 0.0
+    for n, grad in enumerate(grads):
+        base, lot = (n % 3) * width, n // 3
+        e = e + nt(grad[...], w_qkv[:, base + cuts[lot] : base + cuts[lot + 1]])
+    z, root = normalized(source[...].astype(F32))
     out[...] = (grad_hidden[...] + norm_back(z, root, e * gains[0:1, :])).astype(BF16)
 
 
@@ -468,14 +494,37 @@
     return pl.BlockSpec(shape, lambda *_: (0,) * len(shape))
 
 
-def call(kernel, tab, inputs, piece_arrays, outs, scratch, grid=(1,), cost=0):
+anywhere = pl.BlockSpec(memory_space=pl.ANY)
+
+
+def call(kernel, tab, inputs, piece_arrays, outs, scratch, grid=(1,), cost=0, aliases=None):
     specs = [spec or whole(a.shape) for a, spec in inputs]
     specs = specs + [pl.BlockSpec(memory_space=pl.ANY) for _ in piece_arrays]
+    blocks = [(a, spec) for a, spec in inputs] + [(o, spec) for o, spec in outs]
+    need = SPARE_BYTES
+    for array, spec in blocks:
+        if spec is anywhere:
+            continue
+        size = jnp.dtype(array.dtype).itemsize
+        for extent in spec.block_shape if spec else array.shape:
+            size *= extent
+        need += 2 * size
+    for buffer in scratch:
+        if hasattr(buffer, "shape") and buffer.dtype in (BF16, F32):
+            size = buffer.dtype.itemsize if hasattr(buffer.dtype, "itemsize") else jnp.dtype(buffer.dtype).itemsize
+            for extent in buffer.shape:
+                size *= extent
+            need += size
     moved = sum(a.size * a.dtype.itemsize for a, _ in inputs) + sum(a.size * a.dtype.itemsize for a in piece_arrays)
-    moved += sum(o.size * o.dtype.itemsize for o, _ in outs)
+    moved += sum(math.prod(o.shape) * jnp.dtype(o.dtype).itemsize for o, _ in outs)
+    inputs = [
+        (pltpu.with_memory_space_constraint(a, pltpu.HBM) if a.size > 2**21 and spec is not None else a, spec)
+        for a, spec in inputs
+    ]
     return pl.pallas_call(
         kernel,
         out_shape=[o for o, _ in outs],
+        input_output_aliases=aliases or {},
         grid_spec=pltpu.PrefetchScalarGridSpec(
             num_scalar_prefetch=1,
             grid=grid,
@@ -484,7 +533,7 @@
             scratch_shapes=scratch,
         ),
         compiler_params=pltpu.CompilerParams(
-            dimension_semantics=("arbitrary",) * len(grid), vmem_limit_bytes=VMEM_BYTES
+            dimension_semantics=("arbitrary",) * len(grid), vmem_limit_bytes=min(need, VMEM_BYTES)
         ),
         cost_estimate=pl.CostEstimate(flops=cost, bytes_accessed=moved, transcendentals=0),
     )(tab, *[a for a, _ in inputs], *piece_arrays)
@@ -533,52 +582,63 @@
     fields_b = [("up", 0, ff // 2, False), ("out", ff // 2, width // 2, False)]
     fields_c = [("down", 0, width // 2, False)]
     swap_core = functools.partial(lax.ppermute, axis_name=AXES, perm=grid.core_swap())
-    tok_got = lax.ppermute(tok_away, "seq", swap_x)
-
     if fast:
-        def sides(side):
-            return (
-                jnp.concatenate([side_of(w_qkv, side), gain_block], axis=1),
-                jnp.concatenate([side_of(w_up, side), side_of(w_out, side)], axis=1),
-                side_of(w_down, side),
-            )
-
-        def with_partner(keep, give):
-            other = swap_core(give)
+        def sides(side, group):
+            if group == 0:
+                return jnp.concatenate([side_of(w_qkv, side), gain_block], axis=1)
+            if group == 1:
+                return jnp.concatenate([side_of(w_up, side), side_of(w_out, side)], axis=1)
+            return side_of(w_down, side)
+
+        def with_partner(group):
+            keep, other = sides(core, group), swap_core(sides(1 - core, group))
             return jnp.concatenate(
                 [jnp.where(core == 0, keep, other), jnp.where(core == 0, other, keep)], axis=0
             )
 
-        pieces = [with_partner(k, g) for k, g in zip(sides(core), sides(1 - core))]
-        pieces_a, pieces_b, pieces_c = pieces
-
-        def plane(x_first, y_first):
-            near = exchange(grid, [x_first], "x"), exchange(grid, [y_first], "y")
-            straight = exchange(grid, [x_first], "y"), exchange(grid, [y_first], "x")
-            return near, straight
-
-        def corners(near):
-            return exchange(grid, near[0], "y") + exchange(grid, near[1], "x")
+        tok_away, w_qkv = together(tok_away, w_qkv)
+        tok_first = lax.ppermute(tok_away[: half // 2], "seq", swap_x)
+        piece_a = with_partner(0)
+        piece_a, w_up, w_out, w_down = together(piece_a, w_up, w_out, w_down)
+        piece_b, piece_c = with_partner(1), with_partner(2)
+
+        def near_of(lots):
+            return [exchange(grid, [lot], axis) for lot, axis in zip(lots, "xy")]
+
+        def widened(lots, near):
+            return [joined_parts([lot] + moved) for lot, moved in zip(lots, near)]
+
+        def far_of(wide):
+            far = []
+            for lot, axis in zip(wide, "yx"):
+                far += exchange(grid, [lot], axis)
+            return far
+
+        def flat(groups):
+            return [part for group in groups for part in group]
 
         def finish(mine, fields):
             mine = [(a, [rel_of(grid, s) for s in spots]) for a, spots in mine]
             theirs = [(swap_core(a), s) for a, s in mine]
             return Pieces(chips, mine, theirs, fields)
 
-        z_a = gather_along_z(grid, pieces_a)
-        near_a, straight_a = plane(*z_a)
-        far_a = corners(near_a)
-        z_b = gather_along_z(grid, after(pieces_b, z_a[0][0], z_a[1][0]))
-        z_c = gather_along_z(grid, after(pieces_c, z_b[0][0], z_b[1][0]))
-        group_a = finish(list(z_a) + near_a[0] + near_a[1] + straight_a[0] + straight_a[1] + far_a, fields_a)
-
-        def held(parts, *earlier):
-            arrays = lax.optimization_barrier(tuple(a for a, _ in parts) + earlier)
-            return [(a, s) for a, (_, s) in zip(arrays, parts)]
-
-        near_b, straight_b = plane(*held(z_b, *[a for a, _ in far_a]))
-        cot_away = after(cot_away, *[a for a, _ in far_a])
-        cot_got = lax.ppermute(cot_away, "seq", swap_x)
+        z_a = gather_along_z(grid, piece_a)
+        arrays, tok_first, piece_b, tok_next = together(arrays_of(z_a), tok_first, piece_b, tok_away[half // 2 :])
+        tok_second = lax.ppermute(tok_next, "seq", swap_x)
+        z_a = lots_of(with_arrays(z_a, arrays), 2)
+        near_a = near_of(z_a)
+        z_b = gather_along_z(grid, piece_b)
+        arrays, tok_second = together(arrays_of(flat(near_a)), tok_second)
+        tok_got = jnp.concatenate([tok_first, tok_second], axis=0)
+        wide_a = widened(z_a, [[part] for part in with_arrays(flat(near_a), arrays)])
+        far_a = far_of(wide_a)
+        all_a = wide_a + far_a
+        arrays_a, z_own, piece_c = together(arrays_of(all_a), z_b[0][0], piece_c)
+        z_b = with_arrays(z_b, [z_own] + arrays_of(z_b[1:]))
+        group_a = finish(with_arrays(all_a, arrays_a), fields_a)
+        arrays_b = lax.optimization_barrier(arrays_of(z_b))
+        z_b = lots_of(with_arrays(z_b, arrays_b), 2)
+        near_b = near_of(z_b)
     else:
         full = [lax.all_gather(w, AXES, axis=0, tiled=True) for w in (w_qkv, w_out, w_up, w_down, gain_block)]
 
@@ -592,6 +652,7 @@
         group_a = natural([full[0], full[4]], fields_a)
         group_b = natural([full[2], full[1]], fields_b)
         group_c = natural([full[3]], fields_c)
+        tok_got = lax.ppermute(tok_away, "seq", swap_x)
         cot_got = lax.ppermute(cot_away, "seq", swap_x)
 
     sds = jax.ShapeDtypeStruct
@@ -617,6 +678,12 @@
         cost=2 * rows * width * 3 * width,
     )
 
+    if fast:
+        packed, arrays_b, piece_c = together(packed, arrays_of(flat(near_b)), piece_c)
+        wide_b = widened(z_b, [[part] for part in with_arrays(flat(near_b), arrays_b)])
+        far_b = far_of(wide_b)
+        z_c = gather_along_z(grid, piece_c)
+
     clip_blocks = half // 256
     by_clip = lambda a: a.reshape(2, clip_blocks, 256, a.shape[1])
     heads_at = lambda base: pl.BlockSpec((2, 1, 256, 256), lambda b, g, t: (0, b, 0, base + g))
@@ -624,9 +691,6 @@
     clip_shape = low(2, clip_blocks, 256, width)
     step = width // 256
     qkv_in = [(by_clip(packed), heads_at(0)), (by_clip(packed), heads_at(step)), (by_clip(packed), heads_at(2 * step))]
-    if fast:
-        qkv_in = [(after(a, *[x for x, _ in near_b[0] + near_b[1]]), s) for a, s in qkv_in[:1]] + qkv_in[1:]
-        far_b = corners(near_b)
     attended, log_totals = call(
         functools.partial(attend_kernel, chips),
         tab,
@@ -640,9 +704,12 @@
     attended = attended.reshape(rows, width)
 
     if fast:
-        parts_b = list(z_b) + near_b[0] + near_b[1] + straight_b[0] + straight_b[1] + far_b
-        group_b = finish(parts_b, fields_b)
-        near_c, straight_c = plane(*held(z_c, *[a for a, _ in far_b]))
+        all_b = wide_b + far_b
+        attended, arrays_b, arrays_c = together(attended, arrays_of(all_b), arrays_of(z_c))
+        group_b = finish(with_arrays(all_b, arrays_b), fields_b)
+        z_c = lots_of(with_arrays(z_c, arrays_c), grid.nz)
+        near_c = exchange(grid, z_c, "x")
+        straight_c = exchange(grid, z_c, "y")
 
     hidden, normed_second = call(
         functools.partial(middle_kernel, group_b, len(group_b.arrays), chips),
@@ -655,78 +722,33 @@
         cost=2 * rows * width * width,
     )
 
+    steps = ff // width
+
+    def up_part_of(first, count, normed, earlier):
+        to = pl.BlockSpec((rows, width), lambda j, t: (0, first + j))
+        return call(
+            functools.partial(up_kernel, group_b, len(group_b.arrays), chips, first),
+            tab,
+            [(normed, None)] + [(a, anywhere) for a in earlier],
+            group_b.arrays,
+            [(pltpu.HBM((rows, ff), BF16), to), (pltpu.HBM((rows, ff), BF16), to)],
+            [vmem((width, ff), BF16), dma((group_b.copies(("up",)),))],
+            grid=(count,),
+            cost=2 * rows * width * width * count,
+            aliases={2: 0, 3: 1} if earlier else None,
+        )
+
+    active, slope = up_part_of(0, steps // 2, normed_second, [])
     if fast:
-        normed_up = after(normed_second, *[x for x, _ in near_c[0] + near_c[1]])
-        far_c = corners(near_c)
-    else:
-        normed_up = normed_second
-    steps = ff // width
-    down_out = low(chips, rows_c, width // 2)
-    active, slope, down_mine, down_other = call(
-        functools.partial(up_kernel, group_b, len(group_b.arrays), chips, rows_c),
-        tab,
-        [(normed_up, None), (cot_own, None), (cot_got, None)],
-        group_b.arrays,
-        [(low(rows, ff), chunk), (low(rows, ff), chunk), (down_out, None), (down_out, None)],
-        [vmem((width, ff), BF16), dma((group_b.copies(("up",)),))],
-        grid=(steps,),
-        cost=4 * rows * width * ff,
-    )
-
-    def sums(mine, other):
-        if fast:
-            total = scatter_sum(grid, mine, other)
-            height = total.shape[0] // 2
-            keep = lax.dynamic_slice(total, (core * height, 0), (height, total.shape[1]))
-            away = lax.dynamic_slice(total, ((1 - core) * height, 0), (height, total.shape[1]))
-            got = swap_core(away.astype(BF16)).astype(F32)
-            return jnp.where(core == 0, keep, got), jnp.where(core == 0, got, keep)
-        whole_sum = jnp.concatenate([mine[0], other[0]], axis=1)
-        total = lax.psum_scatter(whole_sum, AXES, scatter_dimension=0, tiled=True).astype(F32)
-        return total[:, : total.shape[1] // 2], total[:, total.shape[1] // 2 :]
-
-    left, right = sums(down_mine, down_other)
-    owned_down = jnp.concatenate([left, right], axis=1)
-
+        active, slope, normed_second, arrays_c, cot_away = together(active, slope, normed_second, arrays_of(near_c), cot_away)
+        near_c = with_arrays(near_c, arrays_c)
+        far_c = exchange(grid, near_c, "y")
+        cot_got = lax.ppermute(cot_away, "seq", swap_x)
+    active, slope = up_part_of(steps // 2, steps - steps // 2, normed_second, [active, slope])
     if fast:
-        group_c = finish(list(z_c) + near_c[0] + near_c[1] + straight_c[0] + straight_c[1] + far_c, fields_c)
-    up_out = low(chips, rows_a, ff // 2)
-    grad_up, up_mine, up_other = call(
-        functools.partial(down_back_kernel, group_c, len(group_c.arrays), chips, rows_a),
-        tab,
-        [(cot_own, None), (cot_got, None), (normed_second, None), (slope, chunk)],
-        group_c.arrays,
-        [(low(rows, ff), chunk), (up_out, None), (up_out, None)],
-        [vmem((ff, width), BF16), dma((group_c.copies(("down",)),))],
-        grid=(steps,),
-        cost=4 * rows * width * ff,
-    )
-    small_out = low(chips, rows_a, width // 2)
-    grad_hidden, grad_att, out_mine, out_other = call(
-        functools.partial(up_back_kernel, group_b, len(group_b.arrays), chips, rows_a),
-        tab,
-        [
-            (grad_up, tile(ff)), (attended, tile(width)), (gains, None), (cot_own, own_tile), (cot_got, got_tile),
-            (hidden, tile(width)),
-        ],
-        group_b.arrays,
-        [(sds((rows, width), F32), tile(width)), (low(rows, width), tile(width)), (small_out, None), (small_out, None)],
-        [vmem((width, ff), BF16), vmem((width, width), BF16), vmem((width, width), F32), dma((group_b.copies(("up", "out")),))],
-        grid=(tiles,),
-        cost=2 * rows * width * ff + 4 * rows * width * width,
-    )
-    left, right = sums(
-        jnp.concatenate([up_mine, out_mine], axis=2), jnp.concatenate([up_other, out_other], axis=2)
-    )
-    owned_up = jnp.concatenate([left[:, : ff // 2], right[:, : ff // 2]], axis=1)
-    owned_out = jnp.concatenate([left[:, ff // 2 :], right[:, ff // 2 :]], axis=1)
-
-    def joined(both):
-        own, away = both[:half], both[half:]
-        back = lax.ppermute(away, "seq", swap_x)
-        first = mx == 0
-        return jnp.concatenate([jnp.where(first, own, back), jnp.where(first, back, own)], axis=0)[None]
-
+        all_c = z_c + near_c + straight_c + far_c
+        active, slope, arrays_c, cot_got = together(active, slope, arrays_of(all_c), cot_got)
+        group_c = finish(with_arrays(all_c, arrays_c), fields_c)
     (outputs,) = call(
         functools.partial(output_kernel, group_c, len(group_c.arrays), chips),
         tab,
@@ -737,46 +759,160 @@
         grid=(tiles,),
         cost=2 * rows * width * ff,
     )
-    output_tokens = joined(outputs)
-
-    grads = call(
-        functools.partial(attend_back_kernel, chips),
+    outputs, active = together(outputs, active)
+    out_back = lax.ppermute(outputs[half:], "seq", swap_x)
+    down_out = low(chips, rows_c, width // 2)
+    down_mine, down_other = call(
+        functools.partial(down_grad_kernel, chips, rows_c),
+        tab,
+        [(active, chunk), (cot_own, None), (cot_got, None)],
+        [],
+        [(down_out, None), (down_out, None)],
+        [],
+        grid=(steps,),
+        cost=2 * rows * width * ff,
+    )
+
+    def steps_of(mine, other, cut):
+        if fast:
+            return scatter_steps(grid, mine, other, cut)
+
+        def plain():
+            whole_sum = jnp.concatenate([mine[0], other[0]], axis=1)
+            for _ in range(4):
+                yield []
+            yield lax.psum_scatter(whole_sum, AXES, scatter_dimension=0, tiled=True).astype(F32)
+
+        return plain()
+
+    def owned(total):
+        if not fast:
+            return total[:, : total.shape[1] // 2], total[:, total.shape[1] // 2 :]
+        height = total.shape[0] // 2
+        keep = lax.dynamic_slice(total, (core * height, 0), (height, total.shape[1]))
+        away = lax.dynamic_slice(total, ((1 - core) * height, 0), (height, total.shape[1]))
+        got = swap_core(away.astype(BF16)).astype(F32)
+        return jnp.where(core == 0, keep, got), jnp.where(core == 0, got, keep)
+
+    down_sum = steps_of(down_mine, down_other, 3)
+    arrived = next(down_sum)
+    def joined(own, back):
+        first = mx == 0
+        return jnp.concatenate([jnp.where(first, own, back), jnp.where(first, back, own)], axis=0)[None]
+
+    up_part = pl.BlockSpec((chips, rows_a, ff // 2), lambda *_: (0, 0, 0))
+    out_part = pl.BlockSpec((chips, rows_a, width // 2), lambda *_: (0, 0, ff // width))
+    up_out = low(chips, rows_a, ff // 2 + width // 2)
+    grad_up, up_mine, up_other = call(
+        functools.partial(down_back_kernel, group_c, len(group_c.arrays), chips, rows_a),
+        tab,
+        [(cot_own, None), (cot_got, None), (normed_second, None), (slope, chunk)],
+        group_c.arrays,
+        [(pltpu.HBM((rows, ff), BF16), chunk), (up_out, up_part), (up_out, up_part)],
+        [vmem((ff, width), BF16), dma((group_c.copies(("down",)),))],
+        grid=(steps,),
+        cost=4 * rows * width * ff,
+    )
+    grad_up, up_mine, up_other, out_back, arrived = together(grad_up, up_mine, up_other, out_back, arrived)
+    arrived = down_sum.send(arrived)
+    grad_hidden, grad_att, up_mine, up_other = call(
+        functools.partial(up_back_kernel, group_b, len(group_b.arrays), chips, rows_a),
         tab,
         [
-            (by_clip(packed), heads_at(0)), (by_clip(packed), heads_at(step)), (by_clip(packed), heads_at(2 * step)),
-            (by_clip(attended), heads_at(0)), (by_clip(grad_att), heads_at(0)), (log_totals, totals_at),
+            (grad_up, tile(ff)), (attended, tile(width)), (gains, None), (cot_own, own_tile), (cot_got, got_tile),
+            (hidden, tile(width)), (up_mine, anywhere), (up_other, anywhere),
         ],
-        [],
-        [(clip_shape, heads_at(0))] * 3,
-        [vmem((512, 512), F32)],
-        grid=(clip_blocks, heads // 4),
-        cost=30 * rows * 512 * width,
+        group_b.arrays,
+        [(sds((rows, width), F32), tile(width)), (low(rows, width), tile(width)), (up_out, out_part), (up_out, out_part)],
+        [vmem((width, ff), BF16), vmem((width, width), BF16), vmem((width, width), F32), dma((group_b.copies(("up", "out")),))],
+        grid=(tiles,),
+        cost=2 * rows * width * ff + 4 * rows * width * width,
+        aliases={7: 2, 8: 3},
     )
-    grads = [g.reshape(rows, width) for g in grads]
+    grad_att, grad_hidden, up_mine, up_other, arrived = together(grad_att, grad_hidden, up_mine, up_other, arrived)
+    arrived = down_sum.send(arrived)
+    up_sum = steps_of(up_mine, up_other, 2)
+    arrived_up = next(up_sum)
+
+    groups = heads // 4
+    group_cut = max(1, groups // 3)
+    cuts = [0, 256 * group_cut, width]
+
+    def attend_back(first, last, grad_att):
+        at = lambda base: pl.BlockSpec((2, 1, 256, 256), lambda b, g, t: (0, b, 0, base + first + g))
+        to = pl.BlockSpec((2, 1, 256, 256), lambda b, g, t: (0, b, 0, g))
+        totals = pl.BlockSpec((4, 1, 512), lambda b, g, t: (b * groups + first + g, 0, 0))
+        shape = low(2, clip_blocks, 256, 256 * (last - first))
+        grads = call(
+            functools.partial(attend_back_kernel, chips),
+            tab,
+            [
+                (by_clip(packed), at(0)), (by_clip(packed), at(step)), (by_clip(packed), at(2 * step)),
+                (by_clip(attended), at(0)), (by_clip(grad_att), at(0)), (log_totals, totals),
+            ],
+            [],
+            [(shape, to)] * 3,
+            [vmem((512, 512), F32)],
+            grid=(clip_blocks, last - first),
+            cost=30 * rows * 512 * 256 * (last - first),
+        )
+        return [g.reshape(rows, 256 * (last - first)) for g in grads]
+
+    grads_a = attend_back(0, group_cut, grad_att)
+    grads_a, grad_att, arrived, arrived_up = together(grads_a, grad_att, arrived, arrived_up)
+    arrived = down_sum.send(arrived)
+    arrived_up = up_sum.send(arrived_up)
+    grads_b = attend_back(group_cut, groups, grad_att)
+    grads_b, arrived, arrived_up = together(grads_b, arrived, arrived_up)
+    output_tokens = joined(outputs[:half], out_back)
+    left, right = owned(down_sum.send(arrived))
+    owned_down = jnp.concatenate([left, right], axis=1)
+    arrived_up = up_sum.send(arrived_up)
     qkv_out = low(chips, rows_a, 3 * width // 2)
     qkv_mine, qkv_other = call(
-        functools.partial(qkv_grad_kernel, chips, rows_a),
+        functools.partial(qkv_grad_kernel, chips, rows_a, cuts),
         tab,
-        [(normed_first, None)] + [(g, None) for g in grads],
+        [(normed_first, None)] + [(g, None) for g in grads_a + grads_b],
         [],
         [(qkv_out, None), (qkv_out, None)],
         [],
         cost=2 * rows * width * 3 * width,
     )
-    left, right = sums(qkv_mine, qkv_other)
+    qkv_mine, qkv_other, grads_a, grads_b = together(qkv_mine, qkv_other, grads_a, grads_b)
+    qkv_sum = steps_of(qkv_mine, qkv_other, 2)
+    arrived = next(qkv_sum)
+
+    def first_back(part, source, grad_hidden):
+        here_tile = lambda columns: pl.BlockSpec((256, columns), lambda i, t: (part * (tiles // 2) + i, 0))
+        return call(
+            functools.partial(first_kernel, group_a, len(group_a.arrays), chips, cuts),
+            tab,
+            [(source, tile(width)), (gains, None), (grad_hidden, here_tile(width))]
+            + [(g, here_tile(g.shape[1])) for g in grads_a + grads_b],
+            group_a.arrays,
+            [(low(half, width), tile(width))],
+            [vmem((width, 3 * width), BF16), dma((group_a.copies(("qkv",)),))],
+            grid=(tiles // 2,),
+            cost=2 * half * width * 3 * width,
+        )[0]
+
+    grad_got = first_back(1, tok_got, grad_hidden)
+    grad_back = lax.ppermute(grad_got, "seq", swap_x)
+    grad_got, arrived, tok_own = together(grad_got, arrived, tok_own)
+    arrived = qkv_sum.send(arrived)
+    grad_own = first_back(0, tok_own, grad_hidden)
+    grad_own, arrived_up = together(grad_own, arrived_up)
+    arrived_up = up_sum.send(arrived_up)
+    grad_own, arrived = together(grad_own, arrived)
+    arrived = qkv_sum.send(arrived)
+    arrived_up, arrived = together(arrived_up, arrived)
+    arrived = qkv_sum.send(arrived)
+    left, right = owned(up_sum.send(arrived_up))
+    owned_up = jnp.concatenate([left[:, : ff // 2], right[:, : ff // 2]], axis=1)
+    owned_out = jnp.concatenate([left[:, ff // 2 :], right[:, ff // 2 :]], axis=1)
+    left, right = owned(qkv_sum.send(arrived))
     owned_qkv = jnp.concatenate([left, right], axis=1)
-
-    (grad_rows,) = call(
-        functools.partial(first_kernel, group_a, len(group_a.arrays), chips),
-        tab,
-        [(tok_own, own_tile), (tok_got, got_tile), (gains, None)] + [(g, tile(width)) for g in grads] + [(grad_hidden, tile(width))],
-        group_a.arrays,
-        [(low(rows, width), tile(width))],
-        [vmem((width, 3 * width), BF16), dma((group_a.copies(("qkv",)),))],
-        grid=(tiles,),
-        cost=2 * rows * width * 3 * width,
-    )
-    grad_tokens = joined(grad_rows)
+    grad_tokens = joined(grad_own, grad_back)
 
     scale = norm_gains.astype(F32)
     first_gain = jnp.sum(w_qkv.astype(F32) * owned_qkv, axis=1) / scale[:, 0]

time: 439 us -> 333 us (0.76)
  waiting for transfers between devices: 156 us -> 78.3 us
  Pallas kernels: 174 us -> 150 us
  other arithmetic: 12.9 us -> 20 us
  starting transfers between devices: 72.1 us -> 65.2 us
    ppermute x33 -> x34, waiting for transfers between devices: 88.3 us -> 38.2 us  [the longest x12 20.2 us: scatter_steps(): lax.ppermute(add_all(pieces[k]).astype(BF16), AXES, grid.shift(axis, k))]
    ppermute x27 -> x20, waiting for transfers between devices: 63.4 us -> 34 us  [exchange(): lax.ppermute(array, AXES, grid.shift(axis, k))]
    pallas_call x10 -> x14, Pallas kernels: 174 us -> 150 us  [call(): pl.pallas_call(kernel, out_shape=[o for o, _ in outs], input_output_alias...]
    convert_element_type x15 -> x13, other arithmetic: 2.3 us -> 10.9 us  [the longest x10 7.68 us: scatter_steps(): add_all(pieces[k]).astype(BF16)]
    ppermute x27 -> x20, starting transfers between devices: 37.8 us -> 30.4 us  [exchange(): lax.ppermute(array, AXES, grid.shift(axis, k))]
    unnamed x113 -> x107, local copies, waits for them, and re-layouts: 6.53 us -> 9.84 us
    ppermute x33 -> x34, starting transfers between devices: 30 us -> 30.7 us  [the longest x12 11.9 us: scatter_steps(): lax.ppermute(add_all(pieces[k]).astype(BF16), AXES, grid.shift(axis, k))]
  transfers between devices with their start and end apart: 85 -> 67, of which waited for: 28 -> 27; matrix products, arithmetic and copies ran while one was open for 4% -> 4% of each run, Pallas kernels for 40% -> 37%
where the time goes in v2:
time: 333 us; the launch traced here: 328 us
  Pallas kernels  150 us (45%)
  waiting for transfers between devices  78.3 us (24%)
  starting transfers between devices  65.2 us (20%)
  other arithmetic  20 us (6%)
  local copies, waits for them, and re-layouts  11.9 us (4%)
    pallas_call x14, Pallas kernels, call(): pl.pallas_call(kernel, out_shape=[o for o, _ in outs], input_output_alias...  150 us
    ppermute x20, waiting for transfers between devices, exchange(): lax.ppermute(array, AXES, grid.shift(axis, k))  34 us
    ppermute x20, starting transfers between devices, exchange(): lax.ppermute(array, AXES, grid.shift(axis, k))  30.4 us
    ppermute x12, waiting for transfers between devices, scatter_steps(): lax.ppermute(add_all(pieces[k]).astype(BF16), AXES, grid.shift(axis, k))  20.2 us
    ppermute x12, starting transfers between devices, scatter_steps(): lax.ppermute(add_all(pieces[k]).astype(BF16), AXES, grid.shift(axis, k))  11.9 us
    ppermute x9, starting transfers between devices, scatter_steps(): lax.ppermute(total.astype(BF16), AXES, grid.shift('z', k))  11.7 us
    unnamed x107, local copies, waits for them, and re-layouts  9.84 us
    ppermute x9, waiting for transfers between devices, scatter_steps(): lax.ppermute(total.astype(BF16), AXES, grid.shift('z', k))  8.16 us
  transfers between devices with their start and end apart: 67, of which 27 were waited for; matrix products, arithmetic and copies ran while one was open for 4% of the time, Pallas kernels for 37%

profile of v2, /device:TPU:0, one launch (start us, length us, event | category | flops | bytes accessed | tf_op | source)
XLA Modules:
  0.0 328.1 jit_solution(18166880984736706269)
XLA Ops:
  1.4 1.5 dynamic-slice_bitcast_fusion.2
  3.6 2.6 collective-permute-start.4
  7.0 1.6 collective-permute-start.1
  8.7 2.6 collective-permute-start.2
  11.2 1.3 collective-permute-start.3
  12.8 1.2 collective-permute-done.5
  15.1 4.6 %collective-permute-done.2 = bf16[1,48,1280]{2,1,0:T(8,128)(2,1)S(1)} collective-permute-done((bf16[1,48,1280]{2,1,0:T(8,128)(2,1)S(1)}, bf16[1,48,1280]{2,1,0:T(8,128)(2,1)S(1)}, u32[]{:S(2)}, u32[]{:S(2)}) %collective-permute-start.2) | collective-permute-done | bytes 122912 | tf_op jit(solution)/shard_map/ppermute | solution.py:69
  20.5 1.6 collective-permute-start.7
  22.1 1.4 collective-permute-start.8
  23.5 5.1 %collective-permute-done.6 = bf16[2,48,1280]{2,1,0:T(8,128)(2,1)S(1)} collective-permute-done((bf16[2,48,1280]{2,1,0:T(8,128)(2,1)S(1)}, bf16[2,48,1280]{2,1,0:T(8,128)(2,1)S(1)}, u32[]{:S(2)}, u32[]{:S(2)}) %collective-permute-start.6) | collective-permute-done | bytes 245792 | tf_op jit(solution)/shard_map/ppermute | solution.py:69
  28.7 7.4 %collective-permute-done.8 = bf16[256,768]{1,0:T(8,128)(2,1)S(1)} collective-permute-done((bf16[256,768]{1,0:T(8,128)(2,1)S(1)}, bf16[256,768]{1,0:T(8,128)(2,1)S(1)}, u32[]{:S(2)}, u32[]{:S(2)}) %collective-permute-start.8) | collective-permute-done | bytes 393248 | tf_op jit(solution)/shard_map/ppermute | solution.py:627
  36.1 1.6 collective-permute-start.9
  38.4 3.2 collective-permute-start.16
  42.7 1.4 collective-permute-start.18
  44.2 4.2 %collective-permute-done.9.refs_2_.refs_8_ = bf16[4,48,1280]{2,1,0:T(8,128)(2,1)S(1)} collective-permute-done((bf16[4,48,1280]{2,1,0:T(8,128)(2,1)S(1)}, bf16[4,48,1280]{2,1,0:T(8,128)(2,1)S(1)}, u32[]{:S(2)}, u32[]{:S(2)}) %collective-permute-start.9) | collective-permute-done | bytes 491552 | tf_op jit(solution)/shard_map/ppermute | solution.py:69
  48.4 1.3 collective-permute-done.10.refs_3_.refs_9_
  50.2 3.1 collective-permute-done.17
  53.4 1.5 collective-permute-start.19
  55.7 7.5 %shard_map.135 = (bf16[1024,2304]{1,0:T(8,128)(2,1)S(1)}, bf16[1024,768]{1,0:T(8,128)(2,1)S(1)}, f32[8,768]{1,0:T(8,128)S(1)}) custom-call(s32[34]{0:T(128)S(1)} %stack.140.tab, bf16[512,768]{1,0:T(8,128)(2,1)S(1)} %get-tuple-element.244.own.source, bf16[512,768]{1,0:T(8,128)(2,1)S(1)} %constant_dynamic-update-slice_fusion.got.source, ...), custom_call_target="tpu_custom_call" | custom-call | flops 3623878656 | bytes 11821056 | tf_op jit(solution)/shard_map/pallas_call | solution.py:524
  63.3 2.1 copy-done
  65.8 1.2 collective-permute-start.21
  67.8 4.4 %collective-permute-start.23 = (bf16[1,192,384]{2,1,0:T(8,128)(2,1)S(1)}, bf16[1,192,384]{2,1,0:T(8,128)(2,1)S(1)}, u32[]{:S(2)}, u32[]{:S(2)}) collective-permute-start(bf16[1,192,384]{2,1,0:T(8,128)(2,1)S(1)} %bitcast.285), channel_id=1, source_target_pairs={{0,4},{1,5},{2,6},{3,7},{4,8},{5,9},{6,10},{7,11},{8,12},{9,13},{1... | collective-permute-start | bytes 442376 | tf_op jit(solution)/shard_map/ppermute | solution.py:69
  72.2 2.1 collective-permute-start.24
  75.0 14.8 %shard_map.136 = (bf16[2,2,256,768]{3,2,1,0:T(8,128)(2,1)S(1)}, f32[24,1,512]{2,1,0:T(1,128)S(1)}) custom-call(s32[34]{0:T(128)S(1)} %stack.140.tab, bf16[2,2,256,2304]{3,2,1,0:T(8,128)(2,1)} %bitcast.217, bf16[2,2,256,2304]{3,2,1,0:T(8,128)(2,1)} %bitcast.218, bf16[2,2,256,2304]{3,2,1,0:T(8,128)(2,1)} %bitcast.219), custom_call_target="tpu_custom_call" | custom-call | flops 3221225472 | bytes 15777792 | tf_op jit(solution)/shard_map/pallas_call | solution.py:524
  91.0 1.5 collective-permute-start.30
  95.3 4.2 %shard_map.137 = (f32[1024,768]{1,0:T(8,128)S(1)}, bf16[1024,768]{1,0:T(8,128)(2,1)S(1)}) custom-call(s32[34]{0:T(128)S(1)} %stack.140.tab, bf16[1024,768]{1,0:T(8,128)(2,1)S(1)} %bitcast.226, bf16[512,768]{1,0:T(8,128)(2,1)S(1)} %get-tuple-element.244.own.source, bf16[512,768]{1,0:T(8,128)(2,1)S(1)} %constant_dynamic-update-slice_fusion.got.source, ...), custom_call_target="tpu_custom_call" | custom-call | flops 1207959552 | bytes 13787136 | tf_op jit(solution)/shard_map/pallas_call | solution.py:524
  99.5 11.3 %shard_map.138 = (bf16[1024,3072]{1,0:T(8,128)(2,1)}, bf16[1024,3072]{1,0:T(8,128)(2,1)}) custom-call(s32[34]{0:T(128)S(1)} %stack.140.tab, bf16[1024,768]{1,0:T(8,128)(2,1)S(1)} %get-tuple-element.180.normed, bf16[4,48,1920]{2,1,0:T(8,128)(2,1)S(1)} %constant_dynamic-update-slice_fusion.8.refs_0_.refs_2_, ...), custom_call_target="tpu_custom_call" | custom-call | flops 2415919104 | bytes 20054016 | tf_op jit(solution)/shard_map/pallas_call | solution.py:524
  110.8 1.5 collective-permute-start.33
  113.0 1.4 collective-permute-start.32
  114.4 11.4 %shard_map.139 = (bf16[1024,3072]{1,0:T(8,128)(2,1)}, bf16[1024,3072]{1,0:T(8,128)(2,1)}) custom-call(s32[34]{0:T(128)S(1)} %stack.140.tab, bf16[1024,768]{1,0:T(8,128)(2,1)S(1)} %get-tuple-element.180.normed, bf16[1024,3072]{1,0:T(8,128)(2,1)} %get-tuple-element.181.refs_0_, ...), custom_call_target="tpu_custom_call", output_to_operand_aliasing={{0}: (2, {}), {1}: (3, {})} | custom-call | flops 2415919104 | bytes 32636928 | tf_op jit(solution)/shard_map/pallas_call | solution.py:524
  125.7 2.8 collective-permute-done.31.refs_2_
  128.5 11.5 %collective-permute-done.32.refs_3_ = bf16[4,192,384]{2,1,0:T(8,128)(2,1)S(1)} collective-permute-done((bf16[4,192,384]{2,1,0:T(8,128)(2,1)S(1)}, bf16[4,192,384]{2,1,0:T(8,128)(2,1)S(1)}, u32[]{:S(2)}, u32[]{:S(2)}) %collective-permute-start.32) | collective-permute-done | bytes 589856 | tf_op jit(solution)/shard_map/ppermute | solution.py:69
  144.6 8.9 %shard_map.140 = bf16[1024,768]{1,0:T(8,128)(2,1)S(1)} custom-call(s32[34]{0:T(128)S(1)} %stack.140.tab, bf16[1024,3072]{1,0:T(8,128)(2,1)} %get-tuple-element.199.active, f32[1024,768]{1,0:T(8,128)S(1)} %get-tuple-element.188.hidden, bf16[4,192,384]{2,1,0:T(8,128)(2,1)S(1)} %constant_dynamic-update-slice_fusion.14.refs_0_, ...), custom_call_target="tpu_custom_call" | custom-call | flops 4831838208 | bytes 15728640 | tf_op jit(solution)/shard_map/pallas_call | solution.py:524
  153.5 12.2 %shard_map.142 = (bf16[16,192,384]{2,1,0:T(8,128)(2,1)S(1)}, bf16[16,192,384]{2,1,0:T(8,128)(2,1)}) custom-call(s32[34]{0:T(128)S(1)} %stack.140.tab, bf16[1024,3072]{1,0:T(8,128)(2,1)} %get-tuple-element.199.active, bf16[512,768]{1,0:T(8,128)(2,1)S(1)} %get-tuple-element.285.cot_own, bf16[512,768]{1,0:T(8,128)(2,1)S(1)} %collective-permute-done.33.cot_got), custom_call_target="tpu_custom_call" | custom-call | flops 4831838208 | bytes 12582912 | tf_op jit(solution)/shard_map/pallas_call | solution.py:524
  166.5 18.6 %shard_map.141 = (bf16[1024,3072]{1,0:T(8,128)(2,1)}, bf16[16,48,1920]{2,1,0:T(8,128)(2,1)S(1)}, bf16[16,48,1920]{2,1,0:T(8,128)(2,1)}) custom-call(s32[34]{0:T(128)S(1)} %stack.140.tab, bf16[512,768]{1,0:T(8,128)(2,1)S(1)} %get-tuple-element.285.cot_own, bf16[512,768]{1,0:T(8,128)(2,1)S(1)} %collective-permute-done.33.cot_got, ...), custom_call_target="tpu_custom_call" | custom-call | flops 9663676416 | bytes 26345472 | tf_op jit(solution)/shard_map/pallas_call | solution.py:524
  188.1 1.9 copy-done.34
  190.0 18.4 %shard_map.143 = (f32[1024,768]{1,0:T(8,128)S(1)}, bf16[1024,768]{1,0:T(8,128)(2,1)S(1)}, bf16[16,48,1920]{2,1,0:T(8,128)(2,1)S(1)}, bf16[16,48,1920]{2,1,0:T(8,128)(2,1)}) custom-call(s32[34]{0:T(128)S(1)} %stack.140.tab, bf16[1024,3072]{1,0:T(8,128)(2,1)} %get-tuple-element.202.grad_up, ...), custom_call_target="tpu_custom_call", output_to_operand_aliasing={{2}: (7, {}), {3}: (8, {})} | custom-call | flops 7247757312 | bytes 35020800 | tf_op jit(solution)/shard_map/pallas_call | solution.py:524
  208.4 1.6 copy-done.7
  211.4 1.6 fusion.1
  212.9 1.2 collective-permute-start.42
  216.3 1.4 copy-done.29
  217.7 8.9 %shard_map.144 = (bf16[2,2,256,256]{3,2,1,0:T(8,128)(2,1)S(1)}, bf16[2,2,256,256]{3,2,1,0:T(8,128)(2,1)S(1)}, bf16[2,2,256,256]{3,2,1,0:T(8,128)(2,1)S(1)}) custom-call(s32[34]{0:T(128)S(1)} %stack.140.tab, bf16[2,2,256,2304]{3,2,1,0:T(8,128)(2,1)} %bitcast.220, bf16[2,2,256,2304]{3,2,1,0:T(8,128)(2,1)} %bitcast.221, bf16[2,2,256,2304]{3,2,1,0:T(8,128)(2,1)} %bitcast.222, ...), custom_call_target="tpu_custom_call" | custom-call | flops 4026531840 | bytes 18923520 | tf_op jit(solution)/shard_map/pallas_call | solution.py:524
  226.7 1.3 fusion.2
  228.0 1.4 fusion.3
  229.4 1.6 fusion.21
  231.0 1.8 collective-permute-start.45
  233.7 1.7 collective-permute-start.47
  237.2 15.7 %shard_map.145 = (bf16[2,2,256,512]{3,2,1,0:T(8,128)(2,1)S(1)}, bf16[2,2,256,512]{3,2,1,0:T(8,128)(2,1)S(1)}, bf16[2,2,256,512]{3,2,1,0:T(8,128)(2,1)S(1)}) custom-call(s32[34]{0:T(128)S(1)} %stack.140.tab, bf16[2,2,256,2304]{3,2,1,0:T(8,128)(2,1)} %bitcast.223, bf16[2,2,256,2304]{3,2,1,0:T(8,128)(2,1)} %bitcast.224, bf16[2,2,256,2304]{3,2,1,0:T(8,128)(2,1)} %bitcast.225, ...), custom_call_target="tpu_custom_call" | custom-call | flops 8053063680 | bytes 20496384 | tf_op jit(solution)/shard_map/pallas_call | solution.py:524
  253.8 8.2 %shard_map.146 = (bf16[16,48,1152]{2,1,0:T(8,128)(2,1)S(1)}, bf16[16,48,1152]{2,1,0:T(8,128)(2,1)S(1)}) custom-call(s32[34]{0:T(128)S(1)} %stack.140.tab, bf16[1024,768]{1,0:T(8,128)(2,1)S(1)} %copy-done.36, bf16[1024,256]{1,0:T(8,128)(2,1)S(1)} %bitcast.248, bf16[1024,256]{1,0:T(8,128)(2,1)S(1)} %bitcast.251, bf16[1024,256]{1,0:T(8,128)(2,1)S(1)} %bitcast.254, ...), custom_call_target="tpu_custom_call" | custom-call | flops 3623878656 | bytes 9830400 | tf_op jit(solution)/shard_map/pallas_call | solution.py:524
  262.2 1.2 maximum_bitcast_fusion
  263.5 1.5 fusion.4
  268.4 4.8 %shard_map.147 = bf16[512,768]{1,0:T(8,128)(2,1)S(1)} custom-call(s32[34]{0:T(128)S(1)} %stack.140.tab, bf16[512,768]{1,0:T(8,128)(2,1)S(1)} %copy-done.6, f32[8,768]{1,0:T(8,128)S(1)} %get-tuple-element.168.gains, f32[1024,768]{1,0:T(8,128)S(1)} %get-tuple-element.211.grad_hidden, bf16[1024,256]{1,0:T(8,128)(2,1)S(1)} %bitcast.249, ...), custom_call_target="tpu_custom_call" | custom-call | flops 1811939328 | bytes 13393920 | tf_op jit(solution)/shard_map/pallas_call | solution.py:524
  275.3 4.8 %shard_map.148 = bf16[512,768]{1,0:T(8,128)(2,1)S(1)} custom-call(s32[34]{0:T(128)S(1)} %stack.140.tab, bf16[512,768]{1,0:T(8,128)(2,1)S(1)} %copy-done.2, f32[8,768]{1,0:T(8,128)S(1)} %get-tuple-element.168.gains, f32[1024,768]{1,0:T(8,128)S(1)} %get-tuple-element.211.grad_hidden, bf16[1024,256]{1,0:T(8,128)(2,1)S(1)} %bitcast.250, ...), custom_call_target="tpu_custom_call" | custom-call | flops 1811939328 | bytes 13393920 | tf_op jit(solution)/shard_map/pallas_call | solution.py:524
  282.2 1.4 fusion.13
  283.8 2.1 collective-permute-start.57
  285.9 6.7 %collective-permute-done.53 = bf16[2,2,48,1152]{3,2,1,0:T(8,128)(2,1)S(1)} collective-permute-done((bf16[2,2,48,1152]{3,2,1,0:T(8,128)(2,1)S(1)}, bf16[2,2,48,1152]{3,2,1,0:T(8,128)(2,1)S(1)}, u32[]{:S(2)}, u32[]{:S(2)}) %collective-permute-start.53) | collective-permute-done | bytes 442400 | tf_op jit(solution)/shard_map/ppermute | solution.py:114
  292.6 1.7 collective-permute-start.58
  294.3 8.4 %collective-permute-done.54 = bf16[2,2,48,1152]{3,2,1,0:T(8,128)(2,1)S(1)} collective-permute-done((bf16[2,2,48,1152]{3,2,1,0:T(8,128)(2,1)S(1)}, bf16[2,2,48,1152]{3,2,1,0:T(8,128)(2,1)S(1)}, u32[]{:S(2)}, u32[]{:S(2)}) %collective-permute-start.54) | collective-permute-done | bytes 442400 | tf_op jit(solution)/shard_map/ppermute | solution.py:114
  302.9 1.2 collective-permute-start.59
  305.2 1.2 maximum_bitcast_fusion.1
  306.5 3.5 %collective-permute-done.59 = bf16[2,48,1152]{2,1,0:T(8,128)(2,1)S(1)} collective-permute-done((bf16[2,48,1152]{2,1,0:T(8,128)(2,1)S(1)}, bf16[2,48,1152]{2,1,0:T(8,128)(2,1)S(1)}, u32[]{:S(2)}, u32[]{:S(2)}) %collective-permute-start.59) | collective-permute-done | bytes 221216 | tf_op jit(solution)/shard_map/ppermute | solution.py:114
  312.2 1.7 collective-permute-start.63
  313.9 1.7 collective-permute-start.61
  317.7 7.0 %collective-permute-done.62 = bf16[48,1152]{1,0:T(8,128)(2,1)S(1)} collective-permute-done((bf16[48,1152]{1,0:T(8,128)(2,1)S(1)}, bf16[48,1152]{1,0:T(8,128)(2,1)S(1)}, u32[]{:S(2)}, u32[]{:S(2)}) %collective-permute-start.62) | collective-permute-done | bytes 110624 | tf_op jit(solution)/shard_map/ppermute | solution.py:128
  (255 shorter events, 44.5 us)
Async XLA Ops:
  3.0 3.9 %collective-permute-start = (bf16[24,1280]{1,0:T(8,128)(2,1)S(1)}, bf16[24,1280]{1,0:T(8,128)(2,1)S(1)}, u32[]{:S(2)}, u32[]{:S(2)}) collective-permute-start(bf16[24,1280]{1,0:T(8,128)(2,1)S(1)} %fusion.32), channel_id=1, source_target_pairs={{0,1},{1,0},{2,3},{3,2},{4,5},{5,4},{6,7},{7,6},{8,9},{9,8},{10,11... | collective-permute-start | bytes 184328 | tf_op jit(solution)/shard_map/ppermute | solution.py:594
  3.6 16.1 %collective-permute-start.4 = (bf16[256,768]{1,0:T(8,128)(2,1)S(1)}, bf16[256,768]{1,0:T(8,128)(2,1)S(1)}, u32[]{:S(2)}, u32[]{:S(2)}) collective-permute-start(bf16[256,768]{1,0:T(8,128)(2,1)S(1)} %get-tuple-element.289), channel_id=1, source_target_pairs={{0,16},{16,0},{1,17},{17,1},{2,18},{18,2},{3,19},{19,3},{4,20},{20... | collective-permute-start | bytes 1179656 | tf_op jit(solution)/shard_map/ppermute | solution.py:600
  7.0 8.1 %collective-permute-start.1 = (bf16[1,48,1280]{2,1,0:T(8,128)(2,1)S(1)}, bf16[1,48,1280]{2,1,0:T(8,128)(2,1)S(1)}, u32[]{:S(2)}, u32[]{:S(2)}) collective-permute-start(bf16[1,48,1280]{2,1,0:T(8,128)(2,1)S(1)} %bitcast.280), channel_id=1, source_target_pairs={{0,4},{1,5},{2,6},{3,7},{4,8},{5,9},{6,10},{7,11},{8,12},{9,13},{1... | collective-permute-start | bytes 368648 | tf_op jit(solution)/shard_map/ppermute | solution.py:69
  8.7 11.1 %collective-permute-start.2 = (bf16[1,48,1280]{2,1,0:T(8,128)(2,1)S(1)}, bf16[1,48,1280]{2,1,0:T(8,128)(2,1)S(1)}, u32[]{:S(2)}, u32[]{:S(2)}) collective-permute-start(bf16[1,48,1280]{2,1,0:T(8,128)(2,1)S(1)} %bitcast.281), channel_id=1, source_target_pairs={{0,8},{1,9},{2,10},{3,11},{4,12},{5,13},{6,14},{7,15},{8,0},{9,1},... | collective-permute-start | bytes 368648 | tf_op jit(solution)/shard_map/ppermute | solution.py:69
  11.2 8.5 %collective-permute-start.3 = (bf16[1,48,1280]{2,1,0:T(8,128)(2,1)S(1)}, bf16[1,48,1280]{2,1,0:T(8,128)(2,1)S(1)}, u32[]{:S(2)}, u32[]{:S(2)}) collective-permute-start(bf16[1,48,1280]{2,1,0:T(8,128)(2,1)S(1)} %bitcast.282), channel_id=1, source_target_pairs={{0,12},{1,13},{2,14},{3,15},{4,0},{5,1},{6,2},{7,3},{8,4},{9,5},{1... | collective-permute-start | bytes 368648 | tf_op jit(solution)/shard_map/ppermute | solution.py:69
  14.0 24.4 %collective-permute-start.11 = (bf16[96,384]{1,0:T(8,128)(2,1)S(1)}, bf16[96,384]{1,0:T(8,128)(2,1)S(1)}, u32[]{:S(2)}, u32[]{:S(2)}) collective-permute-start(bf16[96,384]{1,0:T(8,128)(2,1)S(1)} %constant_dynamic-slice_fusion), channel_id=1, source_target_pairs={{0,1},{1,0},{2,3},{3,2},{4,5},{5,4},{6,7},{7,6},{8,9},{9,8},{10,11... | collective-permute-start | bytes 221192 | tf_op jit(solution)/shard_map/ppermute | solution.py:594
  19.8 8.9 %collective-permute-start.6 = (bf16[2,48,1280]{2,1,0:T(8,128)(2,1)S(1)}, bf16[2,48,1280]{2,1,0:T(8,128)(2,1)S(1)}, u32[]{:S(2)}, u32[]{:S(2)}) collective-permute-start(bf16[2,48,1280]{2,1,0:T(8,128)(2,1)S(1)} %pad_maximum_fusion.4), channel_id=1, source_target_pairs={{0,16},{1,17},{2,18},{3,19},{4,20},{5,21},{6,22},{7,23},{8,24},{9,... | collective-permute-start | bytes 737288 | tf_op jit(solution)/shard_map/ppermute | solution.py:69
  20.5 8.2 %collective-permute-start.7 = (bf16[2,48,1280]{2,1,0:T(8,128)(2,1)S(1)}, bf16[2,48,1280]{2,1,0:T(8,128)(2,1)S(1)}, u32[]{:S(2)}, u32[]{:S(2)}) collective-permute-start(bf16[2,48,1280]{2,1,0:T(8,128)(2,1)S(1)} %pad_maximum_fusion.5), channel_id=1, source_target_pairs={{0,2},{1,3},{2,0},{3,1},{4,6},{5,7},{6,4},{7,5},{8,10},{9,11},{10,... | collective-permute-start | bytes 737288 | tf_op jit(solution)/shard_map/ppermute | solution.py:69
  22.1 14.0 %collective-permute-start.8 = (bf16[256,768]{1,0:T(8,128)(2,1)S(1)}, bf16[256,768]{1,0:T(8,128)(2,1)S(1)}, u32[]{:S(2)}, u32[]{:S(2)}) collective-permute-start(bf16[256,768]{1,0:T(8,128)(2,1)S(1)} %get-tuple-element.145), channel_id=1, source_target_pairs={{0,16},{16,0},{1,17},{17,1},{2,18},{18,2},{3,19},{19,3},{4,20},{20... | collective-permute-start | bytes 1179656 | tf_op jit(solution)/shard_map/ppermute | solution.py:627
  36.1 12.3 %collective-permute-start.9 = (bf16[4,48,1280]{2,1,0:T(8,128)(2,1)S(1)}, bf16[4,48,1280]{2,1,0:T(8,128)(2,1)S(1)}, u32[]{:S(2)}, u32[]{:S(2)}) collective-permute-start(bf16[4,48,1280]{2,1,0:T(8,128)(2,1)S(1)} %constant_dynamic-update-slice_fusion.2.refs_0_.refs_6_), channel_id=1, source_target_pairs={{0,2},{1,3},{2,0},{3,1},{4,6},{5,7},{6,4},{7,5},{8,10},{9,11},{10,... | collective-permute-start | bytes 1474568 | tf_op jit(solution)/shard_map/ppermute | solution.py:69
  37.7 12.0 %collective-permute-start.10 = (bf16[4,48,1280]{2,1,0:T(8,128)(2,1)S(1)}, bf16[4,48,1280]{2,1,0:T(8,128)(2,1)S(1)}, u32[]{:S(2)}, u32[]{:S(2)}) collective-permute-start(bf16[4,48,1280]{2,1,0:T(8,128)(2,1)S(1)} %constant_dynamic-update-slice_fusion.5.refs_1_.refs_7_), channel_id=1, source_target_pairs={{0,16},{1,17},{2,18},{3,19},{4,20},{5,21},{6,22},{7,23},{8,24},{9,... | collective-permute-start | bytes 1474568 | tf_op jit(solution)/shard_map/ppermute | solution.py:69
  38.4 11.8 %collective-permute-start.16 = (bf16[1,48,1920]{2,1,0:T(8,128)(2,1)S(1)}, bf16[1,48,1920]{2,1,0:T(8,128)(2,1)S(1)}, u32[]{:S(2)}, u32[]{:S(2)}) collective-permute-start(bf16[1,48,1920]{2,1,0:T(8,128)(2,1)S(1)} %bitcast.275), channel_id=1, source_target_pairs={{0,4},{1,5},{2,6},{3,7},{4,8},{5,9},{6,10},{7,11},{8,12},{9,13},{1... | collective-permute-start | bytes 552968 | tf_op jit(solution)/shard_map/ppermute | solution.py:69
  41.7 11.6 %collective-permute-start.17 = (bf16[1,48,1920]{2,1,0:T(8,128)(2,1)S(1)}, bf16[1,48,1920]{2,1,0:T(8,128)(2,1)S(1)}, u32[]{:S(2)}, u32[]{:S(2)}) collective-permute-start(bf16[1,48,1920]{2,1,0:T(8,128)(2,1)S(1)} %bitcast.276), channel_id=1, source_target_pairs={{0,8},{1,9},{2,10},{3,11},{4,12},{5,13},{6,14},{7,15},{8,0},{9,1},... | collective-permute-start | bytes 552968 | tf_op jit(solution)/shard_map/ppermute | solution.py:69
  42.7 10.6 %collective-permute-start.18 = (bf16[1,48,1920]{2,1,0:T(8,128)(2,1)S(1)}, bf16[1,48,1920]{2,1,0:T(8,128)(2,1)S(1)}, u32[]{:S(2)}, u32[]{:S(2)}) collective-permute-start(bf16[1,48,1920]{2,1,0:T(8,128)(2,1)S(1)} %bitcast.277), channel_id=1, source_target_pairs={{0,12},{1,13},{2,14},{3,15},{4,0},{5,1},{6,2},{7,3},{8,4},{9,5},{1... | collective-permute-start | bytes 552968 | tf_op jit(solution)/shard_map/ppermute | solution.py:69
  49.7 5.3 %collective-permute-start.12 = (bf16[4,48,1280]{2,1,0:T(8,128)(2,1)S(1)}, bf16[4,48,1280]{2,1,0:T(8,128)(2,1)S(1)}, u32[]{:S(2)}, u32[]{:S(2)}) collective-permute-start(bf16[4,48,1280]{2,1,0:T(8,128)(2,1)S(1)} %constant_dynamic-update-slice_fusion.2.refs_0_.refs_6_), channel_id=1, source_target_pairs={{0,1},{1,0},{2,3},{3,2},{4,5},{5,4},{6,7},{7,6},{8,9},{9,8},{10,11... | collective-permute-start | bytes 1474568 | tf_op jit(solution)/shard_map/ppermute | solution.py:622
  49.7 5.9 %collective-permute-start.13 = (bf16[4,48,1280]{2,1,0:T(8,128)(2,1)S(1)}, bf16[4,48,1280]{2,1,0:T(8,128)(2,1)S(1)}, u32[]{:S(2)}, u32[]{:S(2)}) collective-permute-start(bf16[4,48,1280]{2,1,0:T(8,128)(2,1)S(1)} %constant_dynamic-update-slice_fusion.5.refs_1_.refs_7_), channel_id=1, source_target_pairs={{0,1},{1,0},{2,3},{3,2},{4,5},{5,4},{6,7},{7,6},{8,9},{9,8},{10,11... | collective-permute-start | bytes 1474568 | tf_op jit(solution)/shard_map/ppermute | solution.py:622
  50.2 5.4 %collective-permute-start.14 = (bf16[4,48,1280]{2,1,0:T(8,128)(2,1)S(1)}, bf16[4,48,1280]{2,1,0:T(8,128)(2,1)S(1)}, u32[]{:S(2)}, u32[]{:S(2)}) collective-permute-start(bf16[4,48,1280]{2,1,0:T(8,128)(2,1)S(1)} %collective-permute-done.9.refs_2_.refs_8_), channel_id=1, source_target_pairs={{0,1},{1,0},{2,3},{3,2},{4,5},{5,4},{6,7},{7,6},{8,9},{9,8},{10,11... | collective-permute-start | bytes 1474568 | tf_op jit(solution)/shard_map/ppermute | solution.py:622
  53.3 2.3 collective-permute-start.15
  53.4 12.0 %collective-permute-start.19 = (bf16[2,48,1920]{2,1,0:T(8,128)(2,1)S(1)}, bf16[2,48,1920]{2,1,0:T(8,128)(2,1)S(1)}, u32[]{:S(2)}, u32[]{:S(2)}) collective-permute-start(bf16[2,48,1920]{2,1,0:T(8,128)(2,1)S(1)} %pad_maximum_fusion), channel_id=1, source_target_pairs={{0,16},{1,17},{2,18},{3,19},{4,20},{5,21},{6,22},{7,23},{8,24},{9,... | collective-permute-start | bytes 1105928 | tf_op jit(solution)/shard_map/ppermute | solution.py:69
  55.0 10.8 %collective-permute-start.20 = (bf16[2,48,1920]{2,1,0:T(8,128)(2,1)S(1)}, bf16[2,48,1920]{2,1,0:T(8,128)(2,1)S(1)}, u32[]{:S(2)}, u32[]{:S(2)}) collective-permute-start(bf16[2,48,1920]{2,1,0:T(8,128)(2,1)S(1)} %pad_maximum_fusion.1), channel_id=1, source_target_pairs={{0,2},{1,3},{2,0},{3,1},{4,6},{5,7},{6,4},{7,5},{8,10},{9,11},{10,... | collective-permute-start | bytes 1105928 | tf_op jit(solution)/shard_map/ppermute | solution.py:69
  65.8 24.0 %collective-permute-start.21 = (bf16[4,48,1920]{2,1,0:T(8,128)(2,1)S(1)}, bf16[4,48,1920]{2,1,0:T(8,128)(2,1)S(1)}, u32[]{:S(2)}, u32[]{:S(2)}) collective-permute-start(bf16[4,48,1920]{2,1,0:T(8,128)(2,1)S(1)} %constant_dynamic-update-slice_fusion.8.refs_0_.refs_2_), channel_id=1, source_target_pairs={{0,2},{1,3},{2,0},{3,1},{4,6},{5,7},{6,4},{7,5},{8,10},{9,11},{10,... | collective-permute-start | bytes 2211848 | tf_op jit(solution)/shard_map/ppermute | solution.py:69
  67.1 22.7 %collective-permute-start.22 = (bf16[4,48,1920]{2,1,0:T(8,128)(2,1)S(1)}, bf16[4,48,1920]{2,1,0:T(8,128)(2,1)S(1)}, u32[]{:S(2)}, u32[]{:S(2)}) collective-permute-start(bf16[4,48,1920]{2,1,0:T(8,128)(2,1)S(1)} %constant_dynamic-update-slice_fusion.11.refs_1_.refs_3_), channel_id=1, source_target_pairs={{0,16},{1,17},{2,18},{3,19},{4,20},{5,21},{6,22},{7,23},{8,24},{9,... | collective-permute-start | bytes 2211848 | tf_op jit(solution)/shard_map/ppermute | solution.py:69
  67.8 22.0 %collective-permute-start.23 = (bf16[1,192,384]{2,1,0:T(8,128)(2,1)S(1)}, bf16[1,192,384]{2,1,0:T(8,128)(2,1)S(1)}, u32[]{:S(2)}, u32[]{:S(2)}) collective-permute-start(bf16[1,192,384]{2,1,0:T(8,128)(2,1)S(1)} %bitcast.285), channel_id=1, source_target_pairs={{0,4},{1,5},{2,6},{3,7},{4,8},{5,9},{6,10},{7,11},{8,12},{9,13},{1... | collective-permute-start | bytes 442376 | tf_op jit(solution)/shard_map/ppermute | solution.py:69
  72.2 17.6 %collective-permute-start.24 = (bf16[1,192,384]{2,1,0:T(8,128)(2,1)S(1)}, bf16[1,192,384]{2,1,0:T(8,128)(2,1)S(1)}, u32[]{:S(2)}, u32[]{:S(2)}) collective-permute-start(bf16[1,192,384]{2,1,0:T(8,128)(2,1)S(1)} %bitcast.286), channel_id=1, source_target_pairs={{0,8},{1,9},{2,10},{3,11},{4,12},{5,13},{6,14},{7,15},{8,0},{9,1},... | collective-permute-start | bytes 442376 | tf_op jit(solution)/shard_map/ppermute | solution.py:69
  74.3 15.5 %collective-permute-start.25 = (bf16[1,192,384]{2,1,0:T(8,128)(2,1)S(1)}, bf16[1,192,384]{2,1,0:T(8,128)(2,1)S(1)}, u32[]{:S(2)}, u32[]{:S(2)}) collective-permute-start(bf16[1,192,384]{2,1,0:T(8,128)(2,1)S(1)} %bitcast.287), channel_id=1, source_target_pairs={{0,12},{1,13},{2,14},{3,15},{4,0},{5,1},{6,2},{7,3},{8,4},{9,5},{1... | collective-permute-start | bytes 442376 | tf_op jit(solution)/shard_map/ppermute | solution.py:69
  89.8 2.8 collective-permute-start.26
  89.9 3.3 collective-permute-start.27
  90.4 3.8 %collective-permute-start.28 = (bf16[4,48,1920]{2,1,0:T(8,128)(2,1)S(1)}, bf16[4,48,1920]{2,1,0:T(8,128)(2,1)S(1)}, u32[]{:S(2)}, u32[]{:S(2)}) collective-permute-start(bf16[4,48,1920]{2,1,0:T(8,128)(2,1)S(1)} %collective-permute-done.21.refs_2_.refs_4_), channel_id=1, source_target_pairs={{0,1},{1,0},{2,3},{3,2},{4,5},{5,4},{6,7},{7,6},{8,9},{9,8},{10,11... | collective-permute-start | bytes 2211848 | tf_op jit(solution)/shard_map/ppermute | solution.py:622
  90.5 4.8 %collective-permute-start.29 = (bf16[4,48,1920]{2,1,0:T(8,128)(2,1)S(1)}, bf16[4,48,1920]{2,1,0:T(8,128)(2,1)S(1)}, u32[]{:S(2)}, u32[]{:S(2)}) collective-permute-start(bf16[4,48,1920]{2,1,0:T(8,128)(2,1)S(1)} %collective-permute-done.22.refs_3_.refs_5_), channel_id=1, source_target_pairs={{0,1},{1,0},{2,3},{3,2},{4,5},{5,4},{6,7},{7,6},{8,9},{9,8},{10,11... | collective-permute-start | bytes 2211848 | tf_op jit(solution)/shard_map/ppermute | solution.py:622
  91.0 19.8 %collective-permute-start.30 = (bf16[4,192,384]{2,1,0:T(8,128)(2,1)S(1)}, bf16[4,192,384]{2,1,0:T(8,128)(2,1)S(1)}, u32[]{:S(2)}, u32[]{:S(2)}) collective-permute-start(bf16[4,192,384]{2,1,0:T(8,128)(2,1)S(1)} %constant_dynamic-update-slice_fusion.14.refs_0_), channel_id=1, source_target_pairs={{0,16},{1,17},{2,18},{3,19},{4,20},{5,21},{6,22},{7,23},{8,24},{9,... | collective-permute-start | bytes 1769480 | tf_op jit(solution)/shard_map/ppermute | solution.py:69
  110.8 29.2 %collective-permute-start.33 = (bf16[512,768]{1,0:T(8,128)(2,1)S(1)}, bf16[512,768]{1,0:T(8,128)(2,1)S(1)}, u32[]{:S(2)}, u32[]{:S(2)}) collective-permute-start(bf16[512,768]{1,0:T(8,128)(2,1)S(1)} %get-tuple-element.186), channel_id=1, source_target_pairs={{0,16},{16,0},{1,17},{17,1},{2,18},{18,2},{3,19},{19,3},{4,20},{20... | collective-permute-start | bytes 2359304 | tf_op jit(solution)/shard_map/ppermute | solution.py:746
  112.3 16.2 %collective-permute-start.31 = (bf16[4,192,384]{2,1,0:T(8,128)(2,1)S(1)}, bf16[4,192,384]{2,1,0:T(8,128)(2,1)S(1)}, u32[]{:S(2)}, u32[]{:S(2)}) collective-permute-start(bf16[4,192,384]{2,1,0:T(8,128)(2,1)S(1)} %constant_dynamic-update-slice_fusion.14.refs_0_), channel_id=1, source_target_pairs={{0,2},{1,3},{2,0},{3,1},{4,6},{5,7},{6,4},{7,5},{8,10},{9,11},{10,... | collective-permute-start | bytes 1769480 | tf_op jit(solution)/shard_map/ppermute | solution.py:69
  113.0 27.1 %collective-permute-start.32 = (bf16[4,192,384]{2,1,0:T(8,128)(2,1)S(1)}, bf16[4,192,384]{2,1,0:T(8,128)(2,1)S(1)}, u32[]{:S(2)}, u32[]{:S(2)}) collective-permute-start(bf16[4,192,384]{2,1,0:T(8,128)(2,1)S(1)} %collective-permute-done.30.refs_1_), channel_id=1, source_target_pairs={{0,2},{1,3},{2,0},{3,1},{4,6},{5,7},{6,4},{7,5},{8,10},{9,11},{10,... | collective-permute-start | bytes 1769480 | tf_op jit(solution)/shard_map/ppermute | solution.py:69
  140.1 2.8 collective-permute-start.35
  140.6 3.2 collective-permute-start.36
  140.6 4.0 %collective-permute-start.37 = (bf16[4,192,384]{2,1,0:T(8,128)(2,1)S(1)}, bf16[4,192,384]{2,1,0:T(8,128)(2,1)S(1)}, u32[]{:S(2)}, u32[]{:S(2)}) collective-permute-start(bf16[4,192,384]{2,1,0:T(8,128)(2,1)S(1)} %collective-permute-done.32.refs_3_), channel_id=1, source_target_pairs={{0,1},{1,0},{2,3},{3,2},{4,5},{5,4},{6,7},{7,6},{8,9},{9,8},{10,11... | collective-permute-start | bytes 1769480 | tf_op jit(solution)/shard_map/ppermute | solution.py:622
  165.7 20.1 %collective-permute-start.39 = (bf16[16,192,384]{2,1,0:T(8,128)(2,1)}, bf16[16,192,384]{2,1,0:T(8,128)(2,1)S(1)}, u32[]{:S(2)}, u32[]{:S(2)}) collective-permute-start(bf16[16,192,384]{2,1,0:T(8,128)(2,1)} %get-tuple-element.200), channel_id=1, source_target_pairs={{0,1},{1,0},{2,3},{3,2},{4,5},{5,4},{6,7},{7,6},{8,9},{9,8},{10,11... | collective-permute-start | bytes 7077896 | tf_op jit(solution)/shard_map/ppermute | solution.py:98
  165.9 19.9 %collective-permute-start.38 = (bf16[512,768]{1,0:T(8,128)(2,1)S(1)}, bf16[512,768]{1,0:T(8,128)(2,1)S(1)}, u32[]{:S(2)}, u32[]{:S(2)}) collective-permute-start(bf16[512,768]{1,0:T(8,128)(2,1)S(1)} %slice.441), channel_id=1, source_target_pairs={{0,16},{16,0},{1,17},{17,1},{2,18},{18,2},{3,19},{19,3},{4,20},{20... | collective-permute-start | bytes 2359304 | tf_op jit(solution)/shard_map/ppermute | solution.py:763
  186.0 25.3 %collective-permute-start.40 = (bf16[2,3,192,384]{3,2,1,0:T(8,128)(2,1)S(1)}, bf16[2,3,192,384]{3,2,1,0:T(8,128)(2,1)}, u32[]{:S(2)}, u32[]{:S(2)}) collective-permute-start(bf16[2,3,192,384]{3,2,1,0:T(8,128)(2,1)S(1)} %fusion), channel_id=1, source_target_pairs={{0,2},{1,3},{2,0},{3,1},{4,6},{5,7},{6,4},{7,5},{8,10},{9,11},{10,... | collective-permute-start | bytes 2654216 | tf_op jit(solution)/shard_map/ppermute | solution.py:114
  187.2 24.0 %collective-permute-start.41 = (bf16[2,1,192,384]{3,2,1,0:T(8,128)(2,1)S(1)}, bf16[2,1,192,384]{3,2,1,0:T(8,128)(2,1)}, u32[]{:S(2)}, u32[]{:S(2)}) collective-permute-start(bf16[2,1,192,384]{3,2,1,0:T(8,128)(2,1)S(1)} %fusion.16), channel_id=1, source_target_pairs={{0,16},{1,17},{2,18},{3,19},{4,20},{5,21},{6,22},{7,23},{8,24},{9,... | collective-permute-start | bytes 884744 | tf_op jit(solution)/shard_map/ppermute | solution.py:114
  211.3 15.4 %collective-permute-start.44 = (bf16[16,48,1920]{2,1,0:T(8,128)(2,1)}, bf16[16,48,1920]{2,1,0:T(8,128)(2,1)}, u32[]{:S(2)}, u32[]{:S(2)}) collective-permute-start(bf16[16,48,1920]{2,1,0:T(8,128)(2,1)} %get-tuple-element.220), channel_id=1, source_target_pairs={{0,1},{1,0},{2,3},{3,2},{4,5},{5,4},{6,7},{7,6},{8,9},{9,8},{10,11... | collective-permute-start | bytes 8847368 | tf_op jit(solution)/shard_map/ppermute | solution.py:98
  212.9 13.7 %collective-permute-start.42 = (bf16[3,192,384]{2,1,0:T(8,128)(2,1)S(1)}, bf16[3,192,384]{2,1,0:T(8,128)(2,1)S(1)}, u32[]{:S(2)}, u32[]{:S(2)}) collective-permute-start(bf16[3,192,384]{2,1,0:T(8,128)(2,1)S(1)} %fusion.1), channel_id=1, source_target_pairs={{0,16},{1,17},{2,18},{3,19},{4,20},{5,21},{6,22},{7,23},{8,24},{9,... | collective-permute-start | bytes 1327112 | tf_op jit(solution)/shard_map/ppermute | solution.py:114
  215.3 11.4 %collective-permute-start.43 = (bf16[1,192,384]{2,1,0:T(8,128)(2,1)S(1)}, bf16[1,192,384]{2,1,0:T(8,128)(2,1)S(1)}, u32[]{:S(2)}, u32[]{:S(2)}) collective-permute-start(bf16[1,192,384]{2,1,0:T(8,128)(2,1)S(1)} %fusion.23), channel_id=1, source_target_pairs={{0,2},{1,3},{2,0},{3,1},{4,6},{5,7},{6,4},{7,5},{8,10},{9,11},{10,... | collective-permute-start | bytes 442376 | tf_op jit(solution)/shard_map/ppermute | solution.py:114
  231.0 21.9 %collective-permute-start.45 = (bf16[192,384]{1,0:T(8,128)(2,1)S(1)}, bf16[192,384]{1,0:T(8,128)(2,1)S(1)}, u32[]{:S(2)}, u32[]{:S(2)}) collective-permute-start(bf16[192,384]{1,0:T(8,128)(2,1)S(1)} %get-tuple-element.270), channel_id=1, source_target_pairs={{0,4},{1,5},{2,6},{3,7},{4,8},{5,9},{6,10},{7,11},{8,12},{9,13},{1... | collective-permute-start | bytes 442376 | tf_op jit(solution)/shard_map/ppermute | solution.py:128
  232.9 20.1 %collective-permute-start.46 = (bf16[192,384]{1,0:T(8,128)(2,1)S(1)}, bf16[192,384]{1,0:T(8,128)(2,1)S(1)}, u32[]{:S(2)}, u32[]{:S(2)}) collective-permute-start(bf16[192,384]{1,0:T(8,128)(2,1)S(1)} %get-tuple-element.269), channel_id=1, source_target_pairs={{0,8},{1,9},{2,10},{3,11},{4,12},{5,13},{6,14},{7,15},{8,0},{9,1},... | collective-permute-start | bytes 442376 | tf_op jit(solution)/shard_map/ppermute | solution.py:128
  233.7 19.3 %collective-permute-start.47 = (bf16[192,384]{1,0:T(8,128)(2,1)S(1)}, bf16[192,384]{1,0:T(8,128)(2,1)S(1)}, u32[]{:S(2)}, u32[]{:S(2)}) collective-permute-start(bf16[192,384]{1,0:T(8,128)(2,1)S(1)} %get-tuple-element.274), channel_id=1, source_target_pairs={{0,12},{1,13},{2,14},{3,15},{4,0},{5,1},{6,2},{7,3},{8,4},{9,5},{1... | collective-permute-start | bytes 442376 | tf_op jit(solution)/shard_map/ppermute | solution.py:128
  235.3 17.7 %collective-permute-start.48 = (bf16[2,2,48,1920]{3,2,1,0:T(8,128)(2,1)S(1)}, bf16[2,2,48,1920]{3,2,1,0:T(8,128)(2,1)S(1)}, u32[]{:S(2)}, u32[]{:S(2)}) collective-permute-start(bf16[2,2,48,1920]{3,2,1,0:T(8,128)(2,1)S(1)} %fusion.2), channel_id=1, source_target_pairs={{0,2},{1,3},{2,0},{3,1},{4,6},{5,7},{6,4},{7,5},{8,10},{9,11},{10,... | collective-permute-start | bytes 2211848 | tf_op jit(solution)/shard_map/ppermute | solution.py:114
  236.4 17.4 %collective-permute-start.49 = (bf16[2,2,48,1920]{3,2,1,0:T(8,128)(2,1)S(1)}, bf16[2,2,48,1920]{3,2,1,0:T(8,128)(2,1)S(1)}, u32[]{:S(2)}, u32[]{:S(2)}) collective-permute-start(bf16[2,2,48,1920]{3,2,1,0:T(8,128)(2,1)S(1)} %fusion.3), channel_id=1, source_target_pairs={{0,16},{1,17},{2,18},{3,19},{4,20},{5,21},{6,22},{7,23},{8,24},{9,... | collective-permute-start | bytes 2211848 | tf_op jit(solution)/shard_map/ppermute | solution.py:114
  262.0 13.2 %collective-permute-start.50 = (bf16[16,48,1152]{2,1,0:T(8,128)(2,1)S(1)}, bf16[16,48,1152]{2,1,0:T(8,128)(2,1)S(1)}, u32[]{:S(2)}, u32[]{:S(2)}) collective-permute-start(bf16[16,48,1152]{2,1,0:T(8,128)(2,1)S(1)} %get-tuple-element.243), channel_id=1, source_target_pairs={{0,1},{1,0},{2,3},{3,2},{4,5},{5,4},{6,7},{7,6},{8,9},{9,8},{10,11... | collective-permute-start | bytes 5308424 | tf_op jit(solution)/shard_map/ppermute | solution.py:98
  265.1 15.2 %collective-permute-start.51 = (bf16[2,48,1920]{2,1,0:T(8,128)(2,1)S(1)}, bf16[2,48,1920]{2,1,0:T(8,128)(2,1)S(1)}, u32[]{:S(2)}, u32[]{:S(2)}) collective-permute-start(bf16[2,48,1920]{2,1,0:T(8,128)(2,1)S(1)} %get-tuple-element.273), channel_id=1, source_target_pairs={{0,16},{1,17},{2,18},{3,19},{4,20},{5,21},{6,22},{7,23},{8,24},{9,... | collective-permute-start | bytes 1105928 | tf_op jit(solution)/shard_map/ppermute | solution.py:114
  266.0 14.2 %collective-permute-start.52 = (bf16[2,48,1920]{2,1,0:T(8,128)(2,1)S(1)}, bf16[2,48,1920]{2,1,0:T(8,128)(2,1)S(1)}, u32[]{:S(2)}, u32[]{:S(2)}) collective-permute-start(bf16[2,48,1920]{2,1,0:T(8,128)(2,1)S(1)} %get-tuple-element.272), channel_id=1, source_target_pairs={{0,2},{1,3},{2,0},{3,1},{4,6},{5,7},{6,4},{7,5},{8,10},{9,11},{10,... | collective-permute-start | bytes 1105928 | tf_op jit(solution)/shard_map/ppermute | solution.py:114
  268.2 6.2 %collective-permute-start.66 = (bf16[96,384]{1,0:T(8,128)(2,1)S(1)}, bf16[96,384]{1,0:T(8,128)(2,1)S(1)}, u32[]{:S(2)}, u32[]{:S(2)}) collective-permute-start(bf16[96,384]{1,0:T(8,128)(2,1)S(1)} %dynamic-slice_convert_fusion.1), channel_id=1, source_target_pairs={{0,1},{1,0},{2,3},{3,2},{4,5},{5,4},{6,7},{7,6},{8,9},{9,8},{10,11... | collective-permute-start | bytes 221192 | tf_op jit(solution)/shard_map/ppermute | solution.py:794
  273.2 30.8 %collective-permute-start.55 = (bf16[512,768]{1,0:T(8,128)(2,1)S(1)}, bf16[512,768]{1,0:T(8,128)(2,1)S(1)}, u32[]{:S(2)}, u32[]{:S(2)}) collective-permute-start(bf16[512,768]{1,0:T(8,128)(2,1)S(1)} %shard_map.147), channel_id=1, source_target_pairs={{0,16},{16,0},{1,17},{17,1},{2,18},{18,2},{3,19},{19,3},{4,20},{20... | collective-permute-start | bytes 2359304 | tf_op jit(solution)/shard_map/ppermute | solution.py:900
  280.3 12.3 %collective-permute-start.53 = (bf16[2,2,48,1152]{3,2,1,0:T(8,128)(2,1)S(1)}, bf16[2,2,48,1152]{3,2,1,0:T(8,128)(2,1)S(1)}, u32[]{:S(2)}, u32[]{:S(2)}) collective-permute-start(bf16[2,2,48,1152]{3,2,1,0:T(8,128)(2,1)S(1)} %fusion.6), channel_id=1, source_target_pairs={{0,2},{1,3},{2,0},{3,1},{4,6},{5,7},{6,4},{7,5},{8,10},{9,11},{10,... | collective-permute-start | bytes 1327112 | tf_op jit(solution)/shard_map/ppermute | solution.py:114
  281.4 21.3 %collective-permute-start.54 = (bf16[2,2,48,1152]{3,2,1,0:T(8,128)(2,1)S(1)}, bf16[2,2,48,1152]{3,2,1,0:T(8,128)(2,1)S(1)}, u32[]{:S(2)}, u32[]{:S(2)}) collective-permute-start(bf16[2,2,48,1152]{3,2,1,0:T(8,128)(2,1)S(1)} %fusion.7), channel_id=1, source_target_pairs={{0,16},{1,17},{2,18},{3,19},{4,20},{5,21},{6,22},{7,23},{8,24},{9,... | collective-permute-start | bytes 1327112 | tf_op jit(solution)/shard_map/ppermute | solution.py:114
  283.6 22.8 %collective-permute-start.56 = (bf16[48,1920]{1,0:T(8,128)(2,1)S(1)}, bf16[48,1920]{1,0:T(8,128)(2,1)S(1)}, u32[]{:S(2)}, u32[]{:S(2)}) collective-permute-start(bf16[48,1920]{1,0:T(8,128)(2,1)S(1)} %get-tuple-element.271), channel_id=1, source_target_pairs={{0,4},{1,5},{2,6},{3,7},{4,8},{5,9},{6,10},{7,11},{8,12},{9,13},{1... | collective-permute-start | bytes 552968 | tf_op jit(solution)/shard_map/ppermute | solution.py:128
  283.8 22.6 %collective-permute-start.57 = (bf16[48,1920]{1,0:T(8,128)(2,1)S(1)}, bf16[48,1920]{1,0:T(8,128)(2,1)S(1)}, u32[]{:S(2)}, u32[]{:S(2)}) collective-permute-start(bf16[48,1920]{1,0:T(8,128)(2,1)S(1)} %get-tuple-element.268), channel_id=1, source_target_pairs={{0,8},{1,9},{2,10},{3,11},{4,12},{5,13},{6,14},{7,15},{8,0},{9,1},... | collective-permute-start | bytes 552968 | tf_op jit(solution)/shard_map/ppermute | solution.py:128
  292.6 13.9 %collective-permute-start.58 = (bf16[48,1920]{1,0:T(8,128)(2,1)S(1)}, bf16[48,1920]{1,0:T(8,128)(2,1)S(1)}, u32[]{:S(2)}, u32[]{:S(2)}) collective-permute-start(bf16[48,1920]{1,0:T(8,128)(2,1)S(1)} %get-tuple-element.267), channel_id=1, source_target_pairs={{0,12},{1,13},{2,14},{3,15},{4,0},{5,1},{6,2},{7,3},{8,4},{9,5},{1... | collective-permute-start | bytes 552968 | tf_op jit(solution)/shard_map/ppermute | solution.py:128
  302.9 7.1 %collective-permute-start.59 = (bf16[2,48,1152]{2,1,0:T(8,128)(2,1)S(1)}, bf16[2,48,1152]{2,1,0:T(8,128)(2,1)S(1)}, u32[]{:S(2)}, u32[]{:S(2)}) collective-permute-start(bf16[2,48,1152]{2,1,0:T(8,128)(2,1)S(1)} %get-tuple-element.279), channel_id=1, source_target_pairs={{0,16},{1,17},{2,18},{3,19},{4,20},{5,21},{6,22},{7,23},{8,24},{9,... | collective-permute-start | bytes 663560 | tf_op jit(solution)/shard_map/ppermute | solution.py:114
  304.1 6.7 %collective-permute-start.60 = (bf16[2,48,1152]{2,1,0:T(8,128)(2,1)S(1)}, bf16[2,48,1152]{2,1,0:T(8,128)(2,1)S(1)}, u32[]{:S(2)}, u32[]{:S(2)}) collective-permute-start(bf16[2,48,1152]{2,1,0:T(8,128)(2,1)S(1)} %get-tuple-element.278), channel_id=1, source_target_pairs={{0,2},{1,3},{2,0},{3,1},{4,6},{5,7},{6,4},{7,5},{8,10},{9,11},{10,... | collective-permute-start | bytes 663560 | tf_op jit(solution)/shard_map/ppermute | solution.py:114
  311.9 3.7 %collective-permute-start.65 = (bf16[24,1920]{1,0:T(8,128)(2,1)S(1)}, bf16[24,1920]{1,0:T(8,128)(2,1)S(1)}, u32[]{:S(2)}, u32[]{:S(2)}) collective-permute-start(bf16[24,1920]{1,0:T(8,128)(2,1)S(1)} %dynamic-slice_convert_fusion), channel_id=1, source_target_pairs={{0,1},{1,0},{2,3},{3,2},{4,5},{5,4},{6,7},{7,6},{8,9},{9,8},{10,11... | collective-permute-start | bytes 276488 | tf_op jit(solution)/shard_map/ppermute | solution.py:794
  312.2 5.5 %collective-permute-start.63 = (bf16[48,1152]{1,0:T(8,128)(2,1)S(1)}, bf16[48,1152]{1,0:T(8,128)(2,1)S(1)}, u32[]{:S(2)}, u32[]{:S(2)}) collective-permute-start(bf16[48,1152]{1,0:T(8,128)(2,1)S(1)} %get-tuple-element.276), channel_id=1, source_target_pairs={{0,12},{1,13},{2,14},{3,15},{4,0},{5,1},{6,2},{7,3},{8,4},{9,5},{1... | collective-permute-start | bytes 331784 | tf_op jit(solution)/shard_map/ppermute | solution.py:128
  313.9 10.8 %collective-permute-start.62 = (bf16[48,1152]{1,0:T(8,128)(2,1)S(1)}, bf16[48,1152]{1,0:T(8,128)(2,1)S(1)}, u32[]{:S(2)}, u32[]{:S(2)}) collective-permute-start(bf16[48,1152]{1,0:T(8,128)(2,1)S(1)} %get-tuple-element.275), channel_id=1, source_target_pairs={{0,8},{1,9},{2,10},{3,11},{4,12},{5,13},{6,14},{7,15},{8,0},{9,1},... | collective-permute-start | bytes 331784 | tf_op jit(solution)/shard_map/ppermute | solution.py:128
  313.9 10.8 %collective-permute-start.61 = (bf16[48,1152]{1,0:T(8,128)(2,1)S(1)}, bf16[48,1152]{1,0:T(8,128)(2,1)S(1)}, u32[]{:S(2)}, u32[]{:S(2)}) collective-permute-start(bf16[48,1152]{1,0:T(8,128)(2,1)S(1)} %get-tuple-element.277), channel_id=1, source_target_pairs={{0,4},{1,5},{2,6},{3,7},{4,8},{5,9},{6,10},{7,11},{8,12},{9,13},{1... | collective-permute-start | bytes 331784 | tf_op jit(solution)/shard_map/ppermute | solution.py:128
  (50 other events, 707.6 us)

commit v3 on v2

--- a/solution.py
+++ b/solution.py
@@ -96,7 +96,8 @@
 
 def scatter_steps(grid, mine, other, cut):
     got = lax.ppermute(other, AXES, grid.core_swap())
-    (got,) = yield [got]
+    back = yield [got]
+    (got,), held = (back[0], tuple(back[1:])) if isinstance(back, tuple) else (back, ())
     shape = (grid.ny, grid.nx, grid.nz) + mine.shape[1:]
     mine, got = mine.reshape(shape), got.reshape(shape)
     cut = min(cut, grid.nz)
@@ -110,14 +111,17 @@
             pieces = [
                 [lax.index_in_dim(c, k, dim, keepdims=False) for c in current[n]] for k in range(grid.sizes[axis])
             ]
-            received = [
-                lax.ppermute(add_all(pieces[k]).astype(BF16), AXES, grid.shift(axis, k))
-                for k in range(1, grid.sizes[axis])
+            waiting.append([add_all(pieces[k]).astype(BF16) for k in range(1, grid.sizes[axis])])
+            current[n] = pieces[0]
+        if held:
+            waiting, held = together(waiting, held)
+        for n, (_, _, axes) in enumerate(lots):
+            waiting[n] = [
+                lax.ppermute(total, AXES, grid.shift(axes[step], k + 1)) for k, total in enumerate(waiting[n])
             ]
-            waiting.append(received)
-            current[n] = pieces[0]
-        flat = yield [a for received in waiting for a in received]
-        flat = list(flat)
+        flat = [a for received in waiting for a in received]
+        back = yield (flat, *held) if held else flat
+        flat, held = (back[0], tuple(back[1:])) if isinstance(back, tuple) else (list(back), ())
         for n, received in enumerate(waiting):
             current[n] = current[n] + flat[: len(received)]
             flat = flat[len(received) :]
@@ -206,30 +210,41 @@
         return started
 
 
+def hand_on(scratch, target, sem, step, steps):
+    copy = pltpu.make_async_copy(scratch, target, sem.at[0])
+
+    @pl.when(step == 0)
+    def _():
+        copy.start()
+
+    @pl.when(step == steps - 1)
+    def _():
+        copy.wait()
+
+
 def wait_all(copies):
     for copy in copies:
         copy.wait()
 
 
-def emit(value, side, first_chip, rows, mine, other, columns, tab, chips):
-    rel = side ^ tab[2 * chips]
+def emit(value, first_chip, rows, ref, columns, tab, chips):
     height = value.shape[0]
     low = value.astype(BF16)
-
-    def put(ref):
-        if rows >= height:
-            ref[0, pl.ds(first_chip, height), columns] = low
-        else:
-            for a in range(height // rows):
-                ref[tab[chips + first_chip + a], :, columns] = low[a * rows : (a + 1) * rows]
-
-    @pl.when(rel == 0)
-    def _():
-        put(mine)
-
-    @pl.when(rel != 0)
-    def _():
-        put(other)
+    if rows >= height:
+        ref[0, pl.ds(first_chip, height), columns] = low
+    else:
+        for a in range(height // rows):
+            ref[tab[chips + first_chip + a], :, columns] = low[a * rows : (a + 1) * rows]
+
+
+def by_side(core, mine, other, run):
+    @pl.when(core == 0)
+    def _():
+        run(mine, other)
+
+    @pl.when(core != 0)
+    def _():
+        run(other, mine)
 
 
 def place_of(row, rows, chips):
@@ -238,7 +253,7 @@
 
 def input_kernel(pieces, n_refs, chips, tab, own, got, *refs):
     sources, refs = refs[:n_refs], refs[n_refs:]
-    packed, normed, gains, w_qkv, gain_cols, sems = refs
+    packed, normed, gains, w_whole, w_qkv, gain_cols, sems, w_sem = refs
     i = pl.program_id(0)
     steps = pl.num_programs(0)
     width = own.shape[1]
@@ -260,6 +275,7 @@
     for c in range(3):
         cols = slice(c * width, (c + 1) * width)
         packed[:, cols] = nn(low, w_qkv[:, cols]).astype(BF16)
+    hand_on(w_qkv, w_whole, w_sem, i, steps)
 
 
 def pair_of(ref, n):
@@ -273,44 +289,63 @@
     bias[...] = jnp.where(apart, -1e30, 0.0)
 
 
-def attend_kernel(chips, tab, q_ref, k_ref, v_ref, attended, log_totals, bias):
+def by_class(short, run):
+    @pl.when(short == 0)
+    def _():
+        run(False)
+
+    @pl.when(short != 0)
+    def _():
+        run(True)
+
+
+def attend_kernel(chips, tab, q_ref, k_ref, v_ref, *refs):
+    attended, log_totals, bias = refs[-3:]
+    short = tab[2 * chips + 1]
+
     @pl.when(jnp.logical_and(pl.program_id(0) == 0, pl.program_id(1) == 0))
     def _():
-        fill_bias(bias, tab[2 * chips + 1])
-
-    lane = lax.broadcasted_iota(jnp.int32, (512, 128), 1)
-    for n in range(2):
-        q, k, v = pair_of(q_ref, n), pair_of(k_ref, n), pair_of(v_ref, n)
-        v_t = v.T
-        mixed = []
-        for h in range(2):
-            k_h = jnp.where((lane // 64) == h, k, jnp.zeros_like(k))
-            s = nt(k_h, q) * (SCORE_SCALE * LOG2E) + bias[...]
-            top_score = jnp.max(s, axis=0, keepdims=True)
-            p = jnp.exp2(s - top_score)
-            total = jnp.sum(p, axis=0, keepdims=True)
-            mixed.append(nn(v_t[64 * h : 64 * h + 64, :], p.astype(BF16)) * (1.0 / total))
-            log_totals[2 * n + h] = top_score + jnp.log2(total)
-        out = jnp.concatenate(mixed, axis=0).T.astype(BF16)
-        attended[:, 0, :, 128 * n : 128 * (n + 1)] = out.reshape(2, 256, 128)
-
-
-ERF_P = 0.3275911 * (0.5**0.5)
-ERF_A = (0.254829592 * 0.5, -0.284496736 * 0.5, 1.421413741 * 0.5, -1.453152027 * 0.5, 1.061405429 * 0.5)
+        fill_bias(bias, short)
+
+    def run(masked):
+        lane = lax.broadcasted_iota(jnp.int32, (512, 128), 1)
+        q, k, v = [[pair_of(ref, n) for n in range(2)] for ref in (q_ref, k_ref, v_ref)]
+
+        def head_of(value, h):
+            return jnp.where((lane // 64) == h, value, jnp.zeros_like(value))
+
+        def scores(i):
+            s = nt(head_of(q[i // 2], i % 2), k[i // 2])
+            return s + bias[...] if masked else s
+
+        logs = jnp.zeros((512, 128), F32)
+        mixed = [0.0, 0.0]
+        ahead = scores(0)
+        for i in range(4):
+            s, ahead = ahead, scores(i + 1) if i < 3 else None
+            top_score = jnp.max(s, axis=1, keepdims=True) * (SCORE_SCALE * LOG2E)
+            p = jnp.exp2(s * (SCORE_SCALE * LOG2E) - top_score)
+            total = jnp.sum(p, axis=1, keepdims=True)
+            logs = jnp.where(lane == i, top_score + jnp.log2(total), logs)
+            mixed[i // 2] = mixed[i // 2] + nn(p.astype(BF16), head_of(v[i // 2], i % 2)) * (1.0 / total)
+        for n in range(2):
+            attended[:, 0, :, 128 * n : 128 * (n + 1)] = mixed[n].astype(BF16).reshape(2, 256, 128)
+        turned = logs.T
+        for i in range(4):
+            log_totals[i] = turned[i : i + 1, :]
+
+    by_class(short, run)
 
 
 def gelu_both(u):
-    t = 1.0 / (1.0 + ERF_P * jnp.abs(u))
-    bell = jnp.exp2(u * u * (-0.5 * LOG2E))
-    poly = t * (ERF_A[0] + t * (ERF_A[1] + t * (ERF_A[2] + t * (ERF_A[3] + t * ERF_A[4]))))
-    tail = poly * bell
-    below = jnp.where(u < 0, tail, 1.0 - tail)
-    return u * below, below + u * (bell * 0.3989422804014327)
+    below = 0.5 + 0.5 * lax.erf(u * (0.5**0.5))
+    bell = jnp.exp2(u * u * (-0.5 * LOG2E)) * 0.3989422804014327
+    return u * below, below + u * bell
 
 
 def middle_kernel(pieces, n_refs, chips, tab, attended, own, got, gains, *refs):
     sources, refs = refs[:n_refs], refs[n_refs:]
-    hidden, normed, w_out, sems = refs
+    hidden, normed, w_whole, w_out, sems, w_sem = refs
     i = pl.program_id(0)
 
     @pl.when(i == 0)
@@ -322,76 +357,89 @@
     hidden[...] = h
     z, _ = normalized(h)
     normed[...] = (z * gains[1:2, :]).astype(BF16)
-
-
-def up_kernel(pieces, n_refs, chips, first, tab, normed, *refs):
-    sources, refs = refs[-n_refs - 4 : -4], refs[-4:]
-    active, slope, w_up, sems = refs
-    rows, width = normed.shape
-    j = pl.program_id(0)
-
-    @pl.when(j == 0)
-    def _():
-        wait_all(pieces.start(sources, tab, {"up": w_up}, sems, 0)["up"])
-
-    cols = pl.ds(pl.multiple_of((first + j) * width, 128), width)
-    for i in range(rows // 256):
+    hand_on(w_out, w_whole, w_sem, i, pl.num_programs(0))
+
+
+def up_tiles(normed, weight, active, slope):
+    for i in range(normed.shape[0] // 256):
         rows = slice(256 * i, 256 * (i + 1))
-        a, s = gelu_both(nn(normed[rows, :], w_up[:, cols]))
+        a, s = gelu_both(nn(normed[rows, :], weight))
         active[rows, :] = a.astype(BF16)
         slope[rows, :] = s.astype(BF16)
+
+
+def up_kernel(pieces, n_refs, chips, tab, normed, *refs):
+    sources, refs = refs[:n_refs], refs[n_refs:]
+    active, slope, w_whole, w_up, sems, w_sem = refs
+    width = normed.shape[1]
+    j = pl.program_id(0)
+
+    @pl.when(j == 0)
+    def _():
+        wait_all(pieces.start(sources, tab, {"up": w_up}, sems, 0)["up"])
+
+    up_tiles(normed, w_up[:, pl.ds(pl.multiple_of(j * width, 128), width)], active, slope)
+    hand_on(w_up, w_whole, w_sem, j, pl.num_programs(0))
+
+
+def up_rest_kernel(tab, normed, w_up, _active, _slope, active, slope):
+    up_tiles(normed, w_up[...], active, slope)
 
 
 def down_grad_kernel(chips, rows_down, tab, active, cot_own, cot_got, down_mine, down_other):
     half, width = cot_own.shape
     j = pl.program_id(0)
-    for m in range(2):
-        piece = slice(384 * m, 384 * (m + 1))
-        grad = tn(active[:half, piece], cot_own[...]) + tn(active[half:, piece], cot_got[...])
-        start = place_of(width * j + 384 * m, rows_down, chips)
-        emit(grad[:, : width // 2], 0, start, rows_down, down_mine, down_other, slice(None), tab, chips)
-        emit(grad[:, width // 2 :], 1, start, rows_down, down_mine, down_other, slice(None), tab, chips)
-
-
-def down_back_kernel(pieces, n_refs, chips, rows_up, tab, cot_own, cot_got, normed, slope, *refs):
-    sources, refs = refs[:n_refs], refs[n_refs:]
-    grad_up, up_mine, up_other, w_down, sems = refs
+
+    def run(left, right):
+        for m in range(2):
+            piece = slice(384 * m, 384 * (m + 1))
+            grad = tn(active[:half, piece], cot_own[...]) + tn(active[half:, piece], cot_got[...])
+            start = place_of(width * j + 384 * m, rows_down, chips)
+            emit(grad[:, : width // 2], start, rows_down, left, slice(None), tab, chips)
+            emit(grad[:, width // 2 :], start, rows_down, right, slice(None), tab, chips)
+
+    by_side(tab[2 * chips], down_mine, down_other, run)
+
+
+def down_back_kernel(chips, rows_up, tab, cot_own, cot_got, normed, slope, w_down, grad_up, up_mine, up_other):
     half, width = cot_own.shape
     j = pl.program_id(0)
     steps = pl.num_programs(0)
 
-    @pl.when(j == 0)
-    def _():
-        wait_all(pieces.start(sources, tab, {"down": w_down}, sems, 0)["down"])
-
-    w_rows = pl.ds(pl.multiple_of(j * width, 256), width)
-    for part, cot in enumerate((cot_own, cot_got)):
-        for i in range(half // 256):
-            inner = slice(256 * i, 256 * (i + 1))
-            rows = slice(part * half + 256 * i, part * half + 256 * (i + 1))
-            grad_up[rows, :] = (nt(cot[inner, :], w_down[w_rows, :]) * slope[rows, :].astype(F32)).astype(BF16)
-
-    side = j // (steps // 2)
-    offset = lax.rem(j, steps // 2) * width
-    for m in range(2):
-        grad = tn(normed[:, 384 * m : 384 * (m + 1)], grad_up[...])
-        start = place_of(384 * m, rows_up, chips)
-        emit(grad, side, start, rows_up, up_mine, up_other, pl.ds(pl.multiple_of(offset, 128), width), tab, chips)
-
-
-def up_back_kernel(pieces, n_refs, chips, rows_up, tab, grad_up, attended, gains, cot_own, cot_got, hidden, _mine, _other, *refs):
-    sources, refs = refs[:n_refs], refs[n_refs:]
-    grad_hidden, grad_att, out_mine, out_other, w_up, w_out, total_out, sems = refs
+    offset = pl.multiple_of(lax.rem(j, steps // 2) * width, 128)
+
+    def run(target):
+        for part, cot in enumerate((cot_own, cot_got)):
+            for i in range(half // 256):
+                inner = slice(256 * i, 256 * (i + 1))
+                rows = slice(part * half + 256 * i, part * half + 256 * (i + 1))
+                grad_up[rows, :] = (nt(cot[inner, :], w_down[...]) * slope[rows, :].astype(F32)).astype(BF16)
+        for m in range(2):
+            grad = tn(normed[:, 384 * m : 384 * (m + 1)], grad_up[...])
+            emit(grad, place_of(384 * m, rows_up, chips), rows_up, target, pl.ds(offset, width), tab, chips)
+
+    rel = (j // (steps // 2)) ^ tab[2 * chips]
+
+    @pl.when(rel == 0)
+    def _():
+        run(up_mine)
+
+    @pl.when(rel != 0)
+    def _():
+        run(up_other)
+
+
+def up_back_kernel(
+    chips, rows_up, tab, grad_up, attended, gains, cot_own, cot_got, hidden, _mine, _other, w_up, w_out, *refs
+):
+    grad_hidden, grad_att, out_mine, out_other, total_out = refs
     i = pl.program_id(0)
     steps = pl.num_programs(0)
     width = hidden.shape[1]
 
     @pl.when(i == 0)
     def _():
-        started = pieces.start(sources, tab, {"up": w_up, "out": w_out}, sems, 0)
         total_out[...] = jnp.zeros_like(total_out)
-        wait_all(started["up"])
-        wait_all(started["out"])
 
     cot = jnp.where(i < steps // 2, cot_own[...], cot_got[...]).astype(F32)
     e = nt(grad_up[...], w_up[...])
@@ -404,90 +452,106 @@
 
     @pl.when(i == steps - 1)
     def _():
-        for m in range(2):
-            start = place_of(384 * m, rows_up, chips)
-            for side in range(2):
-                value = total_out[384 * m : 384 * (m + 1), side * (width // 2) : (side + 1) * (width // 2)]
-                emit(value, side, start, rows_up, out_mine, out_other, slice(None), tab, chips)
+        def run(left, right):
+            for m in range(2):
+                start = place_of(384 * m, rows_up, chips)
+                for side, ref in enumerate((left, right)):
+                    value = total_out[384 * m : 384 * (m + 1), side * (width // 2) : (side + 1) * (width // 2)]
+                    emit(value, start, rows_up, ref, slice(None), tab, chips)
+
+        by_side(tab[2 * chips], out_mine, out_other, run)
 
 
 def output_kernel(pieces, n_refs, chips, tab, active, hidden, *refs):
     sources, refs = refs[:n_refs], refs[n_refs:]
-    out, w_down, sems = refs
+    out, w_whole, w_down, sems, w_sem = refs
 
     @pl.when(pl.program_id(0) == 0)
     def _():
         wait_all(pieces.start(sources, tab, {"down": w_down}, sems, 0)["down"])
 
     out[...] = (hidden[...] + nn(active[...], w_down[...])).astype(BF16)
+    hand_on(w_down, w_whole, w_sem, pl.program_id(0), pl.num_programs(0))
 
 
 def attend_back_kernel(chips, tab, q_ref, k_ref, v_ref, o_ref, d_ref, log_totals, grad_q_ref, grad_k_ref, grad_v_ref, bias):
+    short = tab[2 * chips + 1]
+
     @pl.when(jnp.logical_and(pl.program_id(0) == 0, pl.program_id(1) == 0))
     def _():
-        fill_bias(bias, tab[2 * chips + 1])
-
-    lane = lax.broadcasted_iota(jnp.int32, (512, 128), 1)
-    for n in range(2):
-        q, k, v, o, d = [pair_of(r, n) for r in (q_ref, k_ref, v_ref, o_ref, d_ref)]
-        k_t = k.T
-        dots = (o.astype(F32) * d.astype(F32)).T
-        grad_q, grad_k, grad_v = [], [], []
-        for h in range(2):
-            here = (lane // 64) == h
-            zero = jnp.zeros_like(k)
-            s = nt(jnp.where(here, k, zero), q) * (SCORE_SCALE * LOG2E) + bias[...]
-            p = jnp.exp2(s - log_totals[2 * n + h])
-            grad_v.append(nn(p.astype(BF16), jnp.where(here, d, zero)))
-            grad_p = nt(jnp.where(here, v, zero), d)
-            delta = jnp.sum(dots[64 * h : 64 * h + 64, :], axis=0, keepdims=True)
-            grad_s = (p * (grad_p - delta)).astype(BF16)
-            grad_k.append(nn(grad_s, jnp.where(here, q, zero)))
-            grad_q.append(nn(k_t[64 * h : 64 * h + 64, :], grad_s))
-
-        def put(ref, value):
-            ref[:, 0, :, 128 * n : 128 * (n + 1)] = value.astype(BF16).reshape(2, 256, 128)
-
-        put(grad_q_ref, jnp.concatenate(grad_q, axis=0).T * SCORE_SCALE)
-        put(grad_k_ref, (grad_k[0] + grad_k[1]) * SCORE_SCALE)
-        put(grad_v_ref, grad_v[0] + grad_v[1])
+        fill_bias(bias, short)
+
+    def put(ref, n, value):
+        ref[:, 0, :, 128 * n : 128 * (n + 1)] = value.astype(BF16).reshape(2, 256, 128)
+
+    def run(masked):
+        lane = lax.broadcasted_iota(jnp.int32, (512, 128), 1)
+        for n in range(2):
+            q, k, v, o, d = [pair_of(r, n) for r in (q_ref, k_ref, v_ref, o_ref, d_ref)]
+            k_t = k.T
+            dots = (o.astype(F32) * d.astype(F32)).T
+            grad_q, grad_k, grad_v = [], [], []
+            for h in range(2):
+                here = (lane // 64) == h
+                zero = jnp.zeros_like(k)
+                s = nt(jnp.where(here, k, zero), q)
+                if masked:
+                    s = s + bias[...]
+                p = jnp.exp2(s * (SCORE_SCALE * LOG2E) - log_totals[2 * n + h])
+                grad_v.append(nn(p.astype(BF16), jnp.where(here, d, zero)))
+                grad_p = nt(jnp.where(here, v, zero), d)
+                delta = jnp.sum(dots[64 * h : 64 * h + 64, :], axis=0, keepdims=True)
+                grad_s = (p * (grad_p - delta)).astype(BF16)
+                grad_k.append(nn(grad_s, jnp.where(here, q, zero)))
+                grad_q.append(nn(k_t[64 * h : 64 * h + 64, :], grad_s))
+            put(grad_q_ref, n, jnp.concatenate(grad_q, axis=0).T * SCORE_SCALE)
+            put(grad_k_ref, n, (grad_k[0] + grad_k[1]) * SCORE_SCALE)
+            put(grad_v_ref, n, grad_v[0] + grad_v[1])
+
+    by_class(short, run)
 
 
 def qkv_grad_kernel(chips, rows_qkv, cuts, tab, normed, *refs):
     grads, mine, other = refs[:-2], refs[-2], refs[-1]
     width = normed.shape[1]
     wide = 3 * width // 2
-    for n, ref in enumerate(grads):
-        base = (n % 3) * width + cuts[n // 3]
-        size = ref.shape[1]
-        for m in range(2):
-            grad = tn(normed[:, 384 * m : 384 * (m + 1)], ref[...])
-            start = place_of(384 * m, rows_qkv, chips)
-            at = base
-            while at < base + size:
-                side = at // wide
-                end = min(base + size, (side + 1) * wide)
-                columns = slice(at - side * wide, end - side * wide)
-                emit(grad[:, at - base : end - base], side, start, rows_qkv, mine, other, columns, tab, chips)
-                at = end
-
-
-def first_kernel(pieces, n_refs, chips, cuts, tab, source, gains, grad_hidden, *refs):
-    n_grads = 3 * (len(cuts) - 1)
-    grads, sources, refs = refs[:n_grads], refs[n_grads : n_grads + n_refs], refs[n_grads + n_refs :]
-    out, w_qkv, sems = refs
-    width = source.shape[1]
-
-    @pl.when(pl.program_id(0) == 0)
-    def _():
-        wait_all(pieces.start(sources, tab, {"qkv": w_qkv}, sems, 0)["qkv"])
-
+
+    def run(*sides):
+        for n, ref in enumerate(grads):
+            base = (n % 3) * width + cuts[n // 3]
+            size = ref.shape[1]
+            for m in range(2):
+                grad = tn(normed[:, 384 * m : 384 * (m + 1)], ref[...])
+                start = place_of(384 * m, rows_qkv, chips)
+                at = base
+                while at < base + size:
+                    side = at // wide
+                    end = min(base + size, (side + 1) * wide)
+                    columns = slice(at - side * wide, end - side * wide)
+                    emit(grad[:, at - base : end - base], start, rows_qkv, sides[side], columns, tab, chips)
+                    at = end
+
+    by_side(tab[2 * chips], mine, other, run)
+
+
+def first_kernel(cuts, tab, own, got, gains, grad_hidden, w_qkv, *refs):
+    grads, (out_own, out_got) = refs[:-2], refs[-2:]
+    width = own.shape[1]
+    here = pl.program_id(0) < pl.num_programs(0) // 2
     e = 0.0
     for n, grad in enumerate(grads):
         base, lot = (n % 3) * width, n // 3
         e = e + nt(grad[...], w_qkv[:, base + cuts[lot] : base + cuts[lot + 1]])
-    z, root = normalized(source[...].astype(F32))
-    out[...] = (grad_hidden[...] + norm_back(z, root, e * gains[0:1, :])).astype(BF16)
+    z, root = normalized(jnp.where(here, own[...], got[...]).astype(F32))
+    value = (grad_hidden[...] + norm_back(z, root, e * gains[0:1, :])).astype(BF16)
+
+    @pl.when(here)
+    def _():
+        out_own[...] = value
+
+    @pl.when(jnp.logical_not(here))
+    def _():
+        out_got[...] = value
 
 
 def whole(shape):
@@ -499,7 +563,7 @@
 
 def call(kernel, tab, inputs, piece_arrays, outs, scratch, grid=(1,), cost=0, aliases=None):
     specs = [spec or whole(a.shape) for a, spec in inputs]
-    specs = specs + [pl.BlockSpec(memory_space=pl.ANY) for _ in piece_arrays]
+    specs = specs + [pl.BlockSpec(memory_space=pltpu.HBM) for _ in piece_arrays]
     blocks = [(a, spec) for a, spec in inputs] + [(o, spec) for o, spec in outs]
     need = SPARE_BYTES
     for array, spec in blocks:
@@ -597,7 +661,7 @@
             )
 
         tok_away, w_qkv = together(tok_away, w_qkv)
-        tok_first = lax.ppermute(tok_away[: half // 2], "seq", swap_x)
+        tok_got = lax.ppermute(tok_away, "seq", swap_x)
         piece_a = with_partner(0)
         piece_a, w_up, w_out, w_down = together(piece_a, w_up, w_out, w_down)
         piece_b, piece_c = with_partner(1), with_partner(2)
@@ -617,28 +681,33 @@
         def flat(groups):
             return [part for group in groups for part in group]
 
+        def swapped(parts):
+            return [(swap_core(a), s) for a, s in parts]
+
+        def pieces_from(mine, theirs, fields):
+            named = lambda parts: [(a, [rel_of(grid, s) for s in spots]) for a, spots in parts]
+            return Pieces(chips, named(mine), named(theirs), fields)
+
         def finish(mine, fields):
             mine = [(a, [rel_of(grid, s) for s in spots]) for a, spots in mine]
             theirs = [(swap_core(a), s) for a, s in mine]
             return Pieces(chips, mine, theirs, fields)
 
         z_a = gather_along_z(grid, piece_a)
-        arrays, tok_first, piece_b, tok_next = together(arrays_of(z_a), tok_first, piece_b, tok_away[half // 2 :])
-        tok_second = lax.ppermute(tok_next, "seq", swap_x)
+        arrays, tok_got, piece_b = together(arrays_of(z_a), tok_got, piece_b)
         z_a = lots_of(with_arrays(z_a, arrays), 2)
         near_a = near_of(z_a)
         z_b = gather_along_z(grid, piece_b)
-        arrays, tok_second = together(arrays_of(flat(near_a)), tok_second)
-        tok_got = jnp.concatenate([tok_first, tok_second], axis=0)
+        arrays = lax.optimization_barrier(arrays_of(flat(near_a)))
         wide_a = widened(z_a, [[part] for part in with_arrays(flat(near_a), arrays)])
         far_a = far_of(wide_a)
         all_a = wide_a + far_a
         arrays_a, z_own, piece_c = together(arrays_of(all_a), z_b[0][0], piece_c)
         z_b = with_arrays(z_b, [z_own] + arrays_of(z_b[1:]))
         group_a = finish(with_arrays(all_a, arrays_a), fields_a)
-        arrays_b = lax.optimization_barrier(arrays_of(z_b))
-        z_b = lots_of(with_arrays(z_b, arrays_b), 2)
+        z_b = lots_of(with_arrays(z_b, lax.optimization_barrier(arrays_of(z_b))), 2)
         near_b = near_of(z_b)
+        z_c = gather_along_z(grid, piece_c)
     else:
         full = [lax.all_gather(w, AXES, axis=0, tiled=True) for w in (w_qkv, w_out, w_up, w_down, gain_block)]
 
@@ -667,100 +736,115 @@
     chunk = pl.BlockSpec((rows, width), lambda j, t: (0, j))
     low = lambda *shape: sds(shape, BF16)
 
-    packed, normed_first, gains = call(
+    packed, normed_first, gains, whole_qkv = call(
         functools.partial(input_kernel, group_a, len(group_a.arrays), chips),
         tab,
         [(tok_own, own_tile), (tok_got, got_tile)],
         group_a.arrays,
-        [(low(rows, 3 * width), tile(3 * width)), (low(rows, width), tile(width)), (sds((8, width), F32), None)],
-        [vmem((width, 3 * width), BF16), vmem((width, 128), BF16), dma((group_a.copies(("qkv", "gain")),))],
+        [(pltpu.HBM((rows, 3 * width), BF16), tile(3 * width)), (low(rows, width), tile(width)), (sds((8, width), F32), None),
+         (pltpu.HBM((width, 3 * width), BF16), anywhere)],
+        [vmem((width, 3 * width), BF16), vmem((width, 128), BF16), dma((group_a.copies(("qkv", "gain")),)), dma((1,))],
         grid=(tiles,),
         cost=2 * rows * width * 3 * width,
     )
 
     if fast:
-        packed, arrays_b, piece_c = together(packed, arrays_of(flat(near_b)), piece_c)
+        packed, arrays_b, arrays_c = together(packed, arrays_of(flat(near_b)), arrays_of(z_c))
+        z_c = with_arrays(z_c, arrays_c)
         wide_b = widened(z_b, [[part] for part in with_arrays(flat(near_b), arrays_b)])
         far_b = far_of(wide_b)
-        z_c = gather_along_z(grid, piece_c)
+        their_wide_b = swapped(wide_b)
 
     clip_blocks = half // 256
     by_clip = lambda a: a.reshape(2, clip_blocks, 256, a.shape[1])
-    heads_at = lambda base: pl.BlockSpec((2, 1, 256, 256), lambda b, g, t: (0, b, 0, base + g))
-    totals_at = pl.BlockSpec((4, 1, 512), lambda b, g, t: (b * (heads // 4) + g, 0, 0))
     clip_shape = low(2, clip_blocks, 256, width)
     step = width // 256
-    qkv_in = [(by_clip(packed), heads_at(0)), (by_clip(packed), heads_at(step)), (by_clip(packed), heads_at(2 * step))]
-    attended, log_totals = call(
-        functools.partial(attend_kernel, chips),
-        tab,
-        qkv_in,
-        [],
-        [(clip_shape, heads_at(0)), (sds((clip_blocks * heads, 1, 512), F32), totals_at)],
-        [vmem((512, 512), F32)],
-        grid=(clip_blocks, heads // 4),
-        cost=8 * rows * 512 * width,
-    )
+    totals_shape = sds((clip_blocks * heads, 1, 512), F32)
+
+    def attend(first, last, packed, earlier):
+        at = lambda base: pl.BlockSpec((2, 1, 256, 256), lambda b, g, t: (0, first + b, 0, base + g))
+        totals = pl.BlockSpec((4, 1, 512), lambda b, g, t: ((first + b) * (heads // 4) + g, 0, 0))
+        return call(
+            functools.partial(attend_kernel, chips),
+            tab,
+            [(by_clip(packed), at(0)), (by_clip(packed), at(step)), (by_clip(packed), at(2 * step))]
+            + [(a, anywhere) for a in earlier],
+            [],
+            [(clip_shape, at(0)), (totals_shape, totals)],
+            [vmem((512, 512), F32)],
+            grid=(last - first, heads // 4),
+            cost=8 * rows * 512 * width * (last - first) // clip_blocks,
+            aliases={4: 0, 5: 1} if earlier else None,
+        )
+
+    attended, log_totals = attend(0, clip_blocks, packed, [])
     attended = attended.reshape(rows, width)
 
     if fast:
-        all_b = wide_b + far_b
-        attended, arrays_b, arrays_c = together(attended, arrays_of(all_b), arrays_of(z_c))
-        group_b = finish(with_arrays(all_b, arrays_b), fields_b)
-        z_c = lots_of(with_arrays(z_c, arrays_c), grid.nz)
+        attended, arrays_b, arrays_w, arrays_c = together(
+            attended, arrays_of(far_b), arrays_of(their_wide_b), arrays_of(z_c)
+        )
+        far_b, their_wide_b = with_arrays(far_b, arrays_b), with_arrays(their_wide_b, arrays_w)
+        group_b = pieces_from(wide_b + far_b, their_wide_b + swapped(far_b), fields_b)
+        z_c = [joined_parts(with_arrays(z_c, arrays_c))]
         near_c = exchange(grid, z_c, "x")
         straight_c = exchange(grid, z_c, "y")
 
-    hidden, normed_second = call(
+    hidden, normed_second, whole_out = call(
         functools.partial(middle_kernel, group_b, len(group_b.arrays), chips),
         tab,
         [(attended, tile(width)), (tok_own, own_tile), (tok_got, got_tile), (gains, None)],
         group_b.arrays,
-        [(sds((rows, width), F32), tile(width)), (low(rows, width), tile(width))],
-        [vmem((width, width), BF16), dma((group_b.copies(("out",)),))],
+        [
+            (sds((rows, width), F32), tile(width)), (low(rows, width), tile(width)),
+            (pltpu.HBM((width, width), BF16), anywhere),
+        ],
+        [vmem((width, width), BF16), dma((group_b.copies(("out",)),)), dma((1,))],
         grid=(tiles,),
         cost=2 * rows * width * width,
     )
 
     steps = ff // width
 
-    def up_part_of(first, count, normed, earlier):
-        to = pl.BlockSpec((rows, width), lambda j, t: (0, first + j))
-        return call(
-            functools.partial(up_kernel, group_b, len(group_b.arrays), chips, first),
-            tab,
-            [(normed, None)] + [(a, anywhere) for a in earlier],
-            group_b.arrays,
-            [(pltpu.HBM((rows, ff), BF16), to), (pltpu.HBM((rows, ff), BF16), to)],
-            [vmem((width, ff), BF16), dma((group_b.copies(("up",)),))],
-            grid=(count,),
-            cost=2 * rows * width * width * count,
-            aliases={2: 0, 3: 1} if earlier else None,
+    split_up = steps // 2
+    wide_hbm = pltpu.HBM((rows, ff), BF16)
+    active, slope, whole_up = call(
+        functools.partial(up_kernel, group_b, len(group_b.arrays), chips),
+        tab,
+        [(normed_second, None)],
+        group_b.arrays,
+        [(wide_hbm, chunk), (wide_hbm, chunk), (pltpu.HBM((width, ff), BF16), anywhere)],
+        [vmem((width, ff), BF16), dma((group_b.copies(("up",)),)), dma((1,))],
+        grid=(split_up,),
+        cost=2 * rows * width * width * split_up,
+    )
+    if fast:
+        active, slope, normed_second, arrays_c, arrays_s, cot_away = together(
+            active, slope, normed_second, arrays_of(near_c), arrays_of(straight_c), cot_away
         )
-
-    active, slope = up_part_of(0, steps // 2, normed_second, [])
-    if fast:
-        active, slope, normed_second, arrays_c, cot_away = together(active, slope, normed_second, arrays_of(near_c), cot_away)
-        near_c = with_arrays(near_c, arrays_c)
+        near_c, straight_c = with_arrays(near_c, arrays_c), with_arrays(straight_c, arrays_s)
         far_c = exchange(grid, near_c, "y")
         cot_got = lax.ppermute(cot_away, "seq", swap_x)
-    active, slope = up_part_of(steps // 2, steps - steps // 2, normed_second, [active, slope])
+    rest = pl.BlockSpec((rows, width), lambda j, t: (0, split_up + j))
+    active, slope = call(
+        up_rest_kernel,
+        tab,
+        [
+            (normed_second, None), (whole_up, pl.BlockSpec((width, width), lambda j, t: (0, split_up + j))),
+            (active, anywhere), (slope, anywhere),
+        ],
+        [],
+        [(wide_hbm, rest), (wide_hbm, rest)],
+        [],
+        grid=(steps - split_up,),
+        cost=2 * rows * width * width * (steps - split_up),
+        aliases={3: 0, 4: 1},
+    )
     if fast:
         all_c = z_c + near_c + straight_c + far_c
         active, slope, arrays_c, cot_got = together(active, slope, arrays_of(all_c), cot_got)
-        group_c = finish(with_arrays(all_c, arrays_c), fields_c)
-    (outputs,) = call(
-        functools.partial(output_kernel, group_c, len(group_c.arrays), chips),
-        tab,
-        [(active, tile(ff)), (hidden, tile(width))],
-        group_c.arrays,
-        [(low(rows, width), tile(width))],
-        [vmem((ff, width), BF16), dma((group_c.copies(("down",)),))],
-        grid=(tiles,),
-        cost=2 * rows * width * ff,
-    )
-    outputs, active = together(outputs, active)
-    out_back = lax.ppermute(outputs[half:], "seq", swap_x)
+        all_c = with_arrays(all_c, arrays_c)
+        theirs_c = swapped(all_c)
     down_out = low(chips, rows_c, width // 2)
     down_mine, down_other = call(
         functools.partial(down_grad_kernel, chips, rows_c),
@@ -779,8 +863,9 @@
 
         def plain():
             whole_sum = jnp.concatenate([mine[0], other[0]], axis=1)
-            for _ in range(4):
-                yield []
+            back = yield []
+            for _ in range(3):
+                back = yield back
             yield lax.psum_scatter(whole_sum, AXES, scatter_dimension=0, tiled=True).astype(F32)
 
         return plain()
@@ -794,8 +879,23 @@
         got = swap_core(away.astype(BF16)).astype(F32)
         return jnp.where(core == 0, keep, got), jnp.where(core == 0, got, keep)
 
-    down_sum = steps_of(down_mine, down_other, 3)
+    if fast:
+        down_mine, down_other, active, arrays_c = together(down_mine, down_other, active, arrays_of(theirs_c))
+        group_c = pieces_from(all_c, with_arrays(theirs_c, arrays_c), fields_c)
+    outputs, whole_down = call(
+        functools.partial(output_kernel, group_c, len(group_c.arrays), chips),
+        tab,
+        [(active, tile(ff)), (hidden, tile(width))],
+        group_c.arrays,
+        [(low(rows, width), tile(width)), (pltpu.HBM((ff, width), BF16), anywhere)],
+        [vmem((ff, width), BF16), dma((group_c.copies(("down",)),)), dma((1,))],
+        grid=(tiles,),
+        cost=2 * rows * width * ff,
+    )
+    down_sum = steps_of(down_mine, down_other, 2)
     arrived = next(down_sum)
+    outputs, arrived, slope = together(outputs, arrived, slope)
+    arrived = down_sum.send(arrived)
     def joined(own, back):
         first = mx == 0
         return jnp.concatenate([jnp.where(first, own, back), jnp.where(first, back, own)], axis=0)[None]
@@ -804,32 +904,41 @@
     out_part = pl.BlockSpec((chips, rows_a, width // 2), lambda *_: (0, 0, ff // width))
     up_out = low(chips, rows_a, ff // 2 + width // 2)
     grad_up, up_mine, up_other = call(
-        functools.partial(down_back_kernel, group_c, len(group_c.arrays), chips, rows_a),
+        functools.partial(down_back_kernel, chips, rows_a),
         tab,
-        [(cot_own, None), (cot_got, None), (normed_second, None), (slope, chunk)],
-        group_c.arrays,
+        [
+            (cot_own, None), (cot_got, None), (normed_second, None), (slope, chunk),
+            (whole_down, pl.BlockSpec((width, width), lambda j, t: (j, 0))),
+        ],
+        [],
         [(pltpu.HBM((rows, ff), BF16), chunk), (up_out, up_part), (up_out, up_part)],
-        [vmem((ff, width), BF16), dma((group_c.copies(("down",)),))],
+        [],
         grid=(steps,),
         cost=4 * rows * width * ff,
     )
-    grad_up, up_mine, up_other, out_back, arrived = together(grad_up, up_mine, up_other, out_back, arrived)
+    grad_up, up_mine, up_other, arrived = together(grad_up, up_mine, up_other, arrived)
     arrived = down_sum.send(arrived)
+    quarter = half // 2
+    out_first = lax.ppermute(outputs[half : half + quarter], "seq", swap_x)
     grad_hidden, grad_att, up_mine, up_other = call(
-        functools.partial(up_back_kernel, group_b, len(group_b.arrays), chips, rows_a),
+        functools.partial(up_back_kernel, chips, rows_a),
         tab,
         [
             (grad_up, tile(ff)), (attended, tile(width)), (gains, None), (cot_own, own_tile), (cot_got, got_tile),
             (hidden, tile(width)), (up_mine, anywhere), (up_other, anywhere),
+            (whole_up, None), (whole_out, None),
         ],
-        group_b.arrays,
+        [],
         [(sds((rows, width), F32), tile(width)), (low(rows, width), tile(width)), (up_out, out_part), (up_out, out_part)],
-        [vmem((width, ff), BF16), vmem((width, width), BF16), vmem((width, width), F32), dma((group_b.copies(("up", "out")),))],
+        [vmem((width, width), F32)],
         grid=(tiles,),
         cost=2 * rows * width * ff + 4 * rows * width * width,
         aliases={7: 2, 8: 3},
     )
-    grad_att, grad_hidden, up_mine, up_other, arrived = together(grad_att, grad_hidden, up_mine, up_other, arrived)
+    grad_att, grad_hidden, up_mine, up_other, arrived, out_first, out_next = together(
+        grad_att, grad_hidden, up_mine, up_other, arrived, out_first, outputs[half + quarter :]
+    )
+    out_second = lax.ppermute(out_next, "seq", swap_x)
     arrived = down_sum.send(arrived)
     up_sum = steps_of(up_mine, up_other, 2)
     arrived_up = next(up_sum)
@@ -859,15 +968,13 @@
         return [g.reshape(rows, 256 * (last - first)) for g in grads]
 
     grads_a = attend_back(0, group_cut, grad_att)
-    grads_a, grad_att, arrived, arrived_up = together(grads_a, grad_att, arrived, arrived_up)
-    arrived = down_sum.send(arrived)
+    grads_a, grad_att, arrived_up, out_second = together(grads_a, grad_att, arrived_up, out_second)
     arrived_up = up_sum.send(arrived_up)
     grads_b = attend_back(group_cut, groups, grad_att)
-    grads_b, arrived, arrived_up = together(grads_b, arrived, arrived_up)
-    output_tokens = joined(outputs[:half], out_back)
+    grads_b, arrived_up, arrived = together(grads_b, arrived_up, arrived)
     left, right = owned(down_sum.send(arrived))
     owned_down = jnp.concatenate([left, right], axis=1)
-    arrived_up = up_sum.send(arrived_up)
+    arrived_up, grads_b, normed_first = up_sum.send((arrived_up, grads_b, normed_first))
     qkv_out = low(chips, rows_a, 3 * width // 2)
     qkv_mine, qkv_other = call(
         functools.partial(qkv_grad_kernel, chips, rows_a, cuts),
@@ -882,34 +989,31 @@
     qkv_sum = steps_of(qkv_mine, qkv_other, 2)
     arrived = next(qkv_sum)
 
-    def first_back(part, source, grad_hidden):
-        here_tile = lambda columns: pl.BlockSpec((256, columns), lambda i, t: (part * (tiles // 2) + i, 0))
-        return call(
-            functools.partial(first_kernel, group_a, len(group_a.arrays), chips, cuts),
-            tab,
-            [(source, tile(width)), (gains, None), (grad_hidden, here_tile(width))]
-            + [(g, here_tile(g.shape[1])) for g in grads_a + grads_b],
-            group_a.arrays,
-            [(low(half, width), tile(width))],
-            [vmem((width, 3 * width), BF16), dma((group_a.copies(("qkv",)),))],
-            grid=(tiles // 2,),
-            cost=2 * half * width * 3 * width,
-        )[0]
-
-    grad_got = first_back(1, tok_got, grad_hidden)
+    tok_own, arrived, arrived_up = together(tok_own, arrived, arrived_up)
+    arrived_up = up_sum.send(arrived_up)
+    arrived = qkv_sum.send(arrived)
+    grad_own, grad_got = call(
+        functools.partial(first_kernel, cuts),
+        tab,
+        [
+            (tok_own, own_tile), (tok_got, got_tile), (gains, None), (grad_hidden, tile(width)), (whole_qkv, None),
+        ]
+        + [(g, tile(g.shape[1])) for g in grads_a + grads_b],
+        [],
+        [(low(half, width), own_tile), (low(half, width), got_tile)],
+        [],
+        grid=(tiles,),
+        cost=2 * rows * width * 3 * width,
+    )
+    grad_got, grad_own, arrived = together(grad_got, grad_own, arrived)
+    arrived = qkv_sum.send(arrived)
     grad_back = lax.ppermute(grad_got, "seq", swap_x)
-    grad_got, arrived, tok_own = together(grad_got, arrived, tok_own)
-    arrived = qkv_sum.send(arrived)
-    grad_own = first_back(0, tok_own, grad_hidden)
-    grad_own, arrived_up = together(grad_own, arrived_up)
-    arrived_up = up_sum.send(arrived_up)
-    grad_own, arrived = together(grad_own, arrived)
-    arrived = qkv_sum.send(arrived)
-    arrived_up, arrived = together(arrived_up, arrived)
+    arrived_up, arrived, out_first, out_second = together(arrived_up, arrived, out_first, out_second)
     arrived = qkv_sum.send(arrived)
     left, right = owned(up_sum.send(arrived_up))
     owned_up = jnp.concatenate([left[:, : ff // 2], right[:, : ff // 2]], axis=1)
     owned_out = jnp.concatenate([left[:, ff // 2 :], right[:, ff // 2 :]], axis=1)
+    output_tokens = joined(outputs[:half], jnp.concatenate([out_first, out_second], axis=0))
     left, right = owned(qkv_sum.send(arrived))
     owned_qkv = jnp.concatenate([left, right], axis=1)
     grad_tokens = joined(grad_own, grad_back)

time: 333 us -> 291 us (0.87)
  Pallas kernels: 150 us -> 126 us
  waiting for transfers between devices: 78.3 us -> 58.1 us
    pallas_call x14 -> x13, Pallas kernels: 150 us -> 126 us  [call(): pl.pallas_call(kernel, out_shape=[o for o, _ in outs], input_output_alias...]
    ppermute x15 -> x23, waiting for transfers between devices: 28.2 us -> 19.4 us  [the longest x12 13 us: scatter_steps(): lax.ppermute(total, AXES, grid.shift(axes[step], k + 1))]
    ppermute x9, waiting for transfers between devices: 8.16 us -> 0.85 us  [scatter_steps(): lax.ppermute(total.astype(BF16), AXES, grid.shift('z', k))]
    ppermute x12 -> x4, waiting for transfers between devices: 6.13 us -> 0.01 us  [finish(): theirs = [(swap_core(a), s) for a, s in mine]]
    ppermute x15 -> x23, starting transfers between devices: 16.6 us -> 19.7 us  [the longest x12 13.8 us: scatter_steps(): lax.ppermute(total, AXES, grid.shift(axes[step], k + 1))]
    unnamed x107 -> x99, local copies, waits for them, and re-layouts: 9.84 us -> 7.96 us
    convert_element_type x10 -> x9, other arithmetic: 7.68 us -> 6.26 us  [scatter_steps(): add_all(pieces[k]).astype(BF16)]
  transfers between devices with their start and end apart: 67 -> 67, of which waited for: 27 -> 22; matrix products, arithmetic and copies ran while one was open for 4% -> 7% of each run, Pallas kernels for 37% -> 42%
where the time goes in v3:
time: 291 us; the launch traced here: 287 us
  Pallas kernels  126 us (43%)
  starting transfers between devices  67.8 us (23%)
  waiting for transfers between devices  58.1 us (20%)
  other arithmetic  22.4 us (8%)
  local copies, waits for them, and re-layouts  10 us (3%)
  between operations  3.05 us (1%)
    pallas_call x13, Pallas kernels, call(): pl.pallas_call(kernel, out_shape=[o for o, _ in outs], input_output_alias...  126 us
    ppermute x20, waiting for transfers between devices, exchange(): lax.ppermute(array, AXES, grid.shift(axis, k))  33.9 us
    ppermute x20, starting transfers between devices, exchange(): lax.ppermute(array, AXES, grid.shift(axis, k))  29.8 us
    ppermute x9, starting transfers between devices, scatter_steps(): lax.ppermute(total.astype(BF16), AXES, grid.shift('z', k))  14.2 us
    ppermute x12, starting transfers between devices, scatter_steps(): lax.ppermute(total, AXES, grid.shift(axes[step], k + 1))  13.8 us
    ppermute x12, waiting for transfers between devices, scatter_steps(): lax.ppermute(total, AXES, grid.shift(axes[step], k + 1))  13 us
    unnamed x99, local copies, waits for them, and re-layouts  7.96 us
    convert_element_type x9, other arithmetic, scatter_steps(): add_all(pieces[k]).astype(BF16)  6.26 us
  transfers between devices with their start and end apart: 67, of which 22 were waited for; matrix products, arithmetic and copies ran while one was open for 7% of the time, Pallas kernels for 42%

profile of v3, /device:TPU:0, one launch (start us, length us, event | category | flops | bytes accessed | tf_op | source)
XLA Modules:
  0.0 287.4 jit_solution(16792002560515438280)
XLA Ops:
  1.5 1.5 dynamic-slice_bitcast_fusion.2
  3.6 2.6 collective-permute-start.4
  6.5 1.6 collective-permute-start.1
  8.1 2.6 collective-permute-start.2
  10.7 1.3 collective-permute-start.3
  12.1 2.4 collective-permute-done.1
  14.5 4.8 %collective-permute-done.2 = bf16[1,48,1280]{2,1,0:T(8,128)(2,1)S(1)} collective-permute-done((bf16[1,48,1280]{2,1,0:T(8,128)(2,1)S(1)}, bf16[1,48,1280]{2,1,0:T(8,128)(2,1)S(1)}, u32[]{:S(2)}, u32[]{:S(2)}) %collective-permute-start.2) | collective-permute-done | bytes 122912 | tf_op jit(solution)/shard_map/ppermute | solution.py:69
  19.3 5.0 %collective-permute-done.4.got = bf16[512,768]{1,0:T(8,128)(2,1)S(1)} collective-permute-done((bf16[512,768]{1,0:T(8,128)(2,1)S(1)}, bf16[512,768]{1,0:T(8,128)(2,1)S(1)}, u32[]{:S(2)}, u32[]{:S(2)}) %collective-permute-start.4) | collective-permute-done | bytes 786464 | tf_op jit(solution)/shard_map/ppermute | solution.py:664
  24.3 1.8 collective-permute-start.6
  26.2 1.6 collective-permute-start.7
  27.8 4.3 %collective-permute-done.6 = bf16[2,48,1280]{2,1,0:T(8,128)(2,1)S(1)} collective-permute-done((bf16[2,48,1280]{2,1,0:T(8,128)(2,1)S(1)}, bf16[2,48,1280]{2,1,0:T(8,128)(2,1)S(1)}, u32[]{:S(2)}, u32[]{:S(2)}) %collective-permute-start.6) | collective-permute-done | bytes 245792 | tf_op jit(solution)/shard_map/ppermute | solution.py:69
  32.1 1.4 collective-permute-done.7
  33.5 1.6 collective-permute-start.8
  36.9 1.6 collective-permute-start.15
  38.5 2.6 collective-permute-start.16
  41.1 1.3 collective-permute-start.17
  43.4 1.8 collective-permute-done.8.refs_2_
  45.2 1.4 collective-permute-done.9.refs_3_
  47.1 6.4 %collective-permute-done.16 = bf16[1,48,1920]{2,1,0:T(8,128)(2,1)S(1)} collective-permute-done((bf16[1,48,1920]{2,1,0:T(8,128)(2,1)S(1)}, bf16[1,48,1920]{2,1,0:T(8,128)(2,1)S(1)}, u32[]{:S(2)}, u32[]{:S(2)}) %collective-permute-start.16) | collective-permute-done | bytes 184352 | tf_op jit(solution)/shard_map/ppermute | solution.py:69
  53.6 1.6 collective-permute-start.18
  55.9 4.5 %collective-permute-start.20 = (bf16[1,192,384]{2,1,0:T(8,128)(2,1)S(1)}, bf16[1,192,384]{2,1,0:T(8,128)(2,1)S(1)}, u32[]{:S(2)}, u32[]{:S(2)}) collective-permute-start(bf16[1,192,384]{2,1,0:T(8,128)(2,1)S(1)} %bitcast.283), channel_id=1, source_target_pairs={{0,4},{1,5},{2,6},{3,7},{4,8},{5,9},{6,10},{7,11},{8,12},{9,13},{1... | collective-permute-start | bytes 442376 | tf_op jit(solution)/shard_map/ppermute | solution.py:69
  60.4 1.6 collective-permute-start.21
  63.1 9.0 %shard_map.135 = (bf16[1024,2304]{1,0:T(8,128)(2,1)}, bf16[1024,768]{1,0:T(8,128)(2,1)S(1)}, f32[8,768]{1,0:T(8,128)S(1)}, bf16[768,2304]{1,0:T(8,128)(2,1)}) custom-call(s32[34]{0:T(128)S(1)} %stack.140.tab, bf16[512,768]{1,0:T(8,128)(2,1)S(1)} %get-tuple-element.288.own, bf16[512,768]{1,0:T(8,128)(2,1)S(1)} %collective-permute-done.4.got, ...), custom_call_target="tpu_custom_call" | custom-call | flops 3623878656 | bytes 15360000 | tf_op jit(solution)/shard_map/pallas_call | solution.py:588
  72.2 1.6 collective-permute-start.23
  74.9 13.1 %shard_map.136 = (bf16[2,2,256,768]{3,2,1,0:T(8,128)(2,1)S(1)}, f32[24,1,512]{2,1,0:T(1,128)S(1)}) custom-call(s32[34]{0:T(128)S(1)} %stack.140.tab, bf16[2,2,256,2304]{3,2,1,0:T(8,128)(2,1)} %bitcast.254, bf16[2,2,256,2304]{3,2,1,0:T(8,128)(2,1)} %bitcast.255, bf16[2,2,256,2304]{3,2,1,0:T(8,128)(2,1)} %bitcast.256), custom_call_target="tpu_custom_call" | custom-call | flops 3221225472 | bytes 15777792 | tf_op jit(solution)/shard_map/pallas_call | solution.py:588
  88.1 2.2 collective-permute-done.23.refs_2_
  90.2 1.3 collective-permute-done.24.refs_3_
  94.8 4.2 %shard_map.137 = (f32[1024,768]{1,0:T(8,128)S(1)}, bf16[1024,768]{1,0:T(8,128)(2,1)S(1)}, bf16[768,768]{1,0:T(8,128)(2,1)}) custom-call(s32[34]{0:T(128)S(1)} %stack.140.tab, bf16[1024,768]{1,0:T(8,128)(2,1)S(1)} %bitcast.223, bf16[512,768]{1,0:T(8,128)(2,1)S(1)} %get-tuple-element.288.own, bf16[512,768]{1,0:T(8,128)(2,1)S(1)} %collective-permute-done.4.got, ...), custom_call_target="tpu_custom_call" | custom-call | flops 1207959552 | bytes 14966784 | tf_op jit(solution)/shard_map/pallas_call | solution.py:588
  99.0 7.3 %shard_map.138 = (bf16[1024,3072]{1,0:T(8,128)(2,1)}, bf16[1024,3072]{1,0:T(8,128)(2,1)}, bf16[768,3072]{1,0:T(8,128)(2,1)}) custom-call(s32[34]{0:T(128)S(1)} %stack.140.tab, bf16[1024,768]{1,0:T(8,128)(2,1)S(1)} %get-tuple-element.207.normed, bf16[4,48,1920]{2,1,0:T(8,128)(2,1)S(1)} %constant_dynamic-update-slice_fusion.6.refs_0_, ...), custom_call_target="tpu_custom_call" | custom-call | flops 2415919104 | bytes 24772608 | tf_op jit(solution)/shard_map/pallas_call | solution.py:588
  107.8 1.5 collective-permute-start.32
  109.8 7.0 %shard_map.139 = (bf16[1024,3072]{1,0:T(8,128)(2,1)}, bf16[1024,3072]{1,0:T(8,128)(2,1)}) custom-call(s32[34]{0:T(128)S(1)} %stack.140.tab, bf16[1024,768]{1,0:T(8,128)(2,1)S(1)} %get-tuple-element.207.normed, bf16[768,3072]{1,0:T(8,128)(2,1)} %get-tuple-element.208.w_up, ...), custom_call_target="tpu_custom_call", output_to_operand_aliasing={{0}: (3, {}), {1}: (4, {})} | custom-call | flops 2415919104 | bytes 31457280 | tf_op jit(solution)/shard_map/pallas_call | solution.py:588
  116.8 6.4 %collective-permute-done.31.refs_3_ = bf16[4,192,384]{2,1,0:T(8,128)(2,1)S(1)} collective-permute-done((bf16[4,192,384]{2,1,0:T(8,128)(2,1)S(1)}, bf16[4,192,384]{2,1,0:T(8,128)(2,1)S(1)}, u32[]{:S(2)}, u32[]{:S(2)}) %collective-permute-start.31) | collective-permute-done | bytes 589856 | tf_op jit(solution)/shard_map/ppermute | solution.py:69
  123.2 3.1 %collective-permute-done.32.cot_got = bf16[512,768]{1,0:T(8,128)(2,1)S(1)} collective-permute-done((bf16[512,768]{1,0:T(8,128)(2,1)S(1)}, bf16[512,768]{1,0:T(8,128)(2,1)S(1)}, u32[]{:S(2)}, u32[]{:S(2)}) %collective-permute-start.32) | collective-permute-done | bytes 786464 | tf_op jit(solution)/shard_map/ppermute | solution.py:827
  127.3 8.3 %shard_map.140 = (bf16[16,192,384]{2,1,0:T(8,128)(2,1)S(1)}, bf16[16,192,384]{2,1,0:T(8,128)(2,1)S(1)}) custom-call(s32[34]{0:T(128)S(1)} %stack.140.tab, bf16[1024,3072]{1,0:T(8,128)(2,1)} %get-tuple-element.224.active, bf16[512,768]{1,0:T(8,128)(2,1)S(1)} %get-tuple-element.341.cot_own, bf16[512,768]{1,0:T(8,128)(2,1)S(1)} %collective-permute-done.32.cot_got), custom_call_target="tpu_custom_call" | custom-call | flops 4831838208 | bytes 12582912 | tf_op jit(solution)/shard_map/pallas_call | solution.py:588
  135.7 9.4 %shard_map.141 = (bf16[1024,768]{1,0:T(8,128)(2,1)S(1)}, bf16[3072,768]{1,0:T(8,128)(2,1)}) custom-call(s32[34]{0:T(128)S(1)} %stack.140.tab, bf16[1024,3072]{1,0:T(8,128)(2,1)} %get-tuple-element.224.active, f32[1024,768]{1,0:T(8,128)S(1)} %get-tuple-element.225.hidden, bf16[4,192,384]{2,1,0:T(8,128)(2,1)S(1)} %constant_dynamic-update-slice_fusion.12.refs_0_, ...), custom_call_target="tpu_custom_call" | custom-call | flops 4831838208 | bytes 20447232 | tf_op jit(solution)/shard_map/pallas_call | solution.py:588
  146.0 1.4 collective-permute-start.39
  148.1 14.3 %shard_map.142 = (bf16[1024,3072]{1,0:T(8,128)(2,1)}, bf16[16,48,1920]{2,1,0:T(8,128)(2,1)S(1)}, bf16[16,48,1920]{2,1,0:T(8,128)(2,1)S(1)}) custom-call(s32[34]{0:T(128)S(1)} %stack.140.tab, bf16[512,768]{1,0:T(8,128)(2,1)S(1)} %get-tuple-element.341.cot_own, bf16[512,768]{1,0:T(8,128)(2,1)S(1)} %collective-permute-done.32.cot_got, ...), custom_call_target="tpu_custom_call" | custom-call | flops 9663676416 | bytes 26345472 | tf_op jit(solution)/shard_map/pallas_call | solution.py:588
  162.7 1.5 collective-permute-start.40
  164.2 1.5 collective-permute-start.41
  165.7 16.7 %shard_map.143 = (f32[1024,768]{1,0:T(8,128)S(1)}, bf16[1024,768]{1,0:T(8,128)(2,1)S(1)}, bf16[16,48,1920]{2,1,0:T(8,128)(2,1)S(1)}, bf16[16,48,1920]{2,1,0:T(8,128)(2,1)S(1)}) custom-call(s32[34]{0:T(128)S(1)} %stack.140.tab, bf16[1024,3072]{1,0:T(8,128)(2,1)} %get-tuple-element.241.grad_up, ...), custom_call_target="tpu_custom_call", output_to_operand_aliasing={{2}: (7, {}), {3}: (8, {})} | custom-call | flops 7247757312 | bytes 35020800 | tf_op jit(solution)/shard_map/pallas_call | solution.py:588
  183.2 1.8 fusion.21
  185.0 3.8 %collective-permute-start.47 = (bf16[192,384]{1,0:T(8,128)(2,1)S(1)}, bf16[192,384]{1,0:T(8,128)(2,1)S(1)}, u32[]{:S(2)}, u32[]{:S(2)}) collective-permute-start(bf16[192,384]{1,0:T(8,128)(2,1)S(1)} %get-tuple-element.326), channel_id=1, source_target_pairs={{0,4},{1,5},{2,6},{3,7},{4,8},{5,9},{6,10},{7,11},{8,12},{9,13},{1... | collective-permute-start | bytes 442376 | tf_op jit(solution)/shard_map/ppermute | solution.py:132
  188.8 2.4 collective-permute-start.49
  191.2 8.7 %shard_map.144 = (bf16[2,2,256,256]{3,2,1,0:T(8,128)(2,1)S(1)}, bf16[2,2,256,256]{3,2,1,0:T(8,128)(2,1)S(1)}, bf16[2,2,256,256]{3,2,1,0:T(8,128)(2,1)S(1)}) custom-call(s32[34]{0:T(128)S(1)} %stack.140.tab, bf16[2,2,256,2304]{3,2,1,0:T(8,128)(2,1)} %bitcast.257, bf16[2,2,256,2304]{3,2,1,0:T(8,128)(2,1)} %bitcast.258, bf16[2,2,256,2304]{3,2,1,0:T(8,128)(2,1)} %bitcast.259, ...), custom_call_target="tpu_custom_call" | custom-call | flops 4026531840 | bytes 18923520 | tf_op jit(solution)/shard_map/pallas_call | solution.py:588
  201.3 1.4 collective-permute-start.46
  202.7 16.0 %shard_map.145 = (bf16[2,2,256,512]{3,2,1,0:T(8,128)(2,1)S(1)}, bf16[2,2,256,512]{3,2,1,0:T(8,128)(2,1)S(1)}, bf16[2,2,256,512]{3,2,1,0:T(8,128)(2,1)S(1)}) custom-call(s32[34]{0:T(128)S(1)} %stack.140.tab, bf16[2,2,256,2304]{3,2,1,0:T(8,128)(2,1)} %bitcast.260, bf16[2,2,256,2304]{3,2,1,0:T(8,128)(2,1)} %bitcast.261, bf16[2,2,256,2304]{3,2,1,0:T(8,128)(2,1)} %bitcast.262, ...), custom_call_target="tpu_custom_call" | custom-call | flops 8053063680 | bytes 20496384 | tf_op jit(solution)/shard_map/pallas_call | solution.py:588
  218.9 1.5 fusion.2
  220.4 6.0 %shard_map.146 = (bf16[16,48,1152]{2,1,0:T(8,128)(2,1)S(1)}, bf16[16,48,1152]{2,1,0:T(8,128)(2,1)}) custom-call(s32[34]{0:T(128)S(1)} %stack.140.tab, bf16[1024,768]{1,0:T(8,128)(2,1)S(1)} %get-tuple-element.272.normed, bf16[1024,256]{1,0:T(8,128)(2,1)S(1)} %bitcast.242, bf16[1024,256]{1,0:T(8,128)(2,1)S(1)} %bitcast.244, bf16[1024,256]{1,0:T(8,128)(2,1)S(1)} %bitcast.246, ...), custom_call_target="tpu_custom_call" | custom-call | flops 3623878656 | bytes 9830400 | tf_op jit(solution)/shard_map/pallas_call | solution.py:588
  227.7 1.3 collective-permute-start.51
  229.0 1.4 collective-permute-start.52
  230.4 1.4 fusion.20
  231.9 7.0 %collective-permute-done.51 = bf16[2,48,1920]{2,1,0:T(8,128)(2,1)S(1)} collective-permute-done((bf16[2,48,1920]{2,1,0:T(8,128)(2,1)}, bf16[2,48,1920]{2,1,0:T(8,128)(2,1)S(1)}, u32[]{:S(2)}, u32[]{:S(2)}) %collective-permute-start.51) | collective-permute-done | bytes 368672 | tf_op jit(solution)/shard_map/ppermute | solution.py:120
  239.9 1.3 fusion.8
  241.3 1.3 fusion.9
  242.6 1.5 collective-permute-start.56
  245.0 1.8 fusion.15
  246.8 2.5 collective-permute-start.54
  250.6 2.0 copy-done.20
  252.6 1.9 copy-done.22
  254.4 6.2 %shard_map.147 = (bf16[512,768]{1,0:T(8,128)(2,1)S(1)}, bf16[512,768]{1,0:T(8,128)(2,1)S(1)}) custom-call(s32[34]{0:T(128)S(1)} %stack.140.tab, bf16[512,768]{1,0:T(8,128)(2,1)S(1)} %get-tuple-element.288.own, bf16[512,768]{1,0:T(8,128)(2,1)S(1)} %copy-done.6, f32[8,768]{1,0:T(8,128)S(1)} %get-tuple-element.195.gains, f32[1024,768]{1,0:T(8,128)S(1)} %copy-done.22, ...), custom_call_target="tpu_custom_call" | custom-call | flops 3623878656 | bytes 14573568 | tf_op jit(solution)/shard_map/pallas_call | solution.py:588
  260.7 1.4 collective-permute-start.55
  266.7 5.0 %collective-permute-done.58 = bf16[2,48,1152]{2,1,0:T(8,128)(2,1)S(1)} collective-permute-done((bf16[2,48,1152]{2,1,0:T(8,128)(2,1)S(1)}, bf16[2,48,1152]{2,1,0:T(8,128)(2,1)S(1)}, u32[]{:S(2)}, u32[]{:S(2)}) %collective-permute-start.58) | collective-permute-done | bytes 221216 | tf_op jit(solution)/shard_map/ppermute | solution.py:120
  273.6 1.5 collective-permute-start.62
  275.2 1.9 collective-permute-start.61
  (244 shorter events, 38.4 us)
Async XLA Ops:
  3.1 3.1 %collective-permute-start = (bf16[24,1280]{1,0:T(8,128)(2,1)S(1)}, bf16[24,1280]{1,0:T(8,128)(2,1)S(1)}, u32[]{:S(2)}, u32[]{:S(2)}) collective-permute-start(bf16[24,1280]{1,0:T(8,128)(2,1)S(1)} %fusion.32), channel_id=1, source_target_pairs={{0,1},{1,0},{2,3},{3,2},{4,5},{5,4},{6,7},{7,6},{8,9},{9,8},{10,11... | collective-permute-start | bytes 184328 | tf_op jit(solution)/shard_map/ppermute | solution.py:658
  3.6 20.7 %collective-permute-start.4 = (bf16[512,768]{1,0:T(8,128)(2,1)S(1)}, bf16[512,768]{1,0:T(8,128)(2,1)S(1)}, u32[]{:S(2)}, u32[]{:S(2)}) collective-permute-start(bf16[512,768]{1,0:T(8,128)(2,1)S(1)} %get-tuple-element.163), channel_id=1, source_target_pairs={{0,16},{16,0},{1,17},{17,1},{2,18},{18,2},{3,19},{19,3},{4,20},{20... | collective-permute-start | bytes 2359304 | tf_op jit(solution)/shard_map/ppermute | solution.py:664
  6.3 5.7 %collective-permute-start.5 = (bf16[24,1920]{1,0:T(8,128)(2,1)S(1)}, bf16[24,1920]{1,0:T(8,128)(2,1)S(1)}, u32[]{:S(2)}, u32[]{:S(2)}) collective-permute-start(bf16[24,1920]{1,0:T(8,128)(2,1)S(1)} %pad_maximum_fusion.11), channel_id=1, source_target_pairs={{0,1},{1,0},{2,3},{3,2},{4,5},{5,4},{6,7},{7,6},{8,9},{9,8},{10,11... | collective-permute-start | bytes 276488 | tf_op jit(solution)/shard_map/ppermute | solution.py:658
  6.5 8.0 %collective-permute-start.1 = (bf16[1,48,1280]{2,1,0:T(8,128)(2,1)S(1)}, bf16[1,48,1280]{2,1,0:T(8,128)(2,1)S(1)}, u32[]{:S(2)}, u32[]{:S(2)}) collective-permute-start(bf16[1,48,1280]{2,1,0:T(8,128)(2,1)S(1)} %bitcast.278), channel_id=1, source_target_pairs={{0,4},{1,5},{2,6},{3,7},{4,8},{5,9},{6,10},{7,11},{8,12},{9,13},{1... | collective-permute-start | bytes 368648 | tf_op jit(solution)/shard_map/ppermute | solution.py:69
  8.1 11.2 %collective-permute-start.2 = (bf16[1,48,1280]{2,1,0:T(8,128)(2,1)S(1)}, bf16[1,48,1280]{2,1,0:T(8,128)(2,1)S(1)}, u32[]{:S(2)}, u32[]{:S(2)}) collective-permute-start(bf16[1,48,1280]{2,1,0:T(8,128)(2,1)S(1)} %bitcast.279), channel_id=1, source_target_pairs={{0,8},{1,9},{2,10},{3,11},{4,12},{5,13},{6,14},{7,15},{8,0},{9,1},... | collective-permute-start | bytes 368648 | tf_op jit(solution)/shard_map/ppermute | solution.py:69
  10.7 8.6 %collective-permute-start.3 = (bf16[1,48,1280]{2,1,0:T(8,128)(2,1)S(1)}, bf16[1,48,1280]{2,1,0:T(8,128)(2,1)S(1)}, u32[]{:S(2)}, u32[]{:S(2)}) collective-permute-start(bf16[1,48,1280]{2,1,0:T(8,128)(2,1)S(1)} %bitcast.280), channel_id=1, source_target_pairs={{0,12},{1,13},{2,14},{3,15},{4,0},{5,1},{6,2},{7,3},{8,4},{9,5},{1... | collective-permute-start | bytes 368648 | tf_op jit(solution)/shard_map/ppermute | solution.py:69
  24.3 7.8 %collective-permute-start.6 = (bf16[2,48,1280]{2,1,0:T(8,128)(2,1)S(1)}, bf16[2,48,1280]{2,1,0:T(8,128)(2,1)S(1)}, u32[]{:S(2)}, u32[]{:S(2)}) collective-permute-start(bf16[2,48,1280]{2,1,0:T(8,128)(2,1)S(1)} %pad_maximum_fusion.4), channel_id=1, source_target_pairs={{0,16},{1,17},{2,18},{3,19},{4,20},{5,21},{6,22},{7,23},{8,24},{9,... | collective-permute-start | bytes 737288 | tf_op jit(solution)/shard_map/ppermute | solution.py:69
  26.2 7.3 %collective-permute-start.7 = (bf16[2,48,1280]{2,1,0:T(8,128)(2,1)S(1)}, bf16[2,48,1280]{2,1,0:T(8,128)(2,1)S(1)}, u32[]{:S(2)}, u32[]{:S(2)}) collective-permute-start(bf16[2,48,1280]{2,1,0:T(8,128)(2,1)S(1)} %pad_maximum_fusion.5), channel_id=1, source_target_pairs={{0,2},{1,3},{2,0},{3,1},{4,6},{5,7},{6,4},{7,5},{8,10},{9,11},{10,... | collective-permute-start | bytes 737288 | tf_op jit(solution)/shard_map/ppermute | solution.py:69
  33.5 11.7 %collective-permute-start.8 = (bf16[4,48,1280]{2,1,0:T(8,128)(2,1)S(1)}, bf16[4,48,1280]{2,1,0:T(8,128)(2,1)S(1)}, u32[]{:S(2)}, u32[]{:S(2)}) collective-permute-start(bf16[4,48,1280]{2,1,0:T(8,128)(2,1)S(1)} %constant_dynamic-update-slice_fusion.refs_0_), channel_id=1, source_target_pairs={{0,2},{1,3},{2,0},{3,1},{4,6},{5,7},{6,4},{7,5},{8,10},{9,11},{10,... | collective-permute-start | bytes 1474568 | tf_op jit(solution)/shard_map/ppermute | solution.py:69
  35.1 11.5 %collective-permute-start.9 = (bf16[4,48,1280]{2,1,0:T(8,128)(2,1)S(1)}, bf16[4,48,1280]{2,1,0:T(8,128)(2,1)}, u32[]{:S(2)}, u32[]{:S(2)}) collective-permute-start(bf16[4,48,1280]{2,1,0:T(8,128)(2,1)S(1)} %constant_dynamic-update-slice_fusion.3.refs_1_), channel_id=1, source_target_pairs={{0,16},{1,17},{2,18},{3,19},{4,20},{5,21},{6,22},{7,23},{8,24},{9,... | collective-permute-start | bytes 1474568 | tf_op jit(solution)/shard_map/ppermute | solution.py:69
  35.7 5.3 %collective-permute-start.10 = (bf16[96,384]{1,0:T(8,128)(2,1)S(1)}, bf16[96,384]{1,0:T(8,128)(2,1)}, u32[]{:S(2)}, u32[]{:S(2)}) collective-permute-start(bf16[96,384]{1,0:T(8,128)(2,1)S(1)} %constant_dynamic-slice_fusion), channel_id=1, source_target_pairs={{0,1},{1,0},{2,3},{3,2},{4,5},{5,4},{6,7},{7,6},{8,9},{9,8},{10,11... | collective-permute-start | bytes 221192 | tf_op jit(solution)/shard_map/ppermute | solution.py:658
  36.9 10.3 %collective-permute-start.15 = (bf16[1,48,1920]{2,1,0:T(8,128)(2,1)S(1)}, bf16[1,48,1920]{2,1,0:T(8,128)(2,1)S(1)}, u32[]{:S(2)}, u32[]{:S(2)}) collective-permute-start(bf16[1,48,1920]{2,1,0:T(8,128)(2,1)S(1)} %bitcast.273), channel_id=1, source_target_pairs={{0,4},{1,5},{2,6},{3,7},{4,8},{5,9},{6,10},{7,11},{8,12},{9,13},{1... | collective-permute-start | bytes 552968 | tf_op jit(solution)/shard_map/ppermute | solution.py:69
  38.5 15.1 %collective-permute-start.16 = (bf16[1,48,1920]{2,1,0:T(8,128)(2,1)S(1)}, bf16[1,48,1920]{2,1,0:T(8,128)(2,1)S(1)}, u32[]{:S(2)}, u32[]{:S(2)}) collective-permute-start(bf16[1,48,1920]{2,1,0:T(8,128)(2,1)S(1)} %bitcast.274), channel_id=1, source_target_pairs={{0,8},{1,9},{2,10},{3,11},{4,12},{5,13},{6,14},{7,15},{8,0},{9,1},... | collective-permute-start | bytes 552968 | tf_op jit(solution)/shard_map/ppermute | solution.py:69
  41.1 12.5 %collective-permute-start.17 = (bf16[1,48,1920]{2,1,0:T(8,128)(2,1)S(1)}, bf16[1,48,1920]{2,1,0:T(8,128)(2,1)S(1)}, u32[]{:S(2)}, u32[]{:S(2)}) collective-permute-start(bf16[1,48,1920]{2,1,0:T(8,128)(2,1)S(1)} %bitcast.275), channel_id=1, source_target_pairs={{0,12},{1,13},{2,14},{3,15},{4,0},{5,1},{6,2},{7,3},{8,4},{9,5},{1... | collective-permute-start | bytes 552968 | tf_op jit(solution)/shard_map/ppermute | solution.py:69
  46.6 8.7 %collective-permute-start.11 = (bf16[4,48,1280]{2,1,0:T(8,128)(2,1)S(1)}, bf16[4,48,1280]{2,1,0:T(8,128)(2,1)S(1)}, u32[]{:S(2)}, u32[]{:S(2)}) collective-permute-start(bf16[4,48,1280]{2,1,0:T(8,128)(2,1)S(1)} %constant_dynamic-update-slice_fusion.refs_0_), channel_id=1, source_target_pairs={{0,1},{1,0},{2,3},{3,2},{4,5},{5,4},{6,7},{7,6},{8,9},{9,8},{10,11... | collective-permute-start | bytes 1474568 | tf_op jit(solution)/shard_map/ppermute | solution.py:693
  46.6 9.3 %collective-permute-start.12 = (bf16[4,48,1280]{2,1,0:T(8,128)(2,1)S(1)}, bf16[4,48,1280]{2,1,0:T(8,128)(2,1)S(1)}, u32[]{:S(2)}, u32[]{:S(2)}) collective-permute-start(bf16[4,48,1280]{2,1,0:T(8,128)(2,1)S(1)} %constant_dynamic-update-slice_fusion.3.refs_1_), channel_id=1, source_target_pairs={{0,1},{1,0},{2,3},{3,2},{4,5},{5,4},{6,7},{7,6},{8,9},{9,8},{10,11... | collective-permute-start | bytes 1474568 | tf_op jit(solution)/shard_map/ppermute | solution.py:693
  47.1 13.2 %collective-permute-start.13 = (bf16[4,48,1280]{2,1,0:T(8,128)(2,1)S(1)}, bf16[4,48,1280]{2,1,0:T(8,128)(2,1)S(1)}, u32[]{:S(2)}, u32[]{:S(2)}) collective-permute-start(bf16[4,48,1280]{2,1,0:T(8,128)(2,1)S(1)} %collective-permute-done.8.refs_2_), channel_id=1, source_target_pairs={{0,1},{1,0},{2,3},{3,2},{4,5},{5,4},{6,7},{7,6},{8,9},{9,8},{10,11... | collective-permute-start | bytes 1474568 | tf_op jit(solution)/shard_map/ppermute | solution.py:693
  53.6 8.4 %collective-permute-start.14 = (bf16[4,48,1280]{2,1,0:T(8,128)(2,1)}, bf16[4,48,1280]{2,1,0:T(8,128)(2,1)S(1)}, u32[]{:S(2)}, u32[]{:S(2)}) collective-permute-start(bf16[4,48,1280]{2,1,0:T(8,128)(2,1)} %collective-permute-done.9.refs_3_), channel_id=1, source_target_pairs={{0,1},{1,0},{2,3},{3,2},{4,5},{5,4},{6,7},{7,6},{8,9},{9,8},{10,11... | collective-permute-start | bytes 1474568 | tf_op jit(solution)/shard_map/ppermute | solution.py:693
  53.6 18.5 %collective-permute-start.18 = (bf16[2,48,1920]{2,1,0:T(8,128)(2,1)S(1)}, bf16[2,48,1920]{2,1,0:T(8,128)(2,1)S(1)}, u32[]{:S(2)}, u32[]{:S(2)}) collective-permute-start(bf16[2,48,1920]{2,1,0:T(8,128)(2,1)S(1)} %pad_maximum_fusion), channel_id=1, source_target_pairs={{0,16},{1,17},{2,18},{3,19},{4,20},{5,21},{6,22},{7,23},{8,24},{9,... | collective-permute-start | bytes 1105928 | tf_op jit(solution)/shard_map/ppermute | solution.py:69
  55.3 16.9 %collective-permute-start.19 = (bf16[2,48,1920]{2,1,0:T(8,128)(2,1)S(1)}, bf16[2,48,1920]{2,1,0:T(8,128)(2,1)S(1)}, u32[]{:S(2)}, u32[]{:S(2)}) collective-permute-start(bf16[2,48,1920]{2,1,0:T(8,128)(2,1)S(1)} %pad_maximum_fusion.1), channel_id=1, source_target_pairs={{0,2},{1,3},{2,0},{3,1},{4,6},{5,7},{6,4},{7,5},{8,10},{9,11},{10,... | collective-permute-start | bytes 1105928 | tf_op jit(solution)/shard_map/ppermute | solution.py:69
  55.9 16.2 %collective-permute-start.20 = (bf16[1,192,384]{2,1,0:T(8,128)(2,1)S(1)}, bf16[1,192,384]{2,1,0:T(8,128)(2,1)S(1)}, u32[]{:S(2)}, u32[]{:S(2)}) collective-permute-start(bf16[1,192,384]{2,1,0:T(8,128)(2,1)S(1)} %bitcast.283), channel_id=1, source_target_pairs={{0,4},{1,5},{2,6},{3,7},{4,8},{5,9},{6,10},{7,11},{8,12},{9,13},{1... | collective-permute-start | bytes 442376 | tf_op jit(solution)/shard_map/ppermute | solution.py:69
  60.4 11.8 %collective-permute-start.21 = (bf16[1,192,384]{2,1,0:T(8,128)(2,1)S(1)}, bf16[1,192,384]{2,1,0:T(8,128)(2,1)S(1)}, u32[]{:S(2)}, u32[]{:S(2)}) collective-permute-start(bf16[1,192,384]{2,1,0:T(8,128)(2,1)S(1)} %bitcast.284), channel_id=1, source_target_pairs={{0,8},{1,9},{2,10},{3,11},{4,12},{5,13},{6,14},{7,15},{8,0},{9,1},... | collective-permute-start | bytes 442376 | tf_op jit(solution)/shard_map/ppermute | solution.py:69
  62.0 10.2 %collective-permute-start.22 = (bf16[1,192,384]{2,1,0:T(8,128)(2,1)S(1)}, bf16[1,192,384]{2,1,0:T(8,128)(2,1)S(1)}, u32[]{:S(2)}, u32[]{:S(2)}) collective-permute-start(bf16[1,192,384]{2,1,0:T(8,128)(2,1)S(1)} %bitcast.285), channel_id=1, source_target_pairs={{0,12},{1,13},{2,14},{3,15},{4,0},{5,1},{6,2},{7,3},{8,4},{9,5},{1... | collective-permute-start | bytes 442376 | tf_op jit(solution)/shard_map/ppermute | solution.py:69
  72.2 18.0 %collective-permute-start.23 = (bf16[4,48,1920]{2,1,0:T(8,128)(2,1)S(1)}, bf16[4,48,1920]{2,1,0:T(8,128)(2,1)S(1)}, u32[]{:S(2)}, u32[]{:S(2)}) collective-permute-start(bf16[4,48,1920]{2,1,0:T(8,128)(2,1)S(1)} %constant_dynamic-update-slice_fusion.6.refs_0_), channel_id=1, source_target_pairs={{0,2},{1,3},{2,0},{3,1},{4,6},{5,7},{6,4},{7,5},{8,10},{9,11},{10,... | collective-permute-start | bytes 2211848 | tf_op jit(solution)/shard_map/ppermute | solution.py:69
  73.8 17.7 %collective-permute-start.24 = (bf16[4,48,1920]{2,1,0:T(8,128)(2,1)S(1)}, bf16[4,48,1920]{2,1,0:T(8,128)(2,1)S(1)}, u32[]{:S(2)}, u32[]{:S(2)}) collective-permute-start(bf16[4,48,1920]{2,1,0:T(8,128)(2,1)S(1)} %constant_dynamic-update-slice_fusion.9.refs_1_), channel_id=1, source_target_pairs={{0,16},{1,17},{2,18},{3,19},{4,20},{5,21},{6,22},{7,23},{8,24},{9,... | collective-permute-start | bytes 2211848 | tf_op jit(solution)/shard_map/ppermute | solution.py:69
  74.4 17.1 %collective-permute-start.25 = (bf16[4,48,1920]{2,1,0:T(8,128)(2,1)S(1)}, bf16[4,48,1920]{2,1,0:T(8,128)(2,1)S(1)}, u32[]{:S(2)}, u32[]{:S(2)}) collective-permute-start(bf16[4,48,1920]{2,1,0:T(8,128)(2,1)S(1)} %constant_dynamic-update-slice_fusion.6.refs_0_), channel_id=1, source_target_pairs={{0,1},{1,0},{2,3},{3,2},{4,5},{5,4},{6,7},{7,6},{8,9},{9,8},{10,11... | collective-permute-start | bytes 2211848 | tf_op jit(solution)/shard_map/ppermute | solution.py:685
  74.4 17.1 %collective-permute-start.26 = (bf16[4,48,1920]{2,1,0:T(8,128)(2,1)S(1)}, bf16[4,48,1920]{2,1,0:T(8,128)(2,1)S(1)}, u32[]{:S(2)}, u32[]{:S(2)}) collective-permute-start(bf16[4,48,1920]{2,1,0:T(8,128)(2,1)S(1)} %constant_dynamic-update-slice_fusion.9.refs_1_), channel_id=1, source_target_pairs={{0,1},{1,0},{2,3},{3,2},{4,5},{5,4},{6,7},{7,6},{8,9},{9,8},{10,11... | collective-permute-start | bytes 2211848 | tf_op jit(solution)/shard_map/ppermute | solution.py:685
  91.6 3.3 %collective-permute-start.28 = (bf16[4,48,1920]{2,1,0:T(8,128)(2,1)S(1)}, bf16[4,48,1920]{2,1,0:T(8,128)(2,1)S(1)}, u32[]{:S(2)}, u32[]{:S(2)}) collective-permute-start(bf16[4,48,1920]{2,1,0:T(8,128)(2,1)S(1)} %collective-permute-done.24.refs_3_), channel_id=1, source_target_pairs={{0,1},{1,0},{2,3},{3,2},{4,5},{5,4},{6,7},{7,6},{8,9},{9,8},{10,11... | collective-permute-start | bytes 2211848 | tf_op jit(solution)/shard_map/ppermute | solution.py:685
  92.2 15.4 %collective-permute-start.29 = (bf16[4,192,384]{2,1,0:T(8,128)(2,1)S(1)}, bf16[4,192,384]{2,1,0:T(8,128)(2,1)S(1)}, u32[]{:S(2)}, u32[]{:S(2)}) collective-permute-start(bf16[4,192,384]{2,1,0:T(8,128)(2,1)S(1)} %constant_dynamic-update-slice_fusion.12.refs_0_), channel_id=1, source_target_pairs={{0,16},{1,17},{2,18},{3,19},{4,20},{5,21},{6,22},{7,23},{8,24},{9,... | collective-permute-start | bytes 1769480 | tf_op jit(solution)/shard_map/ppermute | solution.py:69
  92.8 15.0 %collective-permute-start.30 = (bf16[4,192,384]{2,1,0:T(8,128)(2,1)S(1)}, bf16[4,192,384]{2,1,0:T(8,128)(2,1)S(1)}, u32[]{:S(2)}, u32[]{:S(2)}) collective-permute-start(bf16[4,192,384]{2,1,0:T(8,128)(2,1)S(1)} %constant_dynamic-update-slice_fusion.12.refs_0_), channel_id=1, source_target_pairs={{0,2},{1,3},{2,0},{3,1},{4,6},{5,7},{6,4},{7,5},{8,10},{9,11},{10,... | collective-permute-start | bytes 1769480 | tf_op jit(solution)/shard_map/ppermute | solution.py:69
  107.8 18.4 %collective-permute-start.32 = (bf16[512,768]{1,0:T(8,128)(2,1)S(1)}, bf16[512,768]{1,0:T(8,128)(2,1)S(1)}, u32[]{:S(2)}, u32[]{:S(2)}) collective-permute-start(bf16[512,768]{1,0:T(8,128)(2,1)S(1)} %get-tuple-element.215), channel_id=1, source_target_pairs={{0,16},{16,0},{1,17},{17,1},{2,18},{18,2},{3,19},{19,3},{4,20},{20... | collective-permute-start | bytes 2359304 | tf_op jit(solution)/shard_map/ppermute | solution.py:827
  109.3 13.9 %collective-permute-start.31 = (bf16[4,192,384]{2,1,0:T(8,128)(2,1)S(1)}, bf16[4,192,384]{2,1,0:T(8,128)(2,1)S(1)}, u32[]{:S(2)}, u32[]{:S(2)}) collective-permute-start(bf16[4,192,384]{2,1,0:T(8,128)(2,1)S(1)} %collective-permute-done.29.refs_1_), channel_id=1, source_target_pairs={{0,2},{1,3},{2,0},{3,1},{4,6},{5,7},{6,4},{7,5},{8,10},{9,11},{10,... | collective-permute-start | bytes 1769480 | tf_op jit(solution)/shard_map/ppermute | solution.py:69
  126.3 9.3 %collective-permute-start.33 = (bf16[4,192,384]{2,1,0:T(8,128)(2,1)S(1)}, bf16[4,192,384]{2,1,0:T(8,128)(2,1)S(1)}, u32[]{:S(2)}, u32[]{:S(2)}) collective-permute-start(bf16[4,192,384]{2,1,0:T(8,128)(2,1)S(1)} %constant_dynamic-update-slice_fusion.12.refs_0_), channel_id=1, source_target_pairs={{0,1},{1,0},{2,3},{3,2},{4,5},{5,4},{6,7},{7,6},{8,9},{9,8},{10,11... | collective-permute-start | bytes 1769480 | tf_op jit(solution)/shard_map/ppermute | solution.py:685
  126.3 9.3 %collective-permute-start.34 = (bf16[4,192,384]{2,1,0:T(8,128)(2,1)S(1)}, bf16[4,192,384]{2,1,0:T(8,128)(2,1)S(1)}, u32[]{:S(2)}, u32[]{:S(2)}) collective-permute-start(bf16[4,192,384]{2,1,0:T(8,128)(2,1)S(1)} %collective-permute-done.29.refs_1_), channel_id=1, source_target_pairs={{0,1},{1,0},{2,3},{3,2},{4,5},{5,4},{6,7},{7,6},{8,9},{9,8},{10,11... | collective-permute-start | bytes 1769480 | tf_op jit(solution)/shard_map/ppermute | solution.py:685
  126.8 8.8 %collective-permute-start.35 = (bf16[4,192,384]{2,1,0:T(8,128)(2,1)S(1)}, bf16[4,192,384]{2,1,0:T(8,128)(2,1)S(1)}, u32[]{:S(2)}, u32[]{:S(2)}) collective-permute-start(bf16[4,192,384]{2,1,0:T(8,128)(2,1)S(1)} %collective-permute-done.30.refs_2_), channel_id=1, source_target_pairs={{0,1},{1,0},{2,3},{3,2},{4,5},{5,4},{6,7},{7,6},{8,9},{9,8},{10,11... | collective-permute-start | bytes 1769480 | tf_op jit(solution)/shard_map/ppermute | solution.py:685
  126.8 8.8 %collective-permute-start.36 = (bf16[4,192,384]{2,1,0:T(8,128)(2,1)S(1)}, bf16[4,192,384]{2,1,0:T(8,128)(2,1)S(1)}, u32[]{:S(2)}, u32[]{:S(2)}) collective-permute-start(bf16[4,192,384]{2,1,0:T(8,128)(2,1)S(1)} %collective-permute-done.31.refs_3_), channel_id=1, source_target_pairs={{0,1},{1,0},{2,3},{3,2},{4,5},{5,4},{6,7},{7,6},{8,9},{9,8},{10,11... | collective-permute-start | bytes 1769480 | tf_op jit(solution)/shard_map/ppermute | solution.py:685
  135.6 9.5 %collective-permute-start.37 = (bf16[16,192,384]{2,1,0:T(8,128)(2,1)S(1)}, bf16[16,192,384]{2,1,0:T(8,128)(2,1)S(1)}, u32[]{:S(2)}, u32[]{:S(2)}) collective-permute-start(bf16[16,192,384]{2,1,0:T(8,128)(2,1)S(1)} %get-tuple-element.231), channel_id=1, source_target_pairs={{0,1},{1,0},{2,3},{3,2},{4,5},{5,4},{6,7},{7,6},{8,9},{9,8},{10,11... | collective-permute-start | bytes 7077896 | tf_op jit(solution)/shard_map/ppermute | solution.py:98
  145.4 17.0 %collective-permute-start.38 = (bf16[2,2,192,384]{3,2,1,0:T(8,128)(2,1)S(1)}, bf16[2,2,192,384]{3,2,1,0:T(8,128)(2,1)S(1)}, u32[]{:S(2)}, u32[]{:S(2)}) collective-permute-start(bf16[2,2,192,384]{3,2,1,0:T(8,128)(2,1)S(1)} %fusion.4), channel_id=1, source_target_pairs={{0,2},{1,3},{2,0},{3,1},{4,6},{5,7},{6,4},{7,5},{8,10},{9,11},{10,... | collective-permute-start | bytes 1769480 | tf_op jit(solution)/shard_map/ppermute | solution.py:120
  146.0 16.5 %collective-permute-start.39 = (bf16[2,2,192,384]{3,2,1,0:T(8,128)(2,1)S(1)}, bf16[2,2,192,384]{3,2,1,0:T(8,128)(2,1)S(1)}, u32[]{:S(2)}, u32[]{:S(2)}) collective-permute-start(bf16[2,2,192,384]{3,2,1,0:T(8,128)(2,1)S(1)} %fusion.5), channel_id=1, source_target_pairs={{0,16},{1,17},{2,18},{3,19},{4,20},{5,21},{6,22},{7,23},{8,24},{9,... | collective-permute-start | bytes 1769480 | tf_op jit(solution)/shard_map/ppermute | solution.py:120
  147.5 34.9 %collective-permute-start.42 = (bf16[256,768]{1,0:T(8,128)(2,1)S(1)}, bf16[256,768]{1,0:T(8,128)(2,1)S(1)}, u32[]{:S(2)}, u32[]{:S(2)}) collective-permute-start(bf16[256,768]{1,0:T(8,128)(2,1)S(1)} %get-tuple-element.339), channel_id=1, source_target_pairs={{0,16},{16,0},{1,17},{17,1},{2,18},{18,2},{3,19},{19,3},{4,20},{20... | collective-permute-start | bytes 1179656 | tf_op jit(solution)/shard_map/ppermute | solution.py:922
  162.7 19.7 %collective-permute-start.40 = (bf16[2,192,384]{2,1,0:T(8,128)(2,1)S(1)}, bf16[2,192,384]{2,1,0:T(8,128)(2,1)S(1)}, u32[]{:S(2)}, u32[]{:S(2)}) collective-permute-start(bf16[2,192,384]{2,1,0:T(8,128)(2,1)S(1)} %get-tuple-element.328), channel_id=1, source_target_pairs={{0,16},{1,17},{2,18},{3,19},{4,20},{5,21},{6,22},{7,23},{8,24},{9,... | collective-permute-start | bytes 884744 | tf_op jit(solution)/shard_map/ppermute | solution.py:120
  164.2 18.3 %collective-permute-start.41 = (bf16[2,192,384]{2,1,0:T(8,128)(2,1)S(1)}, bf16[2,192,384]{2,1,0:T(8,128)(2,1)S(1)}, u32[]{:S(2)}, u32[]{:S(2)}) collective-permute-start(bf16[2,192,384]{2,1,0:T(8,128)(2,1)S(1)} %get-tuple-element.327), channel_id=1, source_target_pairs={{0,2},{1,3},{2,0},{3,1},{4,6},{5,7},{6,4},{7,5},{8,10},{9,11},{10,... | collective-permute-start | bytes 884744 | tf_op jit(solution)/shard_map/ppermute | solution.py:120
  182.5 17.5 %collective-permute-start.43 = (bf16[16,48,1920]{2,1,0:T(8,128)(2,1)S(1)}, bf16[16,48,1920]{2,1,0:T(8,128)(2,1)S(1)}, u32[]{:S(2)}, u32[]{:S(2)}) collective-permute-start(bf16[16,48,1920]{2,1,0:T(8,128)(2,1)S(1)} %get-tuple-element.257), channel_id=1, source_target_pairs={{0,1},{1,0},{2,3},{3,2},{4,5},{5,4},{6,7},{7,6},{8,9},{9,8},{10,11... | collective-permute-start | bytes 8847368 | tf_op jit(solution)/shard_map/ppermute | solution.py:98
  182.5 17.4 %collective-permute-start.44 = (bf16[256,768]{1,0:T(8,128)(2,1)S(1)}, bf16[256,768]{1,0:T(8,128)(2,1)S(1)}, u32[]{:S(2)}, u32[]{:S(2)}) collective-permute-start(bf16[256,768]{1,0:T(8,128)(2,1)S(1)} %get-tuple-element.258), channel_id=1, source_target_pairs={{0,16},{16,0},{1,17},{17,1},{2,18},{18,2},{3,19},{19,3},{4,20},{20... | collective-permute-start | bytes 1179656 | tf_op jit(solution)/shard_map/ppermute | solution.py:941
  185.0 33.8 %collective-permute-start.47 = (bf16[192,384]{1,0:T(8,128)(2,1)S(1)}, bf16[192,384]{1,0:T(8,128)(2,1)S(1)}, u32[]{:S(2)}, u32[]{:S(2)}) collective-permute-start(bf16[192,384]{1,0:T(8,128)(2,1)S(1)} %get-tuple-element.326), channel_id=1, source_target_pairs={{0,4},{1,5},{2,6},{3,7},{4,8},{5,9},{6,10},{7,11},{8,12},{9,13},{1... | collective-permute-start | bytes 442376 | tf_op jit(solution)/shard_map/ppermute | solution.py:132
  188.8 30.0 %collective-permute-start.48 = (bf16[192,384]{1,0:T(8,128)(2,1)S(1)}, bf16[192,384]{1,0:T(8,128)(2,1)S(1)}, u32[]{:S(2)}, u32[]{:S(2)}) collective-permute-start(bf16[192,384]{1,0:T(8,128)(2,1)S(1)} %get-tuple-element.325), channel_id=1, source_target_pairs={{0,8},{1,9},{2,10},{3,11},{4,12},{5,13},{6,14},{7,15},{8,0},{9,1},... | collective-permute-start | bytes 442376 | tf_op jit(solution)/shard_map/ppermute | solution.py:132
  188.8 30.0 %collective-permute-start.49 = (bf16[192,384]{1,0:T(8,128)(2,1)S(1)}, bf16[192,384]{1,0:T(8,128)(2,1)S(1)}, u32[]{:S(2)}, u32[]{:S(2)}) collective-permute-start(bf16[192,384]{1,0:T(8,128)(2,1)S(1)} %get-tuple-element.324), channel_id=1, source_target_pairs={{0,12},{1,13},{2,14},{3,15},{4,0},{5,1},{6,2},{7,3},{8,4},{9,5},{1... | collective-permute-start | bytes 442376 | tf_op jit(solution)/shard_map/ppermute | solution.py:132
  200.8 18.0 %collective-permute-start.45 = (bf16[2,2,48,1920]{3,2,1,0:T(8,128)(2,1)S(1)}, bf16[2,2,48,1920]{3,2,1,0:T(8,128)(2,1)S(1)}, u32[]{:S(2)}, u32[]{:S(2)}) collective-permute-start(bf16[2,2,48,1920]{3,2,1,0:T(8,128)(2,1)S(1)} %fusion), channel_id=1, source_target_pairs={{0,2},{1,3},{2,0},{3,1},{4,6},{5,7},{6,4},{7,5},{8,10},{9,11},{10,... | collective-permute-start | bytes 2211848 | tf_op jit(solution)/shard_map/ppermute | solution.py:120
  201.3 17.6 %collective-permute-start.46 = (bf16[2,2,48,1920]{3,2,1,0:T(8,128)(2,1)S(1)}, bf16[2,2,48,1920]{3,2,1,0:T(8,128)(2,1)S(1)}, u32[]{:S(2)}, u32[]{:S(2)}) collective-permute-start(bf16[2,2,48,1920]{3,2,1,0:T(8,128)(2,1)S(1)} %fusion.1), channel_id=1, source_target_pairs={{0,16},{1,17},{2,18},{3,19},{4,20},{5,21},{6,22},{7,23},{8,24},{9,... | collective-permute-start | bytes 2211848 | tf_op jit(solution)/shard_map/ppermute | solution.py:120
  227.7 12.2 %collective-permute-start.50 = (bf16[16,48,1152]{2,1,0:T(8,128)(2,1)}, bf16[16,48,1152]{2,1,0:T(8,128)(2,1)}, u32[]{:S(2)}, u32[]{:S(2)}) collective-permute-start(bf16[16,48,1152]{2,1,0:T(8,128)(2,1)} %get-tuple-element.281), channel_id=1, source_target_pairs={{0,1},{1,0},{2,3},{3,2},{4,5},{5,4},{6,7},{7,6},{8,9},{9,8},{10,11... | collective-permute-start | bytes 5308424 | tf_op jit(solution)/shard_map/ppermute | solution.py:98
  227.7 11.2 %collective-permute-start.51 = (bf16[2,48,1920]{2,1,0:T(8,128)(2,1)}, bf16[2,48,1920]{2,1,0:T(8,128)(2,1)S(1)}, u32[]{:S(2)}, u32[]{:S(2)}) collective-permute-start(bf16[2,48,1920]{2,1,0:T(8,128)(2,1)} %get-tuple-element.282), channel_id=1, source_target_pairs={{0,16},{1,17},{2,18},{3,19},{4,20},{5,21},{6,22},{7,23},{8,24},{9,... | collective-permute-start | bytes 1105928 | tf_op jit(solution)/shard_map/ppermute | solution.py:120
  229.0 10.9 %collective-permute-start.52 = (bf16[2,48,1920]{2,1,0:T(8,128)(2,1)}, bf16[2,48,1920]{2,1,0:T(8,128)(2,1)S(1)}, u32[]{:S(2)}, u32[]{:S(2)}) collective-permute-start(bf16[2,48,1920]{2,1,0:T(8,128)(2,1)} %get-tuple-element.283), channel_id=1, source_target_pairs={{0,2},{1,3},{2,0},{3,1},{4,6},{5,7},{6,4},{7,5},{8,10},{9,11},{10,... | collective-permute-start | bytes 1105928 | tf_op jit(solution)/shard_map/ppermute | solution.py:120
  231.8 32.7 %collective-permute-start.66 = (bf16[96,384]{1,0:T(8,128)(2,1)S(1)}, bf16[96,384]{1,0:T(8,128)(2,1)S(1)}, u32[]{:S(2)}, u32[]{:S(2)}) collective-permute-start(bf16[96,384]{1,0:T(8,128)(2,1)S(1)} %dynamic-slice_convert_fusion.1), channel_id=1, source_target_pairs={{0,1},{1,0},{2,3},{3,2},{4,5},{5,4},{6,7},{7,6},{8,9},{9,8},{10,11... | collective-permute-start | bytes 221192 | tf_op jit(solution)/shard_map/ppermute | solution.py:879
  242.6 18.1 %collective-permute-start.56 = (bf16[2,2,48,1152]{3,2,1,0:T(8,128)(2,1)S(1)}, bf16[2,2,48,1152]{3,2,1,0:T(8,128)(2,1)S(1)}, u32[]{:S(2)}, u32[]{:S(2)}) collective-permute-start(bf16[2,2,48,1152]{3,2,1,0:T(8,128)(2,1)S(1)} %fusion.8), channel_id=1, source_target_pairs={{0,2},{1,3},{2,0},{3,1},{4,6},{5,7},{6,4},{7,5},{8,10},{9,11},{10,... | collective-permute-start | bytes 1327112 | tf_op jit(solution)/shard_map/ppermute | solution.py:120
  244.1 18.0 %collective-permute-start.57 = (bf16[2,2,48,1152]{3,2,1,0:T(8,128)(2,1)S(1)}, bf16[2,2,48,1152]{3,2,1,0:T(8,128)(2,1)S(1)}, u32[]{:S(2)}, u32[]{:S(2)}) collective-permute-start(bf16[2,2,48,1152]{3,2,1,0:T(8,128)(2,1)S(1)} %fusion.9), channel_id=1, source_target_pairs={{0,16},{1,17},{2,18},{3,19},{4,20},{5,21},{6,22},{7,23},{8,24},{9,... | collective-permute-start | bytes 1327112 | tf_op jit(solution)/shard_map/ppermute | solution.py:120
  246.7 19.1 %collective-permute-start.53 = (bf16[48,1920]{1,0:T(8,128)(2,1)S(1)}, bf16[48,1920]{1,0:T(8,128)(2,1)S(1)}, u32[]{:S(2)}, u32[]{:S(2)}) collective-permute-start(bf16[48,1920]{1,0:T(8,128)(2,1)S(1)} %get-tuple-element.321), channel_id=1, source_target_pairs={{0,4},{1,5},{2,6},{3,7},{4,8},{5,9},{6,10},{7,11},{8,12},{9,13},{1... | collective-permute-start | bytes 552968 | tf_op jit(solution)/shard_map/ppermute | solution.py:132
  246.8 19.9 %collective-permute-start.54 = (bf16[48,1920]{1,0:T(8,128)(2,1)S(1)}, bf16[48,1920]{1,0:T(8,128)(2,1)S(1)}, u32[]{:S(2)}, u32[]{:S(2)}) collective-permute-start(bf16[48,1920]{1,0:T(8,128)(2,1)S(1)} %get-tuple-element.320), channel_id=1, source_target_pairs={{0,8},{1,9},{2,10},{3,11},{4,12},{5,13},{6,14},{7,15},{8,0},{9,1},... | collective-permute-start | bytes 552968 | tf_op jit(solution)/shard_map/ppermute | solution.py:132
  260.7 6.0 %collective-permute-start.55 = (bf16[48,1920]{1,0:T(8,128)(2,1)S(1)}, bf16[48,1920]{1,0:T(8,128)(2,1)S(1)}, u32[]{:S(2)}, u32[]{:S(2)}) collective-permute-start(bf16[48,1920]{1,0:T(8,128)(2,1)S(1)} %get-tuple-element.319), channel_id=1, source_target_pairs={{0,12},{1,13},{2,14},{3,15},{4,0},{5,1},{6,2},{7,3},{8,4},{9,5},{1... | collective-permute-start | bytes 552968 | tf_op jit(solution)/shard_map/ppermute | solution.py:132
  263.3 8.4 %collective-permute-start.58 = (bf16[2,48,1152]{2,1,0:T(8,128)(2,1)S(1)}, bf16[2,48,1152]{2,1,0:T(8,128)(2,1)S(1)}, u32[]{:S(2)}, u32[]{:S(2)}) collective-permute-start(bf16[2,48,1152]{2,1,0:T(8,128)(2,1)S(1)} %get-tuple-element.333), channel_id=1, source_target_pairs={{0,16},{1,17},{2,18},{3,19},{4,20},{5,21},{6,22},{7,23},{8,24},{9,... | collective-permute-start | bytes 663560 | tf_op jit(solution)/shard_map/ppermute | solution.py:120
  264.5 7.2 %collective-permute-start.59 = (bf16[2,48,1152]{2,1,0:T(8,128)(2,1)S(1)}, bf16[2,48,1152]{2,1,0:T(8,128)(2,1)S(1)}, u32[]{:S(2)}, u32[]{:S(2)}) collective-permute-start(bf16[2,48,1152]{2,1,0:T(8,128)(2,1)S(1)} %get-tuple-element.332), channel_id=1, source_target_pairs={{0,2},{1,3},{2,0},{3,1},{4,6},{5,7},{6,4},{7,5},{8,10},{9,11},{10,... | collective-permute-start | bytes 663560 | tf_op jit(solution)/shard_map/ppermute | solution.py:120
  265.9 19.9 %collective-permute-start.60 = (bf16[512,768]{1,0:T(8,128)(2,1)S(1)}, bf16[512,768]{1,0:T(8,128)(2,1)S(1)}, u32[]{:S(2)}, u32[]{:S(2)}) collective-permute-start(bf16[512,768]{1,0:T(8,128)(2,1)S(1)} %get-tuple-element.306), channel_id=1, source_target_pairs={{0,16},{16,0},{1,17},{17,1},{2,18},{18,2},{3,19},{19,3},{4,20},{20... | collective-permute-start | bytes 2359304 | tf_op jit(solution)/shard_map/ppermute | solution.py:1010
  273.0 7.9 %collective-permute-start.63 = (bf16[48,1152]{1,0:T(8,128)(2,1)S(1)}, bf16[48,1152]{1,0:T(8,128)(2,1)S(1)}, u32[]{:S(2)}, u32[]{:S(2)}) collective-permute-start(bf16[48,1152]{1,0:T(8,128)(2,1)S(1)} %get-tuple-element.330), channel_id=1, source_target_pairs={{0,12},{1,13},{2,14},{3,15},{4,0},{5,1},{6,2},{7,3},{8,4},{9,5},{1... | collective-permute-start | bytes 331784 | tf_op jit(solution)/shard_map/ppermute | solution.py:132
  273.6 7.2 %collective-permute-start.62 = (bf16[48,1152]{1,0:T(8,128)(2,1)S(1)}, bf16[48,1152]{1,0:T(8,128)(2,1)S(1)}, u32[]{:S(2)}, u32[]{:S(2)}) collective-permute-start(bf16[48,1152]{1,0:T(8,128)(2,1)S(1)} %get-tuple-element.329), channel_id=1, source_target_pairs={{0,8},{1,9},{2,10},{3,11},{4,12},{5,13},{6,14},{7,15},{8,0},{9,1},... | collective-permute-start | bytes 331784 | tf_op jit(solution)/shard_map/ppermute | solution.py:132
  275.2 6.5 %collective-permute-start.61 = (bf16[48,1152]{1,0:T(8,128)(2,1)S(1)}, bf16[48,1152]{1,0:T(8,128)(2,1)S(1)}, u32[]{:S(2)}, u32[]{:S(2)}) collective-permute-start(bf16[48,1152]{1,0:T(8,128)(2,1)S(1)} %get-tuple-element.331), channel_id=1, source_target_pairs={{0,4},{1,5},{2,6},{3,7},{4,8},{5,9},{6,10},{7,11},{8,12},{9,13},{1... | collective-permute-start | bytes 331784 | tf_op jit(solution)/shard_map/ppermute | solution.py:132
  (46 other events, 530.0 us)

commit v4 on v3

--- a/solution.py
+++ b/solution.py
@@ -128,9 +128,13 @@
     final = []
     for k in range(grid.nz):
         n = 0 if k < lots[0][1] else 1
-        total = add_all([c[k - lots[n][0]] for c in current[n]])
-        final.append(total if k == 0 else lax.ppermute(total.astype(BF16), AXES, grid.shift("z", k)))
-    final[1:] = yield final[1:]
+        final.append(add_all([c[k - lots[n][0]] for c in current[n]]))
+    leaving = [total.astype(BF16) for total in final[1:]]
+    if held:
+        leaving, held = together(leaving, held)
+    flat = [lax.ppermute(total, AXES, grid.shift("z", k + 1)) for k, total in enumerate(leaving)]
+    back = yield (flat, *held) if held else flat
+    final[1:] = back[0] if isinstance(back, tuple) else back
     yield add_all(final)
 
 
@@ -561,7 +565,7 @@
 anywhere = pl.BlockSpec(memory_space=pl.ANY)
 
 
-def call(kernel, tab, inputs, piece_arrays, outs, scratch, grid=(1,), cost=0, aliases=None):
+def call(kernel, tab, inputs, piece_arrays, outs, scratch, grid=(1,), cost=0, aliases=None, stay=()):
     specs = [spec or whole(a.shape) for a, spec in inputs]
     specs = specs + [pl.BlockSpec(memory_space=pltpu.HBM) for _ in piece_arrays]
     blocks = [(a, spec) for a, spec in inputs] + [(o, spec) for o, spec in outs]
@@ -582,8 +586,8 @@
     moved = sum(a.size * a.dtype.itemsize for a, _ in inputs) + sum(a.size * a.dtype.itemsize for a in piece_arrays)
     moved += sum(math.prod(o.shape) * jnp.dtype(o.dtype).itemsize for o, _ in outs)
     inputs = [
-        (pltpu.with_memory_space_constraint(a, pltpu.HBM) if a.size > 2**21 and spec is not None else a, spec)
-        for a, spec in inputs
+        (pltpu.with_memory_space_constraint(a, pltpu.HBM) if n in stay or a.size > 2**21 and spec is not None else a, spec)
+        for n, (a, spec) in enumerate(inputs)
     ]
     return pl.pallas_call(
         kernel,
@@ -661,7 +665,8 @@
             )
 
         tok_away, w_qkv = together(tok_away, w_qkv)
-        tok_got = lax.ppermute(tok_away, "seq", swap_x)
+        most = 3 * half // 4
+        tok_first = lax.ppermute(tok_away[:most], "seq", swap_x)
         piece_a = with_partner(0)
         piece_a, w_up, w_out, w_down = together(piece_a, w_up, w_out, w_down)
         piece_b, piece_c = with_partner(1), with_partner(2)
@@ -694,7 +699,8 @@
             return Pieces(chips, mine, theirs, fields)
 
         z_a = gather_along_z(grid, piece_a)
-        arrays, tok_got, piece_b = together(arrays_of(z_a), tok_got, piece_b)
+        arrays, tok_first, tok_next, piece_b = together(arrays_of(z_a), tok_first, tok_away[most:], piece_b)
+        tok_second = lax.ppermute(tok_next, "seq", swap_x)
         z_a = lots_of(with_arrays(z_a, arrays), 2)
         near_a = near_of(z_a)
         z_b = gather_along_z(grid, piece_b)
@@ -703,6 +709,7 @@
         far_a = far_of(wide_a)
         all_a = wide_a + far_a
         arrays_a, z_own, piece_c = together(arrays_of(all_a), z_b[0][0], piece_c)
+        tok_got = jnp.concatenate([tok_first, tok_second], axis=0)
         z_b = with_arrays(z_b, [z_own] + arrays_of(z_b[1:]))
         group_a = finish(with_arrays(all_a, arrays_a), fields_a)
         z_b = lots_of(with_arrays(z_b, lax.optimization_barrier(arrays_of(z_b))), 2)
@@ -929,7 +936,7 @@
             (whole_up, None), (whole_out, None),
         ],
         [],
-        [(sds((rows, width), F32), tile(width)), (low(rows, width), tile(width)), (up_out, out_part), (up_out, out_part)],
+        [(pltpu.HBM((rows, width), F32), tile(width)), (low(rows, width), tile(width)), (up_out, out_part), (up_out, out_part)],
         [vmem((width, width), F32)],
         grid=(tiles,),
         cost=2 * rows * width * ff + 4 * rows * width * width,
@@ -951,7 +958,7 @@
         at = lambda base: pl.BlockSpec((2, 1, 256, 256), lambda b, g, t: (0, b, 0, base + first + g))
         to = pl.BlockSpec((2, 1, 256, 256), lambda b, g, t: (0, b, 0, g))
         totals = pl.BlockSpec((4, 1, 512), lambda b, g, t: (b * groups + first + g, 0, 0))
-        shape = low(2, clip_blocks, 256, 256 * (last - first))
+        shape = pltpu.HBM((2, clip_blocks, 256, 256 * (last - first)), BF16)
         grads = call(
             functools.partial(attend_back_kernel, chips),
             tab,
@@ -972,8 +979,7 @@
     arrived_up = up_sum.send(arrived_up)
     grads_b = attend_back(group_cut, groups, grad_att)
     grads_b, arrived_up, arrived = together(grads_b, arrived_up, arrived)
-    left, right = owned(down_sum.send(arrived))
-    owned_down = jnp.concatenate([left, right], axis=1)
+    arrived_down = arrived
     arrived_up, grads_b, normed_first = up_sum.send((arrived_up, grads_b, normed_first))
     qkv_out = low(chips, rows_a, 3 * width // 2)
     qkv_mine, qkv_other = call(
@@ -984,14 +990,16 @@
         [(qkv_out, None), (qkv_out, None)],
         [],
         cost=2 * rows * width * 3 * width,
-    )
-    qkv_mine, qkv_other, grads_a, grads_b = together(qkv_mine, qkv_other, grads_a, grads_b)
+        stay=tuple(range(1, 7)),
+    )
+    qkv_mine, qkv_other, grads_a, grads_b, tok_own, arrived_up = together(
+        qkv_mine, qkv_other, grads_a, grads_b, tok_own, arrived_up
+    )
+    arrived_up, tok_got = up_sum.send((arrived_up, tok_got))
     qkv_sum = steps_of(qkv_mine, qkv_other, 2)
     arrived = next(qkv_sum)
-
-    tok_own, arrived, arrived_up = together(tok_own, arrived, arrived_up)
-    arrived_up = up_sum.send(arrived_up)
-    arrived = qkv_sum.send(arrived)
+    arrived, tok_own = qkv_sum.send((arrived, tok_own))
+
     grad_own, grad_got = call(
         functools.partial(first_kernel, cuts),
         tab,
@@ -1004,12 +1012,20 @@
         [],
         grid=(tiles,),
         cost=2 * rows * width * 3 * width,
-    )
-    grad_got, grad_own, arrived = together(grad_got, grad_own, arrived)
+        stay=(3, 4) + tuple(range(5, 11)),
+    )
+    grad_got, grad_own, arrived, arrived_up, arrived_down = together(
+        grad_got, grad_own, arrived, arrived_up, arrived_down
+    )
     arrived = qkv_sum.send(arrived)
+    arrived, grad_got = together(arrived, grad_got)
     grad_back = lax.ppermute(grad_got, "seq", swap_x)
-    arrived_up, arrived, out_first, out_second = together(arrived_up, arrived, out_first, out_second)
+    arrived_up, arrived, arrived_down, out_first, out_second = together(
+        arrived_up, arrived, arrived_down, out_first, out_second
+    )
     arrived = qkv_sum.send(arrived)
+    left, right = owned(down_sum.send(arrived_down))
+    owned_down = jnp.concatenate([left, right], axis=1)
     left, right = owned(up_sum.send(arrived_up))
     owned_up = jnp.concatenate([left[:, : ff // 2], right[:, : ff // 2]], axis=1)
     owned_out = jnp.concatenate([left[:, ff // 2 :], right[:, ff // 2 :]], axis=1)

time: 291 us -> 284 us (0.976)
  Pallas kernels: 126 us -> 132 us
  other arithmetic: 22.4 us -> 16.5 us
  waiting for transfers between devices: 58.1 us -> 53.2 us
  local copies, waits for them, and re-layouts: 10 us -> 6.57 us
    ppermute x12, waiting for transfers between devices: 13 us -> 5.47 us  [scatter_steps(): lax.ppermute(total, AXES, grid.shift(axes[step], k + 1))]
    pallas_call x13, Pallas kernels: 126 us -> 132 us  [call(): pl.pallas_call(kernel, out_shape=[o for o, _ in outs], input_output_alias...]
    unnamed x99 -> x92, local copies, waits for them, and re-layouts: 7.96 us -> 3.04 us
    ppermute x3, waiting for transfers between devices: 0.01 us -> 3.69 us  [scatter_steps(): got = lax.ppermute(other, AXES, grid.core_swap())]
    ppermute x10 -> x11, starting transfers between devices: 16.8 us -> 19.4 us  [the longest x9 15.3 us: scatter_steps(): lax.ppermute(total, AXES, grid.shift('z', k + 1))]
    ppermute x10 -> x11, waiting for transfers between devices: 5.82 us -> 3.55 us  [the longest x9 3.55 us: scatter_steps(): lax.ppermute(total, AXES, grid.shift('z', k + 1))]
  transfers between devices with their start and end apart: 67 -> 68, of which waited for: 22 -> 25; matrix products, arithmetic and copies ran while one was open for 7% -> 5% of each run, Pallas kernels for 42% -> 47%
where the time goes in v4:
time: 284 us; the launch traced here: 281 us
  Pallas kernels  132 us (46%)
  starting transfers between devices  69.9 us (25%)
  waiting for transfers between devices  53.2 us (19%)
  other arithmetic  16.5 us (6%)
  local copies, waits for them, and re-layouts  6.57 us (2%)
    pallas_call x13, Pallas kernels, call(): pl.pallas_call(kernel, out_shape=[o for o, _ in outs], input_output_alias...  132 us
    ppermute x20, waiting for transfers between devices, exchange(): lax.ppermute(array, AXES, grid.shift(axis, k))  33.7 us
    ppermute x20, starting transfers between devices, exchange(): lax.ppermute(array, AXES, grid.shift(axis, k))  28.9 us
    ppermute x9, starting transfers between devices, scatter_steps(): lax.ppermute(total, AXES, grid.shift('z', k + 1))  15.3 us
    ppermute x12, starting transfers between devices, scatter_steps(): lax.ppermute(total, AXES, grid.shift(axes[step], k + 1))  13.7 us
  transfers between devices with their start and end apart: 68, of which 25 were waited for; matrix products, arithmetic and copies ran while one was open for 5% of the time, Pallas kernels for 47%

profile of v4, /device:TPU:0, one launch (start us, length us, event | category | flops | bytes accessed | tf_op | source)
XLA Modules:
  0.0 280.5 jit_solution(15399782104863763039)
XLA Ops:
  1.4 1.5 dynamic-slice_bitcast_fusion.2
  3.6 2.6 collective-permute-start.4
  7.7 1.6 collective-permute-start.1
  9.3 2.6 collective-permute-start.2
  11.9 1.3 collective-permute-start.3
  14.1 1.2 collective-permute-done.5
  15.8 4.6 %collective-permute-done.2 = bf16[1,48,1280]{2,1,0:T(8,128)(2,1)S(1)} collective-permute-done((bf16[1,48,1280]{2,1,0:T(8,128)(2,1)S(1)}, bf16[1,48,1280]{2,1,0:T(8,128)(2,1)S(1)}, u32[]{:S(2)}, u32[]{:S(2)}) %collective-permute-start.2) | collective-permute-done | bytes 122912 | tf_op jit(solution)/shard_map/ppermute | solution.py:69
  20.4 1.5 collective-permute-start.6
  22.6 1.6 collective-permute-start.8
  24.2 8.4 %collective-permute-done.7 = bf16[2,48,1280]{2,1,0:T(8,128)(2,1)S(1)} collective-permute-done((bf16[2,48,1280]{2,1,0:T(8,128)(2,1)S(1)}, bf16[2,48,1280]{2,1,0:T(8,128)(2,1)S(1)}, u32[]{:S(2)}, u32[]{:S(2)}) %collective-permute-start.7) | collective-permute-done | bytes 245792 | tf_op jit(solution)/shard_map/ppermute | solution.py:69
  32.6 1.6 collective-permute-start.9
  34.2 1.3 collective-permute-start.10
  35.6 2.6 collective-permute-start.16
  38.2 1.6 collective-permute-start.17
  39.8 1.3 collective-permute-start.18
  41.3 3.6 %collective-permute-done.9.refs_2_ = bf16[4,48,1280]{2,1,0:T(8,128)(2,1)S(1)} collective-permute-done((bf16[4,48,1280]{2,1,0:T(8,128)(2,1)S(1)}, bf16[4,48,1280]{2,1,0:T(8,128)(2,1)S(1)}, u32[]{:S(2)}, u32[]{:S(2)}) %collective-permute-start.9) | collective-permute-done | bytes 491552 | tf_op jit(solution)/shard_map/ppermute | solution.py:69
  44.9 1.3 collective-permute-done.10.refs_3_
  46.7 3.6 %collective-permute-done.17 = bf16[1,48,1920]{2,1,0:T(8,128)(2,1)S(1)} collective-permute-done((bf16[1,48,1920]{2,1,0:T(8,128)(2,1)S(1)}, bf16[1,48,1920]{2,1,0:T(8,128)(2,1)S(1)}, u32[]{:S(2)}, u32[]{:S(2)}) %collective-permute-start.17) | collective-permute-done | bytes 184352 | tf_op jit(solution)/shard_map/ppermute | solution.py:69
  52.1 4.5 %collective-permute-start.21 = (bf16[1,192,384]{2,1,0:T(8,128)(2,1)S(1)}, bf16[1,192,384]{2,1,0:T(8,128)(2,1)S(1)}, u32[]{:S(2)}, u32[]{:S(2)}) collective-permute-start(bf16[1,192,384]{2,1,0:T(8,128)(2,1)S(1)} %bitcast.278), channel_id=1, source_target_pairs={{0,4},{1,5},{2,6},{3,7},{4,8},{5,9},{6,10},{7,11},{8,12},{9,13},{1... | collective-permute-start | bytes 442376 | tf_op jit(solution)/shard_map/ppermute | solution.py:69
  56.6 2.1 collective-permute-start.22
  59.3 8.6 %shard_map.135 = (bf16[1024,2304]{1,0:T(8,128)(2,1)}, bf16[1024,768]{1,0:T(8,128)(2,1)S(1)}, f32[8,768]{1,0:T(8,128)S(1)}, bf16[768,2304]{1,0:T(8,128)(2,1)}) custom-call(s32[34]{0:T(128)S(1)} %stack.140.tab, bf16[512,768]{1,0:T(8,128)(2,1)S(1)} %get-tuple-element.306.own, bf16[512,768]{1,0:T(8,128)(2,1)S(1)} %constant_dynamic-update-slice_fusion.got, ...), custom_call_target="tpu_custom_call" | custom-call | flops 3623878656 | bytes 15360000 | tf_op jit(solution)/shard_map/pallas_call | solution.py:592
  68.6 1.6 collective-permute-start.24
  71.4 13.1 %shard_map.136 = (bf16[2,2,256,768]{3,2,1,0:T(8,128)(2,1)S(1)}, f32[24,1,512]{2,1,0:T(1,128)S(1)}) custom-call(s32[34]{0:T(128)S(1)} %stack.140.tab, bf16[2,2,256,2304]{3,2,1,0:T(8,128)(2,1)} %bitcast.244, bf16[2,2,256,2304]{3,2,1,0:T(8,128)(2,1)} %bitcast.245, bf16[2,2,256,2304]{3,2,1,0:T(8,128)(2,1)} %bitcast.246), custom_call_target="tpu_custom_call" | custom-call | flops 3221225472 | bytes 15777792 | tf_op jit(solution)/shard_map/pallas_call | solution.py:592
  84.5 2.5 collective-permute-done.24.refs_2_
  87.0 1.3 collective-permute-done.25.refs_3_
  91.6 4.2 %shard_map.137 = (f32[1024,768]{1,0:T(8,128)S(1)}, bf16[1024,768]{1,0:T(8,128)(2,1)S(1)}, bf16[768,768]{1,0:T(8,128)(2,1)}) custom-call(s32[34]{0:T(128)S(1)} %stack.140.tab, bf16[1024,768]{1,0:T(8,128)(2,1)S(1)} %bitcast.223, bf16[512,768]{1,0:T(8,128)(2,1)S(1)} %get-tuple-element.306.own, bf16[512,768]{1,0:T(8,128)(2,1)S(1)} %constant_dynamic-update-slice_fusion.got, ...), custom_call_target="tpu_custom_call" | custom-call | flops 1207959552 | bytes 14966784 | tf_op jit(solution)/shard_map/pallas_call | solution.py:592
  95.8 7.4 %shard_map.138 = (bf16[1024,3072]{1,0:T(8,128)(2,1)}, bf16[1024,3072]{1,0:T(8,128)(2,1)}, bf16[768,3072]{1,0:T(8,128)(2,1)}) custom-call(s32[34]{0:T(128)S(1)} %stack.140.tab, bf16[1024,768]{1,0:T(8,128)(2,1)S(1)} %get-tuple-element.227.normed, bf16[4,48,1920]{2,1,0:T(8,128)(2,1)S(1)} %constant_dynamic-update-slice_fusion.8.refs_0_, ...), custom_call_target="tpu_custom_call" | custom-call | flops 2415919104 | bytes 24772608 | tf_op jit(solution)/shard_map/pallas_call | solution.py:592
  103.2 1.1 collective-permute-done.30.refs_1_
  104.6 1.4 collective-permute-start.33
  106.6 7.2 %shard_map.139 = (bf16[1024,3072]{1,0:T(8,128)(2,1)}, bf16[1024,3072]{1,0:T(8,128)(2,1)}) custom-call(s32[34]{0:T(128)S(1)} %stack.140.tab, bf16[1024,768]{1,0:T(8,128)(2,1)S(1)} %get-tuple-element.227.normed, bf16[768,3072]{1,0:T(8,128)(2,1)} %get-tuple-element.228.w_up, ...), custom_call_target="tpu_custom_call", output_to_operand_aliasing={{0}: (3, {}), {1}: (4, {})} | custom-call | flops 2415919104 | bytes 31457280 | tf_op jit(solution)/shard_map/pallas_call | solution.py:592
  113.8 6.1 %collective-permute-done.32.refs_3_ = bf16[4,192,384]{2,1,0:T(8,128)(2,1)S(1)} collective-permute-done((bf16[4,192,384]{2,1,0:T(8,128)(2,1)S(1)}, bf16[4,192,384]{2,1,0:T(8,128)(2,1)S(1)}, u32[]{:S(2)}, u32[]{:S(2)}) %collective-permute-start.32) | collective-permute-done | bytes 589856 | tf_op jit(solution)/shard_map/ppermute | solution.py:69
  119.9 3.1 %collective-permute-done.33.cot_got = bf16[512,768]{1,0:T(8,128)(2,1)S(1)} collective-permute-done((bf16[512,768]{1,0:T(8,128)(2,1)S(1)}, bf16[512,768]{1,0:T(8,128)(2,1)S(1)}, u32[]{:S(2)}, u32[]{:S(2)}) %collective-permute-start.33) | collective-permute-done | bytes 786464 | tf_op jit(solution)/shard_map/ppermute | solution.py:834
  124.0 8.4 %shard_map.140 = (bf16[16,192,384]{2,1,0:T(8,128)(2,1)S(1)}, bf16[16,192,384]{2,1,0:T(8,128)(2,1)S(1)}) custom-call(s32[34]{0:T(128)S(1)} %stack.140.tab, bf16[1024,3072]{1,0:T(8,128)(2,1)} %get-tuple-element.244.active, bf16[512,768]{1,0:T(8,128)(2,1)S(1)} %get-tuple-element.379.cot_own, bf16[512,768]{1,0:T(8,128)(2,1)S(1)} %collective-permute-done.33.cot_got), custom_call_target="tpu_custom_call" | custom-call | flops 4831838208 | bytes 12582912 | tf_op jit(solution)/shard_map/pallas_call | solution.py:592
  132.5 9.4 %shard_map.141 = (bf16[1024,768]{1,0:T(8,128)(2,1)S(1)}, bf16[3072,768]{1,0:T(8,128)(2,1)}) custom-call(s32[34]{0:T(128)S(1)} %stack.140.tab, bf16[1024,3072]{1,0:T(8,128)(2,1)} %get-tuple-element.244.active, f32[1024,768]{1,0:T(8,128)S(1)} %get-tuple-element.245.hidden, bf16[4,192,384]{2,1,0:T(8,128)(2,1)S(1)} %constant_dynamic-update-slice_fusion.14.refs_0_, ...), custom_call_target="tpu_custom_call" | custom-call | flops 4831838208 | bytes 20447232 | tf_op jit(solution)/shard_map/pallas_call | solution.py:592
  142.8 1.4 collective-permute-start.40
  145.0 14.9 %shard_map.142 = (bf16[1024,3072]{1,0:T(8,128)(2,1)}, bf16[16,48,1920]{2,1,0:T(8,128)(2,1)S(1)}, bf16[16,48,1920]{2,1,0:T(8,128)(2,1)S(1)}) custom-call(s32[34]{0:T(128)S(1)} %stack.140.tab, bf16[512,768]{1,0:T(8,128)(2,1)S(1)} %get-tuple-element.379.cot_own, bf16[512,768]{1,0:T(8,128)(2,1)S(1)} %collective-permute-done.33.cot_got, ...), custom_call_target="tpu_custom_call" | custom-call | flops 9663676416 | bytes 26345472 | tf_op jit(solution)/shard_map/pallas_call | solution.py:592
  160.1 1.5 collective-permute-start.41
  161.6 1.5 collective-permute-start.42
  163.1 16.1 %shard_map.143 = (f32[1024,768]{1,0:T(8,128)}, bf16[1024,768]{1,0:T(8,128)(2,1)S(1)}, bf16[16,48,1920]{2,1,0:T(8,128)(2,1)S(1)}, bf16[16,48,1920]{2,1,0:T(8,128)(2,1)S(1)}) custom-call(s32[34]{0:T(128)S(1)} %stack.140.tab, bf16[1024,3072]{1,0:T(8,128)(2,1)} %get-tuple-element.261.grad_up, ...), custom_call_target="tpu_custom_call", output_to_operand_aliasing={{2}: (7, {}), {3}: (8, {})} | custom-call | flops 7247757312 | bytes 35020800 | tf_op jit(solution)/shard_map/pallas_call | solution.py:592
  180.3 3.8 %collective-permute-start.48 = (bf16[192,384]{1,0:T(8,128)(2,1)S(1)}, bf16[192,384]{1,0:T(8,128)(2,1)S(1)}, u32[]{:S(2)}, u32[]{:S(2)}) collective-permute-start(bf16[192,384]{1,0:T(8,128)(2,1)S(1)} %get-tuple-element.364), channel_id=1, source_target_pairs={{0,4},{1,5},{2,6},{3,7},{4,8},{5,9},{6,10},{7,11},{8,12},{9,13},{1... | collective-permute-start | bytes 442376 | tf_op jit(solution)/shard_map/ppermute | solution.py:135
  184.0 2.4 collective-permute-start.50
  186.5 9.5 %shard_map.144 = (bf16[2,2,256,256]{3,2,1,0:T(8,128)(2,1)}, bf16[2,2,256,256]{3,2,1,0:T(8,128)(2,1)}, bf16[2,2,256,256]{3,2,1,0:T(8,128)(2,1)}) custom-call(s32[34]{0:T(128)S(1)} %stack.140.tab, bf16[2,2,256,2304]{3,2,1,0:T(8,128)(2,1)} %bitcast.247, bf16[2,2,256,2304]{3,2,1,0:T(8,128)(2,1)} %bitcast.248, bf16[2,2,256,2304]{3,2,1,0:T(8,128)(2,1)} %bitcast.249, ...), custom_call_target="tpu_custom_call" | custom-call | flops 4026531840 | bytes 18923520 | tf_op jit(solution)/shard_map/pallas_call | solution.py:592
  197.0 1.4 collective-permute-start.47
  198.4 16.7 %shard_map.145 = (bf16[2,2,256,512]{3,2,1,0:T(8,128)(2,1)}, bf16[2,2,256,512]{3,2,1,0:T(8,128)(2,1)}, bf16[2,2,256,512]{3,2,1,0:T(8,128)(2,1)}) custom-call(s32[34]{0:T(128)S(1)} %stack.140.tab, bf16[2,2,256,2304]{3,2,1,0:T(8,128)(2,1)} %bitcast.250, bf16[2,2,256,2304]{3,2,1,0:T(8,128)(2,1)} %bitcast.251, bf16[2,2,256,2304]{3,2,1,0:T(8,128)(2,1)} %bitcast.252, ...), custom_call_target="tpu_custom_call" | custom-call | flops 8053063680 | bytes 20496384 | tf_op jit(solution)/shard_map/pallas_call | solution.py:592
  216.4 1.5 collective-permute-start.52
  218.0 7.0 %shard_map.146 = (bf16[16,48,1152]{2,1,0:T(8,128)(2,1)S(1)}, bf16[16,48,1152]{2,1,0:T(8,128)(2,1)S(1)}) custom-call(s32[34]{0:T(128)S(1)} %stack.140.tab, bf16[1024,768]{1,0:T(8,128)(2,1)S(1)} %copy-done.9, bf16[1024,256]{1,0:T(8,128)(2,1)} %bitcast.282, bf16[1024,256]{1,0:T(8,128)(2,1)} %bitcast.284, bf16[1024,256]{1,0:T(8,128)(2,1)} %bitcast.286, ...), custom_call_target="tpu_custom_call" | custom-call | flops 3623878656 | bytes 9830400 | tf_op jit(solution)/shard_map/pallas_call | solution.py:592
  225.4 3.7 %collective-permute-done.53 = bf16[16,48,1152]{2,1,0:T(8,128)(2,1)S(1)} collective-permute-done((bf16[16,48,1152]{2,1,0:T(8,128)(2,1)S(1)}, bf16[16,48,1152]{2,1,0:T(8,128)(2,1)S(1)}, u32[]{:S(2)}, u32[]{:S(2)}) %collective-permute-start.53) | collective-permute-done | bytes 1769504 | tf_op jit(solution)/shard_map/ppermute | solution.py:98
  229.4 1.5 collective-permute-start.54
  230.9 1.4 collective-permute-start.55
  232.7 2.2 collective-permute-start.57
  235.0 1.6 collective-permute-start.58
  236.6 9.2 %shard_map.147 = (bf16[512,768]{1,0:T(8,128)(2,1)S(1)}, bf16[512,768]{1,0:T(8,128)(2,1)S(1)}) custom-call(s32[34]{0:T(128)S(1)} %stack.140.tab, bf16[512,768]{1,0:T(8,128)(2,1)S(1)} %get-tuple-element.306.own, bf16[512,768]{1,0:T(8,128)(2,1)S(1)} %constant_dynamic-update-slice_fusion.got, f32[8,768]{1,0:T(8,128)S(1)} %get-tuple-element.215.gains, ...), custom_call_target="tpu_custom_call" | custom-call | flops 3623878656 | bytes 14573568 | tf_op jit(solution)/shard_map/pallas_call | solution.py:592
  245.8 2.9 %collective-permute-done.57 = bf16[48,1920]{1,0:T(8,128)(2,1)S(1)} collective-permute-done((bf16[48,1920]{1,0:T(8,128)(2,1)S(1)}, bf16[48,1920]{1,0:T(8,128)(2,1)S(1)}, u32[]{:S(2)}, u32[]{:S(2)}) %collective-permute-start.57) | collective-permute-done | bytes 184352 | tf_op jit(solution)/shard_map/ppermute | solution.py:135
  248.8 2.1 fusion.10
  252.9 4.4 %collective-permute-done.59 = bf16[2,48,1152]{2,1,0:T(8,128)(2,1)} collective-permute-done((bf16[2,48,1152]{2,1,0:T(8,128)(2,1)}, bf16[2,48,1152]{2,1,0:T(8,128)(2,1)}, u32[]{:S(2)}, u32[]{:S(2)}) %collective-permute-start.59) | collective-permute-done | bytes 221216 | tf_op jit(solution)/shard_map/ppermute | solution.py:120
  258.9 1.5 collective-permute-start.61
  260.4 1.5 fusion.25
  262.0 3.8 %collective-permute-start.64 = (bf16[48,1152]{1,0:T(8,128)(2,1)S(1)}, bf16[48,1152]{1,0:T(8,128)(2,1)S(1)}, u32[]{:S(2)}, u32[]{:S(2)}) collective-permute-start(bf16[48,1152]{1,0:T(8,128)(2,1)S(1)} %get-tuple-element.368), channel_id=1, source_target_pairs={{0,12},{1,13},{2,14},{3,15},{4,0},{5,1},{6,2},{7,3},{8,4},{9,5},{1... | collective-permute-start | bytes 331784 | tf_op jit(solution)/shard_map/ppermute | solution.py:135
  265.8 1.4 collective-permute-start.63
  267.2 1.1 fusion.20
  269.5 1.3 fusion.14
  270.8 1.2 maximum_bitcast_fusion
  275.0 1.2 fusion.29
  279.0 1.2 maximum_bitcast_fusion.1
  (243 shorter events, 30.8 us)
Async XLA Ops:
  3.0 4.6 %collective-permute-start = (bf16[24,1280]{1,0:T(8,128)(2,1)S(1)}, bf16[24,1280]{1,0:T(8,128)(2,1)S(1)}, u32[]{:S(2)}, u32[]{:S(2)}) collective-permute-start(bf16[24,1280]{1,0:T(8,128)(2,1)S(1)} %fusion.32), channel_id=1, source_target_pairs={{0,1},{1,0},{2,3},{3,2},{4,5},{5,4},{6,7},{7,6},{8,9},{9,8},{10,11... | collective-permute-start | bytes 184328 | tf_op jit(solution)/shard_map/ppermute | solution.py:662
  3.6 16.8 %collective-permute-start.4 = (bf16[384,768]{1,0:T(8,128)(2,1)S(1)}, bf16[384,768]{1,0:T(8,128)(2,1)S(1)}, u32[]{:S(2)}, u32[]{:S(2)}) collective-permute-start(bf16[384,768]{1,0:T(8,128)(2,1)S(1)} %slice.453), channel_id=1, source_target_pairs={{0,16},{16,0},{1,17},{17,1},{2,18},{18,2},{3,19},{19,3},{4,20},{20... | collective-permute-start | bytes 1769480 | tf_op jit(solution)/shard_map/ppermute | solution.py:669
  7.7 8.1 %collective-permute-start.1 = (bf16[1,48,1280]{2,1,0:T(8,128)(2,1)S(1)}, bf16[1,48,1280]{2,1,0:T(8,128)(2,1)S(1)}, u32[]{:S(2)}, u32[]{:S(2)}) collective-permute-start(bf16[1,48,1280]{2,1,0:T(8,128)(2,1)S(1)} %bitcast.273), channel_id=1, source_target_pairs={{0,4},{1,5},{2,6},{3,7},{4,8},{5,9},{6,10},{7,11},{8,12},{9,13},{1... | collective-permute-start | bytes 368648 | tf_op jit(solution)/shard_map/ppermute | solution.py:69
  9.3 11.1 %collective-permute-start.2 = (bf16[1,48,1280]{2,1,0:T(8,128)(2,1)S(1)}, bf16[1,48,1280]{2,1,0:T(8,128)(2,1)S(1)}, u32[]{:S(2)}, u32[]{:S(2)}) collective-permute-start(bf16[1,48,1280]{2,1,0:T(8,128)(2,1)S(1)} %bitcast.274), channel_id=1, source_target_pairs={{0,8},{1,9},{2,10},{3,11},{4,12},{5,13},{6,14},{7,15},{8,0},{9,1},... | collective-permute-start | bytes 368648 | tf_op jit(solution)/shard_map/ppermute | solution.py:69
  11.9 8.5 %collective-permute-start.3 = (bf16[1,48,1280]{2,1,0:T(8,128)(2,1)S(1)}, bf16[1,48,1280]{2,1,0:T(8,128)(2,1)S(1)}, u32[]{:S(2)}, u32[]{:S(2)}) collective-permute-start(bf16[1,48,1280]{2,1,0:T(8,128)(2,1)S(1)} %bitcast.275), channel_id=1, source_target_pairs={{0,12},{1,13},{2,14},{3,15},{4,0},{5,1},{6,2},{7,3},{8,4},{9,5},{1... | collective-permute-start | bytes 368648 | tf_op jit(solution)/shard_map/ppermute | solution.py:69
  15.4 20.2 %collective-permute-start.11 = (bf16[96,384]{1,0:T(8,128)(2,1)S(1)}, bf16[96,384]{1,0:T(8,128)(2,1)S(1)}, u32[]{:S(2)}, u32[]{:S(2)}) collective-permute-start(bf16[96,384]{1,0:T(8,128)(2,1)S(1)} %constant_dynamic-slice_fusion), channel_id=1, source_target_pairs={{0,1},{1,0},{2,3},{3,2},{4,5},{5,4},{6,7},{7,6},{8,9},{9,8},{10,11... | collective-permute-start | bytes 221192 | tf_op jit(solution)/shard_map/ppermute | solution.py:662
  20.4 19.4 %collective-permute-start.6 = (bf16[128,768]{1,0:T(8,128)(2,1)}, bf16[128,768]{1,0:T(8,128)(2,1)S(1)}, u32[]{:S(2)}, u32[]{:S(2)}) collective-permute-start(bf16[128,768]{1,0:T(8,128)(2,1)} %slice.454), channel_id=1, source_target_pairs={{0,16},{16,0},{1,17},{17,1},{2,18},{18,2},{3,19},{19,3},{4,20},{20... | collective-permute-start | bytes 589832 | tf_op jit(solution)/shard_map/ppermute | solution.py:703
  21.9 10.7 %collective-permute-start.7 = (bf16[2,48,1280]{2,1,0:T(8,128)(2,1)S(1)}, bf16[2,48,1280]{2,1,0:T(8,128)(2,1)S(1)}, u32[]{:S(2)}, u32[]{:S(2)}) collective-permute-start(bf16[2,48,1280]{2,1,0:T(8,128)(2,1)S(1)} %pad_maximum_fusion.4), channel_id=1, source_target_pairs={{0,16},{1,17},{2,18},{3,19},{4,20},{5,21},{6,22},{7,23},{8,24},{9,... | collective-permute-start | bytes 737288 | tf_op jit(solution)/shard_map/ppermute | solution.py:69
  22.6 10.0 %collective-permute-start.8 = (bf16[2,48,1280]{2,1,0:T(8,128)(2,1)S(1)}, bf16[2,48,1280]{2,1,0:T(8,128)(2,1)S(1)}, u32[]{:S(2)}, u32[]{:S(2)}) collective-permute-start(bf16[2,48,1280]{2,1,0:T(8,128)(2,1)S(1)} %pad_maximum_fusion.5), channel_id=1, source_target_pairs={{0,2},{1,3},{2,0},{3,1},{4,6},{5,7},{6,4},{7,5},{8,10},{9,11},{10,... | collective-permute-start | bytes 737288 | tf_op jit(solution)/shard_map/ppermute | solution.py:69
  32.6 12.3 %collective-permute-start.9 = (bf16[4,48,1280]{2,1,0:T(8,128)(2,1)S(1)}, bf16[4,48,1280]{2,1,0:T(8,128)(2,1)S(1)}, u32[]{:S(2)}, u32[]{:S(2)}) collective-permute-start(bf16[4,48,1280]{2,1,0:T(8,128)(2,1)S(1)} %constant_dynamic-update-slice_fusion.2.refs_0_), channel_id=1, source_target_pairs={{0,2},{1,3},{2,0},{3,1},{4,6},{5,7},{6,4},{7,5},{8,10},{9,11},{10,... | collective-permute-start | bytes 1474568 | tf_op jit(solution)/shard_map/ppermute | solution.py:69
  34.2 12.0 %collective-permute-start.10 = (bf16[4,48,1280]{2,1,0:T(8,128)(2,1)S(1)}, bf16[4,48,1280]{2,1,0:T(8,128)(2,1)S(1)}, u32[]{:S(2)}, u32[]{:S(2)}) collective-permute-start(bf16[4,48,1280]{2,1,0:T(8,128)(2,1)S(1)} %constant_dynamic-update-slice_fusion.5.refs_1_), channel_id=1, source_target_pairs={{0,16},{1,17},{2,18},{3,19},{4,20},{5,21},{6,22},{7,23},{8,24},{9,... | collective-permute-start | bytes 1474568 | tf_op jit(solution)/shard_map/ppermute | solution.py:69
  35.6 11.1 %collective-permute-start.16 = (bf16[1,48,1920]{2,1,0:T(8,128)(2,1)S(1)}, bf16[1,48,1920]{2,1,0:T(8,128)(2,1)S(1)}, u32[]{:S(2)}, u32[]{:S(2)}) collective-permute-start(bf16[1,48,1920]{2,1,0:T(8,128)(2,1)S(1)} %bitcast.268), channel_id=1, source_target_pairs={{0,4},{1,5},{2,6},{3,7},{4,8},{5,9},{6,10},{7,11},{8,12},{9,13},{1... | collective-permute-start | bytes 552968 | tf_op jit(solution)/shard_map/ppermute | solution.py:69
  38.2 12.1 %collective-permute-start.17 = (bf16[1,48,1920]{2,1,0:T(8,128)(2,1)S(1)}, bf16[1,48,1920]{2,1,0:T(8,128)(2,1)S(1)}, u32[]{:S(2)}, u32[]{:S(2)}) collective-permute-start(bf16[1,48,1920]{2,1,0:T(8,128)(2,1)S(1)} %bitcast.269), channel_id=1, source_target_pairs={{0,8},{1,9},{2,10},{3,11},{4,12},{5,13},{6,14},{7,15},{8,0},{9,1},... | collective-permute-start | bytes 552968 | tf_op jit(solution)/shard_map/ppermute | solution.py:69
  39.8 10.5 %collective-permute-start.18 = (bf16[1,48,1920]{2,1,0:T(8,128)(2,1)S(1)}, bf16[1,48,1920]{2,1,0:T(8,128)(2,1)S(1)}, u32[]{:S(2)}, u32[]{:S(2)}) collective-permute-start(bf16[1,48,1920]{2,1,0:T(8,128)(2,1)S(1)} %bitcast.270), channel_id=1, source_target_pairs={{0,12},{1,13},{2,14},{3,15},{4,0},{5,1},{6,2},{7,3},{8,4},{9,5},{1... | collective-permute-start | bytes 552968 | tf_op jit(solution)/shard_map/ppermute | solution.py:69
  46.2 5.3 %collective-permute-start.12 = (bf16[4,48,1280]{2,1,0:T(8,128)(2,1)S(1)}, bf16[4,48,1280]{2,1,0:T(8,128)(2,1)S(1)}, u32[]{:S(2)}, u32[]{:S(2)}) collective-permute-start(bf16[4,48,1280]{2,1,0:T(8,128)(2,1)S(1)} %constant_dynamic-update-slice_fusion.2.refs_0_), channel_id=1, source_target_pairs={{0,1},{1,0},{2,3},{3,2},{4,5},{5,4},{6,7},{7,6},{8,9},{9,8},{10,11... | collective-permute-start | bytes 1474568 | tf_op jit(solution)/shard_map/ppermute | solution.py:698
  46.2 5.9 %collective-permute-start.13 = (bf16[4,48,1280]{2,1,0:T(8,128)(2,1)S(1)}, bf16[4,48,1280]{2,1,0:T(8,128)(2,1)S(1)}, u32[]{:S(2)}, u32[]{:S(2)}) collective-permute-start(bf16[4,48,1280]{2,1,0:T(8,128)(2,1)S(1)} %constant_dynamic-update-slice_fusion.5.refs_1_), channel_id=1, source_target_pairs={{0,1},{1,0},{2,3},{3,2},{4,5},{5,4},{6,7},{7,6},{8,9},{9,8},{10,11... | collective-permute-start | bytes 1474568 | tf_op jit(solution)/shard_map/ppermute | solution.py:698
  46.7 9.9 %collective-permute-start.14 = (bf16[4,48,1280]{2,1,0:T(8,128)(2,1)S(1)}, bf16[4,48,1280]{2,1,0:T(8,128)(2,1)S(1)}, u32[]{:S(2)}, u32[]{:S(2)}) collective-permute-start(bf16[4,48,1280]{2,1,0:T(8,128)(2,1)S(1)} %collective-permute-done.9.refs_2_), channel_id=1, source_target_pairs={{0,1},{1,0},{2,3},{3,2},{4,5},{5,4},{6,7},{7,6},{8,9},{9,8},{10,11... | collective-permute-start | bytes 1474568 | tf_op jit(solution)/shard_map/ppermute | solution.py:698
  50.3 8.4 %collective-permute-start.15 = (bf16[4,48,1280]{2,1,0:T(8,128)(2,1)S(1)}, bf16[4,48,1280]{2,1,0:T(8,128)(2,1)S(1)}, u32[]{:S(2)}, u32[]{:S(2)}) collective-permute-start(bf16[4,48,1280]{2,1,0:T(8,128)(2,1)S(1)} %collective-permute-done.10.refs_3_), channel_id=1, source_target_pairs={{0,1},{1,0},{2,3},{3,2},{4,5},{5,4},{6,7},{7,6},{8,9},{9,8},{10,11... | collective-permute-start | bytes 1474568 | tf_op jit(solution)/shard_map/ppermute | solution.py:698
  50.4 18.1 %collective-permute-start.19 = (bf16[2,48,1920]{2,1,0:T(8,128)(2,1)S(1)}, bf16[2,48,1920]{2,1,0:T(8,128)(2,1)S(1)}, u32[]{:S(2)}, u32[]{:S(2)}) collective-permute-start(bf16[2,48,1920]{2,1,0:T(8,128)(2,1)S(1)} %pad_maximum_fusion), channel_id=1, source_target_pairs={{0,16},{1,17},{2,18},{3,19},{4,20},{5,21},{6,22},{7,23},{8,24},{9,... | collective-permute-start | bytes 1105928 | tf_op jit(solution)/shard_map/ppermute | solution.py:69
  51.5 17.0 %collective-permute-start.20 = (bf16[2,48,1920]{2,1,0:T(8,128)(2,1)S(1)}, bf16[2,48,1920]{2,1,0:T(8,128)(2,1)S(1)}, u32[]{:S(2)}, u32[]{:S(2)}) collective-permute-start(bf16[2,48,1920]{2,1,0:T(8,128)(2,1)S(1)} %pad_maximum_fusion.1), channel_id=1, source_target_pairs={{0,2},{1,3},{2,0},{3,1},{4,6},{5,7},{6,4},{7,5},{8,10},{9,11},{10,... | collective-permute-start | bytes 1105928 | tf_op jit(solution)/shard_map/ppermute | solution.py:69
  52.1 15.8 %collective-permute-start.21 = (bf16[1,192,384]{2,1,0:T(8,128)(2,1)S(1)}, bf16[1,192,384]{2,1,0:T(8,128)(2,1)S(1)}, u32[]{:S(2)}, u32[]{:S(2)}) collective-permute-start(bf16[1,192,384]{2,1,0:T(8,128)(2,1)S(1)} %bitcast.278), channel_id=1, source_target_pairs={{0,4},{1,5},{2,6},{3,7},{4,8},{5,9},{6,10},{7,11},{8,12},{9,13},{1... | collective-permute-start | bytes 442376 | tf_op jit(solution)/shard_map/ppermute | solution.py:69
  56.6 11.9 %collective-permute-start.22 = (bf16[1,192,384]{2,1,0:T(8,128)(2,1)S(1)}, bf16[1,192,384]{2,1,0:T(8,128)(2,1)S(1)}, u32[]{:S(2)}, u32[]{:S(2)}) collective-permute-start(bf16[1,192,384]{2,1,0:T(8,128)(2,1)S(1)} %bitcast.279), channel_id=1, source_target_pairs={{0,8},{1,9},{2,10},{3,11},{4,12},{5,13},{6,14},{7,15},{8,0},{9,1},... | collective-permute-start | bytes 442376 | tf_op jit(solution)/shard_map/ppermute | solution.py:69
  58.7 9.8 %collective-permute-start.23 = (bf16[1,192,384]{2,1,0:T(8,128)(2,1)S(1)}, bf16[1,192,384]{2,1,0:T(8,128)(2,1)S(1)}, u32[]{:S(2)}, u32[]{:S(2)}) collective-permute-start(bf16[1,192,384]{2,1,0:T(8,128)(2,1)S(1)} %bitcast.280), channel_id=1, source_target_pairs={{0,12},{1,13},{2,14},{3,15},{4,0},{5,1},{6,2},{7,3},{8,4},{9,5},{1... | collective-permute-start | bytes 442376 | tf_op jit(solution)/shard_map/ppermute | solution.py:69
  68.6 18.4 %collective-permute-start.24 = (bf16[4,48,1920]{2,1,0:T(8,128)(2,1)S(1)}, bf16[4,48,1920]{2,1,0:T(8,128)(2,1)S(1)}, u32[]{:S(2)}, u32[]{:S(2)}) collective-permute-start(bf16[4,48,1920]{2,1,0:T(8,128)(2,1)S(1)} %constant_dynamic-update-slice_fusion.8.refs_0_), channel_id=1, source_target_pairs={{0,2},{1,3},{2,0},{3,1},{4,6},{5,7},{6,4},{7,5},{8,10},{9,11},{10,... | collective-permute-start | bytes 2211848 | tf_op jit(solution)/shard_map/ppermute | solution.py:69
  70.2 18.1 %collective-permute-start.25 = (bf16[4,48,1920]{2,1,0:T(8,128)(2,1)S(1)}, bf16[4,48,1920]{2,1,0:T(8,128)(2,1)S(1)}, u32[]{:S(2)}, u32[]{:S(2)}) collective-permute-start(bf16[4,48,1920]{2,1,0:T(8,128)(2,1)S(1)} %constant_dynamic-update-slice_fusion.11.refs_1_), channel_id=1, source_target_pairs={{0,16},{1,17},{2,18},{3,19},{4,20},{5,21},{6,22},{7,23},{8,24},{9,... | collective-permute-start | bytes 2211848 | tf_op jit(solution)/shard_map/ppermute | solution.py:69
  70.9 17.4 %collective-permute-start.26 = (bf16[4,48,1920]{2,1,0:T(8,128)(2,1)S(1)}, bf16[4,48,1920]{2,1,0:T(8,128)(2,1)S(1)}, u32[]{:S(2)}, u32[]{:S(2)}) collective-permute-start(bf16[4,48,1920]{2,1,0:T(8,128)(2,1)S(1)} %constant_dynamic-update-slice_fusion.8.refs_0_), channel_id=1, source_target_pairs={{0,1},{1,0},{2,3},{3,2},{4,5},{5,4},{6,7},{7,6},{8,9},{9,8},{10,11... | collective-permute-start | bytes 2211848 | tf_op jit(solution)/shard_map/ppermute | solution.py:690
  70.9 17.4 %collective-permute-start.27 = (bf16[4,48,1920]{2,1,0:T(8,128)(2,1)S(1)}, bf16[4,48,1920]{2,1,0:T(8,128)(2,1)S(1)}, u32[]{:S(2)}, u32[]{:S(2)}) collective-permute-start(bf16[4,48,1920]{2,1,0:T(8,128)(2,1)S(1)} %constant_dynamic-update-slice_fusion.11.refs_1_), channel_id=1, source_target_pairs={{0,1},{1,0},{2,3},{3,2},{4,5},{5,4},{6,7},{7,6},{8,9},{9,8},{10,11... | collective-permute-start | bytes 2211848 | tf_op jit(solution)/shard_map/ppermute | solution.py:690
  88.3 3.3 %collective-permute-start.29 = (bf16[4,48,1920]{2,1,0:T(8,128)(2,1)S(1)}, bf16[4,48,1920]{2,1,0:T(8,128)(2,1)S(1)}, u32[]{:S(2)}, u32[]{:S(2)}) collective-permute-start(bf16[4,48,1920]{2,1,0:T(8,128)(2,1)S(1)} %collective-permute-done.25.refs_3_), channel_id=1, source_target_pairs={{0,1},{1,0},{2,3},{3,2},{4,5},{5,4},{6,7},{7,6},{8,9},{9,8},{10,11... | collective-permute-start | bytes 2211848 | tf_op jit(solution)/shard_map/ppermute | solution.py:690
  89.0 15.4 %collective-permute-start.30 = (bf16[4,192,384]{2,1,0:T(8,128)(2,1)S(1)}, bf16[4,192,384]{2,1,0:T(8,128)(2,1)S(1)}, u32[]{:S(2)}, u32[]{:S(2)}) collective-permute-start(bf16[4,192,384]{2,1,0:T(8,128)(2,1)S(1)} %constant_dynamic-update-slice_fusion.14.refs_0_), channel_id=1, source_target_pairs={{0,16},{1,17},{2,18},{3,19},{4,20},{5,21},{6,22},{7,23},{8,24},{9,... | collective-permute-start | bytes 1769480 | tf_op jit(solution)/shard_map/ppermute | solution.py:69
  89.6 15.0 %collective-permute-start.31 = (bf16[4,192,384]{2,1,0:T(8,128)(2,1)S(1)}, bf16[4,192,384]{2,1,0:T(8,128)(2,1)S(1)}, u32[]{:S(2)}, u32[]{:S(2)}) collective-permute-start(bf16[4,192,384]{2,1,0:T(8,128)(2,1)S(1)} %constant_dynamic-update-slice_fusion.14.refs_0_), channel_id=1, source_target_pairs={{0,2},{1,3},{2,0},{3,1},{4,6},{5,7},{6,4},{7,5},{8,10},{9,11},{10,... | collective-permute-start | bytes 1769480 | tf_op jit(solution)/shard_map/ppermute | solution.py:69
  104.6 18.4 %collective-permute-start.33 = (bf16[512,768]{1,0:T(8,128)(2,1)S(1)}, bf16[512,768]{1,0:T(8,128)(2,1)S(1)}, u32[]{:S(2)}, u32[]{:S(2)}) collective-permute-start(bf16[512,768]{1,0:T(8,128)(2,1)S(1)} %get-tuple-element.235), channel_id=1, source_target_pairs={{0,16},{16,0},{1,17},{17,1},{2,18},{18,2},{3,19},{19,3},{4,20},{20... | collective-permute-start | bytes 2359304 | tf_op jit(solution)/shard_map/ppermute | solution.py:834
  106.1 13.9 %collective-permute-start.32 = (bf16[4,192,384]{2,1,0:T(8,128)(2,1)S(1)}, bf16[4,192,384]{2,1,0:T(8,128)(2,1)S(1)}, u32[]{:S(2)}, u32[]{:S(2)}) collective-permute-start(bf16[4,192,384]{2,1,0:T(8,128)(2,1)S(1)} %collective-permute-done.30.refs_1_), channel_id=1, source_target_pairs={{0,2},{1,3},{2,0},{3,1},{4,6},{5,7},{6,4},{7,5},{8,10},{9,11},{10,... | collective-permute-start | bytes 1769480 | tf_op jit(solution)/shard_map/ppermute | solution.py:69
  123.0 9.4 %collective-permute-start.34 = (bf16[4,192,384]{2,1,0:T(8,128)(2,1)S(1)}, bf16[4,192,384]{2,1,0:T(8,128)(2,1)S(1)}, u32[]{:S(2)}, u32[]{:S(2)}) collective-permute-start(bf16[4,192,384]{2,1,0:T(8,128)(2,1)S(1)} %constant_dynamic-update-slice_fusion.14.refs_0_), channel_id=1, source_target_pairs={{0,1},{1,0},{2,3},{3,2},{4,5},{5,4},{6,7},{7,6},{8,9},{9,8},{10,11... | collective-permute-start | bytes 1769480 | tf_op jit(solution)/shard_map/ppermute | solution.py:690
  123.0 9.4 %collective-permute-start.35 = (bf16[4,192,384]{2,1,0:T(8,128)(2,1)S(1)}, bf16[4,192,384]{2,1,0:T(8,128)(2,1)S(1)}, u32[]{:S(2)}, u32[]{:S(2)}) collective-permute-start(bf16[4,192,384]{2,1,0:T(8,128)(2,1)S(1)} %collective-permute-done.30.refs_1_), channel_id=1, source_target_pairs={{0,1},{1,0},{2,3},{3,2},{4,5},{5,4},{6,7},{7,6},{8,9},{9,8},{10,11... | collective-permute-start | bytes 1769480 | tf_op jit(solution)/shard_map/ppermute | solution.py:690
  123.5 8.9 %collective-permute-start.36 = (bf16[4,192,384]{2,1,0:T(8,128)(2,1)S(1)}, bf16[4,192,384]{2,1,0:T(8,128)(2,1)S(1)}, u32[]{:S(2)}, u32[]{:S(2)}) collective-permute-start(bf16[4,192,384]{2,1,0:T(8,128)(2,1)S(1)} %collective-permute-done.31.refs_2_), channel_id=1, source_target_pairs={{0,1},{1,0},{2,3},{3,2},{4,5},{5,4},{6,7},{7,6},{8,9},{9,8},{10,11... | collective-permute-start | bytes 1769480 | tf_op jit(solution)/shard_map/ppermute | solution.py:690
  123.5 8.9 %collective-permute-start.37 = (bf16[4,192,384]{2,1,0:T(8,128)(2,1)S(1)}, bf16[4,192,384]{2,1,0:T(8,128)(2,1)S(1)}, u32[]{:S(2)}, u32[]{:S(2)}) collective-permute-start(bf16[4,192,384]{2,1,0:T(8,128)(2,1)S(1)} %collective-permute-done.32.refs_3_), channel_id=1, source_target_pairs={{0,1},{1,0},{2,3},{3,2},{4,5},{5,4},{6,7},{7,6},{8,9},{9,8},{10,11... | collective-permute-start | bytes 1769480 | tf_op jit(solution)/shard_map/ppermute | solution.py:690
  132.4 9.5 %collective-permute-start.38 = (bf16[16,192,384]{2,1,0:T(8,128)(2,1)S(1)}, bf16[16,192,384]{2,1,0:T(8,128)(2,1)S(1)}, u32[]{:S(2)}, u32[]{:S(2)}) collective-permute-start(bf16[16,192,384]{2,1,0:T(8,128)(2,1)S(1)} %get-tuple-element.251), channel_id=1, source_target_pairs={{0,1},{1,0},{2,3},{3,2},{4,5},{5,4},{6,7},{7,6},{8,9},{9,8},{10,11... | collective-permute-start | bytes 7077896 | tf_op jit(solution)/shard_map/ppermute | solution.py:98
  142.3 17.6 %collective-permute-start.39 = (bf16[2,2,192,384]{3,2,1,0:T(8,128)(2,1)S(1)}, bf16[2,2,192,384]{3,2,1,0:T(8,128)(2,1)S(1)}, u32[]{:S(2)}, u32[]{:S(2)}) collective-permute-start(bf16[2,2,192,384]{3,2,1,0:T(8,128)(2,1)S(1)} %fusion.4), channel_id=1, source_target_pairs={{0,2},{1,3},{2,0},{3,1},{4,6},{5,7},{6,4},{7,5},{8,10},{9,11},{10,... | collective-permute-start | bytes 1769480 | tf_op jit(solution)/shard_map/ppermute | solution.py:120
  142.8 17.1 %collective-permute-start.40 = (bf16[2,2,192,384]{3,2,1,0:T(8,128)(2,1)S(1)}, bf16[2,2,192,384]{3,2,1,0:T(8,128)(2,1)S(1)}, u32[]{:S(2)}, u32[]{:S(2)}) collective-permute-start(bf16[2,2,192,384]{3,2,1,0:T(8,128)(2,1)S(1)} %fusion.5), channel_id=1, source_target_pairs={{0,16},{1,17},{2,18},{3,19},{4,20},{5,21},{6,22},{7,23},{8,24},{9,... | collective-permute-start | bytes 1769480 | tf_op jit(solution)/shard_map/ppermute | solution.py:120
  144.3 34.9 %collective-permute-start.43 = (bf16[256,768]{1,0:T(8,128)(2,1)S(1)}, bf16[256,768]{1,0:T(8,128)(2,1)S(1)}, u32[]{:S(2)}, u32[]{:S(2)}) collective-permute-start(bf16[256,768]{1,0:T(8,128)(2,1)S(1)} %get-tuple-element.377), channel_id=1, source_target_pairs={{0,16},{16,0},{1,17},{17,1},{2,18},{18,2},{3,19},{19,3},{4,20},{20... | collective-permute-start | bytes 1179656 | tf_op jit(solution)/shard_map/ppermute | solution.py:929
  160.1 19.1 %collective-permute-start.41 = (bf16[2,192,384]{2,1,0:T(8,128)(2,1)S(1)}, bf16[2,192,384]{2,1,0:T(8,128)(2,1)S(1)}, u32[]{:S(2)}, u32[]{:S(2)}) collective-permute-start(bf16[2,192,384]{2,1,0:T(8,128)(2,1)S(1)} %get-tuple-element.366), channel_id=1, source_target_pairs={{0,16},{1,17},{2,18},{3,19},{4,20},{5,21},{6,22},{7,23},{8,24},{9,... | collective-permute-start | bytes 884744 | tf_op jit(solution)/shard_map/ppermute | solution.py:120
  161.6 17.6 %collective-permute-start.42 = (bf16[2,192,384]{2,1,0:T(8,128)(2,1)S(1)}, bf16[2,192,384]{2,1,0:T(8,128)(2,1)S(1)}, u32[]{:S(2)}, u32[]{:S(2)}) collective-permute-start(bf16[2,192,384]{2,1,0:T(8,128)(2,1)S(1)} %get-tuple-element.365), channel_id=1, source_target_pairs={{0,2},{1,3},{2,0},{3,1},{4,6},{5,7},{6,4},{7,5},{8,10},{9,11},{10,... | collective-permute-start | bytes 884744 | tf_op jit(solution)/shard_map/ppermute | solution.py:120
  179.3 16.7 %collective-permute-start.44 = (bf16[16,48,1920]{2,1,0:T(8,128)(2,1)S(1)}, bf16[16,48,1920]{2,1,0:T(8,128)(2,1)S(1)}, u32[]{:S(2)}, u32[]{:S(2)}) collective-permute-start(bf16[16,48,1920]{2,1,0:T(8,128)(2,1)S(1)} %get-tuple-element.277), channel_id=1, source_target_pairs={{0,1},{1,0},{2,3},{3,2},{4,5},{5,4},{6,7},{7,6},{8,9},{9,8},{10,11... | collective-permute-start | bytes 8847368 | tf_op jit(solution)/shard_map/ppermute | solution.py:98
  179.3 16.6 %collective-permute-start.45 = (bf16[256,768]{1,0:T(8,128)(2,1)S(1)}, bf16[256,768]{1,0:T(8,128)(2,1)S(1)}, u32[]{:S(2)}, u32[]{:S(2)}) collective-permute-start(bf16[256,768]{1,0:T(8,128)(2,1)S(1)} %get-tuple-element.278), channel_id=1, source_target_pairs={{0,16},{16,0},{1,17},{17,1},{2,18},{18,2},{3,19},{19,3},{4,20},{20... | collective-permute-start | bytes 1179656 | tf_op jit(solution)/shard_map/ppermute | solution.py:948
  180.3 34.8 %collective-permute-start.48 = (bf16[192,384]{1,0:T(8,128)(2,1)S(1)}, bf16[192,384]{1,0:T(8,128)(2,1)S(1)}, u32[]{:S(2)}, u32[]{:S(2)}) collective-permute-start(bf16[192,384]{1,0:T(8,128)(2,1)S(1)} %get-tuple-element.364), channel_id=1, source_target_pairs={{0,4},{1,5},{2,6},{3,7},{4,8},{5,9},{6,10},{7,11},{8,12},{9,13},{1... | collective-permute-start | bytes 442376 | tf_op jit(solution)/shard_map/ppermute | solution.py:135
  184.0 31.1 %collective-permute-start.49 = (bf16[192,384]{1,0:T(8,128)(2,1)S(1)}, bf16[192,384]{1,0:T(8,128)(2,1)S(1)}, u32[]{:S(2)}, u32[]{:S(2)}) collective-permute-start(bf16[192,384]{1,0:T(8,128)(2,1)S(1)} %get-tuple-element.363), channel_id=1, source_target_pairs={{0,8},{1,9},{2,10},{3,11},{4,12},{5,13},{6,14},{7,15},{8,0},{9,1},... | collective-permute-start | bytes 442376 | tf_op jit(solution)/shard_map/ppermute | solution.py:135
  184.0 31.1 %collective-permute-start.50 = (bf16[192,384]{1,0:T(8,128)(2,1)S(1)}, bf16[192,384]{1,0:T(8,128)(2,1)S(1)}, u32[]{:S(2)}, u32[]{:S(2)}) collective-permute-start(bf16[192,384]{1,0:T(8,128)(2,1)S(1)} %get-tuple-element.362), channel_id=1, source_target_pairs={{0,12},{1,13},{2,14},{3,15},{4,0},{5,1},{6,2},{7,3},{8,4},{9,5},{1... | collective-permute-start | bytes 442376 | tf_op jit(solution)/shard_map/ppermute | solution.py:135
  196.4 18.8 %collective-permute-start.46 = (bf16[2,2,48,1920]{3,2,1,0:T(8,128)(2,1)S(1)}, bf16[2,2,48,1920]{3,2,1,0:T(8,128)(2,1)S(1)}, u32[]{:S(2)}, u32[]{:S(2)}) collective-permute-start(bf16[2,2,48,1920]{3,2,1,0:T(8,128)(2,1)S(1)} %fusion), channel_id=1, source_target_pairs={{0,2},{1,3},{2,0},{3,1},{4,6},{5,7},{6,4},{7,5},{8,10},{9,11},{10,... | collective-permute-start | bytes 2211848 | tf_op jit(solution)/shard_map/ppermute | solution.py:120
  197.0 18.2 %collective-permute-start.47 = (bf16[2,2,48,1920]{3,2,1,0:T(8,128)(2,1)S(1)}, bf16[2,2,48,1920]{3,2,1,0:T(8,128)(2,1)S(1)}, u32[]{:S(2)}, u32[]{:S(2)}) collective-permute-start(bf16[2,2,48,1920]{3,2,1,0:T(8,128)(2,1)S(1)} %fusion.1), channel_id=1, source_target_pairs={{0,16},{1,17},{2,18},{3,19},{4,20},{5,21},{6,22},{7,23},{8,24},{9,... | collective-permute-start | bytes 2211848 | tf_op jit(solution)/shard_map/ppermute | solution.py:120
  215.5 9.6 %collective-permute-start.51 = (bf16[2,48,1920]{2,1,0:T(8,128)(2,1)S(1)}, bf16[2,48,1920]{2,1,0:T(8,128)(2,1)S(1)}, u32[]{:S(2)}, u32[]{:S(2)}) collective-permute-start(bf16[2,48,1920]{2,1,0:T(8,128)(2,1)S(1)} %get-tuple-element.301), channel_id=1, source_target_pairs={{0,16},{1,17},{2,18},{3,19},{4,20},{5,21},{6,22},{7,23},{8,24},{9,... | collective-permute-start | bytes 1105928 | tf_op jit(solution)/shard_map/ppermute | solution.py:120
  216.4 9.0 %collective-permute-start.52 = (bf16[2,48,1920]{2,1,0:T(8,128)(2,1)S(1)}, bf16[2,48,1920]{2,1,0:T(8,128)(2,1)S(1)}, u32[]{:S(2)}, u32[]{:S(2)}) collective-permute-start(bf16[2,48,1920]{2,1,0:T(8,128)(2,1)S(1)} %get-tuple-element.302), channel_id=1, source_target_pairs={{0,2},{1,3},{2,0},{3,1},{4,6},{5,7},{6,4},{7,5},{8,10},{9,11},{10,... | collective-permute-start | bytes 1105928 | tf_op jit(solution)/shard_map/ppermute | solution.py:120
  225.4 3.7 %collective-permute-start.53 = (bf16[16,48,1152]{2,1,0:T(8,128)(2,1)S(1)}, bf16[16,48,1152]{2,1,0:T(8,128)(2,1)S(1)}, u32[]{:S(2)}, u32[]{:S(2)}) collective-permute-start(bf16[16,48,1152]{2,1,0:T(8,128)(2,1)S(1)} %get-tuple-element.304), channel_id=1, source_target_pairs={{0,1},{1,0},{2,3},{3,2},{4,5},{5,4},{6,7},{7,6},{8,9},{9,8},{10,11... | collective-permute-start | bytes 5308424 | tf_op jit(solution)/shard_map/ppermute | solution.py:98
  229.4 19.4 %collective-permute-start.54 = (bf16[2,2,48,1152]{3,2,1,0:T(8,128)(2,1)S(1)}, bf16[2,2,48,1152]{3,2,1,0:T(8,128)(2,1)}, u32[]{:S(2)}, u32[]{:S(2)}) collective-permute-start(bf16[2,2,48,1152]{3,2,1,0:T(8,128)(2,1)S(1)} %fusion.8), channel_id=1, source_target_pairs={{0,2},{1,3},{2,0},{3,1},{4,6},{5,7},{6,4},{7,5},{8,10},{9,11},{10,... | collective-permute-start | bytes 1327112 | tf_op jit(solution)/shard_map/ppermute | solution.py:120
  230.9 17.8 %collective-permute-start.55 = (bf16[2,2,48,1152]{3,2,1,0:T(8,128)(2,1)S(1)}, bf16[2,2,48,1152]{3,2,1,0:T(8,128)(2,1)S(1)}, u32[]{:S(2)}, u32[]{:S(2)}) collective-permute-start(bf16[2,2,48,1152]{3,2,1,0:T(8,128)(2,1)S(1)} %fusion.9), channel_id=1, source_target_pairs={{0,16},{1,17},{2,18},{3,19},{4,20},{5,21},{6,22},{7,23},{8,24},{9,... | collective-permute-start | bytes 1327112 | tf_op jit(solution)/shard_map/ppermute | solution.py:120
  232.7 13.2 %collective-permute-start.56 = (bf16[48,1920]{1,0:T(8,128)(2,1)S(1)}, bf16[48,1920]{1,0:T(8,128)(2,1)S(1)}, u32[]{:S(2)}, u32[]{:S(2)}) collective-permute-start(bf16[48,1920]{1,0:T(8,128)(2,1)S(1)} %get-tuple-element.322), channel_id=1, source_target_pairs={{0,4},{1,5},{2,6},{3,7},{4,8},{5,9},{6,10},{7,11},{8,12},{9,13},{1... | collective-permute-start | bytes 552968 | tf_op jit(solution)/shard_map/ppermute | solution.py:135
  232.7 16.0 %collective-permute-start.57 = (bf16[48,1920]{1,0:T(8,128)(2,1)S(1)}, bf16[48,1920]{1,0:T(8,128)(2,1)S(1)}, u32[]{:S(2)}, u32[]{:S(2)}) collective-permute-start(bf16[48,1920]{1,0:T(8,128)(2,1)S(1)} %get-tuple-element.323), channel_id=1, source_target_pairs={{0,8},{1,9},{2,10},{3,11},{4,12},{5,13},{6,14},{7,15},{8,0},{9,1},... | collective-permute-start | bytes 552968 | tf_op jit(solution)/shard_map/ppermute | solution.py:135
  235.0 13.8 %collective-permute-start.58 = (bf16[48,1920]{1,0:T(8,128)(2,1)S(1)}, bf16[48,1920]{1,0:T(8,128)(2,1)S(1)}, u32[]{:S(2)}, u32[]{:S(2)}) collective-permute-start(bf16[48,1920]{1,0:T(8,128)(2,1)S(1)} %get-tuple-element.324), channel_id=1, source_target_pairs={{0,12},{1,13},{2,14},{3,15},{4,0},{5,1},{6,2},{7,3},{8,4},{9,5},{1... | collective-permute-start | bytes 552968 | tf_op jit(solution)/shard_map/ppermute | solution.py:135
  250.9 6.3 %collective-permute-start.59 = (bf16[2,48,1152]{2,1,0:T(8,128)(2,1)}, bf16[2,48,1152]{2,1,0:T(8,128)(2,1)}, u32[]{:S(2)}, u32[]{:S(2)}) collective-permute-start(bf16[2,48,1152]{2,1,0:T(8,128)(2,1)} %get-tuple-element.371), channel_id=1, source_target_pairs={{0,16},{1,17},{2,18},{3,19},{4,20},{5,21},{6,22},{7,23},{8,24},{9,... | collective-permute-start | bytes 663560 | tf_op jit(solution)/shard_map/ppermute | solution.py:120
  251.6 6.3 %collective-permute-start.60 = (bf16[2,48,1152]{2,1,0:T(8,128)(2,1)}, bf16[2,48,1152]{2,1,0:T(8,128)(2,1)}, u32[]{:S(2)}, u32[]{:S(2)}) collective-permute-start(bf16[2,48,1152]{2,1,0:T(8,128)(2,1)} %get-tuple-element.370), channel_id=1, source_target_pairs={{0,2},{1,3},{2,0},{3,1},{4,6},{5,7},{6,4},{7,5},{8,10},{9,11},{10,... | collective-permute-start | bytes 663560 | tf_op jit(solution)/shard_map/ppermute | solution.py:120
  258.9 20.0 %collective-permute-start.61 = (bf16[512,768]{1,0:T(8,128)(2,1)}, bf16[512,768]{1,0:T(8,128)(2,1)S(1)}, u32[]{:S(2)}, u32[]{:S(2)}) collective-permute-start(bf16[512,768]{1,0:T(8,128)(2,1)} %copy-done.7), channel_id=1, source_target_pairs={{0,16},{16,0},{1,17},{17,1},{2,18},{18,2},{3,19},{19,3},{4,20},{20... | collective-permute-start | bytes 2359304 | tf_op jit(solution)/shard_map/ppermute | solution.py:1022
  262.0 12.4 %collective-permute-start.64 = (bf16[48,1152]{1,0:T(8,128)(2,1)S(1)}, bf16[48,1152]{1,0:T(8,128)(2,1)S(1)}, u32[]{:S(2)}, u32[]{:S(2)}) collective-permute-start(bf16[48,1152]{1,0:T(8,128)(2,1)S(1)} %get-tuple-element.368), channel_id=1, source_target_pairs={{0,12},{1,13},{2,14},{3,15},{4,0},{5,1},{6,2},{7,3},{8,4},{9,5},{1... | collective-permute-start | bytes 331784 | tf_op jit(solution)/shard_map/ppermute | solution.py:135
  265.8 9.2 %collective-permute-start.63 = (bf16[48,1152]{1,0:T(8,128)(2,1)S(1)}, bf16[48,1152]{1,0:T(8,128)(2,1)S(1)}, u32[]{:S(2)}, u32[]{:S(2)}) collective-permute-start(bf16[48,1152]{1,0:T(8,128)(2,1)S(1)} %get-tuple-element.367), channel_id=1, source_target_pairs={{0,8},{1,9},{2,10},{3,11},{4,12},{5,13},{6,14},{7,15},{8,0},{9,1},... | collective-permute-start | bytes 331784 | tf_op jit(solution)/shard_map/ppermute | solution.py:135
  267.2 7.8 %collective-permute-start.62 = (bf16[48,1152]{1,0:T(8,128)(2,1)S(1)}, bf16[48,1152]{1,0:T(8,128)(2,1)S(1)}, u32[]{:S(2)}, u32[]{:S(2)}) collective-permute-start(bf16[48,1152]{1,0:T(8,128)(2,1)S(1)} %get-tuple-element.369), channel_id=1, source_target_pairs={{0,4},{1,5},{2,6},{3,7},{4,8},{5,9},{6,10},{7,11},{8,12},{9,13},{1... | collective-permute-start | bytes 331784 | tf_op jit(solution)/shard_map/ppermute | solution.py:135
  268.4 3.7 %collective-permute-start.67 = (bf16[96,384]{1,0:T(8,128)(2,1)S(1)}, bf16[96,384]{1,0:T(8,128)(2,1)S(1)}, u32[]{:S(2)}, u32[]{:S(2)}) collective-permute-start(bf16[96,384]{1,0:T(8,128)(2,1)S(1)} %dynamic-slice_convert_fusion.1), channel_id=1, source_target_pairs={{0,1},{1,0},{2,3},{3,2},{4,5},{5,4},{6,7},{7,6},{8,9},{9,8},{10,11... | collective-permute-start | bytes 221192 | tf_op jit(solution)/shard_map/ppermute | solution.py:886
  (43 other events, 518.2 us)

commit v5 on v4

--- a/solution.py
+++ b/solution.py
@@ -490,27 +490,36 @@
 
     def run(masked):
         lane = lax.broadcasted_iota(jnp.int32, (512, 128), 1)
+        q, k, v, o, d = [[pair_of(r, n) for n in range(2)] for r in (q_ref, k_ref, v_ref, o_ref, d_ref)]
+        k_t = [value.T for value in k]
+        dots = [(a.astype(F32) * b.astype(F32)).T for a, b in zip(o, d)]
+
+        def head_of(value, h):
+            return jnp.where((lane // 64) == h, value, jnp.zeros_like(value))
+
+        def first(i):
+            n, h = i // 2, i % 2
+            s = nt(head_of(k[n], h), q[n])
+            return (s + bias[...] if masked else s), nt(head_of(v[n], h), d[n])
+
+        ready = [first(0), first(1)]
+        grad_q, grad_k, grad_v = [[], []], [0.0, 0.0], [0.0, 0.0]
+        for i in range(4):
+            if i < 2:
+                ready.append(first(i + 2))
+            s, grad_p = ready[i]
+            ready[i] = None
+            n, h = i // 2, i % 2
+            delta = jnp.sum(dots[n][64 * h : 64 * h + 64, :], axis=0, keepdims=True)
+            p = jnp.exp2(s * (SCORE_SCALE * LOG2E) - log_totals[i])
+            grad_s = (p * (grad_p - delta)).astype(BF16)
+            grad_v[n] = grad_v[n] + nn(p.astype(BF16), head_of(d[n], h))
+            grad_k[n] = grad_k[n] + nn(grad_s, head_of(q[n], h))
+            grad_q[n].append(nn(k_t[n][64 * h : 64 * h + 64, :], grad_s))
         for n in range(2):
-            q, k, v, o, d = [pair_of(r, n) for r in (q_ref, k_ref, v_ref, o_ref, d_ref)]
-            k_t = k.T
-            dots = (o.astype(F32) * d.astype(F32)).T
-            grad_q, grad_k, grad_v = [], [], []
-            for h in range(2):
-                here = (lane // 64) == h
-                zero = jnp.zeros_like(k)
-                s = nt(jnp.where(here, k, zero), q)
-                if masked:
-                    s = s + bias[...]
-                p = jnp.exp2(s * (SCORE_SCALE * LOG2E) - log_totals[2 * n + h])
-                grad_v.append(nn(p.astype(BF16), jnp.where(here, d, zero)))
-                grad_p = nt(jnp.where(here, v, zero), d)
-                delta = jnp.sum(dots[64 * h : 64 * h + 64, :], axis=0, keepdims=True)
-                grad_s = (p * (grad_p - delta)).astype(BF16)
-                grad_k.append(nn(grad_s, jnp.where(here, q, zero)))
-                grad_q.append(nn(k_t[64 * h : 64 * h + 64, :], grad_s))
-            put(grad_q_ref, n, jnp.concatenate(grad_q, axis=0).T * SCORE_SCALE)
-            put(grad_k_ref, n, (grad_k[0] + grad_k[1]) * SCORE_SCALE)
-            put(grad_v_ref, n, grad_v[0] + grad_v[1])
+            put(grad_q_ref, n, jnp.concatenate(grad_q[n], axis=0).T * SCORE_SCALE)
+            put(grad_k_ref, n, grad_k[n] * SCORE_SCALE)
+            put(grad_v_ref, n, grad_v[n])
 
     by_class(short, run)
 
@@ -665,8 +674,7 @@
             )
 
         tok_away, w_qkv = together(tok_away, w_qkv)
-        most = 3 * half // 4
-        tok_first = lax.ppermute(tok_away[:most], "seq", swap_x)
+        tok_got = lax.ppermute(tok_away, "seq", swap_x)
         piece_a = with_partner(0)
         piece_a, w_up, w_out, w_down = together(piece_a, w_up, w_out, w_down)
         piece_b, piece_c = with_partner(1), with_partner(2)
@@ -699,8 +707,7 @@
             return Pieces(chips, mine, theirs, fields)
 
         z_a = gather_along_z(grid, piece_a)
-        arrays, tok_first, tok_next, piece_b = together(arrays_of(z_a), tok_first, tok_away[most:], piece_b)
-        tok_second = lax.ppermute(tok_next, "seq", swap_x)
+        arrays, tok_got, piece_b = together(arrays_of(z_a), tok_got, piece_b)
         z_a = lots_of(with_arrays(z_a, arrays), 2)
         near_a = near_of(z_a)
         z_b = gather_along_z(grid, piece_b)
@@ -708,12 +715,14 @@
         wide_a = widened(z_a, [[part] for part in with_arrays(flat(near_a), arrays)])
         far_a = far_of(wide_a)
         all_a = wide_a + far_a
-        arrays_a, z_own, piece_c = together(arrays_of(all_a), z_b[0][0], piece_c)
-        tok_got = jnp.concatenate([tok_first, tok_second], axis=0)
+        arrays_a, z_own, piece_c, cot_away, cot_own = together(
+            arrays_of(all_a), z_b[0][0], piece_c, cot_away, cot_own
+        )
         z_b = with_arrays(z_b, [z_own] + arrays_of(z_b[1:]))
         group_a = finish(with_arrays(all_a, arrays_a), fields_a)
-        z_b = lots_of(with_arrays(z_b, lax.optimization_barrier(arrays_of(z_b))), 2)
-        near_b = near_of(z_b)
+        z_b = lots_of(with_arrays(z_b, lax.optimization_barrier(arrays_of(z_b))), grid.nz)
+        near_b = exchange(grid, z_b, "x")
+        straight_b = exchange(grid, z_b, "y")
         z_c = gather_along_z(grid, piece_c)
     else:
         full = [lax.all_gather(w, AXES, axis=0, tiled=True) for w in (w_qkv, w_out, w_up, w_down, gain_block)]
@@ -756,11 +765,15 @@
     )
 
     if fast:
-        packed, arrays_b, arrays_c = together(packed, arrays_of(flat(near_b)), arrays_of(z_c))
+        packed, arrays_b, arrays_s, arrays_c, cot_away = together(
+            packed, arrays_of(near_b), arrays_of(straight_b), arrays_of(z_c), cot_away
+        )
+        near_b, straight_b = with_arrays(near_b, arrays_b), with_arrays(straight_b, arrays_s)
         z_c = with_arrays(z_c, arrays_c)
-        wide_b = widened(z_b, [[part] for part in with_arrays(flat(near_b), arrays_b)])
-        far_b = far_of(wide_b)
-        their_wide_b = swapped(wide_b)
+        early_b = z_b + near_b + straight_b
+        far_b = exchange(grid, near_b, "y")
+        cot_got = lax.ppermute(cot_away, "seq", swap_x)
+        their_early_b = swapped(early_b)
 
     clip_blocks = half // 256
     by_clip = lambda a: a.reshape(2, clip_blocks, 256, a.shape[1])
@@ -788,11 +801,11 @@
     attended = attended.reshape(rows, width)
 
     if fast:
-        attended, arrays_b, arrays_w, arrays_c = together(
-            attended, arrays_of(far_b), arrays_of(their_wide_b), arrays_of(z_c)
+        attended, arrays_b, arrays_w, arrays_c, cot_got = together(
+            attended, arrays_of(far_b), arrays_of(their_early_b), arrays_of(z_c), cot_got
         )
-        far_b, their_wide_b = with_arrays(far_b, arrays_b), with_arrays(their_wide_b, arrays_w)
-        group_b = pieces_from(wide_b + far_b, their_wide_b + swapped(far_b), fields_b)
+        far_b, their_early_b = with_arrays(far_b, arrays_b), with_arrays(their_early_b, arrays_w)
+        group_b = pieces_from(early_b + far_b, their_early_b + swapped(far_b), fields_b)
         z_c = [joined_parts(with_arrays(z_c, arrays_c))]
         near_c = exchange(grid, z_c, "x")
         straight_c = exchange(grid, z_c, "y")
@@ -826,12 +839,11 @@
         cost=2 * rows * width * width * split_up,
     )
     if fast:
-        active, slope, normed_second, arrays_c, arrays_s, cot_away = together(
-            active, slope, normed_second, arrays_of(near_c), arrays_of(straight_c), cot_away
+        active, slope, normed_second, arrays_c, arrays_s = together(
+            active, slope, normed_second, arrays_of(near_c), arrays_of(straight_c)
         )
         near_c, straight_c = with_arrays(near_c, arrays_c), with_arrays(straight_c, arrays_s)
         far_c = exchange(grid, near_c, "y")
-        cot_got = lax.ppermute(cot_away, "seq", swap_x)
     rest = pl.BlockSpec((rows, width), lambda j, t: (0, split_up + j))
     active, slope = call(
         up_rest_kernel,
@@ -848,10 +860,10 @@
         aliases={3: 0, 4: 1},
     )
     if fast:
-        all_c = z_c + near_c + straight_c + far_c
-        active, slope, arrays_c, cot_got = together(active, slope, arrays_of(all_c), cot_got)
-        all_c = with_arrays(all_c, arrays_c)
-        theirs_c = swapped(all_c)
+        early_c = z_c + near_c + straight_c
+        active, slope, arrays_c = together(active, slope, arrays_of(early_c))
+        early_c = with_arrays(early_c, arrays_c)
+        their_early_c = swapped(early_c)
     down_out = low(chips, rows_c, width // 2)
     down_mine, down_other = call(
         functools.partial(down_grad_kernel, chips, rows_c),
@@ -887,8 +899,13 @@
         return jnp.where(core == 0, keep, got), jnp.where(core == 0, got, keep)
 
     if fast:
-        down_mine, down_other, active, arrays_c = together(down_mine, down_other, active, arrays_of(theirs_c))
-        group_c = pieces_from(all_c, with_arrays(theirs_c, arrays_c), fields_c)
+        down_mine, down_other, active, arrays_c, arrays_w = together(
+            down_mine, down_other, active, arrays_of(far_c), arrays_of(their_early_c)
+        )
+        far_c, their_early_c = with_arrays(far_c, arrays_c), with_arrays(their_early_c, arrays_w)
+        their_far_c = swapped(far_c)
+        down_mine, down_other, arrays_w = together(down_mine, down_other, arrays_of(their_far_c))
+        group_c = pieces_from(early_c + far_c, their_early_c + with_arrays(their_far_c, arrays_w), fields_c)
     outputs, whole_down = call(
         functools.partial(output_kernel, group_c, len(group_c.arrays), chips),
         tab,
@@ -995,7 +1012,7 @@
     qkv_mine, qkv_other, grads_a, grads_b, tok_own, arrived_up = together(
         qkv_mine, qkv_other, grads_a, grads_b, tok_own, arrived_up
     )
-    arrived_up, tok_got = up_sum.send((arrived_up, tok_got))
+    arrived_up, tok_got, qkv_mine, qkv_other = up_sum.send((arrived_up, tok_got, qkv_mine, qkv_other))
     qkv_sum = steps_of(qkv_mine, qkv_other, 2)
     arrived = next(qkv_sum)
     arrived, tok_own = qkv_sum.send((arrived, tok_own))

time: 284 us -> 282 us (level)
  local copies, waits for them, and re-layouts: 6.57 us -> 10.6 us
  waiting for transfers between devices: 53.2 us -> 49.5 us
  Pallas kernels: 132 us -> 129 us
    ppermute x20 -> x19, waiting for transfers between devices: 33.7 us -> 23.5 us  [exchange(): lax.ppermute(array, AXES, grid.shift(axis, k))]
    ppermute x2 -> x1, waiting for transfers between devices: 0.01 us -> 5.4 us  [body(): tok_got = lax.ppermute(tok_away, 'seq', swap_x)]
    ppermute x12, waiting for transfers between devices: 5.47 us -> 9.33 us  [scatter_steps(): lax.ppermute(total, AXES, grid.shift(axes[step], k + 1))]
    ppermute x1, waiting for transfers between devices: 3.07 us -> 0.01 us  [body(): cot_got = lax.ppermute(cot_away, 'seq', swap_x)]
    ppermute x12, starting transfers between devices: 13.7 us -> 10.8 us  [scatter_steps(): lax.ppermute(total, AXES, grid.shift(axes[step], k + 1))]
    unnamed x92 -> x116, local copies, waits for them, and re-layouts: 3.04 us -> 5.96 us
    ppermute x20 -> x19, starting transfers between devices: 28.9 us -> 31.7 us  [exchange(): lax.ppermute(array, AXES, grid.shift(axis, k))]
  transfers between devices with their start and end apart: 68 -> 66, of which waited for: 25 -> 24; matrix products, arithmetic and copies ran while one was open for 5% -> 7% of each run, Pallas kernels for 47% -> 46%
where the time goes in v5:
time: 282 us; the launch traced here: 278 us
  Pallas kernels  129 us (46%)
  starting transfers between devices  68.7 us (24%)
  waiting for transfers between devices  49.5 us (18%)
  other arithmetic  17.8 us (6%)
  local copies, waits for them, and re-layouts  10.6 us (4%)
    pallas_call x13, Pallas kernels, call(): pl.pallas_call(kernel, out_shape=[o for o, _ in outs], input_output_alias...  129 us
    ppermute x19, starting transfers between devices, exchange(): lax.ppermute(array, AXES, grid.shift(axis, k))  31.7 us
    ppermute x19, waiting for transfers between devices, exchange(): lax.ppermute(array, AXES, grid.shift(axis, k))  23.5 us
    ppermute x9, starting transfers between devices, scatter_steps(): lax.ppermute(total, AXES, grid.shift('z', k + 1))  15 us
    ppermute x12, starting transfers between devices, scatter_steps(): lax.ppermute(total, AXES, grid.shift(axes[step], k + 1))  10.8 us
    ppermute x12, waiting for transfers between devices, scatter_steps(): lax.ppermute(total, AXES, grid.shift(axes[step], k + 1))  9.33 us
    unnamed x116, local copies, waits for them, and re-layouts  5.96 us
  transfers between devices with their start and end apart: 66, of which 24 were waited for; matrix products, arithmetic and copies ran while one was open for 7% of the time, Pallas kernels for 46%

profile of v5, /device:TPU:0, one launch (start us, length us, event | category | flops | bytes accessed | tf_op | source)
XLA Modules:
  0.0 278.2 jit_solution(4030846003128254226)
XLA Ops:
  1.5 1.5 dynamic-slice_bitcast_fusion.2
  3.6 2.6 collective-permute-start.4
  6.2 1.6 collective-permute-start.1
  7.9 2.6 collective-permute-start.2
  10.5 1.3 collective-permute-start.3
  14.3 4.6 %collective-permute-done.2 = bf16[1,48,1280]{2,1,0:T(8,128)(2,1)S(1)} collective-permute-done((bf16[1,48,1280]{2,1,0:T(8,128)(2,1)S(1)}, bf16[1,48,1280]{2,1,0:T(8,128)(2,1)S(1)}, u32[]{:S(2)}, u32[]{:S(2)}) %collective-permute-start.2) | collective-permute-done | bytes 122912 | tf_op jit(solution)/shard_map/ppermute | solution.py:69
  18.9 5.4 %collective-permute-done.4.got = bf16[512,768]{1,0:T(8,128)(2,1)S(1)} collective-permute-done((bf16[512,768]{1,0:T(8,128)(2,1)S(1)}, bf16[512,768]{1,0:T(8,128)(2,1)S(1)}, u32[]{:S(2)}, u32[]{:S(2)}) %collective-permute-start.4) | collective-permute-done | bytes 786464 | tf_op jit(solution)/shard_map/ppermute | solution.py:677
  24.3 1.8 collective-permute-start.6
  26.9 1.6 collective-permute-start.7
  29.1 3.0 %collective-permute-done.6 = bf16[2,48,1280]{2,1,0:T(8,128)(2,1)S(1)} collective-permute-done((bf16[2,48,1280]{2,1,0:T(8,128)(2,1)S(1)}, bf16[2,48,1280]{2,1,0:T(8,128)(2,1)S(1)}, u32[]{:S(2)}, u32[]{:S(2)}) %collective-permute-start.6) | collective-permute-done | bytes 245792 | tf_op jit(solution)/shard_map/ppermute | solution.py:69
  32.1 2.1 collective-permute-done.7
  34.2 1.6 collective-permute-start.8
  38.3 1.6 collective-permute-start.15
  39.9 2.6 collective-permute-start.16
  42.5 1.3 collective-permute-start.17
  44.5 1.4 collective-permute-done.8.refs_2_
  46.0 2.2 collective-permute-done.9.refs_3_
  48.6 3.9 %collective-permute-done.16 = bf16[1,48,1920]{2,1,0:T(8,128)(2,1)S(1)} collective-permute-done((bf16[1,48,1920]{2,1,0:T(8,128)(2,1)S(1)}, bf16[1,48,1920]{2,1,0:T(8,128)(2,1)S(1)}, u32[]{:S(2)}, u32[]{:S(2)}) %collective-permute-start.16) | collective-permute-done | bytes 184352 | tf_op jit(solution)/shard_map/ppermute | solution.py:69
  52.7 1.6 collective-permute-start.18
  56.3 4.5 %collective-permute-start.20 = (bf16[1,192,384]{2,1,0:T(8,128)(2,1)}, bf16[1,192,384]{2,1,0:T(8,128)(2,1)S(1)}, u32[]{:S(2)}, u32[]{:S(2)}) collective-permute-start(bf16[1,192,384]{2,1,0:T(8,128)(2,1)} %bitcast.277), channel_id=1, source_target_pairs={{0,4},{1,5},{2,6},{3,7},{4,8},{5,9},{6,10},{7,11},{8,12},{9,13},{1... | collective-permute-start | bytes 442376 | tf_op jit(solution)/shard_map/ppermute | solution.py:69
  60.8 1.6 collective-permute-start.21
  64.4 9.4 %shard_map.135 = (bf16[1024,2304]{1,0:T(8,128)(2,1)}, bf16[1024,768]{1,0:T(8,128)(2,1)S(1)}, f32[8,768]{1,0:T(8,128)S(1)}, bf16[768,2304]{1,0:T(8,128)(2,1)}) custom-call(s32[34]{0:T(128)S(1)} %stack.140.tab, bf16[512,768]{1,0:T(8,128)(2,1)S(1)} %get-tuple-element.318.own, bf16[512,768]{1,0:T(8,128)(2,1)S(1)} %collective-permute-done.4.got, ...), custom_call_target="tpu_custom_call" | custom-call | flops 3623878656 | bytes 15360000 | tf_op jit(solution)/shard_map/pallas_call | solution.py:601
  74.6 1.5 collective-permute-start.23
  76.6 13.1 %shard_map.136 = (bf16[2,2,256,768]{3,2,1,0:T(8,128)(2,1)S(1)}, f32[24,1,512]{2,1,0:T(1,128)S(1)}) custom-call(s32[34]{0:T(128)S(1)} %stack.140.tab, bf16[2,2,256,2304]{3,2,1,0:T(8,128)(2,1)} %bitcast.244, bf16[2,2,256,2304]{3,2,1,0:T(8,128)(2,1)} %bitcast.245, bf16[2,2,256,2304]{3,2,1,0:T(8,128)(2,1)} %bitcast.246), custom_call_target="tpu_custom_call" | custom-call | flops 3221225472 | bytes 15777792 | tf_op jit(solution)/shard_map/pallas_call | solution.py:601
  89.7 3.8 %collective-permute-done.23.refs_3_ = bf16[4,48,1920]{2,1,0:T(8,128)(2,1)S(1)} collective-permute-done((bf16[4,48,1920]{2,1,0:T(8,128)(2,1)S(1)}, bf16[4,48,1920]{2,1,0:T(8,128)(2,1)S(1)}, u32[]{:S(2)}, u32[]{:S(2)}) %collective-permute-start.23) | collective-permute-done | bytes 737312 | tf_op jit(solution)/shard_map/ppermute | solution.py:69
  93.7 1.5 collective-permute-start.29
  95.2 1.5 collective-permute-start.30
  96.7 4.7 %shard_map.137 = (f32[1024,768]{1,0:T(8,128)S(1)}, bf16[1024,768]{1,0:T(8,128)(2,1)S(1)}, bf16[768,768]{1,0:T(8,128)(2,1)}) custom-call(s32[34]{0:T(128)S(1)} %stack.140.tab, bf16[1024,768]{1,0:T(8,128)(2,1)S(1)} %bitcast.223, bf16[512,768]{1,0:T(8,128)(2,1)S(1)} %get-tuple-element.318.own, bf16[512,768]{1,0:T(8,128)(2,1)S(1)} %collective-permute-done.4.got, ...), custom_call_target="tpu_custom_call" | custom-call | flops 1207959552 | bytes 14966784 | tf_op jit(solution)/shard_map/pallas_call | solution.py:601
  101.4 7.6 %shard_map.138 = (bf16[1024,3072]{1,0:T(8,128)(2,1)}, bf16[1024,3072]{1,0:T(8,128)(2,1)}, bf16[768,3072]{1,0:T(8,128)(2,1)}) custom-call(s32[34]{0:T(128)S(1)} %stack.140.tab, bf16[1024,768]{1,0:T(8,128)(2,1)S(1)} %get-tuple-element.233.normed, bf16[4,48,1920]{2,1,0:T(8,128)(2,1)S(1)} %constant_dynamic-update-slice_fusion.6.refs_0_, ...), custom_call_target="tpu_custom_call" | custom-call | flops 2415919104 | bytes 24772608 | tf_op jit(solution)/shard_map/pallas_call | solution.py:601
  110.6 1.5 collective-permute-start.31
  112.2 7.0 %shard_map.139 = (bf16[1024,3072]{1,0:T(8,128)(2,1)}, bf16[1024,3072]{1,0:T(8,128)(2,1)}) custom-call(s32[34]{0:T(128)S(1)} %stack.140.tab, bf16[1024,768]{1,0:T(8,128)(2,1)S(1)} %get-tuple-element.233.normed, bf16[768,3072]{1,0:T(8,128)(2,1)} %get-tuple-element.234.w_up, ...), custom_call_target="tpu_custom_call", output_to_operand_aliasing={{0}: (3, {}), {1}: (4, {})} | custom-call | flops 2415919104 | bytes 31457280 | tf_op jit(solution)/shard_map/pallas_call | solution.py:601
  119.7 8.2 %shard_map.140 = (bf16[16,192,384]{2,1,0:T(8,128)(2,1)S(1)}, bf16[16,192,384]{2,1,0:T(8,128)(2,1)S(1)}) custom-call(s32[34]{0:T(128)S(1)} %stack.140.tab, bf16[1024,3072]{1,0:T(8,128)(2,1)} %get-tuple-element.249.active, bf16[512,768]{1,0:T(8,128)(2,1)S(1)} %copy-done.4, bf16[512,768]{1,0:T(8,128)(2,1)S(1)} %collective-permute-done.27.cot_got), custom_call_target="tpu_custom_call" | custom-call | flops 4831838208 | bytes 12582912 | tf_op jit(solution)/shard_map/pallas_call | solution.py:601
  128.5 1.6 collective-permute-done.35.refs_7_
  130.5 9.4 %shard_map.141 = (bf16[1024,768]{1,0:T(8,128)(2,1)S(1)}, bf16[3072,768]{1,0:T(8,128)(2,1)}) custom-call(s32[34]{0:T(128)S(1)} %stack.140.tab, bf16[1024,3072]{1,0:T(8,128)(2,1)} %get-tuple-element.249.active, f32[1024,768]{1,0:T(8,128)S(1)} %get-tuple-element.250.hidden, bf16[4,192,384]{2,1,0:T(8,128)(2,1)S(1)} %constant_dynamic-update-slice_fusion.10.refs_0_, ...), custom_call_target="tpu_custom_call" | custom-call | flops 4831838208 | bytes 20447232 | tf_op jit(solution)/shard_map/pallas_call | solution.py:601
  142.2 1.4 collective-permute-start.41
  143.6 14.6 %shard_map.142 = (bf16[1024,3072]{1,0:T(8,128)(2,1)}, bf16[16,48,1920]{2,1,0:T(8,128)(2,1)S(1)}, bf16[16,48,1920]{2,1,0:T(8,128)(2,1)S(1)}) custom-call(s32[34]{0:T(128)S(1)} %stack.140.tab, bf16[512,768]{1,0:T(8,128)(2,1)S(1)} %copy-done.4, bf16[512,768]{1,0:T(8,128)(2,1)S(1)} %collective-permute-done.27.cot_got, ...), custom_call_target="tpu_custom_call" | custom-call | flops 9663676416 | bytes 26345472 | tf_op jit(solution)/shard_map/pallas_call | solution.py:601
  158.2 1.5 fusion.6
  160.4 1.5 collective-permute-start.40
  161.8 15.8 %shard_map.143 = (f32[1024,768]{1,0:T(8,128)}, bf16[1024,768]{1,0:T(8,128)(2,1)S(1)}, bf16[16,48,1920]{2,1,0:T(8,128)(2,1)S(1)}, bf16[16,48,1920]{2,1,0:T(8,128)(2,1)S(1)}) custom-call(s32[34]{0:T(128)S(1)} %stack.140.tab, bf16[1024,3072]{1,0:T(8,128)(2,1)} %get-tuple-element.269.grad_up, ...), custom_call_target="tpu_custom_call", output_to_operand_aliasing={{2}: (7, {}), {3}: (8, {})} | custom-call | flops 7247757312 | bytes 35020800 | tf_op jit(solution)/shard_map/pallas_call | solution.py:601
  178.5 1.5 collective-permute-start.43
  180.0 1.3 fusion.21
  181.3 2.8 collective-permute-start.46
  184.1 2.1 collective-permute-start.47
  186.5 8.7 %shard_map.144 = (bf16[2,2,256,256]{3,2,1,0:T(8,128)(2,1)}, bf16[2,2,256,256]{3,2,1,0:T(8,128)(2,1)}, bf16[2,2,256,256]{3,2,1,0:T(8,128)(2,1)}) custom-call(s32[34]{0:T(128)S(1)} %stack.140.tab, bf16[2,2,256,2304]{3,2,1,0:T(8,128)(2,1)} %bitcast.247, bf16[2,2,256,2304]{3,2,1,0:T(8,128)(2,1)} %bitcast.248, bf16[2,2,256,2304]{3,2,1,0:T(8,128)(2,1)} %bitcast.249, ...), custom_call_target="tpu_custom_call" | custom-call | flops 4026531840 | bytes 18923520 | tf_op jit(solution)/shard_map/pallas_call | solution.py:601
  195.6 1.6 collective-permute-start.44
  197.7 14.6 %shard_map.145 = (bf16[2,2,256,512]{3,2,1,0:T(8,128)(2,1)}, bf16[2,2,256,512]{3,2,1,0:T(8,128)(2,1)}, bf16[2,2,256,512]{3,2,1,0:T(8,128)(2,1)}) custom-call(s32[34]{0:T(128)S(1)} %stack.140.tab, bf16[2,2,256,2304]{3,2,1,0:T(8,128)(2,1)} %bitcast.250, bf16[2,2,256,2304]{3,2,1,0:T(8,128)(2,1)} %bitcast.251, bf16[2,2,256,2304]{3,2,1,0:T(8,128)(2,1)} %bitcast.252, ...), custom_call_target="tpu_custom_call" | custom-call | flops 8053063680 | bytes 20496384 | tf_op jit(solution)/shard_map/pallas_call | solution.py:601
  212.3 1.8 collective-permute-done.44
  216.7 7.0 %shard_map.146 = (bf16[16,48,1152]{2,1,0:T(8,128)(2,1)S(1)}, bf16[16,48,1152]{2,1,0:T(8,128)(2,1)S(1)}) custom-call(s32[34]{0:T(128)S(1)} %stack.140.tab, bf16[1024,768]{1,0:T(8,128)(2,1)S(1)} %get-tuple-element.300.normed, bf16[1024,256]{1,0:T(8,128)(2,1)} %bitcast.281, bf16[1024,256]{1,0:T(8,128)(2,1)} %bitcast.283, bf16[1024,256]{1,0:T(8,128)(2,1)} %bitcast.285, ...), custom_call_target="tpu_custom_call" | custom-call | flops 3623878656 | bytes 9830400 | tf_op jit(solution)/shard_map/pallas_call | solution.py:601
  223.8 1.3 collective-permute-done.49
  225.7 3.7 %collective-permute-done.51 = bf16[16,48,1152]{2,1,0:T(8,128)(2,1)S(1)} collective-permute-done((bf16[16,48,1152]{2,1,0:T(8,128)(2,1)S(1)}, bf16[16,48,1152]{2,1,0:T(8,128)(2,1)S(1)}, u32[]{:S(2)}, u32[]{:S(2)}) %collective-permute-start.51) | collective-permute-done | bytes 1769504 | tf_op jit(solution)/shard_map/ppermute | solution.py:98
  230.2 1.5 collective-permute-start.53
  232.4 1.3 collective-permute-start.55
  233.7 2.1 collective-permute-start.56
  235.8 9.2 %shard_map.147 = (bf16[512,768]{1,0:T(8,128)(2,1)S(1)}, bf16[512,768]{1,0:T(8,128)(2,1)S(1)}) custom-call(s32[34]{0:T(128)S(1)} %stack.140.tab, bf16[512,768]{1,0:T(8,128)(2,1)S(1)} %get-tuple-element.318.own, bf16[512,768]{1,0:T(8,128)(2,1)S(1)} %copy-done.8, f32[8,768]{1,0:T(8,128)S(1)} %get-tuple-element.221.gains, ...), custom_call_target="tpu_custom_call" | custom-call | flops 3623878656 | bytes 14573568 | tf_op jit(solution)/shard_map/pallas_call | solution.py:601
  245.1 2.7 collective-permute-done.55
  249.6 1.5 collective-permute-start.58
  251.1 4.3 %collective-permute-done.57 = bf16[2,48,1152]{2,1,0:T(8,128)(2,1)} collective-permute-done((bf16[2,48,1152]{2,1,0:T(8,128)(2,1)}, bf16[2,48,1152]{2,1,0:T(8,128)(2,1)}, u32[]{:S(2)}, u32[]{:S(2)}) %collective-permute-start.57) | collective-permute-done | bytes 221216 | tf_op jit(solution)/shard_map/ppermute | solution.py:120
  255.9 1.6 collective-permute-start.59
  257.5 1.5 fusion.25
  259.0 4.0 %collective-permute-start.62 = (bf16[48,1152]{1,0:T(8,128)(2,1)S(1)}, bf16[48,1152]{1,0:T(8,128)(2,1)S(1)}, u32[]{:S(2)}, u32[]{:S(2)}) collective-permute-start(bf16[48,1152]{1,0:T(8,128)(2,1)S(1)} %get-tuple-element.378), channel_id=1, source_target_pairs={{0,12},{1,13},{2,14},{3,15},{4,0},{5,1},{6,2},{7,3},{8,4},{9,5},{1... | collective-permute-start | bytes 331784 | tf_op jit(solution)/shard_map/ppermute | solution.py:135
  263.0 1.8 collective-permute-start.61
  267.1 1.3 fusion.14
  268.4 1.2 maximum_bitcast_fusion
  276.8 1.2 maximum_bitcast_fusion.1
  (257 shorter events, 38.4 us)
Async XLA Ops:
  3.1 3.1 %collective-permute-start = (bf16[24,1280]{1,0:T(8,128)(2,1)S(1)}, bf16[24,1280]{1,0:T(8,128)(2,1)S(1)}, u32[]{:S(2)}, u32[]{:S(2)}) collective-permute-start(bf16[24,1280]{1,0:T(8,128)(2,1)S(1)} %fusion.32), channel_id=1, source_target_pairs={{0,1},{1,0},{2,3},{3,2},{4,5},{5,4},{6,7},{7,6},{8,9},{9,8},{10,11... | collective-permute-start | bytes 184328 | tf_op jit(solution)/shard_map/ppermute | solution.py:671
  3.6 20.7 %collective-permute-start.4 = (bf16[512,768]{1,0:T(8,128)(2,1)S(1)}, bf16[512,768]{1,0:T(8,128)(2,1)S(1)}, u32[]{:S(2)}, u32[]{:S(2)}) collective-permute-start(bf16[512,768]{1,0:T(8,128)(2,1)S(1)} %get-tuple-element.187), channel_id=1, source_target_pairs={{0,16},{16,0},{1,17},{17,1},{2,18},{18,2},{3,19},{19,3},{4,20},{20... | collective-permute-start | bytes 2359304 | tf_op jit(solution)/shard_map/ppermute | solution.py:677
  6.2 8.1 %collective-permute-start.1 = (bf16[1,48,1280]{2,1,0:T(8,128)(2,1)S(1)}, bf16[1,48,1280]{2,1,0:T(8,128)(2,1)S(1)}, u32[]{:S(2)}, u32[]{:S(2)}) collective-permute-start(bf16[1,48,1280]{2,1,0:T(8,128)(2,1)S(1)} %bitcast.268), channel_id=1, source_target_pairs={{0,4},{1,5},{2,6},{3,7},{4,8},{5,9},{6,10},{7,11},{8,12},{9,13},{1... | collective-permute-start | bytes 368648 | tf_op jit(solution)/shard_map/ppermute | solution.py:69
  7.9 11.0 %collective-permute-start.2 = (bf16[1,48,1280]{2,1,0:T(8,128)(2,1)S(1)}, bf16[1,48,1280]{2,1,0:T(8,128)(2,1)S(1)}, u32[]{:S(2)}, u32[]{:S(2)}) collective-permute-start(bf16[1,48,1280]{2,1,0:T(8,128)(2,1)S(1)} %bitcast.269), channel_id=1, source_target_pairs={{0,8},{1,9},{2,10},{3,11},{4,12},{5,13},{6,14},{7,15},{8,0},{9,1},... | collective-permute-start | bytes 368648 | tf_op jit(solution)/shard_map/ppermute | solution.py:69
  10.5 8.5 %collective-permute-start.3 = (bf16[1,48,1280]{2,1,0:T(8,128)(2,1)S(1)}, bf16[1,48,1280]{2,1,0:T(8,128)(2,1)S(1)}, u32[]{:S(2)}, u32[]{:S(2)}) collective-permute-start(bf16[1,48,1280]{2,1,0:T(8,128)(2,1)S(1)} %bitcast.270), channel_id=1, source_target_pairs={{0,12},{1,13},{2,14},{3,15},{4,0},{5,1},{6,2},{7,3},{8,4},{9,5},{1... | collective-permute-start | bytes 368648 | tf_op jit(solution)/shard_map/ppermute | solution.py:69
  11.9 1.4 collective-permute-start.5
  13.2 29.2 %collective-permute-start.10 = (bf16[96,384]{1,0:T(8,128)(2,1)S(1)}, bf16[96,384]{1,0:T(8,128)(2,1)S(1)}, u32[]{:S(2)}, u32[]{:S(2)}) collective-permute-start(bf16[96,384]{1,0:T(8,128)(2,1)S(1)} %constant_dynamic-slice_fusion), channel_id=1, source_target_pairs={{0,1},{1,0},{2,3},{3,2},{4,5},{5,4},{6,7},{7,6},{8,9},{9,8},{10,11... | collective-permute-start | bytes 221192 | tf_op jit(solution)/shard_map/ppermute | solution.py:671
  24.3 7.8 %collective-permute-start.6 = (bf16[2,48,1280]{2,1,0:T(8,128)(2,1)S(1)}, bf16[2,48,1280]{2,1,0:T(8,128)(2,1)S(1)}, u32[]{:S(2)}, u32[]{:S(2)}) collective-permute-start(bf16[2,48,1280]{2,1,0:T(8,128)(2,1)S(1)} %pad_maximum_fusion.2), channel_id=1, source_target_pairs={{0,16},{1,17},{2,18},{3,19},{4,20},{5,21},{6,22},{7,23},{8,24},{9,... | collective-permute-start | bytes 737288 | tf_op jit(solution)/shard_map/ppermute | solution.py:69
  26.9 7.3 %collective-permute-start.7 = (bf16[2,48,1280]{2,1,0:T(8,128)(2,1)S(1)}, bf16[2,48,1280]{2,1,0:T(8,128)(2,1)S(1)}, u32[]{:S(2)}, u32[]{:S(2)}) collective-permute-start(bf16[2,48,1280]{2,1,0:T(8,128)(2,1)S(1)} %pad_maximum_fusion.3), channel_id=1, source_target_pairs={{0,2},{1,3},{2,0},{3,1},{4,6},{5,7},{6,4},{7,5},{8,10},{9,11},{10,... | collective-permute-start | bytes 737288 | tf_op jit(solution)/shard_map/ppermute | solution.py:69
  34.2 11.8 %collective-permute-start.8 = (bf16[4,48,1280]{2,1,0:T(8,128)(2,1)S(1)}, bf16[4,48,1280]{2,1,0:T(8,128)(2,1)}, u32[]{:S(2)}, u32[]{:S(2)}) collective-permute-start(bf16[4,48,1280]{2,1,0:T(8,128)(2,1)S(1)} %constant_dynamic-update-slice_fusion.refs_0_), channel_id=1, source_target_pairs={{0,2},{1,3},{2,0},{3,1},{4,6},{5,7},{6,4},{7,5},{8,10},{9,11},{10,... | collective-permute-start | bytes 1474568 | tf_op jit(solution)/shard_map/ppermute | solution.py:69
  36.5 11.6 %collective-permute-start.9 = (bf16[4,48,1280]{2,1,0:T(8,128)(2,1)}, bf16[4,48,1280]{2,1,0:T(8,128)(2,1)}, u32[]{:S(2)}, u32[]{:S(2)}) collective-permute-start(bf16[4,48,1280]{2,1,0:T(8,128)(2,1)} %constant_dynamic-update-slice_fusion.3.refs_1_), channel_id=1, source_target_pairs={{0,16},{1,17},{2,18},{3,19},{4,20},{5,21},{6,22},{7,23},{8,24},{9,... | collective-permute-start | bytes 1474568 | tf_op jit(solution)/shard_map/ppermute | solution.py:69
  38.3 10.4 %collective-permute-start.15 = (bf16[1,48,1920]{2,1,0:T(8,128)(2,1)S(1)}, bf16[1,48,1920]{2,1,0:T(8,128)(2,1)S(1)}, u32[]{:S(2)}, u32[]{:S(2)}) collective-permute-start(bf16[1,48,1920]{2,1,0:T(8,128)(2,1)S(1)} %bitcast.273), channel_id=1, source_target_pairs={{0,4},{1,5},{2,6},{3,7},{4,8},{5,9},{6,10},{7,11},{8,12},{9,13},{1... | collective-permute-start | bytes 552968 | tf_op jit(solution)/shard_map/ppermute | solution.py:69
  39.9 12.7 %collective-permute-start.16 = (bf16[1,48,1920]{2,1,0:T(8,128)(2,1)S(1)}, bf16[1,48,1920]{2,1,0:T(8,128)(2,1)S(1)}, u32[]{:S(2)}, u32[]{:S(2)}) collective-permute-start(bf16[1,48,1920]{2,1,0:T(8,128)(2,1)S(1)} %bitcast.274), channel_id=1, source_target_pairs={{0,8},{1,9},{2,10},{3,11},{4,12},{5,13},{6,14},{7,15},{8,0},{9,1},... | collective-permute-start | bytes 552968 | tf_op jit(solution)/shard_map/ppermute | solution.py:69
  42.5 10.1 %collective-permute-start.17 = (bf16[1,48,1920]{2,1,0:T(8,128)(2,1)S(1)}, bf16[1,48,1920]{2,1,0:T(8,128)(2,1)S(1)}, u32[]{:S(2)}, u32[]{:S(2)}) collective-permute-start(bf16[1,48,1920]{2,1,0:T(8,128)(2,1)S(1)} %bitcast.275), channel_id=1, source_target_pairs={{0,12},{1,13},{2,14},{3,15},{4,0},{5,1},{6,2},{7,3},{8,4},{9,5},{1... | collective-permute-start | bytes 552968 | tf_op jit(solution)/shard_map/ppermute | solution.py:69
  48.1 6.1 %collective-permute-start.11 = (bf16[4,48,1280]{2,1,0:T(8,128)(2,1)S(1)}, bf16[4,48,1280]{2,1,0:T(8,128)(2,1)S(1)}, u32[]{:S(2)}, u32[]{:S(2)}) collective-permute-start(bf16[4,48,1280]{2,1,0:T(8,128)(2,1)S(1)} %constant_dynamic-update-slice_fusion.refs_0_), channel_id=1, source_target_pairs={{0,1},{1,0},{2,3},{3,2},{4,5},{5,4},{6,7},{7,6},{8,9},{9,8},{10,11... | collective-permute-start | bytes 1474568 | tf_op jit(solution)/shard_map/ppermute | solution.py:706
  48.1 8.2 %collective-permute-start.12 = (bf16[4,48,1280]{2,1,0:T(8,128)(2,1)}, bf16[4,48,1280]{2,1,0:T(8,128)(2,1)}, u32[]{:S(2)}, u32[]{:S(2)}) collective-permute-start(bf16[4,48,1280]{2,1,0:T(8,128)(2,1)} %constant_dynamic-update-slice_fusion.3.refs_1_), channel_id=1, source_target_pairs={{0,1},{1,0},{2,3},{3,2},{4,5},{5,4},{6,7},{7,6},{8,9},{9,8},{10,11... | collective-permute-start | bytes 1474568 | tf_op jit(solution)/shard_map/ppermute | solution.py:706
  48.6 12.2 %collective-permute-start.13 = (bf16[4,48,1280]{2,1,0:T(8,128)(2,1)}, bf16[4,48,1280]{2,1,0:T(8,128)(2,1)}, u32[]{:S(2)}, u32[]{:S(2)}) collective-permute-start(bf16[4,48,1280]{2,1,0:T(8,128)(2,1)} %collective-permute-done.8.refs_2_), channel_id=1, source_target_pairs={{0,1},{1,0},{2,3},{3,2},{4,5},{5,4},{6,7},{7,6},{8,9},{9,8},{10,11... | collective-permute-start | bytes 1474568 | tf_op jit(solution)/shard_map/ppermute | solution.py:706
  52.6 9.8 %collective-permute-start.14 = (bf16[4,48,1280]{2,1,0:T(8,128)(2,1)}, bf16[4,48,1280]{2,1,0:T(8,128)(2,1)}, u32[]{:S(2)}, u32[]{:S(2)}) collective-permute-start(bf16[4,48,1280]{2,1,0:T(8,128)(2,1)} %collective-permute-done.9.refs_3_), channel_id=1, source_target_pairs={{0,1},{1,0},{2,3},{3,2},{4,5},{5,4},{6,7},{7,6},{8,9},{9,8},{10,11... | collective-permute-start | bytes 1474568 | tf_op jit(solution)/shard_map/ppermute | solution.py:706
  52.7 21.2 %collective-permute-start.18 = (bf16[4,48,1920]{2,1,0:T(8,128)(2,1)S(1)}, bf16[4,48,1920]{2,1,0:T(8,128)(2,1)S(1)}, u32[]{:S(2)}, u32[]{:S(2)}) collective-permute-start(bf16[4,48,1920]{2,1,0:T(8,128)(2,1)S(1)} %constant_dynamic-update-slice_fusion.6.refs_0_), channel_id=1, source_target_pairs={{0,16},{1,17},{2,18},{3,19},{4,20},{5,21},{6,22},{7,23},{8,24},{9,... | collective-permute-start | bytes 2211848 | tf_op jit(solution)/shard_map/ppermute | solution.py:69
  55.1 18.8 %collective-permute-start.19 = (bf16[4,48,1920]{2,1,0:T(8,128)(2,1)S(1)}, bf16[4,48,1920]{2,1,0:T(8,128)(2,1)}, u32[]{:S(2)}, u32[]{:S(2)}) collective-permute-start(bf16[4,48,1920]{2,1,0:T(8,128)(2,1)S(1)} %constant_dynamic-update-slice_fusion.6.refs_0_), channel_id=1, source_target_pairs={{0,2},{1,3},{2,0},{3,1},{4,6},{5,7},{6,4},{7,5},{8,10},{9,11},{10,... | collective-permute-start | bytes 2211848 | tf_op jit(solution)/shard_map/ppermute | solution.py:69
  56.3 17.5 %collective-permute-start.20 = (bf16[1,192,384]{2,1,0:T(8,128)(2,1)}, bf16[1,192,384]{2,1,0:T(8,128)(2,1)S(1)}, u32[]{:S(2)}, u32[]{:S(2)}) collective-permute-start(bf16[1,192,384]{2,1,0:T(8,128)(2,1)} %bitcast.277), channel_id=1, source_target_pairs={{0,4},{1,5},{2,6},{3,7},{4,8},{5,9},{6,10},{7,11},{8,12},{9,13},{1... | collective-permute-start | bytes 442376 | tf_op jit(solution)/shard_map/ppermute | solution.py:69
  60.8 13.1 %collective-permute-start.21 = (bf16[1,192,384]{2,1,0:T(8,128)(2,1)}, bf16[1,192,384]{2,1,0:T(8,128)(2,1)S(1)}, u32[]{:S(2)}, u32[]{:S(2)}) collective-permute-start(bf16[1,192,384]{2,1,0:T(8,128)(2,1)} %bitcast.278), channel_id=1, source_target_pairs={{0,8},{1,9},{2,10},{3,11},{4,12},{5,13},{6,14},{7,15},{8,0},{9,1},... | collective-permute-start | bytes 442376 | tf_op jit(solution)/shard_map/ppermute | solution.py:69
  62.4 11.4 %collective-permute-start.22 = (bf16[1,192,384]{2,1,0:T(8,128)(2,1)}, bf16[1,192,384]{2,1,0:T(8,128)(2,1)S(1)}, u32[]{:S(2)}, u32[]{:S(2)}) collective-permute-start(bf16[1,192,384]{2,1,0:T(8,128)(2,1)} %bitcast.279), channel_id=1, source_target_pairs={{0,12},{1,13},{2,14},{3,15},{4,0},{5,1},{6,2},{7,3},{8,4},{9,5},{1... | collective-permute-start | bytes 442376 | tf_op jit(solution)/shard_map/ppermute | solution.py:69
  73.9 19.6 %collective-permute-start.27 = (bf16[512,768]{1,0:T(8,128)(2,1)S(1)}, bf16[512,768]{1,0:T(8,128)(2,1)S(1)}, u32[]{:S(2)}, u32[]{:S(2)}) collective-permute-start(bf16[512,768]{1,0:T(8,128)(2,1)S(1)} %copy-done.17), channel_id=1, source_target_pairs={{0,16},{16,0},{1,17},{17,1},{2,18},{18,2},{3,19},{19,3},{4,20},{20... | collective-permute-start | bytes 2359304 | tf_op jit(solution)/shard_map/ppermute | solution.py:775
  74.6 15.1 %collective-permute-start.24 = (bf16[4,48,1920]{2,1,0:T(8,128)(2,1)S(1)}, bf16[4,48,1920]{2,1,0:T(8,128)(2,1)S(1)}, u32[]{:S(2)}, u32[]{:S(2)}) collective-permute-start(bf16[4,48,1920]{2,1,0:T(8,128)(2,1)S(1)} %constant_dynamic-update-slice_fusion.6.refs_0_), channel_id=1, source_target_pairs={{0,1},{1,0},{2,3},{3,2},{4,5},{5,4},{6,7},{7,6},{8,9},{9,8},{10,11... | collective-permute-start | bytes 2211848 | tf_op jit(solution)/shard_map/ppermute | solution.py:698
  74.6 18.9 %collective-permute-start.23 = (bf16[4,48,1920]{2,1,0:T(8,128)(2,1)S(1)}, bf16[4,48,1920]{2,1,0:T(8,128)(2,1)S(1)}, u32[]{:S(2)}, u32[]{:S(2)}) collective-permute-start(bf16[4,48,1920]{2,1,0:T(8,128)(2,1)S(1)} %collective-permute-done.18.refs_1_), channel_id=1, source_target_pairs={{0,2},{1,3},{2,0},{3,1},{4,6},{5,7},{6,4},{7,5},{8,10},{9,11},{10,... | collective-permute-start | bytes 2211848 | tf_op jit(solution)/shard_map/ppermute | solution.py:69
  76.0 17.4 %collective-permute-start.25 = (bf16[4,48,1920]{2,1,0:T(8,128)(2,1)S(1)}, bf16[4,48,1920]{2,1,0:T(8,128)(2,1)S(1)}, u32[]{:S(2)}, u32[]{:S(2)}) collective-permute-start(bf16[4,48,1920]{2,1,0:T(8,128)(2,1)S(1)} %collective-permute-done.18.refs_1_), channel_id=1, source_target_pairs={{0,1},{1,0},{2,3},{3,2},{4,5},{5,4},{6,7},{7,6},{8,9},{9,8},{10,11... | collective-permute-start | bytes 2211848 | tf_op jit(solution)/shard_map/ppermute | solution.py:698
  76.3 17.2 %collective-permute-start.26 = (bf16[4,48,1920]{2,1,0:T(8,128)(2,1)}, bf16[4,48,1920]{2,1,0:T(8,128)(2,1)S(1)}, u32[]{:S(2)}, u32[]{:S(2)}) collective-permute-start(bf16[4,48,1920]{2,1,0:T(8,128)(2,1)} %collective-permute-done.19.refs_2_), channel_id=1, source_target_pairs={{0,1},{1,0},{2,3},{3,2},{4,5},{5,4},{6,7},{7,6},{8,9},{9,8},{10,11... | collective-permute-start | bytes 2211848 | tf_op jit(solution)/shard_map/ppermute | solution.py:698
  93.5 3.2 %collective-permute-start.28 = (bf16[4,48,1920]{2,1,0:T(8,128)(2,1)S(1)}, bf16[4,48,1920]{2,1,0:T(8,128)(2,1)S(1)}, u32[]{:S(2)}, u32[]{:S(2)}) collective-permute-start(bf16[4,48,1920]{2,1,0:T(8,128)(2,1)S(1)} %collective-permute-done.23.refs_3_), channel_id=1, source_target_pairs={{0,1},{1,0},{2,3},{3,2},{4,5},{5,4},{6,7},{7,6},{8,9},{9,8},{10,11... | collective-permute-start | bytes 2211848 | tf_op jit(solution)/shard_map/ppermute | solution.py:698
  93.7 15.8 %collective-permute-start.29 = (bf16[4,192,384]{2,1,0:T(8,128)(2,1)S(1)}, bf16[4,192,384]{2,1,0:T(8,128)(2,1)S(1)}, u32[]{:S(2)}, u32[]{:S(2)}) collective-permute-start(bf16[4,192,384]{2,1,0:T(8,128)(2,1)S(1)} %constant_dynamic-update-slice_fusion.10.refs_0_), channel_id=1, source_target_pairs={{0,16},{1,17},{2,18},{3,19},{4,20},{5,21},{6,22},{7,23},{8,24},{9,... | collective-permute-start | bytes 1769480 | tf_op jit(solution)/shard_map/ppermute | solution.py:69
  95.2 15.4 %collective-permute-start.30 = (bf16[4,192,384]{2,1,0:T(8,128)(2,1)S(1)}, bf16[4,192,384]{2,1,0:T(8,128)(2,1)S(1)}, u32[]{:S(2)}, u32[]{:S(2)}) collective-permute-start(bf16[4,192,384]{2,1,0:T(8,128)(2,1)S(1)} %constant_dynamic-update-slice_fusion.10.refs_0_), channel_id=1, source_target_pairs={{0,2},{1,3},{2,0},{3,1},{4,6},{5,7},{6,4},{7,5},{8,10},{9,11},{10,... | collective-permute-start | bytes 1769480 | tf_op jit(solution)/shard_map/ppermute | solution.py:69
  110.6 17.2 %collective-permute-start.31 = (bf16[4,192,384]{2,1,0:T(8,128)(2,1)S(1)}, bf16[4,192,384]{2,1,0:T(8,128)(2,1)S(1)}, u32[]{:S(2)}, u32[]{:S(2)}) collective-permute-start(bf16[4,192,384]{2,1,0:T(8,128)(2,1)S(1)} %collective-permute-done.29.refs_1_), channel_id=1, source_target_pairs={{0,2},{1,3},{2,0},{3,1},{4,6},{5,7},{6,4},{7,5},{8,10},{9,11},{10,... | collective-permute-start | bytes 1769480 | tf_op jit(solution)/shard_map/ppermute | solution.py:69
  119.2 8.7 %collective-permute-start.32 = (bf16[4,192,384]{2,1,0:T(8,128)(2,1)S(1)}, bf16[4,192,384]{2,1,0:T(8,128)(2,1)S(1)}, u32[]{:S(2)}, u32[]{:S(2)}) collective-permute-start(bf16[4,192,384]{2,1,0:T(8,128)(2,1)S(1)} %constant_dynamic-update-slice_fusion.10.refs_0_), channel_id=1, source_target_pairs={{0,1},{1,0},{2,3},{3,2},{4,5},{5,4},{6,7},{7,6},{8,9},{9,8},{10,11... | collective-permute-start | bytes 1769480 | tf_op jit(solution)/shard_map/ppermute | solution.py:698
  119.2 8.7 %collective-permute-start.33 = (bf16[4,192,384]{2,1,0:T(8,128)(2,1)S(1)}, bf16[4,192,384]{2,1,0:T(8,128)(2,1)S(1)}, u32[]{:S(2)}, u32[]{:S(2)}) collective-permute-start(bf16[4,192,384]{2,1,0:T(8,128)(2,1)S(1)} %collective-permute-done.29.refs_1_), channel_id=1, source_target_pairs={{0,1},{1,0},{2,3},{3,2},{4,5},{5,4},{6,7},{7,6},{8,9},{9,8},{10,11... | collective-permute-start | bytes 1769480 | tf_op jit(solution)/shard_map/ppermute | solution.py:698
  119.7 8.2 %collective-permute-start.34 = (bf16[4,192,384]{2,1,0:T(8,128)(2,1)S(1)}, bf16[4,192,384]{2,1,0:T(8,128)(2,1)S(1)}, u32[]{:S(2)}, u32[]{:S(2)}) collective-permute-start(bf16[4,192,384]{2,1,0:T(8,128)(2,1)S(1)} %collective-permute-done.30.refs_2_), channel_id=1, source_target_pairs={{0,1},{1,0},{2,3},{3,2},{4,5},{5,4},{6,7},{7,6},{8,9},{9,8},{10,11... | collective-permute-start | bytes 1769480 | tf_op jit(solution)/shard_map/ppermute | solution.py:698
  127.9 2.2 collective-permute-start.35
  130.1 9.8 %collective-permute-start.36 = (bf16[16,192,384]{2,1,0:T(8,128)(2,1)S(1)}, bf16[16,192,384]{2,1,0:T(8,128)(2,1)S(1)}, u32[]{:S(2)}, u32[]{:S(2)}) collective-permute-start(bf16[16,192,384]{2,1,0:T(8,128)(2,1)S(1)} %get-tuple-element.259), channel_id=1, source_target_pairs={{0,1},{1,0},{2,3},{3,2},{4,5},{5,4},{6,7},{7,6},{8,9},{9,8},{10,11... | collective-permute-start | bytes 7077896 | tf_op jit(solution)/shard_map/ppermute | solution.py:98
  140.2 18.0 %collective-permute-start.37 = (bf16[2,2,192,384]{3,2,1,0:T(8,128)(2,1)S(1)}, bf16[2,2,192,384]{3,2,1,0:T(8,128)(2,1)S(1)}, u32[]{:S(2)}, u32[]{:S(2)}) collective-permute-start(bf16[2,2,192,384]{3,2,1,0:T(8,128)(2,1)S(1)} %fusion.4), channel_id=1, source_target_pairs={{0,2},{1,3},{2,0},{3,1},{4,6},{5,7},{6,4},{7,5},{8,10},{9,11},{10,... | collective-permute-start | bytes 1769480 | tf_op jit(solution)/shard_map/ppermute | solution.py:120
  140.8 17.4 %collective-permute-start.38 = (bf16[2,2,192,384]{3,2,1,0:T(8,128)(2,1)S(1)}, bf16[2,2,192,384]{3,2,1,0:T(8,128)(2,1)S(1)}, u32[]{:S(2)}, u32[]{:S(2)}) collective-permute-start(bf16[2,2,192,384]{3,2,1,0:T(8,128)(2,1)S(1)} %fusion.5), channel_id=1, source_target_pairs={{0,16},{1,17},{2,18},{3,19},{4,20},{5,21},{6,22},{7,23},{8,24},{9,... | collective-permute-start | bytes 1769480 | tf_op jit(solution)/shard_map/ppermute | solution.py:120
  142.2 35.5 %collective-permute-start.41 = (bf16[256,768]{1,0:T(8,128)(2,1)S(1)}, bf16[256,768]{1,0:T(8,128)(2,1)S(1)}, u32[]{:S(2)}, u32[]{:S(2)}) collective-permute-start(bf16[256,768]{1,0:T(8,128)(2,1)S(1)} %get-tuple-element.387), channel_id=1, source_target_pairs={{0,16},{16,0},{1,17},{17,1},{2,18},{18,2},{3,19},{19,3},{4,20},{20... | collective-permute-start | bytes 1179656 | tf_op jit(solution)/shard_map/ppermute | solution.py:946
  159.7 18.0 %collective-permute-start.39 = (bf16[2,192,384]{2,1,0:T(8,128)(2,1)S(1)}, bf16[2,192,384]{2,1,0:T(8,128)(2,1)S(1)}, u32[]{:S(2)}, u32[]{:S(2)}) collective-permute-start(bf16[2,192,384]{2,1,0:T(8,128)(2,1)S(1)} %get-tuple-element.376), channel_id=1, source_target_pairs={{0,16},{1,17},{2,18},{3,19},{4,20},{5,21},{6,22},{7,23},{8,24},{9,... | collective-permute-start | bytes 884744 | tf_op jit(solution)/shard_map/ppermute | solution.py:120
  160.4 17.4 %collective-permute-start.40 = (bf16[2,192,384]{2,1,0:T(8,128)(2,1)S(1)}, bf16[2,192,384]{2,1,0:T(8,128)(2,1)S(1)}, u32[]{:S(2)}, u32[]{:S(2)}) collective-permute-start(bf16[2,192,384]{2,1,0:T(8,128)(2,1)S(1)} %get-tuple-element.375), channel_id=1, source_target_pairs={{0,2},{1,3},{2,0},{3,1},{4,6},{5,7},{6,4},{7,5},{8,10},{9,11},{10,... | collective-permute-start | bytes 884744 | tf_op jit(solution)/shard_map/ppermute | solution.py:120
  178.4 16.7 %collective-permute-start.42 = (bf16[16,48,1920]{2,1,0:T(8,128)(2,1)S(1)}, bf16[16,48,1920]{2,1,0:T(8,128)(2,1)S(1)}, u32[]{:S(2)}, u32[]{:S(2)}) collective-permute-start(bf16[16,48,1920]{2,1,0:T(8,128)(2,1)S(1)} %get-tuple-element.285), channel_id=1, source_target_pairs={{0,1},{1,0},{2,3},{3,2},{4,5},{5,4},{6,7},{7,6},{8,9},{9,8},{10,11... | collective-permute-start | bytes 8847368 | tf_op jit(solution)/shard_map/ppermute | solution.py:98
  178.5 16.7 %collective-permute-start.43 = (bf16[256,768]{1,0:T(8,128)(2,1)S(1)}, bf16[256,768]{1,0:T(8,128)(2,1)S(1)}, u32[]{:S(2)}, u32[]{:S(2)}) collective-permute-start(bf16[256,768]{1,0:T(8,128)(2,1)S(1)} %copy-done.29), channel_id=1, source_target_pairs={{0,16},{16,0},{1,17},{17,1},{2,18},{18,2},{3,19},{19,3},{4,20},{20... | collective-permute-start | bytes 1179656 | tf_op jit(solution)/shard_map/ppermute | solution.py:965
  181.3 30.9 %collective-permute-start.46 = (bf16[192,384]{1,0:T(8,128)(2,1)S(1)}, bf16[192,384]{1,0:T(8,128)(2,1)S(1)}, u32[]{:S(2)}, u32[]{:S(2)}) collective-permute-start(bf16[192,384]{1,0:T(8,128)(2,1)S(1)} %get-tuple-element.374), channel_id=1, source_target_pairs={{0,4},{1,5},{2,6},{3,7},{4,8},{5,9},{6,10},{7,11},{8,12},{9,13},{1... | collective-permute-start | bytes 442376 | tf_op jit(solution)/shard_map/ppermute | solution.py:135
  184.1 28.2 %collective-permute-start.47 = (bf16[192,384]{1,0:T(8,128)(2,1)S(1)}, bf16[192,384]{1,0:T(8,128)(2,1)S(1)}, u32[]{:S(2)}, u32[]{:S(2)}) collective-permute-start(bf16[192,384]{1,0:T(8,128)(2,1)S(1)} %get-tuple-element.373), channel_id=1, source_target_pairs={{0,8},{1,9},{2,10},{3,11},{4,12},{5,13},{6,14},{7,15},{8,0},{9,1},... | collective-permute-start | bytes 442376 | tf_op jit(solution)/shard_map/ppermute | solution.py:135
  186.2 26.1 %collective-permute-start.48 = (bf16[192,384]{1,0:T(8,128)(2,1)S(1)}, bf16[192,384]{1,0:T(8,128)(2,1)S(1)}, u32[]{:S(2)}, u32[]{:S(2)}) collective-permute-start(bf16[192,384]{1,0:T(8,128)(2,1)S(1)} %get-tuple-element.372), channel_id=1, source_target_pairs={{0,12},{1,13},{2,14},{3,15},{4,0},{5,1},{6,2},{7,3},{8,4},{9,5},{1... | collective-permute-start | bytes 442376 | tf_op jit(solution)/shard_map/ppermute | solution.py:135
  195.6 18.5 %collective-permute-start.44 = (bf16[2,2,48,1920]{3,2,1,0:T(8,128)(2,1)S(1)}, bf16[2,2,48,1920]{3,2,1,0:T(8,128)(2,1)S(1)}, u32[]{:S(2)}, u32[]{:S(2)}) collective-permute-start(bf16[2,2,48,1920]{3,2,1,0:T(8,128)(2,1)S(1)} %fusion), channel_id=1, source_target_pairs={{0,2},{1,3},{2,0},{3,1},{4,6},{5,7},{6,4},{7,5},{8,10},{9,11},{10,... | collective-permute-start | bytes 2211848 | tf_op jit(solution)/shard_map/ppermute | solution.py:120
  197.2 18.2 %collective-permute-start.45 = (bf16[2,2,48,1920]{3,2,1,0:T(8,128)(2,1)S(1)}, bf16[2,2,48,1920]{3,2,1,0:T(8,128)(2,1)S(1)}, u32[]{:S(2)}, u32[]{:S(2)}) collective-permute-start(bf16[2,2,48,1920]{3,2,1,0:T(8,128)(2,1)S(1)} %fusion.1), channel_id=1, source_target_pairs={{0,16},{1,17},{2,18},{3,19},{4,20},{5,21},{6,22},{7,23},{8,24},{9,... | collective-permute-start | bytes 2211848 | tf_op jit(solution)/shard_map/ppermute | solution.py:120
  215.6 9.4 %collective-permute-start.49 = (bf16[2,48,1920]{2,1,0:T(8,128)(2,1)S(1)}, bf16[2,48,1920]{2,1,0:T(8,128)(2,1)S(1)}, u32[]{:S(2)}, u32[]{:S(2)}) collective-permute-start(bf16[2,48,1920]{2,1,0:T(8,128)(2,1)S(1)} %get-tuple-element.309), channel_id=1, source_target_pairs={{0,16},{1,17},{2,18},{3,19},{4,20},{5,21},{6,22},{7,23},{8,24},{9,... | collective-permute-start | bytes 1105928 | tf_op jit(solution)/shard_map/ppermute | solution.py:120
  216.2 9.1 %collective-permute-start.50 = (bf16[2,48,1920]{2,1,0:T(8,128)(2,1)S(1)}, bf16[2,48,1920]{2,1,0:T(8,128)(2,1)S(1)}, u32[]{:S(2)}, u32[]{:S(2)}) collective-permute-start(bf16[2,48,1920]{2,1,0:T(8,128)(2,1)S(1)} %get-tuple-element.310), channel_id=1, source_target_pairs={{0,2},{1,3},{2,0},{3,1},{4,6},{5,7},{6,4},{7,5},{8,10},{9,11},{10,... | collective-permute-start | bytes 1105928 | tf_op jit(solution)/shard_map/ppermute | solution.py:120
  225.6 3.8 %collective-permute-start.51 = (bf16[16,48,1152]{2,1,0:T(8,128)(2,1)S(1)}, bf16[16,48,1152]{2,1,0:T(8,128)(2,1)S(1)}, u32[]{:S(2)}, u32[]{:S(2)}) collective-permute-start(bf16[16,48,1152]{2,1,0:T(8,128)(2,1)S(1)} %get-tuple-element.316), channel_id=1, source_target_pairs={{0,1},{1,0},{2,3},{3,2},{4,5},{5,4},{6,7},{7,6},{8,9},{9,8},{10,11... | collective-permute-start | bytes 5308424 | tf_op jit(solution)/shard_map/ppermute | solution.py:98
  229.6 18.2 %collective-permute-start.52 = (bf16[2,2,48,1152]{3,2,1,0:T(8,128)(2,1)S(1)}, bf16[2,2,48,1152]{3,2,1,0:T(8,128)(2,1)S(1)}, u32[]{:S(2)}, u32[]{:S(2)}) collective-permute-start(bf16[2,2,48,1152]{3,2,1,0:T(8,128)(2,1)S(1)} %fusion.8), channel_id=1, source_target_pairs={{0,2},{1,3},{2,0},{3,1},{4,6},{5,7},{6,4},{7,5},{8,10},{9,11},{10,... | collective-permute-start | bytes 1327112 | tf_op jit(solution)/shard_map/ppermute | solution.py:120
  230.2 17.6 %collective-permute-start.53 = (bf16[2,2,48,1152]{3,2,1,0:T(8,128)(2,1)S(1)}, bf16[2,2,48,1152]{3,2,1,0:T(8,128)(2,1)S(1)}, u32[]{:S(2)}, u32[]{:S(2)}) collective-permute-start(bf16[2,2,48,1152]{3,2,1,0:T(8,128)(2,1)S(1)} %fusion.9), channel_id=1, source_target_pairs={{0,16},{1,17},{2,18},{3,19},{4,20},{5,21},{6,22},{7,23},{8,24},{9,... | collective-permute-start | bytes 1327112 | tf_op jit(solution)/shard_map/ppermute | solution.py:120
  231.8 13.3 %collective-permute-start.54 = (bf16[48,1920]{1,0:T(8,128)(2,1)S(1)}, bf16[48,1920]{1,0:T(8,128)(2,1)S(1)}, u32[]{:S(2)}, u32[]{:S(2)}) collective-permute-start(bf16[48,1920]{1,0:T(8,128)(2,1)S(1)} %get-tuple-element.332), channel_id=1, source_target_pairs={{0,4},{1,5},{2,6},{3,7},{4,8},{5,9},{6,10},{7,11},{8,12},{9,13},{1... | collective-permute-start | bytes 552968 | tf_op jit(solution)/shard_map/ppermute | solution.py:135
  232.4 15.4 %collective-permute-start.55 = (bf16[48,1920]{1,0:T(8,128)(2,1)S(1)}, bf16[48,1920]{1,0:T(8,128)(2,1)S(1)}, u32[]{:S(2)}, u32[]{:S(2)}) collective-permute-start(bf16[48,1920]{1,0:T(8,128)(2,1)S(1)} %get-tuple-element.333), channel_id=1, source_target_pairs={{0,8},{1,9},{2,10},{3,11},{4,12},{5,13},{6,14},{7,15},{8,0},{9,1},... | collective-permute-start | bytes 552968 | tf_op jit(solution)/shard_map/ppermute | solution.py:135
  233.7 14.1 %collective-permute-start.56 = (bf16[48,1920]{1,0:T(8,128)(2,1)S(1)}, bf16[48,1920]{1,0:T(8,128)(2,1)S(1)}, u32[]{:S(2)}, u32[]{:S(2)}) collective-permute-start(bf16[48,1920]{1,0:T(8,128)(2,1)S(1)} %get-tuple-element.334), channel_id=1, source_target_pairs={{0,12},{1,13},{2,14},{3,15},{4,0},{5,1},{6,2},{7,3},{8,4},{9,5},{1... | collective-permute-start | bytes 552968 | tf_op jit(solution)/shard_map/ppermute | solution.py:135
  249.0 6.4 %collective-permute-start.57 = (bf16[2,48,1152]{2,1,0:T(8,128)(2,1)}, bf16[2,48,1152]{2,1,0:T(8,128)(2,1)}, u32[]{:S(2)}, u32[]{:S(2)}) collective-permute-start(bf16[2,48,1152]{2,1,0:T(8,128)(2,1)} %get-tuple-element.381), channel_id=1, source_target_pairs={{0,16},{1,17},{2,18},{3,19},{4,20},{5,21},{6,22},{7,23},{8,24},{9,... | collective-permute-start | bytes 663560 | tf_op jit(solution)/shard_map/ppermute | solution.py:120
  249.6 6.3 %collective-permute-start.58 = (bf16[2,48,1152]{2,1,0:T(8,128)(2,1)}, bf16[2,48,1152]{2,1,0:T(8,128)(2,1)}, u32[]{:S(2)}, u32[]{:S(2)}) collective-permute-start(bf16[2,48,1152]{2,1,0:T(8,128)(2,1)} %get-tuple-element.380), channel_id=1, source_target_pairs={{0,2},{1,3},{2,0},{3,1},{4,6},{5,7},{6,4},{7,5},{8,10},{9,11},{10,... | collective-permute-start | bytes 663560 | tf_op jit(solution)/shard_map/ppermute | solution.py:120
  255.9 20.8 %collective-permute-start.59 = (bf16[512,768]{1,0:T(8,128)(2,1)}, bf16[512,768]{1,0:T(8,128)(2,1)S(1)}, u32[]{:S(2)}, u32[]{:S(2)}) collective-permute-start(bf16[512,768]{1,0:T(8,128)(2,1)} %copy-done.10), channel_id=1, source_target_pairs={{0,16},{16,0},{1,17},{17,1},{2,18},{18,2},{3,19},{19,3},{4,20},{20... | collective-permute-start | bytes 2359304 | tf_op jit(solution)/shard_map/ppermute | solution.py:1039
  259.0 12.9 %collective-permute-start.62 = (bf16[48,1152]{1,0:T(8,128)(2,1)S(1)}, bf16[48,1152]{1,0:T(8,128)(2,1)S(1)}, u32[]{:S(2)}, u32[]{:S(2)}) collective-permute-start(bf16[48,1152]{1,0:T(8,128)(2,1)S(1)} %get-tuple-element.378), channel_id=1, source_target_pairs={{0,12},{1,13},{2,14},{3,15},{4,0},{5,1},{6,2},{7,3},{8,4},{9,5},{1... | collective-permute-start | bytes 331784 | tf_op jit(solution)/shard_map/ppermute | solution.py:135
  263.0 9.7 %collective-permute-start.61 = (bf16[48,1152]{1,0:T(8,128)(2,1)S(1)}, bf16[48,1152]{1,0:T(8,128)(2,1)S(1)}, u32[]{:S(2)}, u32[]{:S(2)}) collective-permute-start(bf16[48,1152]{1,0:T(8,128)(2,1)S(1)} %get-tuple-element.377), channel_id=1, source_target_pairs={{0,8},{1,9},{2,10},{3,11},{4,12},{5,13},{6,14},{7,15},{8,0},{9,1},... | collective-permute-start | bytes 331784 | tf_op jit(solution)/shard_map/ppermute | solution.py:135
  264.8 8.0 %collective-permute-start.60 = (bf16[48,1152]{1,0:T(8,128)(2,1)S(1)}, bf16[48,1152]{1,0:T(8,128)(2,1)S(1)}, u32[]{:S(2)}, u32[]{:S(2)}) collective-permute-start(bf16[48,1152]{1,0:T(8,128)(2,1)S(1)} %get-tuple-element.379), channel_id=1, source_target_pairs={{0,4},{1,5},{2,6},{3,7},{4,8},{5,9},{6,10},{7,11},{8,12},{9,13},{1... | collective-permute-start | bytes 331784 | tf_op jit(solution)/shard_map/ppermute | solution.py:135
  266.0 3.7 %collective-permute-start.65 = (bf16[96,384]{1,0:T(8,128)(2,1)S(1)}, bf16[96,384]{1,0:T(8,128)(2,1)S(1)}, u32[]{:S(2)}, u32[]{:S(2)}) collective-permute-start(bf16[96,384]{1,0:T(8,128)(2,1)S(1)} %dynamic-slice_convert_fusion.1), channel_id=1, source_target_pairs={{0,1},{1,0},{2,3},{3,2},{4,5},{5,4},{6,7},{7,6},{8,9},{9,8},{10,11... | collective-permute-start | bytes 221192 | tf_op jit(solution)/shard_map/ppermute | solution.py:898
  (54 other events, 625.1 us)

commit v6 on v5

--- a/solution.py
+++ b/solution.py
@@ -17,7 +17,7 @@
 BF16 = jnp.bfloat16
 F32 = jnp.float32
 VMEM_BYTES = 58 * 1024 * 1024
-SPARE_BYTES = 10 * 1024 * 1024
+SPARE_BYTES = 8 * 1024 * 1024
 
 
 class Grid:

time: 282 us -> 281 us (level)
    unnamed x116 -> x114, local copies, waits for them, and re-layouts: 5.96 us -> 6.3 us
  transfers between devices with their start and end apart: 66 -> 66, of which waited for: 24 -> 23; matrix products, arithmetic and copies ran while one was open for 7% -> 6% of each run, Pallas kernels for 46% -> 47%
where the time goes in v6:
time: 281 us; the launch traced here: 277 us
  Pallas kernels  131 us (47%)
  starting transfers between devices  69.4 us (25%)
  waiting for transfers between devices  47.6 us (17%)
  other arithmetic  16.3 us (6%)
  local copies, waits for them, and re-layouts  10.1 us (4%)
    pallas_call x13, Pallas kernels, call(): pl.pallas_call(kernel, out_shape=[o for o, _ in outs], input_output_alias...  131 us
    ppermute x19, starting transfers between devices, exchange(): lax.ppermute(array, AXES, grid.shift(axis, k))  31.7 us
    ppermute x19, waiting for transfers between devices, exchange(): lax.ppermute(array, AXES, grid.shift(axis, k))  22.8 us
    ppermute x9, starting transfers between devices, scatter_steps(): lax.ppermute(total, AXES, grid.shift('z', k + 1))  15 us
    ppermute x12, starting transfers between devices, scatter_steps(): lax.ppermute(total, AXES, grid.shift(axes[step], k + 1))  11.2 us
    ppermute x12, waiting for transfers between devices, scatter_steps(): lax.ppermute(total, AXES, grid.shift(axes[step], k + 1))  7.69 us
    unnamed x114, local copies, waits for them, and re-layouts  6.3 us
  transfers between devices with their start and end apart: 66, of which 23 were waited for; matrix products, arithmetic and copies ran while one was open for 6% of the time, Pallas kernels for 47%

profile of v6, /device:TPU:0, one launch (start us, length us, event | category | flops | bytes accessed | tf_op | source)
XLA Modules:
  0.0 277.1 jit_solution(17321737866817132391)
XLA Ops:
  1.5 1.5 dynamic-slice_bitcast_fusion.2
  3.6 2.6 collective-permute-start.4
  6.2 1.6 collective-permute-start.1
  7.9 2.6 collective-permute-start.2
  10.5 1.3 collective-permute-start.3
  12.0 1.2 collective-permute-done.5
  14.3 4.6 %collective-permute-done.2 = bf16[1,48,1280]{2,1,0:T(8,128)(2,1)S(1)} collective-permute-done((bf16[1,48,1280]{2,1,0:T(8,128)(2,1)S(1)}, bf16[1,48,1280]{2,1,0:T(8,128)(2,1)S(1)}, u32[]{:S(2)}, u32[]{:S(2)}) %collective-permute-start.2) | collective-permute-done | bytes 122912 | tf_op jit(solution)/shard_map/ppermute | solution.py:69
  18.9 5.4 %collective-permute-done.4.got = bf16[512,768]{1,0:T(8,128)(2,1)S(1)} collective-permute-done((bf16[512,768]{1,0:T(8,128)(2,1)S(1)}, bf16[512,768]{1,0:T(8,128)(2,1)S(1)}, u32[]{:S(2)}, u32[]{:S(2)}) %collective-permute-start.4) | collective-permute-done | bytes 786464 | tf_op jit(solution)/shard_map/ppermute | solution.py:677
  24.3 1.8 collective-permute-start.6
  26.9 1.6 collective-permute-start.7
  29.1 3.0 %collective-permute-done.6 = bf16[2,48,1280]{2,1,0:T(8,128)(2,1)S(1)} collective-permute-done((bf16[2,48,1280]{2,1,0:T(8,128)(2,1)S(1)}, bf16[2,48,1280]{2,1,0:T(8,128)(2,1)S(1)}, u32[]{:S(2)}, u32[]{:S(2)}) %collective-permute-start.6) | collective-permute-done | bytes 245792 | tf_op jit(solution)/shard_map/ppermute | solution.py:69
  32.1 2.0 collective-permute-done.7
  34.2 1.6 collective-permute-start.8
  37.0 1.2 dynamic-slice_bitcast_fusion
  38.3 1.6 collective-permute-start.15
  39.8 2.6 collective-permute-start.16
  42.4 1.3 collective-permute-start.17
  44.5 1.4 collective-permute-done.8.refs_2_
  45.9 2.2 collective-permute-done.9.refs_3_
  48.6 3.9 %collective-permute-done.16 = bf16[1,48,1920]{2,1,0:T(8,128)(2,1)S(1)} collective-permute-done((bf16[1,48,1920]{2,1,0:T(8,128)(2,1)S(1)}, bf16[1,48,1920]{2,1,0:T(8,128)(2,1)S(1)}, u32[]{:S(2)}, u32[]{:S(2)}) %collective-permute-start.16) | collective-permute-done | bytes 184352 | tf_op jit(solution)/shard_map/ppermute | solution.py:69
  52.7 1.6 collective-permute-start.18
  56.3 4.5 %collective-permute-start.20 = (bf16[1,192,384]{2,1,0:T(8,128)(2,1)}, bf16[1,192,384]{2,1,0:T(8,128)(2,1)S(1)}, u32[]{:S(2)}, u32[]{:S(2)}) collective-permute-start(bf16[1,192,384]{2,1,0:T(8,128)(2,1)} %bitcast.277), channel_id=1, source_target_pairs={{0,4},{1,5},{2,6},{3,7},{4,8},{5,9},{6,10},{7,11},{8,12},{9,13},{1... | collective-permute-start | bytes 442376 | tf_op jit(solution)/shard_map/ppermute | solution.py:69
  60.8 1.6 collective-permute-start.21
  64.4 9.4 %shard_map.135 = (bf16[1024,2304]{1,0:T(8,128)(2,1)}, bf16[1024,768]{1,0:T(8,128)(2,1)S(1)}, f32[8,768]{1,0:T(8,128)S(1)}, bf16[768,2304]{1,0:T(8,128)(2,1)}) custom-call(s32[34]{0:T(128)S(1)} %stack.140.tab, bf16[512,768]{1,0:T(8,128)(2,1)S(1)} %get-tuple-element.318.own, bf16[512,768]{1,0:T(8,128)(2,1)S(1)} %collective-permute-done.4.got, ...), custom_call_target="tpu_custom_call" | custom-call | flops 3623878656 | bytes 15360000 | tf_op jit(solution)/shard_map/pallas_call | solution.py:601
  74.6 1.5 collective-permute-start.23
  76.5 13.9 %shard_map.136 = (bf16[2,2,256,768]{3,2,1,0:T(8,128)(2,1)S(1)}, f32[24,1,512]{2,1,0:T(1,128)S(1)}) custom-call(s32[34]{0:T(128)S(1)} %stack.140.tab, bf16[2,2,256,2304]{3,2,1,0:T(8,128)(2,1)} %bitcast.244, bf16[2,2,256,2304]{3,2,1,0:T(8,128)(2,1)} %bitcast.245, bf16[2,2,256,2304]{3,2,1,0:T(8,128)(2,1)} %bitcast.246), custom_call_target="tpu_custom_call" | custom-call | flops 3221225472 | bytes 15777792 | tf_op jit(solution)/shard_map/pallas_call | solution.py:601
  90.4 3.1 %collective-permute-done.23.refs_3_ = bf16[4,48,1920]{2,1,0:T(8,128)(2,1)S(1)} collective-permute-done((bf16[4,48,1920]{2,1,0:T(8,128)(2,1)S(1)}, bf16[4,48,1920]{2,1,0:T(8,128)(2,1)S(1)}, u32[]{:S(2)}, u32[]{:S(2)}) %collective-permute-start.23) | collective-permute-done | bytes 737312 | tf_op jit(solution)/shard_map/ppermute | solution.py:69
  93.7 1.5 collective-permute-start.29
  95.2 1.5 collective-permute-start.30
  96.7 4.7 %shard_map.137 = (f32[1024,768]{1,0:T(8,128)S(1)}, bf16[1024,768]{1,0:T(8,128)(2,1)S(1)}, bf16[768,768]{1,0:T(8,128)(2,1)}) custom-call(s32[34]{0:T(128)S(1)} %stack.140.tab, bf16[1024,768]{1,0:T(8,128)(2,1)S(1)} %bitcast.223, bf16[512,768]{1,0:T(8,128)(2,1)S(1)} %get-tuple-element.318.own, bf16[512,768]{1,0:T(8,128)(2,1)S(1)} %collective-permute-done.4.got, ...), custom_call_target="tpu_custom_call" | custom-call | flops 1207959552 | bytes 14966784 | tf_op jit(solution)/shard_map/pallas_call | solution.py:601
  101.4 7.6 %shard_map.138 = (bf16[1024,3072]{1,0:T(8,128)(2,1)}, bf16[1024,3072]{1,0:T(8,128)(2,1)}, bf16[768,3072]{1,0:T(8,128)(2,1)}) custom-call(s32[34]{0:T(128)S(1)} %stack.140.tab, bf16[1024,768]{1,0:T(8,128)(2,1)S(1)} %get-tuple-element.233.normed, bf16[4,48,1920]{2,1,0:T(8,128)(2,1)S(1)} %constant_dynamic-update-slice_fusion.6.refs_0_, ...), custom_call_target="tpu_custom_call" | custom-call | flops 2415919104 | bytes 24772608 | tf_op jit(solution)/shard_map/pallas_call | solution.py:601
  109.5 1.1 collective-permute-done.30.refs_2_
  110.6 1.5 collective-permute-start.31
  112.1 7.0 %shard_map.139 = (bf16[1024,3072]{1,0:T(8,128)(2,1)}, bf16[1024,3072]{1,0:T(8,128)(2,1)}) custom-call(s32[34]{0:T(128)S(1)} %stack.140.tab, bf16[1024,768]{1,0:T(8,128)(2,1)S(1)} %get-tuple-element.233.normed, bf16[768,3072]{1,0:T(8,128)(2,1)} %get-tuple-element.234.w_up, ...), custom_call_target="tpu_custom_call", output_to_operand_aliasing={{0}: (3, {}), {1}: (4, {})} | custom-call | flops 2415919104 | bytes 31457280 | tf_op jit(solution)/shard_map/pallas_call | solution.py:601
  119.6 8.2 %shard_map.140 = (bf16[16,192,384]{2,1,0:T(8,128)(2,1)S(1)}, bf16[16,192,384]{2,1,0:T(8,128)(2,1)S(1)}) custom-call(s32[34]{0:T(128)S(1)} %stack.140.tab, bf16[1024,3072]{1,0:T(8,128)(2,1)} %get-tuple-element.249.active, bf16[512,768]{1,0:T(8,128)(2,1)S(1)} %copy-done.4, bf16[512,768]{1,0:T(8,128)(2,1)S(1)} %collective-permute-done.27.cot_got), custom_call_target="tpu_custom_call" | custom-call | flops 4831838208 | bytes 12582912 | tf_op jit(solution)/shard_map/pallas_call | solution.py:601
  128.4 1.6 collective-permute-done.35.refs_7_
  130.4 9.4 %shard_map.141 = (bf16[1024,768]{1,0:T(8,128)(2,1)S(1)}, bf16[3072,768]{1,0:T(8,128)(2,1)}) custom-call(s32[34]{0:T(128)S(1)} %stack.140.tab, bf16[1024,3072]{1,0:T(8,128)(2,1)} %get-tuple-element.249.active, f32[1024,768]{1,0:T(8,128)S(1)} %get-tuple-element.250.hidden, bf16[4,192,384]{2,1,0:T(8,128)(2,1)S(1)} %constant_dynamic-update-slice_fusion.10.refs_0_, ...), custom_call_target="tpu_custom_call" | custom-call | flops 4831838208 | bytes 20447232 | tf_op jit(solution)/shard_map/pallas_call | solution.py:601
  141.4 1.5 collective-permute-start.41
  142.9 14.6 %shard_map.142 = (bf16[1024,3072]{1,0:T(8,128)(2,1)}, bf16[16,48,1920]{2,1,0:T(8,128)(2,1)S(1)}, bf16[16,48,1920]{2,1,0:T(8,128)(2,1)S(1)}) custom-call(s32[34]{0:T(128)S(1)} %stack.140.tab, bf16[512,768]{1,0:T(8,128)(2,1)S(1)} %copy-done.4, bf16[512,768]{1,0:T(8,128)(2,1)S(1)} %collective-permute-done.27.cot_got, ...), custom_call_target="tpu_custom_call" | custom-call | flops 9663676416 | bytes 26345472 | tf_op jit(solution)/shard_map/pallas_call | solution.py:601
  158.4 1.4 collective-permute-start.40
  159.9 15.8 %shard_map.143 = (f32[1024,768]{1,0:T(8,128)}, bf16[1024,768]{1,0:T(8,128)(2,1)S(1)}, bf16[16,48,1920]{2,1,0:T(8,128)(2,1)S(1)}, bf16[16,48,1920]{2,1,0:T(8,128)(2,1)S(1)}) custom-call(s32[34]{0:T(128)S(1)} %stack.140.tab, bf16[1024,3072]{1,0:T(8,128)(2,1)} %get-tuple-element.269.grad_up, ...), custom_call_target="tpu_custom_call", output_to_operand_aliasing={{2}: (7, {}), {3}: (8, {})} | custom-call | flops 7247757312 | bytes 35020800 | tf_op jit(solution)/shard_map/pallas_call | solution.py:601
  176.5 1.5 collective-permute-start.43
  179.1 2.8 collective-permute-start.46
  181.9 2.1 collective-permute-start.47
  184.3 9.0 %shard_map.144 = (bf16[2,2,256,256]{3,2,1,0:T(8,128)(2,1)}, bf16[2,2,256,256]{3,2,1,0:T(8,128)(2,1)}, bf16[2,2,256,256]{3,2,1,0:T(8,128)(2,1)}) custom-call(s32[34]{0:T(128)S(1)} %stack.140.tab, bf16[2,2,256,2304]{3,2,1,0:T(8,128)(2,1)} %bitcast.247, bf16[2,2,256,2304]{3,2,1,0:T(8,128)(2,1)} %bitcast.248, bf16[2,2,256,2304]{3,2,1,0:T(8,128)(2,1)} %bitcast.249, ...), custom_call_target="tpu_custom_call" | custom-call | flops 4026531840 | bytes 18923520 | tf_op jit(solution)/shard_map/pallas_call | solution.py:601
  194.1 1.5 collective-permute-start.44
  196.2 15.3 %shard_map.145 = (bf16[2,2,256,512]{3,2,1,0:T(8,128)(2,1)}, bf16[2,2,256,512]{3,2,1,0:T(8,128)(2,1)}, bf16[2,2,256,512]{3,2,1,0:T(8,128)(2,1)}) custom-call(s32[34]{0:T(128)S(1)} %stack.140.tab, bf16[2,2,256,2304]{3,2,1,0:T(8,128)(2,1)} %bitcast.250, bf16[2,2,256,2304]{3,2,1,0:T(8,128)(2,1)} %bitcast.251, bf16[2,2,256,2304]{3,2,1,0:T(8,128)(2,1)} %bitcast.252, ...), custom_call_target="tpu_custom_call" | custom-call | flops 8053063680 | bytes 20496384 | tf_op jit(solution)/shard_map/pallas_call | solution.py:601
  214.9 7.0 %shard_map.146 = (bf16[16,48,1152]{2,1,0:T(8,128)(2,1)S(1)}, bf16[16,48,1152]{2,1,0:T(8,128)(2,1)S(1)}) custom-call(s32[34]{0:T(128)S(1)} %stack.140.tab, bf16[1024,768]{1,0:T(8,128)(2,1)S(1)} %get-tuple-element.300.normed, bf16[1024,256]{1,0:T(8,128)(2,1)} %bitcast.281, bf16[1024,256]{1,0:T(8,128)(2,1)} %bitcast.283, bf16[1024,256]{1,0:T(8,128)(2,1)} %bitcast.285, ...), custom_call_target="tpu_custom_call" | custom-call | flops 3623878656 | bytes 9830400 | tf_op jit(solution)/shard_map/pallas_call | solution.py:601
  223.3 3.7 %collective-permute-done.51 = bf16[16,48,1152]{2,1,0:T(8,128)(2,1)S(1)} collective-permute-done((bf16[16,48,1152]{2,1,0:T(8,128)(2,1)S(1)}, bf16[16,48,1152]{2,1,0:T(8,128)(2,1)S(1)}, u32[]{:S(2)}, u32[]{:S(2)}) %collective-permute-start.51) | collective-permute-done | bytes 1769504 | tf_op jit(solution)/shard_map/ppermute | solution.py:98
  228.0 1.4 collective-permute-start.53
  231.1 2.0 collective-permute-start.56
  233.2 9.2 %shard_map.147 = (bf16[512,768]{1,0:T(8,128)(2,1)S(1)}, bf16[512,768]{1,0:T(8,128)(2,1)S(1)}) custom-call(s32[34]{0:T(128)S(1)} %stack.140.tab, bf16[512,768]{1,0:T(8,128)(2,1)S(1)} %get-tuple-element.318.own, bf16[512,768]{1,0:T(8,128)(2,1)S(1)} %copy-done.8, f32[8,768]{1,0:T(8,128)S(1)} %get-tuple-element.221.gains, ...), custom_call_target="tpu_custom_call" | custom-call | flops 3623878656 | bytes 14573568 | tf_op jit(solution)/shard_map/pallas_call | solution.py:601
  242.5 2.8 %collective-permute-done.55 = bf16[48,1920]{1,0:T(8,128)(2,1)S(1)} collective-permute-done((bf16[48,1920]{1,0:T(8,128)(2,1)S(1)}, bf16[48,1920]{1,0:T(8,128)(2,1)S(1)}, u32[]{:S(2)}, u32[]{:S(2)}) %collective-permute-start.55) | collective-permute-done | bytes 184352 | tf_op jit(solution)/shard_map/ppermute | solution.py:135
  247.3 1.4 collective-permute-start.58
  248.7 5.0 %collective-permute-done.57 = bf16[2,48,1152]{2,1,0:T(8,128)(2,1)} collective-permute-done((bf16[2,48,1152]{2,1,0:T(8,128)(2,1)}, bf16[2,48,1152]{2,1,0:T(8,128)(2,1)}, u32[]{:S(2)}, u32[]{:S(2)}) %collective-permute-start.57) | collective-permute-done | bytes 221216 | tf_op jit(solution)/shard_map/ppermute | solution.py:120
  253.9 1.7 collective-permute-start.59
  255.6 1.5 fusion.25
  257.2 3.2 %collective-permute-start.62 = (bf16[48,1152]{1,0:T(8,128)(2,1)S(1)}, bf16[48,1152]{1,0:T(8,128)(2,1)S(1)}, u32[]{:S(2)}, u32[]{:S(2)}) collective-permute-start(bf16[48,1152]{1,0:T(8,128)(2,1)S(1)} %get-tuple-element.378), channel_id=1, source_target_pairs={{0,12},{1,13},{2,14},{3,15},{4,0},{5,1},{6,2},{7,3},{8,4},{9,5},{1... | collective-permute-start | bytes 331784 | tf_op jit(solution)/shard_map/ppermute | solution.py:135
  260.4 2.7 collective-permute-start.61
  265.5 1.3 fusion.14
  266.8 1.2 maximum_bitcast_fusion
  270.3 1.2 collective-permute-done.61
  271.5 1.2 fusion.29
  275.6 1.2 maximum_bitcast_fusion.1
  (255 shorter events, 36.3 us)
Async XLA Ops:
  3.1 3.1 %collective-permute-start = (bf16[24,1280]{1,0:T(8,128)(2,1)S(1)}, bf16[24,1280]{1,0:T(8,128)(2,1)S(1)}, u32[]{:S(2)}, u32[]{:S(2)}) collective-permute-start(bf16[24,1280]{1,0:T(8,128)(2,1)S(1)} %fusion.32), channel_id=1, source_target_pairs={{0,1},{1,0},{2,3},{3,2},{4,5},{5,4},{6,7},{7,6},{8,9},{9,8},{10,11... | collective-permute-start | bytes 184328 | tf_op jit(solution)/shard_map/ppermute | solution.py:671
  3.6 20.7 %collective-permute-start.4 = (bf16[512,768]{1,0:T(8,128)(2,1)S(1)}, bf16[512,768]{1,0:T(8,128)(2,1)S(1)}, u32[]{:S(2)}, u32[]{:S(2)}) collective-permute-start(bf16[512,768]{1,0:T(8,128)(2,1)S(1)} %get-tuple-element.187), channel_id=1, source_target_pairs={{0,16},{16,0},{1,17},{17,1},{2,18},{18,2},{3,19},{19,3},{4,20},{20... | collective-permute-start | bytes 2359304 | tf_op jit(solution)/shard_map/ppermute | solution.py:677
  6.2 8.1 %collective-permute-start.1 = (bf16[1,48,1280]{2,1,0:T(8,128)(2,1)S(1)}, bf16[1,48,1280]{2,1,0:T(8,128)(2,1)S(1)}, u32[]{:S(2)}, u32[]{:S(2)}) collective-permute-start(bf16[1,48,1280]{2,1,0:T(8,128)(2,1)S(1)} %bitcast.268), channel_id=1, source_target_pairs={{0,4},{1,5},{2,6},{3,7},{4,8},{5,9},{6,10},{7,11},{8,12},{9,13},{1... | collective-permute-start | bytes 368648 | tf_op jit(solution)/shard_map/ppermute | solution.py:69
  7.9 11.0 %collective-permute-start.2 = (bf16[1,48,1280]{2,1,0:T(8,128)(2,1)S(1)}, bf16[1,48,1280]{2,1,0:T(8,128)(2,1)S(1)}, u32[]{:S(2)}, u32[]{:S(2)}) collective-permute-start(bf16[1,48,1280]{2,1,0:T(8,128)(2,1)S(1)} %bitcast.269), channel_id=1, source_target_pairs={{0,8},{1,9},{2,10},{3,11},{4,12},{5,13},{6,14},{7,15},{8,0},{9,1},... | collective-permute-start | bytes 368648 | tf_op jit(solution)/shard_map/ppermute | solution.py:69
  10.5 8.5 %collective-permute-start.3 = (bf16[1,48,1280]{2,1,0:T(8,128)(2,1)S(1)}, bf16[1,48,1280]{2,1,0:T(8,128)(2,1)S(1)}, u32[]{:S(2)}, u32[]{:S(2)}) collective-permute-start(bf16[1,48,1280]{2,1,0:T(8,128)(2,1)S(1)} %bitcast.270), channel_id=1, source_target_pairs={{0,12},{1,13},{2,14},{3,15},{4,0},{5,1},{6,2},{7,3},{8,4},{9,5},{1... | collective-permute-start | bytes 368648 | tf_op jit(solution)/shard_map/ppermute | solution.py:69
  11.9 1.4 collective-permute-start.5
  13.2 29.2 %collective-permute-start.10 = (bf16[96,384]{1,0:T(8,128)(2,1)S(1)}, bf16[96,384]{1,0:T(8,128)(2,1)S(1)}, u32[]{:S(2)}, u32[]{:S(2)}) collective-permute-start(bf16[96,384]{1,0:T(8,128)(2,1)S(1)} %constant_dynamic-slice_fusion), channel_id=1, source_target_pairs={{0,1},{1,0},{2,3},{3,2},{4,5},{5,4},{6,7},{7,6},{8,9},{9,8},{10,11... | collective-permute-start | bytes 221192 | tf_op jit(solution)/shard_map/ppermute | solution.py:671
  24.3 7.8 %collective-permute-start.6 = (bf16[2,48,1280]{2,1,0:T(8,128)(2,1)S(1)}, bf16[2,48,1280]{2,1,0:T(8,128)(2,1)S(1)}, u32[]{:S(2)}, u32[]{:S(2)}) collective-permute-start(bf16[2,48,1280]{2,1,0:T(8,128)(2,1)S(1)} %pad_maximum_fusion.2), channel_id=1, source_target_pairs={{0,16},{1,17},{2,18},{3,19},{4,20},{5,21},{6,22},{7,23},{8,24},{9,... | collective-permute-start | bytes 737288 | tf_op jit(solution)/shard_map/ppermute | solution.py:69
  26.9 7.3 %collective-permute-start.7 = (bf16[2,48,1280]{2,1,0:T(8,128)(2,1)S(1)}, bf16[2,48,1280]{2,1,0:T(8,128)(2,1)S(1)}, u32[]{:S(2)}, u32[]{:S(2)}) collective-permute-start(bf16[2,48,1280]{2,1,0:T(8,128)(2,1)S(1)} %pad_maximum_fusion.3), channel_id=1, source_target_pairs={{0,2},{1,3},{2,0},{3,1},{4,6},{5,7},{6,4},{7,5},{8,10},{9,11},{10,... | collective-permute-start | bytes 737288 | tf_op jit(solution)/shard_map/ppermute | solution.py:69
  34.2 11.8 %collective-permute-start.8 = (bf16[4,48,1280]{2,1,0:T(8,128)(2,1)S(1)}, bf16[4,48,1280]{2,1,0:T(8,128)(2,1)}, u32[]{:S(2)}, u32[]{:S(2)}) collective-permute-start(bf16[4,48,1280]{2,1,0:T(8,128)(2,1)S(1)} %constant_dynamic-update-slice_fusion.refs_0_), channel_id=1, source_target_pairs={{0,2},{1,3},{2,0},{3,1},{4,6},{5,7},{6,4},{7,5},{8,10},{9,11},{10,... | collective-permute-start | bytes 1474568 | tf_op jit(solution)/shard_map/ppermute | solution.py:69
  36.5 11.6 %collective-permute-start.9 = (bf16[4,48,1280]{2,1,0:T(8,128)(2,1)}, bf16[4,48,1280]{2,1,0:T(8,128)(2,1)}, u32[]{:S(2)}, u32[]{:S(2)}) collective-permute-start(bf16[4,48,1280]{2,1,0:T(8,128)(2,1)} %constant_dynamic-update-slice_fusion.3.refs_1_), channel_id=1, source_target_pairs={{0,16},{1,17},{2,18},{3,19},{4,20},{5,21},{6,22},{7,23},{8,24},{9,... | collective-permute-start | bytes 1474568 | tf_op jit(solution)/shard_map/ppermute | solution.py:69
  38.3 10.4 %collective-permute-start.15 = (bf16[1,48,1920]{2,1,0:T(8,128)(2,1)S(1)}, bf16[1,48,1920]{2,1,0:T(8,128)(2,1)S(1)}, u32[]{:S(2)}, u32[]{:S(2)}) collective-permute-start(bf16[1,48,1920]{2,1,0:T(8,128)(2,1)S(1)} %bitcast.273), channel_id=1, source_target_pairs={{0,4},{1,5},{2,6},{3,7},{4,8},{5,9},{6,10},{7,11},{8,12},{9,13},{1... | collective-permute-start | bytes 552968 | tf_op jit(solution)/shard_map/ppermute | solution.py:69
  39.8 12.7 %collective-permute-start.16 = (bf16[1,48,1920]{2,1,0:T(8,128)(2,1)S(1)}, bf16[1,48,1920]{2,1,0:T(8,128)(2,1)S(1)}, u32[]{:S(2)}, u32[]{:S(2)}) collective-permute-start(bf16[1,48,1920]{2,1,0:T(8,128)(2,1)S(1)} %bitcast.274), channel_id=1, source_target_pairs={{0,8},{1,9},{2,10},{3,11},{4,12},{5,13},{6,14},{7,15},{8,0},{9,1},... | collective-permute-start | bytes 552968 | tf_op jit(solution)/shard_map/ppermute | solution.py:69
  42.4 10.1 %collective-permute-start.17 = (bf16[1,48,1920]{2,1,0:T(8,128)(2,1)S(1)}, bf16[1,48,1920]{2,1,0:T(8,128)(2,1)S(1)}, u32[]{:S(2)}, u32[]{:S(2)}) collective-permute-start(bf16[1,48,1920]{2,1,0:T(8,128)(2,1)S(1)} %bitcast.275), channel_id=1, source_target_pairs={{0,12},{1,13},{2,14},{3,15},{4,0},{5,1},{6,2},{7,3},{8,4},{9,5},{1... | collective-permute-start | bytes 552968 | tf_op jit(solution)/shard_map/ppermute | solution.py:69
  48.1 6.1 %collective-permute-start.11 = (bf16[4,48,1280]{2,1,0:T(8,128)(2,1)S(1)}, bf16[4,48,1280]{2,1,0:T(8,128)(2,1)S(1)}, u32[]{:S(2)}, u32[]{:S(2)}) collective-permute-start(bf16[4,48,1280]{2,1,0:T(8,128)(2,1)S(1)} %constant_dynamic-update-slice_fusion.refs_0_), channel_id=1, source_target_pairs={{0,1},{1,0},{2,3},{3,2},{4,5},{5,4},{6,7},{7,6},{8,9},{9,8},{10,11... | collective-permute-start | bytes 1474568 | tf_op jit(solution)/shard_map/ppermute | solution.py:706
  48.1 8.2 %collective-permute-start.12 = (bf16[4,48,1280]{2,1,0:T(8,128)(2,1)}, bf16[4,48,1280]{2,1,0:T(8,128)(2,1)}, u32[]{:S(2)}, u32[]{:S(2)}) collective-permute-start(bf16[4,48,1280]{2,1,0:T(8,128)(2,1)} %constant_dynamic-update-slice_fusion.3.refs_1_), channel_id=1, source_target_pairs={{0,1},{1,0},{2,3},{3,2},{4,5},{5,4},{6,7},{7,6},{8,9},{9,8},{10,11... | collective-permute-start | bytes 1474568 | tf_op jit(solution)/shard_map/ppermute | solution.py:706
  48.6 12.2 %collective-permute-start.13 = (bf16[4,48,1280]{2,1,0:T(8,128)(2,1)}, bf16[4,48,1280]{2,1,0:T(8,128)(2,1)}, u32[]{:S(2)}, u32[]{:S(2)}) collective-permute-start(bf16[4,48,1280]{2,1,0:T(8,128)(2,1)} %collective-permute-done.8.refs_2_), channel_id=1, source_target_pairs={{0,1},{1,0},{2,3},{3,2},{4,5},{5,4},{6,7},{7,6},{8,9},{9,8},{10,11... | collective-permute-start | bytes 1474568 | tf_op jit(solution)/shard_map/ppermute | solution.py:706
  52.6 9.8 %collective-permute-start.14 = (bf16[4,48,1280]{2,1,0:T(8,128)(2,1)}, bf16[4,48,1280]{2,1,0:T(8,128)(2,1)}, u32[]{:S(2)}, u32[]{:S(2)}) collective-permute-start(bf16[4,48,1280]{2,1,0:T(8,128)(2,1)} %collective-permute-done.9.refs_3_), channel_id=1, source_target_pairs={{0,1},{1,0},{2,3},{3,2},{4,5},{5,4},{6,7},{7,6},{8,9},{9,8},{10,11... | collective-permute-start | bytes 1474568 | tf_op jit(solution)/shard_map/ppermute | solution.py:706
  52.7 21.2 %collective-permute-start.18 = (bf16[4,48,1920]{2,1,0:T(8,128)(2,1)S(1)}, bf16[4,48,1920]{2,1,0:T(8,128)(2,1)S(1)}, u32[]{:S(2)}, u32[]{:S(2)}) collective-permute-start(bf16[4,48,1920]{2,1,0:T(8,128)(2,1)S(1)} %constant_dynamic-update-slice_fusion.6.refs_0_), channel_id=1, source_target_pairs={{0,16},{1,17},{2,18},{3,19},{4,20},{5,21},{6,22},{7,23},{8,24},{9,... | collective-permute-start | bytes 2211848 | tf_op jit(solution)/shard_map/ppermute | solution.py:69
  55.0 18.8 %collective-permute-start.19 = (bf16[4,48,1920]{2,1,0:T(8,128)(2,1)S(1)}, bf16[4,48,1920]{2,1,0:T(8,128)(2,1)}, u32[]{:S(2)}, u32[]{:S(2)}) collective-permute-start(bf16[4,48,1920]{2,1,0:T(8,128)(2,1)S(1)} %constant_dynamic-update-slice_fusion.6.refs_0_), channel_id=1, source_target_pairs={{0,2},{1,3},{2,0},{3,1},{4,6},{5,7},{6,4},{7,5},{8,10},{9,11},{10,... | collective-permute-start | bytes 2211848 | tf_op jit(solution)/shard_map/ppermute | solution.py:69
  56.3 17.5 %collective-permute-start.20 = (bf16[1,192,384]{2,1,0:T(8,128)(2,1)}, bf16[1,192,384]{2,1,0:T(8,128)(2,1)S(1)}, u32[]{:S(2)}, u32[]{:S(2)}) collective-permute-start(bf16[1,192,384]{2,1,0:T(8,128)(2,1)} %bitcast.277), channel_id=1, source_target_pairs={{0,4},{1,5},{2,6},{3,7},{4,8},{5,9},{6,10},{7,11},{8,12},{9,13},{1... | collective-permute-start | bytes 442376 | tf_op jit(solution)/shard_map/ppermute | solution.py:69
  60.8 13.1 %collective-permute-start.21 = (bf16[1,192,384]{2,1,0:T(8,128)(2,1)}, bf16[1,192,384]{2,1,0:T(8,128)(2,1)S(1)}, u32[]{:S(2)}, u32[]{:S(2)}) collective-permute-start(bf16[1,192,384]{2,1,0:T(8,128)(2,1)} %bitcast.278), channel_id=1, source_target_pairs={{0,8},{1,9},{2,10},{3,11},{4,12},{5,13},{6,14},{7,15},{8,0},{9,1},... | collective-permute-start | bytes 442376 | tf_op jit(solution)/shard_map/ppermute | solution.py:69
  62.4 11.4 %collective-permute-start.22 = (bf16[1,192,384]{2,1,0:T(8,128)(2,1)}, bf16[1,192,384]{2,1,0:T(8,128)(2,1)S(1)}, u32[]{:S(2)}, u32[]{:S(2)}) collective-permute-start(bf16[1,192,384]{2,1,0:T(8,128)(2,1)} %bitcast.279), channel_id=1, source_target_pairs={{0,12},{1,13},{2,14},{3,15},{4,0},{5,1},{6,2},{7,3},{8,4},{9,5},{1... | collective-permute-start | bytes 442376 | tf_op jit(solution)/shard_map/ppermute | solution.py:69
  73.9 19.6 %collective-permute-start.27 = (bf16[512,768]{1,0:T(8,128)(2,1)S(1)}, bf16[512,768]{1,0:T(8,128)(2,1)S(1)}, u32[]{:S(2)}, u32[]{:S(2)}) collective-permute-start(bf16[512,768]{1,0:T(8,128)(2,1)S(1)} %copy-done.17), channel_id=1, source_target_pairs={{0,16},{16,0},{1,17},{17,1},{2,18},{18,2},{3,19},{19,3},{4,20},{20... | collective-permute-start | bytes 2359304 | tf_op jit(solution)/shard_map/ppermute | solution.py:775
  74.6 15.8 %collective-permute-start.24 = (bf16[4,48,1920]{2,1,0:T(8,128)(2,1)S(1)}, bf16[4,48,1920]{2,1,0:T(8,128)(2,1)S(1)}, u32[]{:S(2)}, u32[]{:S(2)}) collective-permute-start(bf16[4,48,1920]{2,1,0:T(8,128)(2,1)S(1)} %constant_dynamic-update-slice_fusion.6.refs_0_), channel_id=1, source_target_pairs={{0,1},{1,0},{2,3},{3,2},{4,5},{5,4},{6,7},{7,6},{8,9},{9,8},{10,11... | collective-permute-start | bytes 2211848 | tf_op jit(solution)/shard_map/ppermute | solution.py:698
  74.6 18.9 %collective-permute-start.23 = (bf16[4,48,1920]{2,1,0:T(8,128)(2,1)S(1)}, bf16[4,48,1920]{2,1,0:T(8,128)(2,1)S(1)}, u32[]{:S(2)}, u32[]{:S(2)}) collective-permute-start(bf16[4,48,1920]{2,1,0:T(8,128)(2,1)S(1)} %collective-permute-done.18.refs_1_), channel_id=1, source_target_pairs={{0,2},{1,3},{2,0},{3,1},{4,6},{5,7},{6,4},{7,5},{8,10},{9,11},{10,... | collective-permute-start | bytes 2211848 | tf_op jit(solution)/shard_map/ppermute | solution.py:69
  76.0 17.4 %collective-permute-start.25 = (bf16[4,48,1920]{2,1,0:T(8,128)(2,1)S(1)}, bf16[4,48,1920]{2,1,0:T(8,128)(2,1)S(1)}, u32[]{:S(2)}, u32[]{:S(2)}) collective-permute-start(bf16[4,48,1920]{2,1,0:T(8,128)(2,1)S(1)} %collective-permute-done.18.refs_1_), channel_id=1, source_target_pairs={{0,1},{1,0},{2,3},{3,2},{4,5},{5,4},{6,7},{7,6},{8,9},{9,8},{10,11... | collective-permute-start | bytes 2211848 | tf_op jit(solution)/shard_map/ppermute | solution.py:698
  76.2 17.2 %collective-permute-start.26 = (bf16[4,48,1920]{2,1,0:T(8,128)(2,1)}, bf16[4,48,1920]{2,1,0:T(8,128)(2,1)S(1)}, u32[]{:S(2)}, u32[]{:S(2)}) collective-permute-start(bf16[4,48,1920]{2,1,0:T(8,128)(2,1)} %collective-permute-done.19.refs_2_), channel_id=1, source_target_pairs={{0,1},{1,0},{2,3},{3,2},{4,5},{5,4},{6,7},{7,6},{8,9},{9,8},{10,11... | collective-permute-start | bytes 2211848 | tf_op jit(solution)/shard_map/ppermute | solution.py:698
  93.5 3.2 %collective-permute-start.28 = (bf16[4,48,1920]{2,1,0:T(8,128)(2,1)S(1)}, bf16[4,48,1920]{2,1,0:T(8,128)(2,1)S(1)}, u32[]{:S(2)}, u32[]{:S(2)}) collective-permute-start(bf16[4,48,1920]{2,1,0:T(8,128)(2,1)S(1)} %collective-permute-done.23.refs_3_), channel_id=1, source_target_pairs={{0,1},{1,0},{2,3},{3,2},{4,5},{5,4},{6,7},{7,6},{8,9},{9,8},{10,11... | collective-permute-start | bytes 2211848 | tf_op jit(solution)/shard_map/ppermute | solution.py:698
  93.7 15.8 %collective-permute-start.29 = (bf16[4,192,384]{2,1,0:T(8,128)(2,1)S(1)}, bf16[4,192,384]{2,1,0:T(8,128)(2,1)S(1)}, u32[]{:S(2)}, u32[]{:S(2)}) collective-permute-start(bf16[4,192,384]{2,1,0:T(8,128)(2,1)S(1)} %constant_dynamic-update-slice_fusion.10.refs_0_), channel_id=1, source_target_pairs={{0,16},{1,17},{2,18},{3,19},{4,20},{5,21},{6,22},{7,23},{8,24},{9,... | collective-permute-start | bytes 1769480 | tf_op jit(solution)/shard_map/ppermute | solution.py:69
  95.2 15.4 %collective-permute-start.30 = (bf16[4,192,384]{2,1,0:T(8,128)(2,1)S(1)}, bf16[4,192,384]{2,1,0:T(8,128)(2,1)S(1)}, u32[]{:S(2)}, u32[]{:S(2)}) collective-permute-start(bf16[4,192,384]{2,1,0:T(8,128)(2,1)S(1)} %constant_dynamic-update-slice_fusion.10.refs_0_), channel_id=1, source_target_pairs={{0,2},{1,3},{2,0},{3,1},{4,6},{5,7},{6,4},{7,5},{8,10},{9,11},{10,... | collective-permute-start | bytes 1769480 | tf_op jit(solution)/shard_map/ppermute | solution.py:69
  110.6 17.2 %collective-permute-start.31 = (bf16[4,192,384]{2,1,0:T(8,128)(2,1)S(1)}, bf16[4,192,384]{2,1,0:T(8,128)(2,1)S(1)}, u32[]{:S(2)}, u32[]{:S(2)}) collective-permute-start(bf16[4,192,384]{2,1,0:T(8,128)(2,1)S(1)} %collective-permute-done.29.refs_1_), channel_id=1, source_target_pairs={{0,2},{1,3},{2,0},{3,1},{4,6},{5,7},{6,4},{7,5},{8,10},{9,11},{10,... | collective-permute-start | bytes 1769480 | tf_op jit(solution)/shard_map/ppermute | solution.py:69
  119.1 8.7 %collective-permute-start.32 = (bf16[4,192,384]{2,1,0:T(8,128)(2,1)S(1)}, bf16[4,192,384]{2,1,0:T(8,128)(2,1)S(1)}, u32[]{:S(2)}, u32[]{:S(2)}) collective-permute-start(bf16[4,192,384]{2,1,0:T(8,128)(2,1)S(1)} %constant_dynamic-update-slice_fusion.10.refs_0_), channel_id=1, source_target_pairs={{0,1},{1,0},{2,3},{3,2},{4,5},{5,4},{6,7},{7,6},{8,9},{9,8},{10,11... | collective-permute-start | bytes 1769480 | tf_op jit(solution)/shard_map/ppermute | solution.py:698
  119.1 8.7 %collective-permute-start.33 = (bf16[4,192,384]{2,1,0:T(8,128)(2,1)S(1)}, bf16[4,192,384]{2,1,0:T(8,128)(2,1)S(1)}, u32[]{:S(2)}, u32[]{:S(2)}) collective-permute-start(bf16[4,192,384]{2,1,0:T(8,128)(2,1)S(1)} %collective-permute-done.29.refs_1_), channel_id=1, source_target_pairs={{0,1},{1,0},{2,3},{3,2},{4,5},{5,4},{6,7},{7,6},{8,9},{9,8},{10,11... | collective-permute-start | bytes 1769480 | tf_op jit(solution)/shard_map/ppermute | solution.py:698
  119.6 8.2 %collective-permute-start.34 = (bf16[4,192,384]{2,1,0:T(8,128)(2,1)S(1)}, bf16[4,192,384]{2,1,0:T(8,128)(2,1)S(1)}, u32[]{:S(2)}, u32[]{:S(2)}) collective-permute-start(bf16[4,192,384]{2,1,0:T(8,128)(2,1)S(1)} %collective-permute-done.30.refs_2_), channel_id=1, source_target_pairs={{0,1},{1,0},{2,3},{3,2},{4,5},{5,4},{6,7},{7,6},{8,9},{9,8},{10,11... | collective-permute-start | bytes 1769480 | tf_op jit(solution)/shard_map/ppermute | solution.py:698
  127.9 2.2 collective-permute-start.35
  130.1 9.8 %collective-permute-start.36 = (bf16[16,192,384]{2,1,0:T(8,128)(2,1)S(1)}, bf16[16,192,384]{2,1,0:T(8,128)(2,1)S(1)}, u32[]{:S(2)}, u32[]{:S(2)}) collective-permute-start(bf16[16,192,384]{2,1,0:T(8,128)(2,1)S(1)} %get-tuple-element.259), channel_id=1, source_target_pairs={{0,1},{1,0},{2,3},{3,2},{4,5},{5,4},{6,7},{7,6},{8,9},{9,8},{10,11... | collective-permute-start | bytes 7077896 | tf_op jit(solution)/shard_map/ppermute | solution.py:98
  140.2 17.3 %collective-permute-start.37 = (bf16[2,2,192,384]{3,2,1,0:T(8,128)(2,1)S(1)}, bf16[2,2,192,384]{3,2,1,0:T(8,128)(2,1)S(1)}, u32[]{:S(2)}, u32[]{:S(2)}) collective-permute-start(bf16[2,2,192,384]{3,2,1,0:T(8,128)(2,1)S(1)} %fusion.4), channel_id=1, source_target_pairs={{0,2},{1,3},{2,0},{3,1},{4,6},{5,7},{6,4},{7,5},{8,10},{9,11},{10,... | collective-permute-start | bytes 1769480 | tf_op jit(solution)/shard_map/ppermute | solution.py:120
  140.7 16.7 %collective-permute-start.38 = (bf16[2,2,192,384]{3,2,1,0:T(8,128)(2,1)S(1)}, bf16[2,2,192,384]{3,2,1,0:T(8,128)(2,1)S(1)}, u32[]{:S(2)}, u32[]{:S(2)}) collective-permute-start(bf16[2,2,192,384]{3,2,1,0:T(8,128)(2,1)S(1)} %fusion.5), channel_id=1, source_target_pairs={{0,16},{1,17},{2,18},{3,19},{4,20},{5,21},{6,22},{7,23},{8,24},{9,... | collective-permute-start | bytes 1769480 | tf_op jit(solution)/shard_map/ppermute | solution.py:120
  141.4 34.3 %collective-permute-start.41 = (bf16[256,768]{1,0:T(8,128)(2,1)S(1)}, bf16[256,768]{1,0:T(8,128)(2,1)S(1)}, u32[]{:S(2)}, u32[]{:S(2)}) collective-permute-start(bf16[256,768]{1,0:T(8,128)(2,1)S(1)} %get-tuple-element.387), channel_id=1, source_target_pairs={{0,16},{16,0},{1,17},{17,1},{2,18},{18,2},{3,19},{19,3},{4,20},{20... | collective-permute-start | bytes 1179656 | tf_op jit(solution)/shard_map/ppermute | solution.py:946
  157.7 18.0 %collective-permute-start.39 = (bf16[2,192,384]{2,1,0:T(8,128)(2,1)S(1)}, bf16[2,192,384]{2,1,0:T(8,128)(2,1)S(1)}, u32[]{:S(2)}, u32[]{:S(2)}) collective-permute-start(bf16[2,192,384]{2,1,0:T(8,128)(2,1)S(1)} %get-tuple-element.376), channel_id=1, source_target_pairs={{0,16},{1,17},{2,18},{3,19},{4,20},{5,21},{6,22},{7,23},{8,24},{9,... | collective-permute-start | bytes 884744 | tf_op jit(solution)/shard_map/ppermute | solution.py:120
  158.4 17.3 %collective-permute-start.40 = (bf16[2,192,384]{2,1,0:T(8,128)(2,1)S(1)}, bf16[2,192,384]{2,1,0:T(8,128)(2,1)S(1)}, u32[]{:S(2)}, u32[]{:S(2)}) collective-permute-start(bf16[2,192,384]{2,1,0:T(8,128)(2,1)S(1)} %get-tuple-element.375), channel_id=1, source_target_pairs={{0,2},{1,3},{2,0},{3,1},{4,6},{5,7},{6,4},{7,5},{8,10},{9,11},{10,... | collective-permute-start | bytes 884744 | tf_op jit(solution)/shard_map/ppermute | solution.py:120
  176.5 16.9 %collective-permute-start.42 = (bf16[16,48,1920]{2,1,0:T(8,128)(2,1)S(1)}, bf16[16,48,1920]{2,1,0:T(8,128)(2,1)S(1)}, u32[]{:S(2)}, u32[]{:S(2)}) collective-permute-start(bf16[16,48,1920]{2,1,0:T(8,128)(2,1)S(1)} %get-tuple-element.285), channel_id=1, source_target_pairs={{0,1},{1,0},{2,3},{3,2},{4,5},{5,4},{6,7},{7,6},{8,9},{9,8},{10,11... | collective-permute-start | bytes 8847368 | tf_op jit(solution)/shard_map/ppermute | solution.py:98
  176.5 16.9 %collective-permute-start.43 = (bf16[256,768]{1,0:T(8,128)(2,1)S(1)}, bf16[256,768]{1,0:T(8,128)(2,1)S(1)}, u32[]{:S(2)}, u32[]{:S(2)}) collective-permute-start(bf16[256,768]{1,0:T(8,128)(2,1)S(1)} %get-tuple-element.286), channel_id=1, source_target_pairs={{0,16},{16,0},{1,17},{17,1},{2,18},{18,2},{3,19},{19,3},{4,20},{20... | collective-permute-start | bytes 1179656 | tf_op jit(solution)/shard_map/ppermute | solution.py:965
  179.1 32.3 %collective-permute-start.46 = (bf16[192,384]{1,0:T(8,128)(2,1)S(1)}, bf16[192,384]{1,0:T(8,128)(2,1)S(1)}, u32[]{:S(2)}, u32[]{:S(2)}) collective-permute-start(bf16[192,384]{1,0:T(8,128)(2,1)S(1)} %get-tuple-element.374), channel_id=1, source_target_pairs={{0,4},{1,5},{2,6},{3,7},{4,8},{5,9},{6,10},{7,11},{8,12},{9,13},{1... | collective-permute-start | bytes 442376 | tf_op jit(solution)/shard_map/ppermute | solution.py:135
  181.9 29.6 %collective-permute-start.47 = (bf16[192,384]{1,0:T(8,128)(2,1)S(1)}, bf16[192,384]{1,0:T(8,128)(2,1)S(1)}, u32[]{:S(2)}, u32[]{:S(2)}) collective-permute-start(bf16[192,384]{1,0:T(8,128)(2,1)S(1)} %get-tuple-element.373), channel_id=1, source_target_pairs={{0,8},{1,9},{2,10},{3,11},{4,12},{5,13},{6,14},{7,15},{8,0},{9,1},... | collective-permute-start | bytes 442376 | tf_op jit(solution)/shard_map/ppermute | solution.py:135
  184.0 27.5 %collective-permute-start.48 = (bf16[192,384]{1,0:T(8,128)(2,1)S(1)}, bf16[192,384]{1,0:T(8,128)(2,1)S(1)}, u32[]{:S(2)}, u32[]{:S(2)}) collective-permute-start(bf16[192,384]{1,0:T(8,128)(2,1)S(1)} %get-tuple-element.372), channel_id=1, source_target_pairs={{0,12},{1,13},{2,14},{3,15},{4,0},{5,1},{6,2},{7,3},{8,4},{9,5},{1... | collective-permute-start | bytes 442376 | tf_op jit(solution)/shard_map/ppermute | solution.py:135
  194.1 18.1 %collective-permute-start.44 = (bf16[2,2,48,1920]{3,2,1,0:T(8,128)(2,1)S(1)}, bf16[2,2,48,1920]{3,2,1,0:T(8,128)(2,1)S(1)}, u32[]{:S(2)}, u32[]{:S(2)}) collective-permute-start(bf16[2,2,48,1920]{3,2,1,0:T(8,128)(2,1)S(1)} %fusion), channel_id=1, source_target_pairs={{0,2},{1,3},{2,0},{3,1},{4,6},{5,7},{6,4},{7,5},{8,10},{9,11},{10,... | collective-permute-start | bytes 2211848 | tf_op jit(solution)/shard_map/ppermute | solution.py:120
  195.6 17.4 %collective-permute-start.45 = (bf16[2,2,48,1920]{3,2,1,0:T(8,128)(2,1)S(1)}, bf16[2,2,48,1920]{3,2,1,0:T(8,128)(2,1)S(1)}, u32[]{:S(2)}, u32[]{:S(2)}) collective-permute-start(bf16[2,2,48,1920]{3,2,1,0:T(8,128)(2,1)S(1)} %fusion.1), channel_id=1, source_target_pairs={{0,16},{1,17},{2,18},{3,19},{4,20},{5,21},{6,22},{7,23},{8,24},{9,... | collective-permute-start | bytes 2211848 | tf_op jit(solution)/shard_map/ppermute | solution.py:120
  213.3 8.6 %collective-permute-start.49 = (bf16[2,48,1920]{2,1,0:T(8,128)(2,1)S(1)}, bf16[2,48,1920]{2,1,0:T(8,128)(2,1)S(1)}, u32[]{:S(2)}, u32[]{:S(2)}) collective-permute-start(bf16[2,48,1920]{2,1,0:T(8,128)(2,1)S(1)} %get-tuple-element.309), channel_id=1, source_target_pairs={{0,16},{1,17},{2,18},{3,19},{4,20},{5,21},{6,22},{7,23},{8,24},{9,... | collective-permute-start | bytes 1105928 | tf_op jit(solution)/shard_map/ppermute | solution.py:120
  214.0 8.9 %collective-permute-start.50 = (bf16[2,48,1920]{2,1,0:T(8,128)(2,1)S(1)}, bf16[2,48,1920]{2,1,0:T(8,128)(2,1)S(1)}, u32[]{:S(2)}, u32[]{:S(2)}) collective-permute-start(bf16[2,48,1920]{2,1,0:T(8,128)(2,1)S(1)} %get-tuple-element.310), channel_id=1, source_target_pairs={{0,2},{1,3},{2,0},{3,1},{4,6},{5,7},{6,4},{7,5},{8,10},{9,11},{10,... | collective-permute-start | bytes 1105928 | tf_op jit(solution)/shard_map/ppermute | solution.py:120
  223.2 3.8 %collective-permute-start.51 = (bf16[16,48,1152]{2,1,0:T(8,128)(2,1)S(1)}, bf16[16,48,1152]{2,1,0:T(8,128)(2,1)S(1)}, u32[]{:S(2)}, u32[]{:S(2)}) collective-permute-start(bf16[16,48,1152]{2,1,0:T(8,128)(2,1)S(1)} %get-tuple-element.316), channel_id=1, source_target_pairs={{0,1},{1,0},{2,3},{3,2},{4,5},{5,4},{6,7},{7,6},{8,9},{9,8},{10,11... | collective-permute-start | bytes 5308424 | tf_op jit(solution)/shard_map/ppermute | solution.py:98
  227.2 18.1 %collective-permute-start.52 = (bf16[2,2,48,1152]{3,2,1,0:T(8,128)(2,1)S(1)}, bf16[2,2,48,1152]{3,2,1,0:T(8,128)(2,1)S(1)}, u32[]{:S(2)}, u32[]{:S(2)}) collective-permute-start(bf16[2,2,48,1152]{3,2,1,0:T(8,128)(2,1)S(1)} %fusion.8), channel_id=1, source_target_pairs={{0,2},{1,3},{2,0},{3,1},{4,6},{5,7},{6,4},{7,5},{8,10},{9,11},{10,... | collective-permute-start | bytes 1327112 | tf_op jit(solution)/shard_map/ppermute | solution.py:120
  228.0 17.4 %collective-permute-start.53 = (bf16[2,2,48,1152]{3,2,1,0:T(8,128)(2,1)S(1)}, bf16[2,2,48,1152]{3,2,1,0:T(8,128)(2,1)S(1)}, u32[]{:S(2)}, u32[]{:S(2)}) collective-permute-start(bf16[2,2,48,1152]{3,2,1,0:T(8,128)(2,1)S(1)} %fusion.9), channel_id=1, source_target_pairs={{0,16},{1,17},{2,18},{3,19},{4,20},{5,21},{6,22},{7,23},{8,24},{9,... | collective-permute-start | bytes 1327112 | tf_op jit(solution)/shard_map/ppermute | solution.py:120
  229.4 13.1 %collective-permute-start.54 = (bf16[48,1920]{1,0:T(8,128)(2,1)S(1)}, bf16[48,1920]{1,0:T(8,128)(2,1)S(1)}, u32[]{:S(2)}, u32[]{:S(2)}) collective-permute-start(bf16[48,1920]{1,0:T(8,128)(2,1)S(1)} %get-tuple-element.332), channel_id=1, source_target_pairs={{0,4},{1,5},{2,6},{3,7},{4,8},{5,9},{6,10},{7,11},{8,12},{9,13},{1... | collective-permute-start | bytes 552968 | tf_op jit(solution)/shard_map/ppermute | solution.py:135
  230.3 15.0 %collective-permute-start.55 = (bf16[48,1920]{1,0:T(8,128)(2,1)S(1)}, bf16[48,1920]{1,0:T(8,128)(2,1)S(1)}, u32[]{:S(2)}, u32[]{:S(2)}) collective-permute-start(bf16[48,1920]{1,0:T(8,128)(2,1)S(1)} %get-tuple-element.333), channel_id=1, source_target_pairs={{0,8},{1,9},{2,10},{3,11},{4,12},{5,13},{6,14},{7,15},{8,0},{9,1},... | collective-permute-start | bytes 552968 | tf_op jit(solution)/shard_map/ppermute | solution.py:135
  231.1 14.2 %collective-permute-start.56 = (bf16[48,1920]{1,0:T(8,128)(2,1)S(1)}, bf16[48,1920]{1,0:T(8,128)(2,1)S(1)}, u32[]{:S(2)}, u32[]{:S(2)}) collective-permute-start(bf16[48,1920]{1,0:T(8,128)(2,1)S(1)} %get-tuple-element.334), channel_id=1, source_target_pairs={{0,12},{1,13},{2,14},{3,15},{4,0},{5,1},{6,2},{7,3},{8,4},{9,5},{1... | collective-permute-start | bytes 552968 | tf_op jit(solution)/shard_map/ppermute | solution.py:135
  246.5 7.2 %collective-permute-start.57 = (bf16[2,48,1152]{2,1,0:T(8,128)(2,1)}, bf16[2,48,1152]{2,1,0:T(8,128)(2,1)}, u32[]{:S(2)}, u32[]{:S(2)}) collective-permute-start(bf16[2,48,1152]{2,1,0:T(8,128)(2,1)} %get-tuple-element.381), channel_id=1, source_target_pairs={{0,16},{1,17},{2,18},{3,19},{4,20},{5,21},{6,22},{7,23},{8,24},{9,... | collective-permute-start | bytes 663560 | tf_op jit(solution)/shard_map/ppermute | solution.py:120
  247.3 6.6 %collective-permute-start.58 = (bf16[2,48,1152]{2,1,0:T(8,128)(2,1)}, bf16[2,48,1152]{2,1,0:T(8,128)(2,1)}, u32[]{:S(2)}, u32[]{:S(2)}) collective-permute-start(bf16[2,48,1152]{2,1,0:T(8,128)(2,1)} %get-tuple-element.380), channel_id=1, source_target_pairs={{0,2},{1,3},{2,0},{3,1},{4,6},{5,7},{6,4},{7,5},{8,10},{9,11},{10,... | collective-permute-start | bytes 663560 | tf_op jit(solution)/shard_map/ppermute | solution.py:120
  253.9 21.5 %collective-permute-start.59 = (bf16[512,768]{1,0:T(8,128)(2,1)}, bf16[512,768]{1,0:T(8,128)(2,1)S(1)}, u32[]{:S(2)}, u32[]{:S(2)}) collective-permute-start(bf16[512,768]{1,0:T(8,128)(2,1)} %copy-done.10), channel_id=1, source_target_pairs={{0,16},{16,0},{1,17},{17,1},{2,18},{18,2},{3,19},{19,3},{4,20},{20... | collective-permute-start | bytes 2359304 | tf_op jit(solution)/shard_map/ppermute | solution.py:1039
  257.2 13.1 %collective-permute-start.62 = (bf16[48,1152]{1,0:T(8,128)(2,1)S(1)}, bf16[48,1152]{1,0:T(8,128)(2,1)S(1)}, u32[]{:S(2)}, u32[]{:S(2)}) collective-permute-start(bf16[48,1152]{1,0:T(8,128)(2,1)S(1)} %get-tuple-element.378), channel_id=1, source_target_pairs={{0,12},{1,13},{2,14},{3,15},{4,0},{5,1},{6,2},{7,3},{8,4},{9,5},{1... | collective-permute-start | bytes 331784 | tf_op jit(solution)/shard_map/ppermute | solution.py:135
  260.4 11.1 %collective-permute-start.61 = (bf16[48,1152]{1,0:T(8,128)(2,1)S(1)}, bf16[48,1152]{1,0:T(8,128)(2,1)S(1)}, u32[]{:S(2)}, u32[]{:S(2)}) collective-permute-start(bf16[48,1152]{1,0:T(8,128)(2,1)S(1)} %get-tuple-element.377), channel_id=1, source_target_pairs={{0,8},{1,9},{2,10},{3,11},{4,12},{5,13},{6,14},{7,15},{8,0},{9,1},... | collective-permute-start | bytes 331784 | tf_op jit(solution)/shard_map/ppermute | solution.py:135
  263.2 8.4 %collective-permute-start.60 = (bf16[48,1152]{1,0:T(8,128)(2,1)S(1)}, bf16[48,1152]{1,0:T(8,128)(2,1)S(1)}, u32[]{:S(2)}, u32[]{:S(2)}) collective-permute-start(bf16[48,1152]{1,0:T(8,128)(2,1)S(1)} %get-tuple-element.379), channel_id=1, source_target_pairs={{0,4},{1,5},{2,6},{3,7},{4,8},{5,9},{6,10},{7,11},{8,12},{9,13},{1... | collective-permute-start | bytes 331784 | tf_op jit(solution)/shard_map/ppermute | solution.py:135
  264.4 3.7 %collective-permute-start.65 = (bf16[96,384]{1,0:T(8,128)(2,1)S(1)}, bf16[96,384]{1,0:T(8,128)(2,1)S(1)}, u32[]{:S(2)}, u32[]{:S(2)}) collective-permute-start(bf16[96,384]{1,0:T(8,128)(2,1)S(1)} %dynamic-slice_convert_fusion.1), channel_id=1, source_target_pairs={{0,1},{1,0},{2,3},{3,2},{4,5},{5,4},{6,7},{7,6},{8,9},{9,8},{10,11... | collective-permute-start | bytes 221192 | tf_op jit(solution)/shard_map/ppermute | solution.py:898
  (53 other events, 614.0 us)
